TPU v7x, 128 devices: a whole 4x4x4 slice. The times are simulated.
128 devices in a mesh: expert: 32 (over x, z, core), tensor: 4 (over y).
Axes of the slice: x: 4, y: 4, z: 4, core: 2. Of those that a mesh axis runs over, the one named last changes fastest.
Arguments:
- stream: bfloat16 [8192, 2048], P('expert'), may hold values from -6 to 6
- segment_ids: int32 [32, 256], P('expert'), may hold values from 0 to 3, never falling along the last dimension, each value on 1 to 128 neighbouring positions
- expert_ids: int32 [8192, 6], P('expert'), may hold values from 0 to 63, all different within a row; in each aligned block of 256 rows (0 to 255, 256 to 511, ...) at most 32 rows name the same one
- first_gain: bfloat16 [2048], P('expert'), may hold values from 0.5 to 1.5
- query_proj: bfloat16 [2048, 3072], P('expert', 'tensor'), may hold values from -0.125 to 0.125
- latent_down: bfloat16 [2048, 576], P('expert'), may hold values from -0.125 to 0.125
- latent_gain: bfloat16 [512], P('expert'), may hold values from 0.5 to 1.5
- latent_up: bfloat16 [512, 4096], P('expert', 'tensor'), may hold values from -0.25 to 0.25
- output_proj: bfloat16 [2048, 2048], P('tensor', 'expert'), may hold values from -1 to 1
- second_gain: bfloat16 [2048], P('expert'), may hold values from 0.5 to 1.5
- router_proj: bfloat16 [2048, 64], P('expert'), may hold values from -0.0625 to 0.0625
- shared_gate: bfloat16 [2048, 2816], P('expert', 'tensor'), may hold values from -0.125 to 0.125
- shared_up: bfloat16 [2048, 2816], P('expert', 'tensor'), may hold values from -0.125 to 0.125
- shared_down: bfloat16 [2816, 2048], P('tensor', 'expert'), may hold values from -0.109375 to 0.109375
- expert_gate: bfloat16 [64, 2048, 1408], P('expert', None, 'tensor'), may hold values from -0.125 to 0.125
- expert_up: bfloat16 [64, 2048, 1408], P('expert', None, 'tensor'), may hold values from -0.125 to 0.125
- expert_down: bfloat16 [64, 1408, 2048], P('expert', 'tensor'), may hold values from -1.75 to 1.75
- cotangent: float32 [8192, 2048], P('expert'), may hold values from -6 to 6
Outputs:
- result: float32 [8192, 2048], P('expert')
- stream_grad: float32 [8192, 2048], P('expert')
- first_gain_grad: float32 [2048], P('expert')
- query_proj_grad: float32 [2048, 3072], P('expert', 'tensor')
- latent_down_grad: float32 [2048, 576], P('expert')
- latent_gain_grad: float32 [512], P('expert')
- latent_up_grad: float32 [512, 4096], P('expert', 'tensor')
- output_proj_grad: float32 [2048, 2048], P('tensor', 'expert')
- second_gain_grad: float32 [2048], P('expert')
- router_proj_grad: float32 [2048, 64], P('expert')
- shared_gate_grad: float32 [2048, 2816], P('expert', 'tensor')
- shared_up_grad: float32 [2048, 2816], P('expert', 'tensor')
- shared_down_grad: float32 [2816, 2048], P('tensor', 'expert')
- expert_gate_grad: float32 [64, 2048, 1408], P('expert', None, 'tensor')
- expert_up_grad: float32 [64, 2048, 1408], P('expert', None, 'tensor')
- expert_down_grad: float32 [64, 1408, 2048], P('expert', 'tensor')
Inputs may be any that keep to these rules, and one draw needn't show every extreme that they name: `expert_ids`: each row names 6 different experts. Among the 256 rows of one index of expert no expert is named by more than 32 rows, a bound that some block reaches. `segment_ids`: within a sequence the numbers never fall; a document holds at most 128 tokens, and one holds exactly that many.
All inputs are finite; a program needn't handle non-finite values.
Results may differ from a plain program's by a relative error of at most 0.018.
Values may be sent and summed in bfloat16 or wider, within the bound.
No kernel may reach another device: no remote copies, remote signals or barrier semaphores. Data moves between devices by JAX's collectives and lax.ppermute only.
A program may use at most 320 MiB of HBM per device.

v0:
```python
import math

import jax
import jax.numpy as jnp
from jax import lax
from jax.sharding import PartitionSpec as P

NOPE = 128
ROPE = 64
VDIM = 128
LATENT = 512
TOPK = 6


EPSILON = 1e-06
ROTARY_BASE = 10000.0


def contract(pattern, left, right):
    return jnp.einsum(pattern, left, right, preferred_element_type=jnp.float32)


def rms_scale(values, gain_vector):
    return (
        values
        * lax.rsqrt(jnp.mean(values * values, axis=-1, keepdims=True) + EPSILON)
        * gain_vector
    )


def rotary_tables(length, rotary_width):
    position = jnp.arange(length).astype(jnp.float32)
    exponent = jnp.arange(rotary_width // 2).astype(jnp.float32) * (2.0 / rotary_width)
    frequency = jnp.exp(-math.log(ROTARY_BASE) * exponent)
    angles = position[:, None] * frequency[None, :]
    angles = jnp.concatenate([angles, angles], axis=-1)
    return (jnp.cos(angles), jnp.sin(angles))


def rotate(values, cosine_table, sine_table):
    halfway = values.shape[-1] // 2
    turned = jnp.concatenate([-values[..., halfway:], values[..., :halfway]], axis=-1)
    return values * cosine_table + turned * sine_table


def silu_parts(pre_values):
    sigmoid_value = jax.nn.sigmoid(pre_values)
    return (pre_values * sigmoid_value, sigmoid_value * (1.0 + pre_values * (1.0 - sigmoid_value)))


def per_device(
    stream,
    segment_ids,
    expert_ids,
    first_gain,
    query_proj,
    latent_down,
    latent_gain,
    latent_up,
    output_proj,
    second_gain,
    router_proj,
    shared_gate,
    shared_up,
    shared_down,
    expert_gate,
    expert_up,
    expert_down,
    cotangent,
):
    gathered = (
        lax.all_gather(first_gain, "expert", axis=0, tiled=True),
        lax.all_gather(query_proj, "expert", axis=0, tiled=True),
        lax.all_gather(latent_down, "expert", axis=0, tiled=True),
        lax.all_gather(latent_gain, "expert", axis=0, tiled=True),
        lax.all_gather(latent_up, "expert", axis=0, tiled=True),
        lax.all_gather(output_proj, "expert", axis=1, tiled=True),
        lax.all_gather(second_gain, "expert", axis=0, tiled=True),
        lax.all_gather(router_proj, "expert", axis=0, tiled=True),
        lax.all_gather(shared_gate, "expert", axis=0, tiled=True),
        lax.all_gather(shared_up, "expert", axis=0, tiled=True),
        lax.all_gather(shared_down, "expert", axis=1, tiled=True),
    )
    (
        gain_first,
        proj_query,
        down_latent,
        gain_latent,
        up_latent,
        proj_output,
        gain_second,
        proj_router,
        gate_shared,
        up_shared,
        down_shared,
    ) = gathered
    token_count = stream.shape[0]
    model_width = stream.shape[1]
    query_width = NOPE + ROPE
    local_heads = proj_query.shape[1] // query_width
    score_scale = query_width ** (-0.5)
    residual = stream.astype(jnp.float32)
    normed_first, first_back = jax.vjp(rms_scale, residual, gain_first.astype(jnp.float32))
    normed_low = normed_first.astype(jnp.bfloat16)
    cosine_table, sine_table = rotary_tables(token_count, ROPE)

    def turn_queries(raw_query):
        return jnp.concatenate(
            [
                raw_query[..., :NOPE],
                rotate(raw_query[..., NOPE:], cosine_table[:, None, :], sine_table[:, None, :]),
            ],
            axis=-1,
        )

    def turn_keys(raw_key):
        return rotate(raw_key, cosine_table, sine_table)

    query_raw = jnp.dot(normed_low, proj_query, preferred_element_type=jnp.float32).reshape(
        token_count, local_heads, query_width
    )
    query_turned, query_back = jax.vjp(turn_queries, query_raw)
    queries = query_turned.astype(jnp.bfloat16)
    compressed = jnp.dot(normed_low, down_latent, preferred_element_type=jnp.float32)
    latent_value, latent_back = jax.vjp(
        rms_scale, compressed[:, :LATENT], gain_latent.astype(jnp.float32)
    )
    latent_low = latent_value.astype(jnp.bfloat16)
    key_turned, key_back = jax.vjp(turn_keys, compressed[:, LATENT:])
    key_rope = key_turned.astype(jnp.bfloat16)
    expanded = (
        jnp.dot(latent_low, up_latent, preferred_element_type=jnp.float32)
        .astype(jnp.bfloat16)
        .reshape(token_count, local_heads, NOPE + VDIM)
    )
    key_nope = expanded[..., :NOPE]
    values = expanded[..., NOPE:]
    positions = jnp.arange(token_count)
    segment = segment_ids[0]
    allowed = (segment[:, None] == segment[None, :]) & (positions[None, :] <= positions[:, None])
    raw_scores = contract("thd,uhd->htu", queries[..., :NOPE], key_nope) + contract(
        "thr,ur->htu", queries[..., NOPE:], key_rope
    )
    attention_probs = jax.nn.softmax(
        jnp.where(allowed[None], raw_scores * score_scale, -1e30), axis=-1
    )
    probs_low = attention_probs.astype(jnp.bfloat16)
    attended = (
        contract("htu,uhv->thv", probs_low, values)
        .astype(jnp.bfloat16)
        .reshape(token_count, local_heads * VDIM)
    )
    attention = lax.psum(
        jnp.dot(attended, proj_output, preferred_element_type=jnp.float32), "tensor"
    )
    middle = residual + attention
    normed_second, second_back = jax.vjp(rms_scale, middle, gain_second.astype(jnp.float32))
    mixed_low = normed_second.astype(jnp.bfloat16)
    logits = jnp.dot(mixed_low, proj_router, preferred_element_type=jnp.float32)
    router_probs, router_back = jax.vjp(lambda logit_in: jax.nn.softmax(logit_in, axis=-1), logits)
    gate_values = jnp.take_along_axis(router_probs, expert_ids, axis=1)
    gate_pre = jnp.dot(mixed_low, gate_shared, preferred_element_type=jnp.float32)
    up_pre = jnp.dot(mixed_low, up_shared, preferred_element_type=jnp.float32)
    gate_act, gate_slope = silu_parts(gate_pre)
    hidden_shared = (gate_act * up_pre).astype(jnp.bfloat16)
    shared_part = jnp.dot(hidden_shared, down_shared, preferred_element_type=jnp.float32)
    local_experts = expert_gate.shape[0]
    owners = lax.axis_size("expert")
    experts_all = proj_router.shape[1]
    capacity = token_count * TOPK * 4 // (3 * experts_all)
    slot_count = experts_all * capacity
    routing_flat = expert_ids.reshape(-1)
    onehot = (routing_flat[:, None] == jnp.arange(experts_all)[None, :]).astype(jnp.int32)
    position = jnp.sum((jnp.cumsum(onehot, axis=0) - onehot) * onehot, axis=1)
    slot_index = (
        routing_flat % local_experts * (owners * capacity)
        + routing_flat // local_experts * capacity
        + position
    )
    pair_token = jnp.arange(token_count * TOPK) // TOPK
    slot_token = jnp.full((slot_count,), token_count, jnp.int32).at[slot_index].set(pair_token)
    slot_gate = jnp.zeros((slot_count,), jnp.float32).at[slot_index].set(gate_values.reshape(-1))
    padded = jnp.concatenate([mixed_low, jnp.zeros((1, model_width), jnp.bfloat16)], axis=0)
    outgoing = padded[slot_token].reshape(local_experts, owners * capacity, model_width)
    arriving = lax.all_to_all(outgoing, "expert", split_axis=1, concat_axis=1, tiled=True)
    gate_exp = contract("erd,edf->erf", arriving, expert_gate)
    up_exp = contract("erd,edf->erf", arriving, expert_up)
    gate_exp_act, gate_exp_slope = silu_parts(gate_exp)
    hidden_exp = (gate_exp_act * up_exp).astype(jnp.bfloat16)
    partial_exp = contract("erf,efd->erd", hidden_exp, expert_down)
    returned = lax.all_to_all(partial_exp, "expert", split_axis=1, concat_axis=1, tiled=True)
    picked = returned.reshape(slot_count, model_width)[slot_index].reshape(
        token_count, TOPK, model_width
    )
    routed_full = jnp.sum(gate_values[..., None] * picked, axis=1)
    branch_out = lax.psum(shared_part + routed_full, "tensor")
    result = middle + branch_out
    gate_part = jnp.sum(cotangent[:, None, :] * picked, axis=-1)
    padded_up = jnp.concatenate([cotangent, jnp.zeros((1, model_width), jnp.float32)], axis=0)
    outgoing_grad = (
        (padded_up[slot_token] * slot_gate[:, None])
        .astype(jnp.bfloat16)
        .reshape(local_experts, owners * capacity, model_width)
    )
    arriving_grad = lax.all_to_all(outgoing_grad, "expert", split_axis=1, concat_axis=1, tiled=True)
    expert_down_grad = contract("erf,erd->efd", hidden_exp, arriving_grad)
    hidden_exp_grad = contract("erd,efd->erf", arriving_grad, expert_down)
    gate_rows_grad = (hidden_exp_grad * up_exp * gate_exp_slope).astype(jnp.bfloat16)
    up_rows_grad = (hidden_exp_grad * gate_exp_act).astype(jnp.bfloat16)
    expert_gate_grad = contract("erd,erf->edf", arriving, gate_rows_grad)
    expert_up_grad = contract("erd,erf->edf", arriving, up_rows_grad)
    rows_back = contract("erf,edf->erd", gate_rows_grad, expert_gate) + contract(
        "erf,edf->erd", up_rows_grad, expert_up
    )
    arrived_back = lax.all_to_all(rows_back, "expert", split_axis=1, concat_axis=1, tiled=True)
    routed_back = jnp.sum(
        arrived_back.reshape(slot_count, model_width)[slot_index].reshape(
            token_count, TOPK, model_width
        ),
        axis=1,
    )
    upstream_low = cotangent.astype(jnp.bfloat16)
    shared_down_grad = contract("tf,td->fd", hidden_shared, upstream_low)
    hidden_shared_grad = contract("td,fd->tf", upstream_low, down_shared)
    gate_shared_low = (hidden_shared_grad * up_pre * gate_slope).astype(jnp.bfloat16)
    up_shared_low = (hidden_shared_grad * gate_act).astype(jnp.bfloat16)
    shared_gate_grad = contract("td,tf->df", mixed_low, gate_shared_low)
    shared_up_grad = contract("td,tf->df", mixed_low, up_shared_low)
    mixed_part = (
        contract("tf,df->td", gate_shared_low, gate_shared)
        + contract("tf,df->td", up_shared_low, up_shared)
        + routed_back
    )
    mixed_sum, gate_total = lax.psum((mixed_part, gate_part), "tensor")
    probs_grad = jnp.sum(
        jnp.where(
            expert_ids[..., None] == jnp.arange(experts_all)[None, None, :],
            gate_total[..., None],
            0.0,
        ),
        axis=1,
    )
    (logits_grad,) = router_back(probs_grad)
    logits_low = logits_grad.astype(jnp.bfloat16)
    router_proj_grad = contract("td,te->de", mixed_low, logits_low)
    mixed_grad = mixed_sum + contract("te,de->td", logits_low, proj_router)
    middle_norm_grad, second_gain_grad = second_back(mixed_grad)
    middle_grad = cotangent + middle_norm_grad
    middle_low = middle_grad.astype(jnp.bfloat16)
    output_proj_grad = contract("tv,td->vd", attended, middle_low)
    attended_grad = (
        contract("td,vd->tv", middle_low, proj_output)
        .astype(jnp.bfloat16)
        .reshape(token_count, local_heads, VDIM)
    )
    value_grad = contract("htu,thv->uhv", probs_low, attended_grad)
    probs_att_grad = contract("thv,uhv->htu", attended_grad, values)
    scores_grad = attention_probs * (
        probs_att_grad - jnp.sum(attention_probs * probs_att_grad, axis=-1, keepdims=True)
    )
    raw_low = (scores_grad * score_scale).astype(jnp.bfloat16)
    queries_grad = jnp.concatenate(
        [contract("htu,uhd->thd", raw_low, key_nope), contract("htu,ur->thr", raw_low, key_rope)],
        axis=-1,
    )
    key_nope_grad = contract("htu,thd->uhd", raw_low, queries[..., :NOPE])
    key_rope_grad = contract("htu,thr->ur", raw_low, queries[..., NOPE:])
    (query_raw_grad,) = query_back(queries_grad)
    query_low = query_raw_grad.astype(jnp.bfloat16).reshape(token_count, local_heads * query_width)
    query_proj_grad = contract("td,tq->dq", normed_low, query_low)
    first_part = contract("tq,dq->td", query_low, proj_query)
    expanded_low = (
        jnp.concatenate([key_nope_grad, value_grad], axis=-1)
        .astype(jnp.bfloat16)
        .reshape(token_count, local_heads * (NOPE + VDIM))
    )
    latent_up_grad = contract("tl,tk->lk", latent_low, expanded_low)
    latent_part = contract("tk,lk->tl", expanded_low, up_latent)
    first_sum, latent_sum, rope_sum = lax.psum((first_part, latent_part, key_rope_grad), "tensor")
    latent_pre_grad, latent_gain_grad = latent_back(latent_sum)
    (rope_pre_grad,) = key_back(rope_sum)
    compressed_low = jnp.concatenate([latent_pre_grad, rope_pre_grad], axis=-1).astype(jnp.bfloat16)
    latent_down_grad = contract("td,tc->dc", normed_low, compressed_low)
    first_grad = first_sum + contract("tc,dc->td", compressed_low, down_latent)
    stream_back, first_gain_grad = first_back(first_grad)
    stream_grad = middle_grad + stream_back
    dense_grads = (
        lax.psum_scatter(first_gain_grad, "expert", scatter_dimension=0, tiled=True),
        lax.psum_scatter(query_proj_grad, "expert", scatter_dimension=0, tiled=True),
        lax.psum_scatter(latent_down_grad, "expert", scatter_dimension=0, tiled=True),
        lax.psum_scatter(latent_gain_grad, "expert", scatter_dimension=0, tiled=True),
        lax.psum_scatter(latent_up_grad, "expert", scatter_dimension=0, tiled=True),
        lax.psum_scatter(output_proj_grad, "expert", scatter_dimension=1, tiled=True),
        lax.psum_scatter(second_gain_grad, "expert", scatter_dimension=0, tiled=True),
        lax.psum_scatter(router_proj_grad, "expert", scatter_dimension=0, tiled=True),
        lax.psum_scatter(shared_gate_grad, "expert", scatter_dimension=0, tiled=True),
        lax.psum_scatter(shared_up_grad, "expert", scatter_dimension=0, tiled=True),
        lax.psum_scatter(shared_down_grad, "expert", scatter_dimension=1, tiled=True),
    )
    return (
        result,
        stream_grad,
        dense_grads[0],
        dense_grads[1],
        dense_grads[2],
        dense_grads[3],
        dense_grads[4],
        dense_grads[5],
        dense_grads[6],
        dense_grads[7],
        dense_grads[8],
        dense_grads[9],
        dense_grads[10],
        expert_gate_grad,
        expert_up_grad,
        expert_down_grad,
    )


def solution(mesh):
    placed = (
        P("expert", None),
        P("expert", None),
        P("expert", None),
        P("expert"),
        P("expert", "tensor"),
        P("expert", None),
        P("expert"),
        P("expert", "tensor"),
        P("tensor", "expert"),
        P("expert"),
        P("expert", None),
        P("expert", "tensor"),
        P("expert", "tensor"),
        P("tensor", "expert"),
        P("expert", None, "tensor"),
        P("expert", None, "tensor"),
        P("expert", "tensor", None),
        P("expert", None),
    )
    return jax.shard_map(
        per_device,
        mesh=mesh,
        in_specs=placed,
        out_specs=(
            P("expert", None),
            P("expert", None),
            P("expert"),
            P("expert", "tensor"),
            P("expert", None),
            P("expert"),
            P("expert", "tensor"),
            P("tensor", "expert"),
            P("expert"),
            P("expert", None),
            P("expert", "tensor"),
            P("expert", "tensor"),
            P("tensor", "expert"),
            P("expert", None, "tensor"),
            P("expert", None, "tensor"),
            P("expert", "tensor", None),
        ),
        check_vma=False,
    )
```

profile of v0, /device:TPU:0, one launch (start us, length us, event | category | flops | bytes accessed | tf_op | source)
XLA Modules:
  0.0 2231.2 jit_solution(10908595985883163919)
XLA Ops:
  17.3 70.7 %all-reduce.16 = (bf16[2048]{0:T(1024)(128)(2,1)S(1)}, bf16[512]{0:T(512)(128)(2,1)S(1)}, bf16[2048]{0:T(1024)(128)(2,1)S(1)}) all-reduce(bf16[2048]{0:T(1024)(128)(2,1)S(1)} %dynamic-update-slice, bf16[512]{0:T(512)(128)(2,1)S(1)} %dynamic-update-slice.1, ...), channel_id=1, replica_groups=mesh['expert'=32,'tensor'=4] {'expert'}, use_global_device_ids=true, to_apply=%add.8 | all-reduce | flops 4608 | bytes 18432
  93.7 8.2 all-gather.10.cloned.1.call-done
  112.2 36.3 %all-gather.12.cloned.1.call-done = bf16[2048,768]{1,0:T(8,128)(2,1)} async-done(((bf16[64,768]{1,0:T(8,128)(2,1)}), bf16[2048,768]{1,0:T(8,128)(2,1)}) %all-gather.12.cloned.1.call-update) | async-done | bytes 3145744 | tf_op jit(solution)/shard_map/all_gather | solution.py:73
  148.5 3.7 fusion.107
  157.7 36.2 %all-gather.14.cloned.1.call-done = bf16[512,2048]{0,1:T(8,128)(2,1)} async-done(((bf16[512,64]{0,1:T(8,128)(2,1)}), bf16[512,2048]{0,1:T(8,128)(2,1)}) %all-gather.14.cloned.1.call-update) | async-done | bytes 2097168 | tf_op jit(solution)/shard_map/all_gather | solution.py:77
  193.9 3.7 fusion.119
  199.1 31.5 %reduce-window.6 = s32[64,12,128]{2,1,0:T(8,128)S(1)} reduce-window(s32[64,12,128]{2,1,0:T(8,128)} %fusion.57, s32[]{:T(128)} %constant.85.clone.1), window={size=1x1x128 pad=0_0x0_0x127_0}, to_apply=%region_8.9 | reduce-window | flops 12484608 | bytes 786436 | tf_op jit(solution)/shard_map/reduce-window
  233.5 6.4 scatter_custom_fusion
  239.9 15.9 all-reduce.21.cloned.1.call-done
  261.7 17.7 gather_fusion
  279.4 16.4 copy.252
  295.8 7.4 all-to-all-start
  306.6 18.2 gather_fusion.2
  324.8 117.5 %all_gather.43 = bf16[2048,64]{1,0:T(8,128)(2,1)S(1)} all-gather(bf16[64,64]{1,0:T(8,128)(2,1)S(1)} %copy-done.77), channel_id=1, replica_groups=mesh['expert'=32,'tensor'=4] {'expert'}, dimensions={0}, use_global_device_ids=true | all-gather | bytes 270336 | tf_op jit(solution)/shard_map/all_gather | solution.py:79
  445.4 12.7 gather_fusion.4
  458.7 6.2 scatter_custom_fusion.1
  464.9 6.5 multiply_convert_fusion
  471.4 24.9 %copy.258 = bf16[2,1024,2048]{2,0,1:T(2,128)(2,1)} copy(bf16[2,1024,2048]{2,1,0:T(8,128)(2,1)S(1)} %multiply_convert_fusion) | data formatting | bytes 16777216 | tf_op jit(solution)/shard_map/convert_element_type | solution.py:202
  496.3 7.3 all-to-all-start.2
  503.6 12.1 fusion.10
  515.8 11.3 fusion.12
  527.1 90.0 %all-to-all-done.2 = bf16[2,1024,2048]{2,0,1:T(2,128)(2,1)} async-done(((bf16[2,1024,2048]{2,0,1:T(2,128)(2,1)}), bf16[2,1024,2048]{2,0,1:T(2,128)(2,1)}, u32[]{:S(2)}, u32[]{:S(2)}) %all-to-all-start.2) | async-done | bytes 8388640 | tf_op jit(solution)/shard_map/all_to_all | solution.py:205
  617.1 14.4 multiply_convert_fusion.1
  631.5 13.1 fusion.124
  644.6 11.7 convolution_add_fusion
  656.3 28.6 %copy.260 = f32[2,1024,2048]{2,0,1:T(2,128)} copy(f32[2,1024,2048]{2,1,0:T(8,128)} %convolution_add_fusion) | data formatting | bytes 33554432 | tf_op jit(solution)/shard_map/add | solution.py:212
  684.9 16.3 all-to-all-start.3
  701.8 6.0 fusion.122
  707.8 21.4 copy.255
  729.2 212.6 %all-to-all-done.3 = f32[2,1024,2048]{2,0,1:T(2,128)} async-done(((f32[2,1024,2048]{2,0,1:T(2,128)}), f32[2,1024,2048]{2,0,1:T(2,128)}, u32[]{:S(2)}, u32[]{:S(2)}) %all-to-all-start.3) | async-done | bytes 16777248 | tf_op jit(solution)/shard_map/all_to_all | solution.py:215
  941.8 36.4 %all-to-all-start.1 = ((f32[2,1024,2048]{2,0,1:T(2,128)}), f32[2,1024,2048]{2,0,1:T(2,128)}, u32[]{:S(2)}, u32[]{:S(2)}) async-start(f32[2,1024,2048]{2,0,1:T(2,128)} %copy.255), calls=%async_computation.1 | async-start | bytes 33554432 | tf_op jit(solution)/shard_map/all_to_all | solution.py:191
  983.2 209.8 %all-gather.18.cloned.1.call-done = bf16[2048,704]{1,0:T(8,128)(2,1)} async-done(((bf16[64,704]{1,0:T(8,128)(2,1)}), bf16[2048,704]{1,0:T(8,128)(2,1)}) %all-gather.18.cloned.1.call-update) | async-done | bytes 2883600 | tf_op jit(solution)/shard_map/all_gather | solution.py:81
  1193.1 4.0 fusion.121
  1197.1 44.5 %all-gather.20.cloned.1.call-done = bf16[704,2048]{0,1:T(8,128)(2,1)} async-done(((bf16[704,64]{0,1:T(8,128)(2,1)}), bf16[704,2048]{0,1:T(8,128)(2,1)}) %all-gather.20.cloned.1.call-update) | async-done | bytes 2883600 | tf_op jit(solution)/shard_map/all_gather | solution.py:82
  1241.6 4.3 multiply_convert_fusion.5
  1247.0 17.7 copy.261
  1264.7 18.3 gather_fusion.3
  1283.0 15.0 reshape.431
  1298.0 9.8 reduce_sum.200
  1307.8 4.9 fusion.15
  1312.9 18.2 copy.256
  1331.0 18.4 gather_fusion.1
  1349.5 15.3 reshape.429
  1364.8 12.0 multiply_reduce_fusion
  1376.8 18.5 psum.52
  1395.6 5.1 convolution_add_fusion.3
  1424.9 3.7 fusion.128
  1429.6 3.6 fusion.129
  1434.2 5.3 fusion.49
  1443.2 3.6 fusion.46
  1448.2 3.7 fusion.105
  1452.3 72.6 %all-reduce.25.cloned.1.call-done = (f32[256,2048]{1,0:T(8,128)}, f32[256,2048]{1,0:T(8,128)}, f32[256,64]{0,1:T(8,128)}, f32[256,512]{0,1:T(8,128)}) async-done(((f32[256,2048]{1,0:T(8,128)}, f32[256,2048]{1,0:T(8,128)}, f32[256,64]{0,1:T(8,128)}, f32[256,512]{0,1:T(8,128)}), (f32[256,2048]{1,0:T(8,128)}, f32[256,2048]{1,0:T(8,128)}, f32[256,64]{0,1:T(8,128)}, ...) | async-done | bytes 4784144 | tf_op jit(solution)/shard_map/psum | solution.py:196
  1529.3 3.4 fusion.69
  1534.2 15.7 fusion.2
  1549.9 16.1 fusion.6
  1565.9 16.0 fusion.8
  1584.7 128.7 %all-reduce.14 = (f32[2048]{0:T(1024)S(1)}, f32[512]{0:T(512)S(1)}, f32[2048]{0:T(1024)S(1)}) all-reduce(f32[2048]{0:T(1024)S(1)} %get-tuple-element.20, f32[512]{0:T(512)S(1)} %get-tuple-element.22, f32[2048]{0:T(1024)S(1)} %get-tuple-element.18), channel_id=2, replica_groups=mesh['expert'=32,'tensor'=4] {'expert'}, use_global_device_ids=true, to_apply=%region_29.30.clone | all-reduce | flops 4608 | bytes 36864
  1714.5 4.0 add.217
  1721.1 75.1 %reduce-scatter.23.cloned.1.call-done = f32[704,64]{0,1:T(8,128)} async-done(((f32[704,2048]{0,1:T(8,128)}), f32[704,64]{0,1:T(8,128)}) %reduce-scatter.23.cloned.1.call-update) | async-done | bytes 180240 | tf_op jit(solution)/shard_map/reduce_scatter | solution.py:298
  1796.1 80.8 %reduce-scatter.17.cloned.1.call-done = f32[64,64]{1,0:T(8,128)} async-done(((f32[2048,64]{1,0:T(8,128)}), f32[64,64]{1,0:T(8,128)}) %reduce-scatter.17.cloned.1.call-update) | async-done | bytes 16400 | tf_op jit(solution)/shard_map/reduce_scatter | solution.py:295
  1876.9 82.6 %reduce-scatter.13.cloned.1.call-done = f32[16,1024]{1,0:T(8,128)} async-done(((f32[512,1024]{1,0:T(8,128)}), f32[16,1024]{1,0:T(8,128)}) %reduce-scatter.13.cloned.1.call-update) | async-done | bytes 65552 | tf_op jit(solution)/shard_map/reduce_scatter | solution.py:292
  1959.6 85.8 %reduce-scatter.15.cloned.1.call-done = f32[512,64]{0,1:T(8,128)} async-done(((f32[512,2048]{0,1:T(8,128)}), f32[512,64]{0,1:T(8,128)}) %reduce-scatter.15.cloned.1.call-update) | async-done | bytes 131088 | tf_op jit(solution)/shard_map/reduce_scatter | solution.py:293
  2045.4 89.8 %reduce-scatter.9.cloned.1.call-done = f32[64,768]{1,0:T(8,128)} async-done(((f32[2048,768]{1,0:T(8,128)}), f32[64,768]{1,0:T(8,128)}) %reduce-scatter.9.cloned.1.call-update) | async-done | bytes 196624 | tf_op jit(solution)/shard_map/reduce_scatter | solution.py:289
  2135.3 88.7 %reduce-scatter.11.cloned.1.call-done = f32[64,576]{1,0:T(8,128)} async-done(((f32[2048,576]{1,0:T(8,128)}), f32[64,576]{1,0:T(8,128)}) %reduce-scatter.11.cloned.1.call-update) | async-done | bytes 147472 | tf_op jit(solution)/shard_map/reduce_scatter | solution.py:290
  (321 shorter events, 96.2 us)
Async XLA Ops:
  7.2 609.9 %copy-start = (bf16[2,352,2048]{2,1,0:T(8,128)(2,1)S(1)}, bf16[2,352,2048]{2,1,0:T(8,128)(2,1)}, u32[]{:S(2)}) copy-start(bf16[2,352,2048]{2,1,0:T(8,128)(2,1)} %param.34) | copy-start | bytes 8650756
  7.2 83.1 %all-gather.8.cloned.1.call-start = ((), (), s32[]{:S(2)}) async-start(), calls=%async_computation.12 | async-start | bytes 2703360 | tf_op jit(solution)/shard_map/all_gather | solution.py:74
  7.9 93.9 %all-gather.10.cloned.1.call-start = ((), (), s32[]{:S(2)}) async-start(), calls=%async_computation.13 | async-start | bytes 1081344 | tf_op jit(solution)/shard_map/all_gather | solution.py:76
  8.7 139.8 %all-gather.12.cloned.1.call-start = ((), (), s32[]{:S(2)}) async-start(), calls=%async_computation.14 | async-start | bytes 3244032 | tf_op jit(solution)/shard_map/all_gather | solution.py:73
  9.4 184.5 %all-gather.14.cloned.1.call-start = ((), (), s32[]{:S(2)}) async-start(), calls=%async_computation.15 | async-start | bytes 2162688 | tf_op jit(solution)/shard_map/all_gather | solution.py:77
  10.0 245.8 %all-reduce.21.cloned.1.call-start = ((), (), s32[]{:S(2)}) async-start(), calls=%async_computation.16 | async-start | bytes 4194304 | tf_op jit(solution)/shard_map/psum | solution.py:153
  12.1 136.4 %copy-start.69 = (f32[256]{0:T(256)}, f32[256]{0:T(256)S(1)}, u32[]{:S(2)}) copy-start(f32[256]{0:T(256)S(1)} %fusion.90) | copy-start | bytes 3076
  88.1 60.5 %copy-start.51 = (f32[2048]{0:T(1024)}, f32[2048]{0:T(1024)S(1)}, u32[]{:S(2)}) copy-start(f32[2048]{0:T(1024)S(1)} %convert_element_type.109) | copy-start | bytes 24580
  88.1 16.3 copy-start.67
  93.5 58.7 %copy-start.14 = (f32[256,576]{0,1:T(8,128)}, f32[256,576]{0,1:T(8,128)S(1)}, u32[]{:S(2)}) copy-start(f32[256,576]{0,1:T(8,128)S(1)} %fusion.109) | copy-start | bytes 1769476
  93.6 16.8 copy-start.82
  93.6 16.8 copy-start.71
  112.2 40.1 %copy-start.53 = (f32[256,64]{0,1:T(8,128)}, f32[256,64]{0,1:T(8,128)S(1)}, u32[]{:S(2)}) copy-start(f32[256,64]{0,1:T(8,128)S(1)} %get-tuple-element.52) | copy-start | bytes 196612
  155.7 41.9 %copy-start.86 = (f32[4,256]{1,0:T(4,128)}, f32[4,256]{1,0:T(4,128)S(1)}, u32[]{:S(2)}) copy-start(f32[4,256]{1,0:T(4,128)S(1)} %get-tuple-element.57) | copy-start | bytes 12292
  157.7 39.9 %copy-start.32 = (bf16[4,128,256]{2,1,0:T(8,128)(2,1)}, bf16[4,128,256]{2,1,0:T(8,128)(2,1)S(1)}, u32[]{:S(2)}) copy-start(bf16[4,128,256]{2,1,0:T(8,128)(2,1)S(1)} %convolution_convert_fusion.4) | copy-start | bytes 786436
  198.2 59.8 %copy-start.65 = (f32[2048]{0:T(1024)}, f32[2048]{0:T(1024)S(1)}, u32[]{:S(2)}) copy-start(f32[2048]{0:T(1024)S(1)} %convert_element_type.120) | copy-start | bytes 24580
  258.0 21.3 copy-start.84
  258.1 21.3 copy-start.78
  295.8 200.5 %all-to-all-start = ((bf16[2,1024,2048]{2,0,1:T(2,128)(2,1)}), bf16[2,1024,2048]{2,0,1:T(2,128)(2,1)}, u32[]{:S(2)}, u32[]{:S(2)}) async-start(bf16[2,1024,2048]{2,0,1:T(2,128)(2,1)} %copy.252), calls=%async_computation | async-start | bytes 16777216 | tf_op jit(solution)/shard_map/all_to_all | solution.py:185
  306.6 18.2 copy-start.77
  458.5 12.9 copy-start.45
  496.3 120.8 %all-to-all-start.2 = ((bf16[2,1024,2048]{2,0,1:T(2,128)(2,1)}), bf16[2,1024,2048]{2,0,1:T(2,128)(2,1)}, u32[]{:S(2)}, u32[]{:S(2)}) async-start(bf16[2,1024,2048]{2,0,1:T(2,128)(2,1)} %copy.258), calls=%async_computation.2 | async-start | bytes 16777216 | tf_op jit(solution)/shard_map/all_to_all | solution.py:205
  503.6 12.2 copy-start.26
  631.5 13.1 copy-start.35
  631.5 13.1 copy-start.27
  684.9 256.9 %all-to-all-start.3 = ((f32[2,1024,2048]{2,0,1:T(2,128)}), f32[2,1024,2048]{2,0,1:T(2,128)}, u32[]{:S(2)}, u32[]{:S(2)}) async-start(f32[2,1024,2048]{2,0,1:T(2,128)} %copy.260), calls=%async_computation.3 | async-start | bytes 33554432 | tf_op jit(solution)/shard_map/all_to_all | solution.py:215
  701.2 278.8 %all-gather.16.cloned.1.call-start = ((), (), s32[]{:S(2)}) async-start(), calls=%async_computation.17 | async-start | bytes 3244032 | tf_op jit(solution)/shard_map/all_gather | solution.py:80
  729.2 250.8 %copy-start.7 = (bf16[256,2048]{1,0:T(8,128)(2,1)S(1)}, bf16[256,2048]{1,0:T(8,128)(2,1)}, u32[]{:S(2)}) copy-start(bf16[256,2048]{1,0:T(8,128)(2,1)} %copy-done.6) | copy-start | bytes 3145732
  941.8 371.1 %all-to-all-start.1 = ((f32[2,1024,2048]{2,0,1:T(2,128)}), f32[2,1024,2048]{2,0,1:T(2,128)}, u32[]{:S(2)}, u32[]{:S(2)}) async-start(f32[2,1024,2048]{2,0,1:T(2,128)} %copy.255), calls=%async_computation.1 | async-start | bytes 33554432 | tf_op jit(solution)/shard_map/all_to_all | solution.py:191
  978.2 214.8 %all-gather.18.cloned.1.call-start = ((), (), s32[]{:S(2)}) async-start(), calls=%async_computation.18 | async-start | bytes 3244032 | tf_op jit(solution)/shard_map/all_gather | solution.py:81
  979.0 262.6 %all-gather.20.cloned.1.call-start = ((), (), s32[]{:S(2)}) async-start(), calls=%async_computation.19 | async-start | bytes 3244032 | tf_op jit(solution)/shard_map/all_gather | solution.py:82
  979.7 420.9 %all-reduce.23.cloned.1.call-start = ((), (), s32[]{:S(2)}) async-start(), calls=%async_computation.20 | async-start | bytes 4194304 | tf_op jit(solution)/shard_map/psum | solution.py:234
  1245.9 18.8 copy-start.41
  1245.9 62.0 %copy-start.37 = (bf16[256,704]{0,1:T(8,128)(2,1)}, bf16[256,704]{0,1:T(8,128)(2,1)S(1)}, u32[]{:S(2)}) copy-start(bf16[256,704]{0,1:T(8,128)(2,1)S(1)} %get-tuple-element.39) | copy-start | bytes 1081348
  1245.9 149.6 %copy-start.29 = (bf16[256,704]{0,1:T(8,128)(2,1)}, bf16[256,704]{0,1:T(8,128)(2,1)S(1)}, u32[]{:S(2)}) copy-start(bf16[256,704]{0,1:T(8,128)(2,1)S(1)} %get-tuple-element.41) | copy-start | bytes 1081348
  1307.8 5.0 copy-start.76
  1312.8 212.1 %all-reduce.25.cloned.1.call-start = ((), (), s32[]{:S(2)}) async-start(), calls=%async_computation.29 | async-start | bytes 9568256 | tf_op jit(solution)/shard_map/psum | solution.py:196
  1349.5 15.3 copy-start.12
  1349.5 15.3 copy-start.46
  1364.8 30.5 %copy-start.64 = (s32[256,6]{0,1:T(8,128)S(1)}, s32[256,6]{0,1:T(8,128)}, u32[]{:S(2)}) copy-start(s32[256,6]{0,1:T(8,128)} %param.20) | copy-start | bytes 18436
  1364.8 30.6 %copy-start.34 = (f32[256,64]{0,1:T(8,128)S(1)}, f32[256,64]{0,1:T(8,128)}, u32[]{:S(2)}) copy-start(f32[256,64]{0,1:T(8,128)} %copy-done.33) | copy-start | bytes 196612
  1364.8 30.6 %copy-start.74 = (f32[256]{0:T(256)S(1)}, f32[256]{0:T(256)}, u32[]{:S(2)}) copy-start(f32[256]{0:T(256)} %copy-done.73) | copy-start | bytes 3076
  1395.5 5.1 copy-start.5
  1395.5 5.1 copy-start.19
  1395.5 5.1 copy-start.66
  1395.5 5.1 copy-start.79
  1423.7 297.4 %reduce-scatter.19.cloned.1.call-start = ((), (), s32[]{:S(2)}) async-start(), calls=%async_computation.26 | async-start | bytes 6488064 | tf_op jit(solution)/shard_map/reduce_scatter | solution.py:296
  1428.7 292.4 %reduce-scatter.21.cloned.1.call-start = ((), (), s32[]{:S(2)}) async-start(), calls=%async_computation.27 | async-start | bytes 6488064 | tf_op jit(solution)/shard_map/reduce_scatter | solution.py:297
  1433.3 362.9 %reduce-scatter.23.cloned.1.call-start = ((), (), s32[]{:S(2)}) async-start(), calls=%async_computation.28 | async-start | bytes 6488064 | tf_op jit(solution)/shard_map/reduce_scatter | solution.py:298
  1439.6 437.3 %reduce-scatter.17.cloned.1.call-start = ((), (), s32[]{:S(2)}) async-start(), calls=%async_computation.25 | async-start | bytes 1081344 | tf_op jit(solution)/shard_map/reduce_scatter | solution.py:295
  1441.2 518.4 %reduce-scatter.13.cloned.1.call-start = ((), (), s32[]{:S(2)}) async-start(), calls=%async_computation.23 | async-start | bytes 2162688 | tf_op jit(solution)/shard_map/reduce_scatter | solution.py:292
  1443.2 602.3 %reduce-scatter.15.cloned.1.call-start = ((), (), s32[]{:S(2)}) async-start(), calls=%async_computation.24 | async-start | bytes 4325376 | tf_op jit(solution)/shard_map/reduce_scatter | solution.py:293
  1446.9 688.4 %reduce-scatter.9.cloned.1.call-start = ((), (), s32[]{:S(2)}) async-start(), calls=%async_computation.21 | async-start | bytes 6488064 | tf_op jit(solution)/shard_map/reduce_scatter | solution.py:289
  1452.0 74.2 %copy-start.83 = (f32[256]{0:T(256)S(1)}, f32[256]{0:T(256)}, u32[]{:S(2)}) copy-start(f32[256]{0:T(256)} %copy-done.82) | copy-start | bytes 3076
  1452.0 74.2 %copy-start.55 = (f32[256,32]{0,1:T(8,128)S(1)}, f32[256,32]{0,1:T(8,128)}, u32[]{:S(2)}) copy-start(f32[256,32]{0,1:T(8,128)} %broadcast_multiply_fusion.1) | copy-start | bytes 98308
  1452.0 772.0 %reduce-scatter.11.cloned.1.call-start = ((), (), s32[]{:S(2)}) async-start(), calls=%async_computation.22 | async-start | bytes 5406720 | tf_op jit(solution)/shard_map/reduce_scatter | solution.py:290
  1534.2 15.7 copy-start.39
  1549.9 16.1 copy-start.36
  1565.9 16.0 copy-start.28
  1565.9 16.0 copy-start.31
  1714.5 4.7 copy-start.3
  1714.5 4.7 copy-start.11
  1714.5 4.7 copy-start.16
  1719.1 504.8 %copy-start.1 = (bf16[2,352,2048]{2,1,0:T(8,128)(2,1)S(1)}, bf16[2,352,2048]{2,1,0:T(8,128)(2,1)}, u32[]{:S(2)}) copy-start(bf16[2,352,2048]{2,1,0:T(8,128)(2,1)} %param.34) | copy-start | bytes 8650756
  (46 other events, 90.3 us)
Sparse Core Ops, SparseCore 0:
  10.3 47.0 all-gather.7
  59.6 42.1 all-gather.9
  104.1 44.4 all-gather.11
  150.6 43.2 all-gather.13
  197.8 58.0 all-reduce.20
  704.3 192.0 all-gather.15
  981.6 211.4 all-gather.17
  1195.6 46.0 all-gather.19
  1312.9 58.2 all-reduce.22
  1423.8 101.0 all-reduce.24
  1529.7 86.1 reduce-scatter.18
  1620.0 85.7 reduce-scatter.20
  1710.6 85.5 reduce-scatter.22
  1800.1 76.8 reduce-scatter.16
  1881.3 78.2 reduce-scatter.12
  1964.1 81.2 reduce-scatter.14
  2049.6 85.6 reduce-scatter.8
  2139.9 84.0 reduce-scatter.10
where the time goes:
time: 2240 us; the launch traced here: 2230 us
  waiting for transfers between devices  1230 us (55%)
  blocking collectives  335 us (15%)
  local copies, waits for them, and re-layouts  287 us (13%)
  matrix products  205 us (9%)
  other arithmetic  82.8 us (4%)
  starting transfers between devices  68.5 us (3%)
    all_to_all x1, waiting for transfers between devices, per_device(): lax.all_to_all(rows_back, 'expert', split_axis=1, concat_axis=1, tiled=True)  213 us
    all_gather x1, waiting for transfers between devices, per_device(): lax.all_gather(shared_up, 'expert', axis=0, tiled=True)  210 us
    unnamed x2, blocking collectives  199 us
    dot_general x34, matrix products, contract(): return jnp.einsum(pattern, left, right, preferred_element_type=jnp.float32)  178 us
    all_gather x1, blocking collectives, per_device(): lax.all_gather(router_proj, 'expert', axis=0, tiled=True)  117 us
    all_to_all x1, waiting for transfers between devices, per_device(): lax.all_to_all(outgoing_grad, 'expert', split_axis=1, concat_axis=1, tile...  90 us
    reduce_scatter x1, waiting for transfers between devices, per_device(): lax.psum_scatter(query_proj_grad, 'expert', scatter_dimension=0, tiled=True)  89.8 us
    reduce_scatter x1, waiting for transfers between devices, per_device(): lax.psum_scatter(latent_down_grad, 'expert', scatter_dimension=0, tiled=T...  88.7 us
  transfers between devices with their start and end apart: 22, of which 15 were waited for; matrix products, arithmetic and copies ran while one was open for 19% of the time, Pallas kernels for 0%

commit v1 on v0

v1 whole, which is shorter than its diff:
```python
import functools
import math

import jax
import jax.numpy as jnp
from jax import lax
from jax.experimental import pallas as pl
from jax.experimental.pallas import tpu as pltpu
from jax.sharding import PartitionSpec as P

NOPE = 128
ROPE = 64
VDIM = 128
LATENT = 512
TOPK = 6
EPSILON = 1e-06
ROTARY_BASE = 10000.0

BF16 = jnp.bfloat16
F32 = jnp.float32
VMEM_BYTES = 60 * 1024 * 1024
LANES = 128
COST_SCALE = 10


def dot_nn(left, right):
    return lax.dot_general(left, right, (((1,), (0,)), ((), ())), preferred_element_type=F32)


def dot_nt(left, right):
    return lax.dot_general(left, right, (((1,), (1,)), ((), ())), preferred_element_type=F32)


def dot_tn(left, right):
    return lax.dot_general(left, right, (((0,), (0,)), ((), ())), preferred_element_type=F32)


def silu_parts(pre_values):
    sigmoid_value = 1.0 / (1.0 + jnp.exp(-pre_values))
    return (pre_values * sigmoid_value, sigmoid_value * (1.0 + pre_values * (1.0 - sigmoid_value)))


def inverse_rms(values):
    return lax.rsqrt(jnp.mean(values * values, axis=-1, keepdims=True) + EPSILON)


def rms_back(values, scale, gain, grad):
    normed = values * scale
    weighted = grad * gain
    return (
        scale * (weighted - normed * jnp.mean(weighted * normed, axis=-1, keepdims=True)),
        grad * normed,
    )


def turned(values):
    width = values.shape[1]
    lane = lax.broadcasted_iota(jnp.int32, values.shape, 1) % ROPE
    half = ROPE // 2
    return jnp.where(
        lane < half, pltpu.roll(values, width - half, 1), pltpu.roll(values, half, 1)
    )


def rotated(values, cosine, sine):
    return values * cosine + turned(values) * sine


def block_at(me, step, count, width):
    return pl.ds(pl.multiple_of(lax.rem(me + step, count) * width, width), width)


def run(kernel, outs, args, flops, scratch=(), name=None, places=None, aliases=None, out_places=None):
    places = places or {}
    out_places = out_places or {}
    in_specs = [pl.BlockSpec(memory_space=places.get(i, pltpu.VMEM)) for i in range(len(args))]
    out_specs = [pl.BlockSpec(memory_space=out_places.get(i, pltpu.VMEM)) for i in range(len(outs))]
    moved = sum(a.size * a.dtype.itemsize for a in args) + sum(
        math.prod(shape) * jnp.dtype(dtype).itemsize for shape, dtype in outs
    )
    return pl.pallas_call(
        kernel,
        in_specs=in_specs,
        out_specs=out_specs,
        out_shape=[jax.ShapeDtypeStruct(shape, dtype) for shape, dtype in outs],
        scratch_shapes=list(scratch),
        input_output_aliases=aliases or {},
        compiler_params=pltpu.CompilerParams(vmem_limit_bytes=VMEM_BYTES),
        cost_estimate=pl.CostEstimate(
            flops=flops // COST_SCALE, bytes_accessed=moved // COST_SCALE, transcendentals=0
        ),
        name=name,
    )(*args)


def routing_kernel(me_ref, ids_ref, cot_ref, t0_ref, t1_ref, low_ref, out_ref):
    choices, tokens = ids_ref.shape
    owners, local, capacity, piece = out_ref.shape
    experts = owners * local
    rows = owners * capacity
    expert = lax.broadcasted_iota(jnp.int32, (experts, tokens), 0)
    chosen = jnp.zeros((experts, tokens), F32)
    for choice in range(choices):
        chosen += jnp.where(ids_ref[choice : choice + 1, :] == expert, 1.0, 0.0)
    before = jnp.where(
        lax.broadcasted_iota(jnp.int32, (tokens, tokens), 0)
        < lax.broadcasted_iota(jnp.int32, (tokens, tokens), 1),
        1.0,
        0.0,
    ).astype(BF16)
    place = dot_nn(chosen.astype(BF16), before)
    place = jnp.where(chosen > 0.5, place, -1.0).astype(BF16)
    low = cot_ref[...].astype(BF16)
    low_ref[...] = low
    mine = cot_ref[:, block_at(me_ref[0], 0, cot_ref.shape[1] // piece, piece)].astype(BF16)
    slot = (lax.broadcasted_iota(jnp.int32, (tokens, rows), 1) % capacity).astype(F32)
    for index, t_ref in ((0, t0_ref), (1, t1_ref)):
        spread = jnp.where(
            lax.broadcasted_iota(jnp.int32, (experts, rows), 0)
            == lax.broadcasted_iota(jnp.int32, (experts, rows), 1) // capacity * local + index,
            1.0,
            0.0,
        ).astype(BF16)
        wanted = dot_tn(place, spread)
        matrix = jnp.where(wanted == slot, 1.0, 0.0).astype(BF16)
        t_ref[...] = matrix
        out_ref[:, index] = dot_tn(matrix, mine).astype(BF16).reshape(owners, capacity, piece)


def attend_kernel(
    me_ref,
    stream_ref,
    w_ref,
    seg_row_ref,
    seg_col_ref,
    cos_ref,
    sin_ref,
    own_ref,
    send1_ref,
    send2_ref,
    send3_ref,
    normed_ref,
    query_ref,
    expanded_ref,
    key_ref,
    latent_ref,
    compressed_ref,
    probs_ref,
    attended_ref,
    gains_ref,
    latent_gain_ref,
):
    heads, tokens, _ = probs_ref.shape
    width = stream_ref.shape[1]
    piece = own_ref.shape[1]
    nope = heads * NOPE
    queries = nope + heads * ROPE
    edge = queries + LATENT + LANES
    outer = edge + heads * VDIM
    owners = 32
    columns = jnp.concatenate(
        [w_ref[:, outer + 2 * NOPE :].astype(F32), jnp.zeros((width, ROPE), F32)], axis=1
    )
    gains = columns.T[:8, :]
    gains_ref[...] = gains
    shard = width // owners
    short = LATENT // owners
    latent_gain = (
        columns.reshape(owners, shard, LANES)[:, :short, :].reshape(LATENT, LANES).T[:8, :]
    )
    latent_gain_ref[...] = latent_gain
    stream = stream_ref[...].astype(F32)
    normed = (stream * inverse_rms(stream) * gains[0:1, :]).astype(BF16)
    normed_ref[...] = normed
    projected = dot_nn(normed, w_ref[:, :edge])
    query_ref[:, :nope] = projected[:, :nope].astype(BF16)
    query_ref[:, nope:] = rotated(projected[:, nope:queries], cos_ref[...], sin_ref[...]).astype(BF16)
    compressed = projected[:, queries : queries + LATENT]
    compressed_ref[...] = compressed
    latent = (compressed * inverse_rms(compressed) * latent_gain[2:3, :]).astype(BF16)
    latent_ref[...] = latent
    raw_key = projected[:, queries + LATENT : edge]
    key = rotated(raw_key, cos_ref[:, :LANES], sin_ref[:, :LANES])
    lane = lax.broadcasted_iota(jnp.int32, key.shape, 1)
    key = jnp.where(lane < ROPE, key, 0.0)
    key_low = key.astype(BF16)
    key_odd = pltpu.roll(key, ROPE, 1).astype(BF16)
    key_ref[...] = key_low
    row = lax.broadcasted_iota(jnp.int32, (tokens, tokens), 0)
    column = lax.broadcasted_iota(jnp.int32, (tokens, tokens), 1)
    allowed = (seg_col_ref[...] == seg_row_ref[...]) & (column <= row)
    scale = (NOPE + ROPE) ** (-0.5)
    for head in range(heads):
        block = slice(head * 2 * NOPE, (head + 1) * 2 * NOPE)
        up = w_ref[:, outer : outer + 2 * NOPE].reshape(owners, heads, short, 2 * NOPE)[:, head]
        up = up.reshape(LATENT, 2 * NOPE)
        expanded = dot_nn(latent, up).astype(BF16)
        expanded_ref[:, block] = expanded
        pair = nope + head // 2 * LANES
        raw = dot_nt(query_ref[:, head * NOPE : (head + 1) * NOPE], expanded[:, :NOPE]) + dot_nt(
            query_ref[:, pair : pair + LANES], key_odd if head % 2 else key_low
        )
        scores = jnp.where(allowed, raw * scale, -1e30)
        weight = jnp.exp(scores - jnp.max(scores, axis=-1, keepdims=True))
        probs = weight / jnp.sum(weight, axis=-1, keepdims=True)
        probs_ref[head] = probs
        attended_ref[:, head * VDIM : (head + 1) * VDIM] = dot_nn(
            probs.astype(BF16), expanded[:, NOPE:]
        ).astype(BF16)
    attended = attended_ref[...]
    for step, out_ref in enumerate((own_ref, send1_ref, send2_ref, send3_ref)):
        part = dot_nt(attended, w_ref[block_at(me_ref[0], step, width // piece, piece), edge:outer])
        out_ref[...] = part.astype(out_ref.dtype)


def dispatch_kernel(
    me_ref, stream_ref, a0_ref, a1_ref, a2_ref, a3_ref, gains_ref, t0_ref, t1_ref, middle_ref, mixed_ref, out_ref
):
    piece = a0_ref.shape[1]
    width = stream_ref.shape[1]
    count = width // piece
    owners, capacity, _ = out_ref.shape
    for step, a_ref in enumerate((a0_ref, a1_ref, a2_ref, a3_ref)):
        place = block_at(me_ref[0], step, count, piece)
        middle_ref[:, place] = stream_ref[:, place].astype(F32) + a_ref[...].astype(F32)
    middle = middle_ref[...]
    mixed = (middle * inverse_rms(middle) * gains_ref[1:2, :]).astype(BF16)
    mixed_ref[...] = mixed
    mine = mixed_ref[:, block_at(me_ref[0], 0, count, piece)]
    out_ref[:, :, width:] = dot_tn(t1_ref[...], mine).astype(BF16).reshape(owners, capacity, piece)
    out_ref[:, :, :width] = dot_tn(t0_ref[...], mixed).astype(BF16).reshape(owners, capacity, width)


def shared_kernel(
    me_ref,
    mixed_ref,
    cot_ref,
    w_ref,
    router_ref,
    own_ref,
    send1_ref,
    send2_ref,
    send3_ref,
    back_ref,
    probs_ref,
    grads_ref,
):
    width = mixed_ref.shape[1]
    piece = own_ref.shape[1]
    hidden_columns = w_ref.shape[1] // 3
    mixed = mixed_ref[...]
    cot = cot_ref[...]
    pre = dot_nn(mixed, w_ref[:, : 2 * hidden_columns])
    gate_pre, up_pre = pre[:, :hidden_columns], pre[:, hidden_columns:]
    act, slope = silu_parts(gate_pre)
    hidden = (act * up_pre).astype(BF16)
    hidden_grad = dot_nn(cot, w_ref[:, 2 * hidden_columns :])
    pair = jnp.concatenate([hidden_grad * up_pre * slope, hidden_grad * act], axis=1).astype(BF16)
    grads_ref[:, : 2 * hidden_columns] = dot_tn(mixed, pair).astype(BF16)
    grads_ref[:, 2 * hidden_columns :] = dot_tn(cot, hidden).astype(BF16)
    back_ref[...] = dot_nt(pair, w_ref[:, : 2 * hidden_columns])
    logits = dot_nn(mixed, router_ref[...])
    lane = lax.broadcasted_iota(jnp.int32, logits.shape, 1)
    logits = jnp.where(lane >= ROPE, logits, -1e30)
    weight = jnp.exp(logits - jnp.max(logits, axis=-1, keepdims=True))
    probs_ref[...] = weight / jnp.sum(weight, axis=-1, keepdims=True)
    for step, out_ref in enumerate((own_ref, send1_ref, send2_ref, send3_ref)):
        place = block_at(me_ref[0], step, width // piece, piece)
        part = dot_nt(hidden, w_ref[place, 2 * hidden_columns :])
        out_ref[...] = part.astype(out_ref.dtype)


def expert_back_kernel(split, *refs):
    if split:
        me_ref, base_ref, x0_ref, x1_ref, x2_ref, x3_ref = refs[:6]
        refs = refs[6:]
    else:
        me_ref, base_ref, x_ref = refs[:3]
        refs = refs[3:]
    c0_ref, c1_ref, c2_ref, c3_ref, wg_ref, wu_ref, wd_ref, router_ref = refs[:8]
    refs = refs[8:]
    if split:
        back_ref, c_ref, hg_ref, gr_ref, ur_ref, x_ref, wide_ref, down_ref, tall_ref = refs
    else:
        back_ref, c_ref, hg_ref, gr_ref, ur_ref, wide_ref, down_ref, tall_ref = refs
    sources, capacity, width = c_ref.shape
    rows = sources * capacity
    piece = c0_ref.shape[-1]
    count = width // piece
    hidden_columns = wd_ref.shape[1]
    padded = down_ref.shape[1]
    me = me_ref[0]

    @pl.when(pl.program_id(0) == 0)
    def _():
        rest = jnp.zeros((padded - hidden_columns, width), BF16)
        gate_up = jnp.concatenate([wg_ref[0], rest, wu_ref[0], rest], axis=0)
        tall_ref[...] = gate_up
        wide_ref[...] = gate_up.T
        down_ref[...] = jnp.concatenate([wd_ref[0], rest], axis=0).T

    for step, p_ref in enumerate((c0_ref, c1_ref, c2_ref, c3_ref)):
        c_ref[:, :, block_at(me, step, count, piece)] = p_ref[:, 0]
    if split:
        for step, p_ref in enumerate((x0_ref, x1_ref, x2_ref, x3_ref)):
            x_ref[:, :, block_at(me, step, count, piece)] = p_ref[...]
    x = x_ref[...].reshape(rows, width)
    expert = base_ref[0] + (1 if split else 0) + ROPE
    logits = dot_nn(x, router_ref[...])
    lane = lax.broadcasted_iota(jnp.int32, logits.shape, 1)
    logits = jnp.where(lane >= ROPE, logits, -1e30)
    weight = jnp.exp(logits - jnp.max(logits, axis=-1, keepdims=True))
    gate = jnp.sum(jnp.where(lane == expert, weight, 0.0), axis=-1, keepdims=True) / jnp.sum(
        weight, axis=-1, keepdims=True
    )
    pre = dot_nn(x, wide_ref[...])
    gate_pre, up_pre = pre[:, :padded], pre[:, padded:]
    hidden_cot = dot_nn(c_ref[...].reshape(rows, width), down_ref[...])
    act, slope = silu_parts(gate_pre)
    hidden = (act * up_pre).astype(BF16).astype(F32)
    gate_grad = jnp.sum(hidden * hidden_cot, axis=-1, keepdims=True)
    hidden_grad = gate * hidden_cot
    gate_rows = (hidden_grad * up_pre * slope).astype(BF16)
    up_rows = (hidden_grad * act).astype(BF16)
    hg_ref[...] = (gate * hidden).astype(BF16)[:, :hidden_columns]
    gr_ref[...] = gate_rows[:, :hidden_columns]
    ur_ref[...] = up_rows[:, :hidden_columns]
    high = gate_grad.astype(BF16).astype(F32)
    low = gate_grad - high
    beside = jnp.where(lane == 0, high, 0.0) + jnp.where(lane == 1, low, 0.0)
    back = dot_nn(jnp.concatenate([gate_rows, up_rows], axis=1), tall_ref[...])
    back_ref[:, :, :width] = back.astype(BF16).reshape(sources, capacity, width)
    back_ref[:, :, width:] = beside.astype(BF16).reshape(sources, capacity, LANES)


def expert_back(split, me, base, xs, cs, wg, wu, wd, router, router_at, chunk):
    owners, local, capacity, piece = cs[0].shape
    hidden, width = wg.shape[1:]
    local_index = 1 if split else 0
    rows = owners * capacity
    padded = -(-hidden // LANES) * LANES
    scalar = pl.BlockSpec(memory_space=pltpu.SMEM)
    row_spec = pl.BlockSpec((chunk * capacity, hidden), lambda c: (c, 0))
    row_shape = jax.ShapeDtypeStruct((rows, hidden), BF16)
    wide_spec = pl.BlockSpec((chunk, capacity, width), lambda c: (c, 0, 0))
    wide_shape = jax.ShapeDtypeStruct((owners, capacity, width), BF16)
    narrow_spec = pl.BlockSpec((chunk, capacity, piece), lambda c: (c, 0, 0))
    own_spec = pl.BlockSpec((chunk, capacity, piece), lambda c: (c, 0, width // piece))
    cot_spec = pl.BlockSpec((chunk, 1, capacity, piece), lambda c: (c, local_index, 0, 0))
    weight_spec = pl.BlockSpec((1, hidden, width), lambda c: (local_index, 0, 0))
    in_specs = [scalar, scalar]
    in_specs += [own_spec] + [narrow_spec] * 3 if split else [wide_spec]
    in_specs += [cot_spec] * 4 + [weight_spec] * 3 + [pl.BlockSpec((width, LANES), lambda c: (0, router_at))]
    out_specs = [pl.BlockSpec((chunk, capacity, width + LANES), lambda c: (c, 0, 0)), wide_spec]
    out_shape = [jax.ShapeDtypeStruct((owners, capacity, width + LANES), BF16), wide_shape]
    last_spec, last_shape = ([wide_spec], [wide_shape]) if split else ([], [])
    return pl.pallas_call(
        functools.partial(expert_back_kernel, split),
        grid=(owners // chunk,),
        in_specs=in_specs,
        out_specs=out_specs + [row_spec] * 3 + last_spec,
        out_shape=out_shape + [row_shape] * 3 + last_shape,
        scratch_shapes=[
            pltpu.VMEM((width, 2 * padded), BF16),
            pltpu.VMEM((width, padded), BF16),
            pltpu.VMEM((2 * padded, width), BF16),
        ],
        compiler_params=pltpu.CompilerParams(vmem_limit_bytes=VMEM_BYTES),
        cost_estimate=pl.CostEstimate(
            flops=100 * rows * hidden * width, bytes_accessed=24 * 1024 * 1024, transcendentals=0
        ),
        name="expert_back",
    )(me, base, *xs, *cs, wg, wu, wd, router)


def expert_out_kernel(hg_ref, wd_ref, out_ref):
    pieces, sources, capacity, piece = out_ref.shape
    out = dot_nn(hg_ref[...], wd_ref[0]).astype(BF16)
    for index in range(pieces):
        out_ref[index] = out[:, index * piece : (index + 1) * piece].reshape(sources, capacity, piece)


def expert_out(expert, hg, wd, owners, pieces, chunk):
    rows, hidden = hg.shape
    width = wd.shape[2]
    capacity = rows // owners
    piece = width // pieces
    return pl.pallas_call(
        expert_out_kernel,
        grid=(owners // chunk,),
        in_specs=[
            pl.BlockSpec((chunk * capacity, hidden), lambda c: (c, 0)),
            pl.BlockSpec((1, hidden, width), lambda c: (expert, 0, 0)),
        ],
        out_specs=pl.BlockSpec((pieces, chunk, capacity, piece), lambda c: (0, c, 0, 0)),
        out_shape=jax.ShapeDtypeStruct((pieces, owners, capacity, piece), BF16),
        compiler_params=pltpu.CompilerParams(vmem_limit_bytes=VMEM_BYTES),
        cost_estimate=pl.CostEstimate(
            flops=rows * hidden * width // 5, bytes_accessed=6 * 1024 * 102, transcendentals=0
        ),
        name="expert_out",
    )(hg, wd)


def expert_grads_kernel(
    x0_ref, c0_ref, hg0_ref, gr0_ref, ur0_ref, x1_ref, c1_ref, hg1_ref, gr1_ref, ur1_ref, dg_ref, du_ref, dd_ref
):
    owners, capacity, piece = x0_ref.shape
    rows = owners * capacity

    def step(x_ref, c_ref, hg_ref, gr_ref, ur_ref):
        x = x_ref[...].reshape(rows, piece)
        dg_ref[0] = dot_tn(gr_ref[...], x)
        du_ref[0] = dot_tn(ur_ref[...], x)
        dd_ref[0] = dot_tn(hg_ref[...], c_ref[...].reshape(rows, piece))

    pl.when(pl.program_id(0) == 0)(lambda: step(x0_ref, c0_ref, hg0_ref, gr0_ref, ur0_ref))
    pl.when(pl.program_id(0) == 1)(lambda: step(x1_ref, c1_ref, hg1_ref, gr1_ref, ur1_ref))


def expert_grads(first, second, pieces):
    owners, capacity, width = first[1].shape
    rows, hidden = first[2].shape
    piece = width // pieces
    row_spec = pl.BlockSpec((rows, hidden), lambda e, j: (0, 0))

    def specs(expert):
        stay = 0 if expert else pieces - 1
        wide = pl.BlockSpec(
            (owners, capacity, piece), lambda e, j: (0, 0, jnp.where(e == expert, j, stay))
        )
        return [wide, wide, row_spec, row_spec, row_spec]

    out_spec = pl.BlockSpec((1, hidden, piece), lambda e, j: (e, 0, j))
    out_shape = jax.ShapeDtypeStruct((2, hidden, width), F32)
    return pl.pallas_call(
        expert_grads_kernel,
        grid=(2, pieces),
        in_specs=specs(0) + specs(1),
        out_specs=[out_spec] * 3,
        out_shape=[out_shape] * 3,
        compiler_params=pltpu.CompilerParams(vmem_limit_bytes=VMEM_BYTES),
        cost_estimate=pl.CostEstimate(
            flops=rows * hidden * width, bytes_accessed=40 * 1024 * 102, transcendentals=0
        ),
        name="expert_grads",
    )(*first, *second)


def combine_kernel(
    me_ref, t0_ref, t1_ref, b0_ref, b1_ref, shared_ref, own_ref, probs_ref, send1_ref, send2_ref, send3_ref
):
    owners, capacity, _ = b0_ref.shape
    rows = owners * capacity
    width = shared_ref.shape[1]
    piece = own_ref.shape[1]
    me = me_ref[0]
    t0, t1 = t0_ref[...], t1_ref[...]
    lane = lax.broadcasted_iota(jnp.int32, (rows, LANES), 1)
    owner = lax.broadcasted_iota(jnp.int32, (rows, LANES), 0) // capacity
    spreads = []
    for index, b_ref in ((0, b0_ref), (1, b1_ref)):
        beside = b_ref[:, :, width:].reshape(rows, LANES).astype(F32)
        expert = 2 * owner + index
        spreads.append(
            (
                jnp.where(lane == expert + ROPE, beside[:, 0:1], 0.0)
                + jnp.where(lane == expert, beside[:, 1:2], 0.0)
            ).astype(BF16)
        )
    probs = dot_nn(t0, spreads[0]) + dot_nn(t1, spreads[1])
    probs = probs + pltpu.roll(probs, ROPE, 1)
    probs_ref[...] = probs
    high = probs.astype(BF16)
    low = (probs - high.astype(F32)).astype(BF16)
    short = lax.broadcasted_iota(jnp.int32, probs.shape, 1)
    message = jnp.where(short >= ROPE, high.astype(F32), low.astype(F32)).astype(BF16)
    for step, out_ref in enumerate((own_ref, send1_ref, send2_ref, send3_ref)):
        place = block_at(me, step, width // piece, piece)
        part = (
            dot_nn(t0, b0_ref[:, :, place].reshape(rows, piece))
            + dot_nn(t1, b1_ref[:, :, place].reshape(rows, piece))
            + shared_ref[:, place]
        )
        if step == 0:
            own_ref[...] = part
        else:
            out_ref[:, :piece] = part.astype(BF16)
            out_ref[:, piece:] = message


def attend_back_kernel(
    me_ref,
    core_ref,
    stream_ref,
    cot_ref,
    middle_ref,
    a0_ref,
    a1_ref,
    a2_ref,
    a3_ref,
    r1_ref,
    r2_ref,
    r3_ref,
    probs_own_ref,
    router_probs_ref,
    w_ref,
    router_ref,
    mixed_ref,
    normed_ref,
    query_ref,
    expanded_ref,
    key_ref,
    latent_ref,
    compressed_ref,
    probs_ref,
    attended_ref,
    gains_ref,
    latent_gain_ref,
    cos_ref,
    sin_ref,
    keep_ref,
    pass_ref,
    middle_grad_ref,
    own_ref,
    send1_ref,
    send2_ref,
    send3_ref,
    scr_ref,
    low_ref,
    wide_ref,
    sems,
):
    heads, tokens, _ = probs_ref.shape
    width = stream_ref.shape[1]
    piece = own_ref.shape[1]
    nope = heads * NOPE
    queries = nope + heads * ROPE
    edge = queries + LATENT + LANES
    outer = edge + heads * VDIM
    owners = 32
    shard = width // owners
    short = LATENT // owners
    count = width // piece
    me = me_ref[0]
    probs_grad = probs_own_ref[...]
    for r_ref in (r1_ref, r2_ref, r3_ref):
        other = r_ref[:, piece:].astype(F32)
        probs_grad = probs_grad + other + pltpu.roll(other, ROPE, 1)
    router_probs = router_probs_ref[...]
    logits_low = (
        router_probs * (probs_grad - jnp.sum(router_probs * probs_grad, axis=-1, keepdims=True))
    ).astype(BF16)
    router_back = dot_nt(logits_low, router_ref[...])
    for step, a_ref in enumerate((a0_ref, a1_ref, a2_ref, a3_ref)):
        wide_ref[:, block_at(me, step, count, piece)] = a_ref[...].astype(F32)
    mixed_grad = wide_ref[...] + router_back
    middle = middle_ref[...]
    norm_grad, second_gain_rows = rms_back(middle, inverse_rms(middle), gains_ref[1:2, :], mixed_grad)
    second_gain_grad = jnp.sum(second_gain_rows, axis=0, keepdims=True)
    middle_grad = cot_ref[...] + norm_grad
    middle_grad_ref[...] = middle_grad
    middle_low = middle_grad.astype(BF16)
    attended_grad = dot_nn(middle_low, w_ref[:, edge:outer]).astype(BF16)
    scale = (NOPE + ROPE) ** (-0.5)
    key_low = key_ref[...]
    key_odd = pltpu.roll(key_low.astype(F32), ROPE, 1).astype(BF16)
    latent = latent_ref[...]
    latent_part = jnp.zeros((tokens, LATENT), F32)
    key_even_grad = jnp.zeros((tokens, LANES), F32)
    key_odd_grad = jnp.zeros((tokens, LANES), F32)
    rope_grads = []
    grads4 = scr_ref.reshape(owners, shard, scr_ref.shape[1])
    for head in range(heads):
        pair = nope + head // 2 * LANES
        expanded = expanded_ref[:, head * 2 * NOPE : (head + 1) * 2 * NOPE]
        probs = probs_ref[head]
        head_grad = attended_grad[:, head * VDIM : (head + 1) * VDIM]
        value_grad = dot_tn(probs.astype(BF16), head_grad)
        probs_att = dot_nt(head_grad, expanded[:, NOPE:])
        scores = probs * (probs_att - jnp.sum(probs * probs_att, axis=-1, keepdims=True))
        raw_low = (scores * scale).astype(BF16)
        low_ref[:, head * NOPE : (head + 1) * NOPE] = dot_nn(raw_low, expanded[:, :NOPE]).astype(BF16)
        turn_grad = dot_nn(raw_low, key_odd if head % 2 else key_low)
        if head % 2:
            rope_grads[-1] = rope_grads[-1] + turn_grad
            key_odd_grad += dot_tn(raw_low, query_ref[:, pair : pair + LANES])
        else:
            rope_grads.append(turn_grad)
            key_even_grad += dot_tn(raw_low, query_ref[:, pair : pair + LANES])
        key_grad = dot_tn(raw_low, query_ref[:, head * NOPE : (head + 1) * NOPE])
        expanded_low = jnp.concatenate([key_grad, value_grad], axis=1).astype(BF16)
        up = w_ref[:, outer : outer + 2 * NOPE].reshape(owners, heads, short, 2 * NOPE)[:, head]
        up = up.reshape(LATENT, 2 * NOPE)
        latent_part += dot_nt(expanded_low, up)
        grads4[:, head * short : (head + 1) * short, outer : outer + 2 * NOPE] = (
            dot_tn(latent, expanded_low).astype(BF16).reshape(owners, short, 2 * NOPE)
        )
    rope_grad = jnp.concatenate(rope_grads, axis=1)
    low_ref[:, nope:queries] = rotated(rope_grad, cos_ref[...], -sin_ref[...]).astype(BF16)
    compressed = compressed_ref[...]
    latent_grad, latent_gain_rows = rms_back(
        compressed, inverse_rms(compressed), latent_gain_ref[2:3, :], latent_part
    )
    latent_gain_grad = jnp.sum(latent_gain_rows, axis=0, keepdims=True)
    low_ref[:, queries : queries + LATENT] = latent_grad.astype(BF16)
    lane = lax.broadcasted_iota(jnp.int32, (tokens, LANES), 1)
    key_grad = jnp.where(lane < ROPE, key_even_grad + pltpu.roll(key_odd_grad, ROPE, 1), 0.0)
    key_grad = rotated(key_grad, cos_ref[:, :LANES], -sin_ref[:, :LANES])
    low_ref[:, queries + LATENT : edge] = jnp.where(lane < ROPE, key_grad, 0.0).astype(BF16)
    low = low_ref[...]
    for step, out_ref in enumerate((own_ref, send1_ref, send2_ref, send3_ref)):
        place = block_at(me, step, count, piece)
        part = dot_nt(low, w_ref[place, :edge])
        wide_ref[:, place] = part
        out_ref[...] = part.astype(out_ref.dtype)
    stream = stream_ref[...].astype(F32)
    first_gain_grad = jnp.sum(wide_ref[...] * (stream * inverse_rms(stream)), axis=0, keepdims=True)
    late = dot_tn(normed_ref[...], low[:, queries:])
    sub = lax.broadcasted_iota(jnp.int32, (LANES, width), 0)
    gain_columns = (
        jnp.where(sub == ROPE, first_gain_grad, 0.0)
        + jnp.where(sub == ROPE + 1, second_gain_grad * (1.0 / count), 0.0)
    ).T
    key_columns = (late[:, LATENT:] + gain_columns).reshape(owners, shard, LANES)
    sub = lax.broadcasted_iota(jnp.int32, (LANES, LATENT), 0)
    latent_columns = jnp.where(sub == ROPE + 2, latent_gain_grad, 0.0).T.reshape(owners, short, LANES)
    grads4[:, :, queries : queries + LATENT] = (
        late[:, :LATENT].astype(BF16).reshape(owners, shard, LATENT)
    )
    grads4[:, :, queries + LATENT : edge] = key_columns.astype(BF16)
    grads4[:, :short, queries + LATENT : edge] = (key_columns[:, :short] + latent_columns).astype(BF16)
    scr_ref[:, edge:outer] = dot_tn(middle_low, attended_ref[...]).astype(BF16)
    scr_ref[:, :queries] = dot_tn(normed_ref[...], low[:, :queries]).astype(BF16)
    router_grad = dot_tn(mixed_ref[...], logits_low)
    scr_ref[:, outer + 2 * NOPE :] = router_grad[:, ROPE:].astype(BF16)
    halves = scr_ref.reshape(owners // 2, 2, shard, scr_ref.shape[1])
    core = core_ref[0]
    first = pltpu.make_async_copy(halves.at[:, 1 - core], pass_ref, sems.at[0])
    second = pltpu.make_async_copy(halves.at[:, core], keep_ref, sems.at[1])
    first.start()
    second.start()
    first.wait()
    second.wait()


def unpack_kernel(parts_ref, query_ref, late_ref, output_ref, up_ref, router_ref):
    heads = up_ref.shape[1] // (2 * NOPE)
    short = up_ref.shape[0]
    nope = heads * NOPE
    queries = nope + heads * ROPE
    edge = queries + LATENT + LANES
    outer = edge + heads * VDIM
    total = jnp.sum(parts_ref[...].astype(F32), axis=0)
    for head in range(heads):
        start = head * (NOPE + ROPE)
        query_ref[:, start : start + NOPE] = total[:, head * NOPE : (head + 1) * NOPE]
        query_ref[:, start + NOPE : start + NOPE + ROPE] = total[
            :, nope + head * ROPE : nope + (head + 1) * ROPE
        ]
        up_ref[:, head * 2 * NOPE : (head + 1) * 2 * NOPE] = total[
            head * short : (head + 1) * short, outer : outer + 2 * NOPE
        ]
    late_ref[...] = total[:, queries:edge]
    output_ref[...] = total[:, edge:outer]
    router_ref[...] = total[:, outer + 2 * NOPE :]


def late_kernel(own_ref, r1_ref, r2_ref, r3_ref, down_ref, gains_ref):
    total = own_ref[...] + r1_ref[...] + r2_ref[...] + r3_ref[...]
    down_ref[...] = total[:, : down_ref.shape[1]]
    columns = total[:, LATENT:]
    columns = jnp.concatenate([columns, jnp.zeros(columns.shape, F32)], axis=0)
    gains_ref[...] = columns.T[ROPE : ROPE + 8, :]


def stream_kernel(me_ref, middle_grad_ref, stream_ref, gains_ref, a0_ref, a1_ref, a2_ref, a3_ref, out_ref, wide_ref):
    piece = a0_ref.shape[1]
    count = stream_ref.shape[1] // piece
    for step, a_ref in enumerate((a0_ref, a1_ref, a2_ref, a3_ref)):
        wide_ref[:, block_at(me_ref[0], step, count, piece)] = a_ref[...].astype(F32)
    stream = stream_ref[...].astype(F32)
    norm_grad, _ = rms_back(stream, inverse_rms(stream), gains_ref[0:1, :], wide_ref[...])
    out_ref[...] = middle_grad_ref[...] + norm_grad


def routed_kernel(t0_ref, t1_ref, o_ref, own_ref, r1_ref, r2_ref, r3_ref, out_ref):
    owners, _, capacity, piece = o_ref.shape
    rows = owners * capacity
    total = own_ref[...]
    for r_ref in (r1_ref, r2_ref, r3_ref):
        total = total + r_ref[...].astype(F32)
    for index, t_ref in ((0, t0_ref), (1, t1_ref)):
        total = total + dot_nn(t_ref[...], o_ref[:, index].reshape(rows, piece))
    out_ref[...] = total.astype(BF16)


def result_kernel(me_ref, middle_ref, a0_ref, a1_ref, a2_ref, a3_ref, out_ref):
    piece = a0_ref.shape[1]
    count = middle_ref.shape[1] // piece
    for step, a_ref in enumerate((a0_ref, a1_ref, a2_ref, a3_ref)):
        place = block_at(me_ref[0], step, count, piece)
        out_ref[:, place] = middle_ref[:, place] + a_ref[...].astype(F32)


def shift(array, step):
    size = lax.axis_size("tensor")
    return lax.ppermute(array, "tensor", [(i, (i + step) % size) for i in range(size)])


def send_blocks(sends):
    return [shift(array, step + 1) for step, array in enumerate(sends)]


def share_small(low):
    size = lax.axis_size("tensor")
    return [low] + [shift(low, size - step) for step in range(1, size)]


def ring_first(rows):
    return shift(rows, 1), shift(rows, lax.axis_size("tensor") - 1)


def ring_second(rows, before, after):
    half = rows.shape[0] // 2
    across = [shift(before[:half], 1), shift(after[half:], lax.axis_size("tensor") - 1)]
    return [rows, after, jnp.concatenate(across, axis=0), before]


def after(array, *others):
    return lax.optimization_barrier((array, *others))[0]


def exchange(rows):
    shape = rows.shape
    return lax.all_to_all(
        rows.reshape(shape[0], -1, shape[-1]), "expert", split_axis=0, concat_axis=0, tiled=True
    ).reshape(shape)


def per_device(
    stream,
    segment_ids,
    expert_ids,
    first_gain,
    query_proj,
    latent_down,
    latent_gain,
    latent_up,
    output_proj,
    second_gain,
    router_proj,
    shared_gate,
    shared_up,
    shared_down,
    expert_gate,
    expert_up,
    expert_down,
    cotangent,
):
    tokens, width = stream.shape
    owners = lax.axis_size("expert")
    tensors = lax.axis_size("tensor")
    shard = query_proj.shape[0]
    heads = query_proj.shape[1] // (NOPE + ROPE)
    short = latent_up.shape[0]
    experts = router_proj.shape[1]
    hidden_columns = shared_gate.shape[1]
    local, _, expert_hidden = expert_gate.shape
    capacity = tokens * TOPK * 4 // (3 * experts)
    rows = owners * capacity
    piece = width // tensors
    nope = heads * NOPE
    queries = nope + heads * ROPE
    edge = queries + LATENT + LANES
    outer = edge + heads * VDIM
    me = lax.axis_index("tensor").astype(jnp.int32).reshape(1)
    base = (lax.axis_index("expert") * local).astype(jnp.int32).reshape(1)
    core = lax.rem(lax.axis_index("expert"), 2).astype(jnp.int32).reshape(1)
    smem = {0: pltpu.SMEM}

    gains = jnp.concatenate(
        [
            first_gain[:, None],
            second_gain[:, None],
            jnp.pad(latent_gain, (0, shard - short))[:, None],
            jnp.zeros((shard, ROPE - 3), BF16),
        ],
        axis=1,
    )
    by_head = query_proj.reshape(shard, heads, NOPE + ROPE)
    pack_one = jnp.concatenate(
        [
            by_head[:, :, :NOPE].reshape(shard, nope),
            by_head[:, :, NOPE:].reshape(shard, heads * ROPE),
            latent_down,
            router_proj,
            output_proj.T,
            latent_up.reshape(short, heads, 2 * NOPE).transpose(1, 0, 2).reshape(shard, 2 * NOPE),
            gains,
        ],
        axis=1,
    )
    pack_two = jnp.concatenate([shared_gate, shared_up, shared_down.T], axis=1)
    one = lax.all_gather(pack_one, "expert", axis=0, tiled=True)
    two = lax.all_gather(pack_two, "expert", axis=0, tiled=True)

    position = jnp.arange(tokens).astype(F32)
    exponent = jnp.arange(ROPE // 2).astype(F32) * (2.0 / ROPE)
    angles = position[:, None] * jnp.exp(-math.log(ROTARY_BASE) * exponent)[None, :]
    cosine = jnp.tile(jnp.cos(angles), (1, 2 * heads))
    sine = jnp.sin(angles)
    sine = jnp.tile(jnp.concatenate([-sine, sine], axis=1), (1, heads))

    t0, t1, cot_low, cot_out = run(
        routing_kernel,
        [
            ((tokens, rows), BF16),
            ((tokens, rows), BF16),
            ((tokens, width), BF16),
            ((owners, local, capacity, piece), BF16),
        ],
        [me, expert_ids.T, cotangent],
        2 * local * tokens * rows * (piece + experts),
        places=smem,
        name="routing",
    )

    cot_own = exchange(cot_out)
    cot_before, cot_after = ring_first(cot_own)
    (
        own,
        send1,
        send2,
        send3,
        normed,
        query,
        expanded,
        key,
        latent,
        compressed,
        probs,
        attended,
        gain_rows,
        latent_gain_rows,
    ) = run(
        attend_kernel,
        [
            ((tokens, piece), F32),
            ((tokens, piece), BF16),
            ((tokens, piece), BF16),
            ((tokens, piece), BF16),
            ((tokens, width), BF16),
            ((tokens, queries), BF16),
            ((tokens, heads * 2 * NOPE), BF16),
            ((tokens, LANES), BF16),
            ((tokens, LATENT), BF16),
            ((tokens, LATENT), F32),
            ((heads, tokens, tokens), F32),
            ((tokens, heads * VDIM), BF16),
            ((8, width), F32),
            ((8, LATENT), F32),
        ],
        [after(me, cot_own), stream, one, segment_ids, segment_ids.T, cosine, sine],
        2 * tokens * width * outer,
        places=smem,
        name="attend",
    )
    got = send_blocks([send1, send2, send3])
    attention = (own + got[0].astype(F32) + got[1].astype(F32) + got[2].astype(F32)).astype(BF16)
    attention = after(attention, cot_before, cot_after)
    middle, mixed, x_out = run(
        dispatch_kernel,
        [
            ((tokens, width), F32),
            ((tokens, width), BF16),
            ((owners, capacity, width + piece), BF16),
        ],
        [me, stream, *share_small(attention), gain_rows, t0, t1],
        2 * tokens * rows * (width + piece),
        places=smem,
        name="dispatch",
    )
    x_in = exchange(x_out)
    cots = ring_second(cot_own, cot_before, cot_after)
    x1s = x_in[:, :, width:]
    x1_before, x1_after = ring_first(x1s)
    x1s = [x_in] + ring_second(x1s, x1_before, x1_after)[1:]
    router_block = one[:, queries + LATENT : edge]
    (
        shared_own,
        shared1,
        shared2,
        shared3,
        shared_back,
        router_probs,
        shared_grads,
    ) = run(
        shared_kernel,
        [
            ((tokens, piece), F32),
            ((tokens, piece), BF16),
            ((tokens, piece), BF16),
            ((tokens, piece), BF16),
            ((tokens, width), F32),
            ((tokens, LANES), F32),
            ((width, 3 * hidden_columns), BF16),
        ],
        [me, mixed, cot_low, two, router_block],
        18 * tokens * width * hidden_columns,
        places=smem,
        name="shared",
    )
    base = after(base, shared_back)

    gate_t = expert_gate.transpose(0, 2, 1)
    up_t = expert_up.transpose(0, 2, 1)
    chunk = owners // 2
    back0, c0, hg0, gr0, ur0 = expert_back(
        False, me, base, [x_in], cots, gate_t, up_t, expert_down, one, edge // LANES - 1, chunk // 2
    )
    back0 = exchange(back0)
    back1, c1, hg1, gr1, ur1, x1 = expert_back(
        True, me, after(base, hg0), x1s, cots, gate_t, up_t, expert_down, one, edge // LANES - 1, chunk // 2
    )
    back1 = exchange(after(back1, back0))
    gr0 = after(gr0, back0)
    gate_grad, up_grad, down_grad = expert_grads(
        (x_in, c0, hg0, gr0, ur0), (x1, c1, hg1, gr1, ur1), tensors
    )
    out0 = expert_out(0, hg0, expert_down, owners, tensors, chunk)
    out1 = expert_out(1, after(hg1, out0), expert_down, owners, tensors, chunk)
    out_rows = [
        lax.psum_scatter(out, "tensor", scatter_dimension=0, tiled=True).reshape(owners, 1, capacity, piece)
        for out in (out0, out1)
    ]

    out_rows = exchange(after(jnp.concatenate(out_rows, axis=1), back1, gate_grad))
    own, probs_own, send1, send2, send3 = run(
        combine_kernel,
        [
            ((tokens, piece), F32),
            ((tokens, LANES), F32),
            ((tokens, piece + LANES), BF16),
            ((tokens, piece + LANES), BF16),
            ((tokens, piece + LANES), BF16),
        ],
        [after(me, out1, gate_grad), t0, t1, back0, back1, shared_back],
        2 * tokens * rows * (width + piece),
        places=smem,
        name="combine",
    )
    got = send_blocks([send1, send2, send3])
    shared_sum = lax.psum_scatter(
        after(shared_grads, own), "expert", scatter_dimension=0, tiled=True
    )
    mixed_sum = (
        own
        + got[0][:, :piece].astype(F32)
        + got[1][:, :piece].astype(F32)
        + got[2][:, :piece].astype(F32)
    ).astype(BF16)
    keep, passed, middle_grad, own, send1, send2, send3 = run(
        attend_back_kernel,
        [
            ((owners // 2, shard, outer + 2 * NOPE + experts), BF16),
            ((owners // 2, shard, outer + 2 * NOPE + experts), BF16),
            ((tokens, width), F32),
            ((tokens, piece), F32),
            ((tokens, piece), BF16),
            ((tokens, piece), BF16),
            ((tokens, piece), BF16),
        ],
        [
            after(me, out_rows),
            core,
            stream,
            cotangent,
            middle,
            *share_small(mixed_sum),
            *got,
            probs_own,
            router_probs,
            one,
            router_block,
            mixed,
            normed,
            query,
            expanded,
            key,
            latent,
            compressed,
            probs,
            attended,
            gain_rows,
            latent_gain_rows,
            cosine,
            sine,
        ],
        2 * tokens * width * (3 * edge + 2 * outer),
        scratch=[
            pltpu.VMEM((width, outer + 2 * NOPE + experts), BF16),
            pltpu.VMEM((tokens, edge), BF16),
            pltpu.VMEM((tokens, width), F32),
            pltpu.SemaphoreType.DMA((2,)),
        ],
        places={0: pltpu.SMEM, 1: pltpu.SMEM},
        out_places={0: pl.ANY, 1: pl.ANY},
        name="attend_back",
    )
    paired = lax.ppermute(passed, "expert", [(i, i ^ 1) for i in range(owners)])
    paired = (keep.astype(F32) + paired.astype(F32)).astype(BF16)
    parts = lax.all_to_all(
        paired,
        "expert",
        split_axis=0,
        concat_axis=0,
        tiled=True,
        axis_index_groups=[[2 * i + c for i in range(owners // 2)] for c in range(2)],
    )
    query_grad, late, output_grad, latent_up_grad, router_grad = run(
        unpack_kernel,
        [
            (query_proj.shape, F32),
            ((shard, edge - queries), F32),
            ((shard, heads * VDIM), F32),
            (latent_up.shape, F32),
            (router_proj.shape, F32),
        ],
        [parts],
        0,
        name="unpack",
    )
    latent_down_grad, gain_grads = run(
        late_kernel,
        [(latent_down.shape, F32), ((8, LANES), F32)],
        [late, *(shift(late, step) for step in range(1, tensors))],
        0,
        name="late",
    )
    got = send_blocks([send1, send2, send3])
    first_sum = (own + got[0].astype(F32) + got[1].astype(F32) + got[2].astype(F32)).astype(BF16)
    (stream_grad,) = run(
        stream_kernel,
        [((tokens, width), F32)],
        [me, middle_grad, stream, gain_rows, *share_small(first_sum)],
        0,
        scratch=[pltpu.VMEM((tokens, width), F32)],
        places=smem,
        name="stream",
    )

    got = send_blocks([shared1, shared2, shared3])
    (branch,) = run(
        routed_kernel,
        [((tokens, piece), BF16)],
        [t0, t1, out_rows, shared_own, *got],
        4 * tokens * rows * piece,
        name="routed",
    )
    (result,) = run(
        result_kernel,
        [((tokens, width), F32)],
        [me, middle, *share_small(branch)],
        0,
        places=smem,
        name="result",
    )

    shared_sum = shared_sum.astype(F32)
    return (
        result,
        stream_grad,
        gain_grads[0, :shard],
        query_grad,
        latent_down_grad,
        gain_grads[2, :short],
        latent_up_grad,
        output_grad.T,
        gain_grads[1, :shard],
        router_grad,
        shared_sum[:, :hidden_columns],
        shared_sum[:, hidden_columns : 2 * hidden_columns],
        shared_sum[:, 2 * hidden_columns :].T,
        gate_grad.transpose(0, 2, 1),
        up_grad.transpose(0, 2, 1),
        down_grad,
    )


def solution(mesh):
    placed = (
        P("expert", None),
        P("expert", None),
        P("expert", None),
        P("expert"),
        P("expert", "tensor"),
        P("expert", None),
        P("expert"),
        P("expert", "tensor"),
        P("tensor", "expert"),
        P("expert"),
        P("expert", None),
        P("expert", "tensor"),
        P("expert", "tensor"),
        P("tensor", "expert"),
        P("expert", None, "tensor"),
        P("expert", None, "tensor"),
        P("expert", "tensor", None),
        P("expert", None),
    )
    return jax.shard_map(
        per_device,
        mesh=mesh,
        in_specs=placed,
        out_specs=(
            P("expert", None),
            P("expert", None),
            P("expert"),
            P("expert", "tensor"),
            P("expert", None),
            P("expert"),
            P("expert", "tensor"),
            P("tensor", "expert"),
            P("expert"),
            P("expert", None),
            P("expert", "tensor"),
            P("expert", "tensor"),
            P("tensor", "expert"),
            P("expert", None, "tensor"),
            P("expert", None, "tensor"),
            P("expert", "tensor", None),
        ),
        check_vma=False,
    )
```

time: 2240 us -> 592 us (0.26)
  waiting for transfers between devices: 1230 us -> 252 us
  blocking collectives: 335 us -> 40 us
  local copies, waits for them, and re-layouts: 287 us -> 29.5 us
  matrix products: 205 us -> 0 us
  Pallas kernels: 0 us -> 151 us
  other arithmetic: 82.8 us -> 12.6 us
    reduce_scatter x8 -> x3, waiting for transfers between devices: 503 us -> 0.04 us  [the longest x2 0.04 us: per_device(): lax.psum_scatter(out, 'tensor', scatter_dimension=0, tiled=True)]
    all_gather x7 -> x2, waiting for transfers between devices: 335 us -> 23.8 us  [the longest x1 23.8 us: per_device(): one = lax.all_gather(pack_one, 'expert', axis=0, tiled=True)]
    dot_general x42 -> x0, matrix products: 205 us -> none  [the longest x34 178 us: contract(): return jnp.einsum(pattern, left, right, preferred_element_type=jnp.float32)]
    unnamed x2 -> x0, blocking collectives: 199 us -> none
    all_to_all x4 -> x5, waiting for transfers between devices: 303 us -> 118 us  [the longest x4 79.7 us: exchange(): lax.all_to_all(rows.reshape(shape[0], -1, shape[-1]), 'expert', split_axi...]
    pallas_call x0 -> x16, Pallas kernels: none -> 151 us  [the longest x11 88.4 us: run(): pl.pallas_call(kernel, in_specs=in_specs, out_specs=out_specs, out_shape=...]
    all_gather x1 -> x0, blocking collectives: 117 us -> none  [per_device(): lax.all_gather(router_proj, 'expert', axis=0, tiled=True)]
    ppermute x0 -> x36, waiting for transfers between devices: none -> 110 us  [the longest x35 102 us: shift(): lax.ppermute(array, 'tensor', [(i, (i + step) % size) for i in range(size)])]
  transfers between devices with their start and end apart: 22 -> 46, of which waited for: 15 -> 26; matrix products, arithmetic and copies ran while one was open for 19% -> 5% of each run, Pallas kernels for 0% -> 26%
where the time goes in v1:
time: 592 us; the launch traced here: 583 us
  waiting for transfers between devices  252 us (43%)
  Pallas kernels  151 us (26%)
  starting transfers between devices  82.7 us (14%)
  blocking collectives  40 us (7%)
  local copies, waits for them, and re-layouts  29.5 us (5%)
  between operations  14.7 us (2%)
  other arithmetic  12.6 us (2%)
    ppermute x35, waiting for transfers between devices, shift(): lax.ppermute(array, 'tensor', [(i, (i + step) % size) for i in range(size)])  102 us
    pallas_call x11, Pallas kernels, run(): pl.pallas_call(kernel, in_specs=in_specs, out_specs=out_specs, out_shape=...  88.4 us
    all_to_all x4, waiting for transfers between devices, exchange(): lax.all_to_all(rows.reshape(shape[0], -1, shape[-1]), 'expert', split_axi...  79.7 us
    ppermute x35, starting transfers between devices, shift(): lax.ppermute(array, 'tensor', [(i, (i + step) % size) for i in range(size)])  48.3 us
    all_to_all x1, blocking collectives, exchange(): lax.all_to_all(rows.reshape(shape[0], -1, shape[-1]), 'expert', split_axi...  40 us
    all_to_all x1, waiting for transfers between devices, per_device(): lax.all_to_all(paired, 'expert', split_axis=0, concat_axis=0, tiled=True,...  37.9 us
    pallas_call x2, Pallas kernels, expert_back(): pl.pallas_call(functools.partial(expert_back_kernel, split), grid=(owners...  32.9 us
    all_to_all x4, starting transfers between devices, exchange(): lax.all_to_all(rows.reshape(shape[0], -1, shape[-1]), 'expert', split_axi...  26.6 us
  transfers between devices with their start and end apart: 46, of which 26 were waited for; matrix products, arithmetic and copies ran while one was open for 5% of the time, Pallas kernels for 26%

profile of v1, /device:TPU:0, one launch (start us, length us, event | category | flops | bytes accessed | tf_op | source)
XLA Modules:
  0.0 582.7 jit_solution(6794907751057246339)
XLA Ops:
  11.5 1.7 concatenate.18
  13.3 1.8 concatenate.20
  15.2 4.7 routing.1
  19.9 40.0 %all_to_all.30 = bf16[32,64,512]{2,1,0:T(8,128)(2,1)S(1)} all-to-all(bf16[32,64,512]{2,1,0:T(8,128)(2,1)} %bitcast.49), channel_id=1, replica_groups=mesh['expert'=32,'tensor'=4] {'expert'}, dimensions={0} | all-to-all | bytes 4194304 | tf_op jit(solution)/shard_map/all_to_all | solution.py:736
  61.0 2.1 collective-permute-start.4
  66.0 23.8 %all-gather.3.cloned.1.call-done.w_ref.refs_10_.refs_13_ = bf16[2048,2240]{1,0:T(8,128)(2,1)} async-done(((bf16[64,2240]{1,0:T(8,128)(2,1)}), bf16[2048,2240]{1,0:T(8,128)(2,1)}) %all-gather.3.cloned.1.call-update) | async-done | bytes 9175056 | tf_op jit(solution)/shard_map/all_gather | solution.py:805
  89.7 11.1 %attend.1 = (f32[256,512]{1,0:T(8,128)}, bf16[256,512]{1,0:T(8,128)(2,1)}, bf16[256,512]{1,0:T(8,128)(2,1)}, bf16[256,512]{1,0:T(8,128)(2,1)}, bf16[256,2048]{1,...) custom-call(s32[1]{0:T(128)} %bitcast.me_ref.refs_0_, ...), custom_call_target="tpu_custom_call" | custom-call | flops 201326592 | bytes 1627136 | tf_op jit(solution)/shard_map/attend/pallas_call | solution.py:81
  102.3 2.7 collective-permute-start.1
  106.5 7.7 %collective-permute-done = bf16[256,512]{1,0:T(8,128)(2,1)S(1)} collective-permute-done((bf16[256,512]{1,0:T(8,128)(2,1)}, bf16[256,512]{1,0:T(8,128)(2,1)S(1)}, u32[]{:S(2)}, u32[]{:S(2)}) %collective-permute-start) | collective-permute-done | bytes 262176 | tf_op jit(solution)/shard_map/ppermute | solution.py:708
  114.2 6.7 %collective-permute-done.1 = bf16[256,512]{1,0:T(8,128)(2,1)S(1)} collective-permute-done((bf16[256,512]{1,0:T(8,128)(2,1)}, bf16[256,512]{1,0:T(8,128)(2,1)S(1)}, u32[]{:S(2)}, u32[]{:S(2)}) %collective-permute-start.1) | collective-permute-done | bytes 262176 | tf_op jit(solution)/shard_map/ppermute | solution.py:708
  122.1 2.0 collective-permute-start.5
  125.6 5.8 %collective-permute-done.5.a1_ref = bf16[256,512]{1,0:T(8,128)(2,1)S(1)} collective-permute-done((bf16[256,512]{1,0:T(8,128)(2,1)S(1)}, bf16[256,512]{1,0:T(8,128)(2,1)S(1)}, u32[]{:S(2)}, u32[]{:S(2)}) %collective-permute-start.5) | collective-permute-done | bytes 262176 | tf_op jit(solution)/shard_map/ppermute | solution.py:708
  131.4 3.4 collective-permute-done.6.a2_ref
  134.8 3.1 collective-permute-done.7.a3_ref
  138.7 6.7 %dispatch.1 = (f32[256,2048]{1,0:T(8,128)}, bf16[256,2048]{1,0:T(8,128)(2,1)}, bf16[32,32,2560]{2,1,0:T(8,128)(2,1)}) custom-call(s32[1]{0:T(128)} %bitcast.me_ref.refs_0_, bf16[256,2048]{1,0:T(8,128)(2,1)} %stream_ref.7, bf16[256,512]{1,0:T(8,128)(2,1)} %copy-done.7, bf16[256,512]{1,0:T(8,128)(2,1)} %copy-done.17, bf16[256,512]{1,0:T(8,128)(2,1)} %copy-done.18, ...), custom_call_target="tpu_custom_call" | custom-call | flops 134217728 | bytes 1159987 | tf_op jit(solution)/shard_map/dispatch/pallas_call | solution.py:81
  145.4 4.9 all-to-all-start.1
  150.3 2.3 slice.71
  153.9 3.3 collective-permute-start.9
  157.2 22.0 %collective-permute-done.8 = bf16[16,2,32,512]{3,2,1,0:T(8,128)(2,1)S(1)} collective-permute-done((bf16[16,2,32,512]{3,2,1,0:T(8,128)(2,1)}, bf16[16,2,32,512]{3,2,1,0:T(8,128)(2,1)S(1)}, u32[]{:S(2)}, u32[]{:S(2)}) %collective-permute-start.8) | collective-permute-done | bytes 1048608 | tf_op jit(solution)/shard_map/ppermute | solution.py:708
  181.1 1.9 slice.70.router_ref
  182.9 16.6 %shared.1 = (f32[256,512]{1,0:T(8,128)}, bf16[256,512]{1,0:T(8,128)(2,1)}, bf16[256,512]{1,0:T(8,128)(2,1)}, bf16[256,512]{1,0:T(8,128)(2,1)}, f32[256,2048]{1,0...) custom-call(s32[1]{0:T(128)} %bitcast.me_ref.refs_0_, bf16[256,2048]{1,0:T(8,128)(2,1)} %get-tuple-element.99.mixed_ref, ...), custom_call_target="tpu_custom_call" | custom-call | flops 664377728 | bytes 2346189 | tf_op jit(solution)/shard_map/shared/pallas_call | solution.py:81
  199.5 15.8 %all-to-all-done.1.refs_2_.x0_ref = bf16[32,32,2560]{2,1,0:T(8,128)(2,1)} async-done(((bf16[32,32,2560]{2,1,0:T(8,128)(2,1)}), bf16[32,32,2560]{2,1,0:T(8,128)(2,1)}, u32[]{:S(2)}, u32[]{:S(2)}) %all-to-all-start.1) | async-done | bytes 5242912 | tf_op jit(solution)/shard_map/all_to_all | solution.py:736
  216.7 3.6 collective-permute-start.10
  220.3 16.3 %expert_back.2 = (bf16[32,32,2176]{2,1,0:T(8,128)(2,1)}, bf16[32,32,2048]{2,1,0:T(8,128)(2,1)}, bf16[1024,352]{1,0:T(8,128)(2,1)}, bf16[1024,352]{1,0:T(8,128)(2,1)}, bf16[1024,352]{1,0:T(8,128)(2,1)}) custom-call(s32[1]{0:T(128)} %bitcast.me_ref.refs_0_, s32[1]{0:T(128)} %bitcast.13.refs_1_, bf16[32,32,2560]{2,1,0:T(8,128)(2,1)} %all-to-all-done.1.refs_2_.x0_ref, ...), custom_call_target="tpu_custom_call" | custom-call | flops 73819750400 | bytes 25165824 | tf_op jit(solution)/shard_map/expert_back/pallas_call | solution.py:357
  236.6 5.4 expert_out.2
  244.1 3.1 collective-permute-start.13
  247.3 8.4 %all-to-all-start.2 = ((bf16[32,32,2176]{2,1,0:T(8,128)(2,1)}), bf16[32,32,2176]{2,1,0:T(8,128)(2,1)}, u32[]{:S(2)}, u32[]{:S(2)}) async-start(bf16[32,32,2176]{2,1,0:T(8,128)(2,1)} %get-tuple-element.109), calls=%async_computation.4 | async-start | bytes 8912896 | tf_op jit(solution)/shard_map/all_to_all | solution.py:736
  255.7 5.9 %collective-permute-done.12 = bf16[16,32,512]{2,1,0:T(8,128)(2,1)S(1)} collective-permute-done((bf16[16,32,512]{2,1,0:T(8,128)(2,1)S(1)}, bf16[16,32,512]{2,1,0:T(8,128)(2,1)S(1)}, u32[]{:S(2)}, u32[]{:S(2)}) %collective-permute-start.12) | collective-permute-done | bytes 524320 | tf_op jit(solution)/shard_map/ppermute | solution.py:708
  261.6 4.7 collective-permute-done.13
  267.3 16.6 %expert_back.3 = (bf16[32,32,2176]{2,1,0:T(8,128)(2,1)}, bf16[32,32,2048]{2,1,0:T(8,128)(2,1)}, bf16[1024,352]{1,0:T(8,128)(2,1)}, bf16[1024,352]{1,0:T(8,128)(2...) custom-call(s32[1]{0:T(128)} %bitcast.me_ref.refs_0_, s32[1]{0:T(128)} %bitcast.13.refs_1_, ...), custom_call_target="tpu_custom_call" | custom-call | flops 73819750400 | bytes 25165824 | tf_op jit(solution)/shard_map/expert_back/pallas_call | solution.py:357
  284.0 5.4 expert_out.3
  289.4 22.4 %all-to-all-done.2.b0_ref = bf16[32,32,2176]{2,1,0:T(8,128)(2,1)} async-done(((bf16[32,32,2176]{2,1,0:T(8,128)(2,1)}), bf16[32,32,2176]{2,1,0:T(8,128)(2,1)}, u32[]{:S(2)}, u32[]{:S(2)}) %all-to-all-start.2) | async-done | bytes 4456480 | tf_op jit(solution)/shard_map/all_to_all | solution.py:736
  311.8 6.6 %all-to-all-start.3 = ((bf16[32,32,2176]{2,1,0:T(8,128)(2,1)}), bf16[32,32,2176]{2,1,0:T(8,128)(2,1)}, u32[]{:S(2)}, u32[]{:S(2)}) async-start(bf16[32,32,2176]{2,1,0:T(8,128)(2,1)} %get-tuple-element.110), calls=%async_computation.5 | async-start | bytes 8912896 | tf_op jit(solution)/shard_map/all_to_all | solution.py:736
  318.6 19.4 %expert_grads.1 = (f32[2,352,2048]{2,1,0:T(8,128)}, f32[2,352,2048]{2,1,0:T(8,128)}, f32[2,352,2048]{2,1,0:T(8,128)}) custom-call(bf16[32,32,2560]{2,1,0:T(8,128)(2,1)} %all-to-all-done.1.refs_2_.x0_ref, bf16[32,32,2048]{2,1,0:T(8,128)(2,1)} %get-tuple-element.111.c0_ref, bf16[1024,352]{1,0:T(8,128)(2,1)} %get-tuple-element.104.hg_ref.hg0_ref, ...), custom_call_target="tpu_custom_call" | custom-call | flops 738197504 | bytes 4177920 | tf_op jit(solution)/shard_map/expert_grads/pallas_call | solution.py:436
  338.0 36.2 %all-to-all-done.3.b1_ref = bf16[32,32,2176]{2,1,0:T(8,128)(2,1)} async-done(((bf16[32,32,2176]{2,1,0:T(8,128)(2,1)}), bf16[32,32,2176]{2,1,0:T(8,128)(2,1)}, u32[]{:S(2)}, u32[]{:S(2)}) %all-to-all-start.3) | async-done | bytes 4456480 | tf_op jit(solution)/shard_map/all_to_all | solution.py:736
  374.2 8.3 %combine.1 = (f32[256,512]{1,0:T(8,128)}, f32[256,128]{1,0:T(8,128)}, bf16[256,640]{1,0:T(8,128)(2,1)}, bf16[256,640]{1,0:T(8,128)(2,1)}, bf16[256,640]{1,0:T(8,128)(2,1)}) custom-call(s32[1]{0:T(128)} %bitcast.me_ref.refs_0_, bf16[256,1024]{1,0:T(8,128)(2,1)} %get-tuple-element.96.t0_ref, bf16[256,1024]{1,0:T(8,128)(2,1)} %get-tuple-element.97.t1_ref, ...), custom_call_target="tpu_custom_call" | custom-call | flops 134217728 | bytes 1369702 | tf_op jit(solution)/shard_map/combine/pallas_call | solution.py:81
  382.6 1.7 pad_maximum_fusion
  385.9 6.7 %all-to-all-start.4 = ((bf16[32,64,512]{2,1,0:T(8,128)(2,1)}), bf16[32,64,512]{2,1,0:T(8,128)(2,1)S(1)}, u32[]{:S(2)}, u32[]{:S(2)}) async-start(bf16[32,64,512]{2,1,0:T(8,128)(2,1)} %bitcast.44), calls=%async_computation.6 | async-start | bytes 4194304 | tf_op jit(solution)/shard_map/all_to_all | solution.py:736
  394.2 1.8 collective-permute-start.22
  395.9 15.1 %collective-permute-done.20.r1_ref = bf16[256,640]{1,0:T(8,128)(2,1)S(1)} collective-permute-done((bf16[256,640]{1,0:T(8,128)(2,1)}, bf16[256,640]{1,0:T(8,128)(2,1)S(1)}, u32[]{:S(2)}, u32[]{:S(2)}) %collective-permute-start.20) | collective-permute-done | bytes 327712 | tf_op jit(solution)/shard_map/ppermute | solution.py:708
  413.0 2.2 collective-permute-start.23
  416.3 5.3 all-to-all-done.4
  421.6 4.5 collective-permute-done.23.a1_ref
  426.1 3.8 collective-permute-done.25.a3_ref
  429.9 23.3 %attend_back.1 = (bf16[16,64,2240]{2,1,0:T(8,128)(2,1)}, bf16[16,64,2240]{2,1,0:T(8,128)(2,1)}, f32[256,2048]{1,0:T(8,128)}, f32[256,512]{1,0:T(8,128)}, bf16[25...) custom-call(s32[1]{0:T(128)} %bitcast.me_ref.refs_0_, s32[1]{0:T(128)} %bitcast.21.core_ref, ...), custom_call_target="tpu_custom_call" | custom-call | flops 845571712 | bytes 3560244 | tf_op jit(solution)/shard_map/attend_back/pallas_call | solution.py:81
  453.3 8.1 %collective-permute-done.32 = bf16[16,64,2240]{2,1,0:T(8,128)(2,1)S(1)} collective-permute-done((bf16[16,64,2240]{2,1,0:T(8,128)(2,1)}, bf16[16,64,2240]{2,1,0:T(8,128)(2,1)S(1)}, u32[]{:S(2)}, u32[]{:S(2)}) %collective-permute-start.32) | collective-permute-done | bytes 4587552 | tf_op jit(solution)/shard_map/ppermute | solution.py:1011
  461.4 6.0 %add_convert_fusion = bf16[16,64,2240]{2,1,0:T(8,128)(2,1)} fusion(bf16[16,64,2240]{2,1,0:T(8,128)(2,1)S(1)} %collective-permute-done.32, bf16[16,64,2240]{2,1,0:T(8,128)(2,1)} %get-tuple-element.147), kind=kLoop, calls=%fused_computation | loop fusion | flops 9175040 | bytes 13762560 | tf_op jit(solution)/shard_map/convert_element_type | solution.py:1012
  467.4 7.3 %all-to-all-start.5 = ((bf16[16,64,2240]{2,1,0:T(8,128)(2,1)}), bf16[16,64,2240]{2,1,0:T(8,128)(2,1)}, u32[]{:S(2)}, u32[]{:S(2)}) async-start(bf16[16,64,2240]{2,1,0:T(8,128)(2,1)} %add_convert_fusion), calls=%async_computation.7 | async-start | bytes 9437184 | tf_op jit(solution)/shard_map/all_to_all | solution.py:1013
  474.8 1.8 collective-permute-start.15
  479.2 2.1 collective-permute-start.27
  481.3 9.5 %collective-permute-done.14.r1_ref = bf16[256,512]{1,0:T(8,128)(2,1)S(1)} collective-permute-done((bf16[256,512]{1,0:T(8,128)(2,1)S(1)}, bf16[256,512]{1,0:T(8,128)(2,1)S(1)}, u32[]{:S(2)}, u32[]{:S(2)}) %collective-permute-start.14) | collective-permute-done | bytes 262176 | tf_op jit(solution)/shard_map/ppermute | solution.py:708
  492.4 3.6 routed.1.a0_ref
  496.1 2.7 collective-permute-start.17
  500.9 2.1 collective-permute-done.28
  504.8 3.8 collective-permute-done.17.a1_ref
  508.6 37.9 %all-to-all-done.5.parts_ref = bf16[16,64,2240]{2,1,0:T(8,128)(2,1)} async-done(((bf16[16,64,2240]{2,1,0:T(8,128)(2,1)}), bf16[16,64,2240]{2,1,0:T(8,128)(2,1)}, u32[]{:S(2)}, u32[]{:S(2)}) %all-to-all-start.5) | async-done | bytes 4587552 | tf_op jit(solution)/shard_map/all_to_all | solution.py:1013
  546.6 4.0 unpack.1
  550.6 3.1 collective-permute-start.33
  553.7 1.9 collective-permute-start.34
  555.6 2.5 collective-permute-start.35
  558.1 3.3 result.1
  562.2 5.0 stream.1
  568.6 1.9 late.1
  573.9 1.8 fusion.1
  (159 shorter events, 42.9 us)
Async XLA Ops:
  7.2 82.5 %all-gather.3.cloned.1.call-start = ((), (), s32[]{:S(2)}) async-start(), calls=%async_computation.9 | async-start | bytes 9732096 | tf_op jit(solution)/shard_map/all_gather | solution.py:805
  13.3 169.6 %all-gather.5.cloned.1.call-start = ((), (), s32[]{:S(2)}) async-start(), calls=%async_computation.10 | async-start | bytes 9191424 | tf_op jit(solution)/shard_map/all_gather | solution.py:806
  15.2 50.0 %copy-start.26 = (s32[1,256]{1,0:T(1,128)S(1)}, s32[1,256]{1,0:T(1,128)}, u32[]{:S(2)}) copy-start(s32[1,256]{1,0:T(1,128)} %seg_row_ref.1) | copy-start | bytes 3076
  59.9 40.8 %copy-start.1 = (bf16[32,64,512]{2,1,0:T(8,128)(2,1)}, bf16[32,64,512]{2,1,0:T(8,128)(2,1)S(1)}, u32[]{:S(2)}) copy-start(bf16[32,64,512]{2,1,0:T(8,128)(2,1)S(1)} %all_to_all.30) | copy-start | bytes 6291460
  59.9 62.1 %collective-permute-start.3 = (bf16[32,2,32,512]{3,2,1,0:T(8,128)(2,1)S(1)}, bf16[32,2,32,512]{3,2,1,0:T(8,128)(2,1)}, u32[]{:S(2)}, u32[]{:S(2)}) collective-permute-start(bf16[32,2,32,512]{3,2,1,0:T(8,128)(2,1)S(1)} %bitcast.45), channel_id=1, source_target_pairs={{0,1},{1,2},{2,3},{3,0},{4,5},{5,6},{6,7},{7,4},{8,9},{9,10},{10,1... | collective-permute-start | bytes 6291464 | tf_op jit(solution)/shard_map/ppermute | solution.py:708
  61.0 61.0 %collective-permute-start.4 = (bf16[32,2,32,512]{3,2,1,0:T(8,128)(2,1)S(1)}, bf16[32,2,32,512]{3,2,1,0:T(8,128)(2,1)}, u32[]{:S(2)}, u32[]{:S(2)}) collective-permute-start(bf16[32,2,32,512]{3,2,1,0:T(8,128)(2,1)S(1)} %bitcast.46), channel_id=1, source_target_pairs={{0,3},{1,0},{2,1},{3,2},{4,7},{5,4},{6,5},{7,6},{8,11},{9,8},{10,9... | collective-permute-start | bytes 6291464 | tf_op jit(solution)/shard_map/ppermute | solution.py:708
  100.8 13.4 %collective-permute-start = (bf16[256,512]{1,0:T(8,128)(2,1)}, bf16[256,512]{1,0:T(8,128)(2,1)S(1)}, u32[]{:S(2)}, u32[]{:S(2)}) collective-permute-start(bf16[256,512]{1,0:T(8,128)(2,1)} %get-tuple-element.91), channel_id=1, source_target_pairs={{0,1},{1,2},{2,3},{3,0},{4,5},{5,6},{6,7},{7,4},{8,9},{9,10},{10,1... | collective-permute-start | bytes 786440 | tf_op jit(solution)/shard_map/ppermute | solution.py:708
  102.3 18.5 %collective-permute-start.1 = (bf16[256,512]{1,0:T(8,128)(2,1)}, bf16[256,512]{1,0:T(8,128)(2,1)S(1)}, u32[]{:S(2)}, u32[]{:S(2)}) collective-permute-start(bf16[256,512]{1,0:T(8,128)(2,1)} %get-tuple-element.92), channel_id=1, source_target_pairs={{0,2},{1,3},{2,0},{3,1},{4,6},{5,7},{6,4},{7,5},{8,10},{9,11},{10,... | collective-permute-start | bytes 786440 | tf_op jit(solution)/shard_map/ppermute | solution.py:708
  105.0 15.8 %collective-permute-start.2 = (bf16[256,512]{1,0:T(8,128)(2,1)}, bf16[256,512]{1,0:T(8,128)(2,1)S(1)}, u32[]{:S(2)}, u32[]{:S(2)}) collective-permute-start(bf16[256,512]{1,0:T(8,128)(2,1)} %get-tuple-element.93), channel_id=1, source_target_pairs={{0,3},{1,0},{2,1},{3,2},{4,7},{5,4},{6,5},{7,6},{8,11},{9,8},{10,9... | collective-permute-start | bytes 786440 | tf_op jit(solution)/shard_map/ppermute | solution.py:708
  122.0 15.9 %copy-start.7 = (bf16[256,512]{1,0:T(8,128)(2,1)}, bf16[256,512]{1,0:T(8,128)(2,1)S(1)}, u32[]{:S(2)}) copy-start(bf16[256,512]{1,0:T(8,128)(2,1)S(1)} %add_convert_fusion.3.a0_ref) | copy-start | bytes 786436
  122.1 9.3 %collective-permute-start.5 = (bf16[256,512]{1,0:T(8,128)(2,1)S(1)}, bf16[256,512]{1,0:T(8,128)(2,1)S(1)}, u32[]{:S(2)}, u32[]{:S(2)}) collective-permute-start(bf16[256,512]{1,0:T(8,128)(2,1)S(1)} %add_convert_fusion.3.a0_ref), channel_id=1, source_target_pairs={{0,3},{1,0},{2,1},{3,2},{4,7},{5,4},{6,5},{7,6},{8,11},{9,8},{10,9... | collective-permute-start | bytes 786440 | tf_op jit(solution)/shard_map/ppermute | solution.py:708
  124.1 10.8 %collective-permute-start.6 = (bf16[256,512]{1,0:T(8,128)(2,1)S(1)}, bf16[256,512]{1,0:T(8,128)(2,1)S(1)}, u32[]{:S(2)}, u32[]{:S(2)}) collective-permute-start(bf16[256,512]{1,0:T(8,128)(2,1)S(1)} %add_convert_fusion.3.a0_ref), channel_id=1, source_target_pairs={{0,2},{1,3},{2,0},{3,1},{4,6},{5,7},{6,4},{7,5},{8,10},{9,11},{10,... | collective-permute-start | bytes 786440 | tf_op jit(solution)/shard_map/ppermute | solution.py:708
  124.6 13.3 %collective-permute-start.7 = (bf16[256,512]{1,0:T(8,128)(2,1)S(1)}, bf16[256,512]{1,0:T(8,128)(2,1)S(1)}, u32[]{:S(2)}, u32[]{:S(2)}) collective-permute-start(bf16[256,512]{1,0:T(8,128)(2,1)S(1)} %add_convert_fusion.3.a0_ref), channel_id=1, source_target_pairs={{0,1},{1,2},{2,3},{3,0},{4,5},{5,6},{6,7},{7,4},{8,9},{9,10},{10,1... | collective-permute-start | bytes 786440 | tf_op jit(solution)/shard_map/ppermute | solution.py:708
  145.4 69.9 %all-to-all-start.1 = ((bf16[32,32,2560]{2,1,0:T(8,128)(2,1)}), bf16[32,32,2560]{2,1,0:T(8,128)(2,1)}, u32[]{:S(2)}, u32[]{:S(2)}) async-start(bf16[32,32,2560]{2,1,0:T(8,128)(2,1)} %get-tuple-element.103), calls=%async_computation.1 | async-start | bytes 10485760 | tf_op jit(solution)/shard_map/all_to_all | solution.py:736
  150.3 232.3 %reduce-scatter.4.cloned.1.call-start = ((), (), s32[]{:S(2)}) async-start(), calls=%async_computation.11 | async-start | bytes 5242880 | tf_op jit(solution)/shard_map/reduce_scatter | solution.py:934
  152.6 26.6 %collective-permute-start.8 = (bf16[16,2,32,512]{3,2,1,0:T(8,128)(2,1)}, bf16[16,2,32,512]{3,2,1,0:T(8,128)(2,1)S(1)}, u32[]{:S(2)}, u32[]{:S(2)}) collective-permute-start(bf16[16,2,32,512]{3,2,1,0:T(8,128)(2,1)} %slice.71), channel_id=1, source_target_pairs={{0,1},{1,2},{2,3},{3,0},{4,5},{5,6},{6,7},{7,4},{8,9},{9,10},{10,1... | collective-permute-start | bytes 3145736 | tf_op jit(solution)/shard_map/ppermute | solution.py:708
  153.9 25.7 %collective-permute-start.9 = (bf16[16,2,32,512]{3,2,1,0:T(8,128)(2,1)S(1)}, bf16[16,2,32,512]{3,2,1,0:T(8,128)(2,1)S(1)}, u32[]{:S(2)}, u32[]{:S(2)}) collective-permute-start(bf16[16,2,32,512]{3,2,1,0:T(8,128)(2,1)S(1)} %slice.72), channel_id=1, source_target_pairs={{0,3},{1,0},{2,1},{3,2},{4,7},{5,4},{6,5},{7,6},{8,11},{9,8},{10,9... | collective-permute-start | bytes 3145736 | tf_op jit(solution)/shard_map/ppermute | solution.py:708
  216.6 26.1 %collective-permute-start.11 = (bf16[32,32,512]{2,1,0:T(8,128)(2,1)S(1)}, bf16[32,32,512]{2,1,0:T(8,128)(2,1)S(1)}, u32[]{:S(2)}, u32[]{:S(2)}) collective-permute-start(bf16[32,32,512]{2,1,0:T(8,128)(2,1)S(1)} %slice.73), channel_id=1, source_target_pairs={{0,1},{1,2},{2,3},{3,0},{4,5},{5,6},{6,7},{7,4},{8,9},{9,10},{10,1... | collective-permute-start | bytes 3145736 | tf_op jit(solution)/shard_map/ppermute | solution.py:708
  216.7 26.1 %collective-permute-start.10 = (bf16[32,32,512]{2,1,0:T(8,128)(2,1)S(1)}, bf16[32,32,512]{2,1,0:T(8,128)(2,1)}, u32[]{:S(2)}, u32[]{:S(2)}) collective-permute-start(bf16[32,32,512]{2,1,0:T(8,128)(2,1)S(1)} %slice.73), channel_id=1, source_target_pairs={{0,3},{1,0},{2,1},{3,2},{4,7},{5,4},{6,5},{7,6},{8,11},{9,8},{10,9... | collective-permute-start | bytes 3145736 | tf_op jit(solution)/shard_map/ppermute | solution.py:708
  242.7 18.8 %collective-permute-start.12 = (bf16[16,32,512]{2,1,0:T(8,128)(2,1)S(1)}, bf16[16,32,512]{2,1,0:T(8,128)(2,1)S(1)}, u32[]{:S(2)}, u32[]{:S(2)}) collective-permute-start(bf16[16,32,512]{2,1,0:T(8,128)(2,1)S(1)} %slice.74), channel_id=1, source_target_pairs={{0,1},{1,2},{2,3},{3,0},{4,5},{5,6},{6,7},{7,4},{8,9},{9,10},{10,1... | collective-permute-start | bytes 1572872 | tf_op jit(solution)/shard_map/ppermute | solution.py:708
  244.1 22.1 %collective-permute-start.13 = (bf16[16,32,512]{2,1,0:T(8,128)(2,1)S(1)}, bf16[16,32,512]{2,1,0:T(8,128)(2,1)S(1)}, u32[]{:S(2)}, u32[]{:S(2)}) collective-permute-start(bf16[16,32,512]{2,1,0:T(8,128)(2,1)S(1)} %slice.75), channel_id=1, source_target_pairs={{0,3},{1,0},{2,1},{3,2},{4,7},{5,4},{6,5},{7,6},{8,11},{9,8},{10,9... | collective-permute-start | bytes 1572872 | tf_op jit(solution)/shard_map/ppermute | solution.py:708
  247.3 64.5 %all-to-all-start.2 = ((bf16[32,32,2176]{2,1,0:T(8,128)(2,1)}), bf16[32,32,2176]{2,1,0:T(8,128)(2,1)}, u32[]{:S(2)}, u32[]{:S(2)}) async-start(bf16[32,32,2176]{2,1,0:T(8,128)(2,1)} %get-tuple-element.109), calls=%async_computation.4 | async-start | bytes 8912896 | tf_op jit(solution)/shard_map/all_to_all | solution.py:736
  255.7 126.9 %reduce-scatter.6.cloned.1.call-start = ((), (), s32[]{:S(2)}) async-start(), calls=%async_computation.12 | async-start | bytes 5242880 | tf_op jit(solution)/shard_map/reduce_scatter | solution.py:934
  311.8 62.5 %all-to-all-start.3 = ((bf16[32,32,2176]{2,1,0:T(8,128)(2,1)}), bf16[32,32,2176]{2,1,0:T(8,128)(2,1)}, u32[]{:S(2)}, u32[]{:S(2)}) async-start(bf16[32,32,2176]{2,1,0:T(8,128)(2,1)} %get-tuple-element.110), calls=%async_computation.5 | async-start | bytes 8912896 | tf_op jit(solution)/shard_map/all_to_all | solution.py:736
  318.4 254.5 %reduce-scatter.8.cloned.1.call-start = ((), (), s32[]{:S(2)}) async-start(), calls=%async_computation.13 | async-start | bytes 9191424 | tf_op jit(solution)/shard_map/reduce_scatter | solution.py:954
  384.3 9.9 %copy-start.27 = (bf16[256,640]{1,0:T(8,128)(2,1)S(1)}, bf16[256,640]{1,0:T(8,128)(2,1)}, u32[]{:S(2)}) copy-start(bf16[256,640]{1,0:T(8,128)(2,1)} %get-tuple-element.130) | copy-start | bytes 983044
  385.9 35.7 %all-to-all-start.4 = ((bf16[32,64,512]{2,1,0:T(8,128)(2,1)}), bf16[32,64,512]{2,1,0:T(8,128)(2,1)S(1)}, u32[]{:S(2)}, u32[]{:S(2)}) async-start(bf16[32,64,512]{2,1,0:T(8,128)(2,1)} %bitcast.44), calls=%async_computation.6 | async-start | bytes 4194304 | tf_op jit(solution)/shard_map/all_to_all | solution.py:736
  392.6 18.4 %collective-permute-start.20 = (bf16[256,640]{1,0:T(8,128)(2,1)}, bf16[256,640]{1,0:T(8,128)(2,1)S(1)}, u32[]{:S(2)}, u32[]{:S(2)}) collective-permute-start(bf16[256,640]{1,0:T(8,128)(2,1)} %get-tuple-element.128), channel_id=1, source_target_pairs={{0,1},{1,2},{2,3},{3,0},{4,5},{5,6},{6,7},{7,4},{8,9},{9,10},{10,1... | collective-permute-start | bytes 983048 | tf_op jit(solution)/shard_map/ppermute | solution.py:708
  392.7 18.3 %collective-permute-start.21 = (bf16[256,640]{1,0:T(8,128)(2,1)}, bf16[256,640]{1,0:T(8,128)(2,1)S(1)}, u32[]{:S(2)}, u32[]{:S(2)}) collective-permute-start(bf16[256,640]{1,0:T(8,128)(2,1)} %get-tuple-element.129), channel_id=1, source_target_pairs={{0,2},{1,3},{2,0},{3,1},{4,6},{5,7},{6,4},{7,5},{8,10},{9,11},{10,... | collective-permute-start | bytes 983048 | tf_op jit(solution)/shard_map/ppermute | solution.py:708
  394.2 17.5 %collective-permute-start.22 = (bf16[256,640]{1,0:T(8,128)(2,1)S(1)}, bf16[256,640]{1,0:T(8,128)(2,1)S(1)}, u32[]{:S(2)}, u32[]{:S(2)}) collective-permute-start(bf16[256,640]{1,0:T(8,128)(2,1)S(1)} %copy-done.27), channel_id=1, source_target_pairs={{0,3},{1,0},{2,1},{3,2},{4,7},{5,4},{6,5},{7,6},{8,11},{9,8},{10,9... | collective-permute-start | bytes 983048 | tf_op jit(solution)/shard_map/ppermute | solution.py:708
  411.0 18.8 %copy-start.2 = (bf16[256,640]{1,0:T(8,128)(2,1)}, bf16[256,640]{1,0:T(8,128)(2,1)S(1)}, u32[]{:S(2)}) copy-start(bf16[256,640]{1,0:T(8,128)(2,1)S(1)} %collective-permute-done.20.r1_ref) | copy-start | bytes 983044
  411.0 18.8 %copy-start.3 = (bf16[256,640]{1,0:T(8,128)(2,1)}, bf16[256,640]{1,0:T(8,128)(2,1)S(1)}, u32[]{:S(2)}) copy-start(bf16[256,640]{1,0:T(8,128)(2,1)S(1)} %collective-permute-done.21.r2_ref) | copy-start | bytes 983044
  411.7 18.2 %copy-start.4 = (bf16[256,640]{1,0:T(8,128)(2,1)}, bf16[256,640]{1,0:T(8,128)(2,1)S(1)}, u32[]{:S(2)}) copy-start(bf16[256,640]{1,0:T(8,128)(2,1)S(1)} %collective-permute-done.22.r3_ref) | copy-start | bytes 983044
  413.0 16.9 %copy-start.5 = (bf16[256,512]{1,0:T(8,128)(2,1)}, bf16[256,512]{1,0:T(8,128)(2,1)S(1)}, u32[]{:S(2)}) copy-start(bf16[256,512]{1,0:T(8,128)(2,1)S(1)} %add_convert_fusion.2.a0_ref) | copy-start | bytes 786436
  413.0 13.1 %collective-permute-start.23 = (bf16[256,512]{1,0:T(8,128)(2,1)S(1)}, bf16[256,512]{1,0:T(8,128)(2,1)}, u32[]{:S(2)}, u32[]{:S(2)}) collective-permute-start(bf16[256,512]{1,0:T(8,128)(2,1)S(1)} %add_convert_fusion.2.a0_ref), channel_id=1, source_target_pairs={{0,3},{1,0},{2,1},{3,2},{4,7},{5,4},{6,5},{7,6},{8,11},{9,8},{10,9... | collective-permute-start | bytes 786440 | tf_op jit(solution)/shard_map/ppermute | solution.py:708
  415.2 10.9 %collective-permute-start.24 = (bf16[256,512]{1,0:T(8,128)(2,1)S(1)}, bf16[256,512]{1,0:T(8,128)(2,1)}, u32[]{:S(2)}, u32[]{:S(2)}) collective-permute-start(bf16[256,512]{1,0:T(8,128)(2,1)S(1)} %add_convert_fusion.2.a0_ref), channel_id=1, source_target_pairs={{0,2},{1,3},{2,0},{3,1},{4,6},{5,7},{6,4},{7,5},{8,10},{9,11},{10,... | collective-permute-start | bytes 786440 | tf_op jit(solution)/shard_map/ppermute | solution.py:708
  415.3 14.5 %collective-permute-start.25 = (bf16[256,512]{1,0:T(8,128)(2,1)S(1)}, bf16[256,512]{1,0:T(8,128)(2,1)}, u32[]{:S(2)}, u32[]{:S(2)}) collective-permute-start(bf16[256,512]{1,0:T(8,128)(2,1)S(1)} %add_convert_fusion.2.a0_ref), channel_id=1, source_target_pairs={{0,1},{1,2},{2,3},{3,0},{4,5},{5,6},{6,7},{7,4},{8,9},{9,10},{10,1... | collective-permute-start | bytes 786440 | tf_op jit(solution)/shard_map/ppermute | solution.py:708
  421.6 31.6 %copy-start = (bf16[32,64,512]{2,1,0:T(8,128)(2,1)}, bf16[32,64,512]{2,1,0:T(8,128)(2,1)S(1)}, u32[]{:S(2)}) copy-start(bf16[32,64,512]{2,1,0:T(8,128)(2,1)S(1)} %all-to-all-done.4) | copy-start | bytes 6291460
  453.2 8.2 %collective-permute-start.32 = (bf16[16,64,2240]{2,1,0:T(8,128)(2,1)}, bf16[16,64,2240]{2,1,0:T(8,128)(2,1)S(1)}, u32[]{:S(2)}, u32[]{:S(2)}) collective-permute-start(bf16[16,64,2240]{2,1,0:T(8,128)(2,1)} %get-tuple-element.148), channel_id=1, source_target_pairs={{0,4},{4,0},{8,12},{12,8},{16,20},{20,16},{24,28},{28,24},{32,36},... | collective-permute-start | bytes 13762568 | tf_op jit(solution)/shard_map/ppermute | solution.py:1011
  467.4 7.4 %copy-start.29 = (bf16[256,512]{1,0:T(8,128)(2,1)S(1)}, bf16[256,512]{1,0:T(8,128)(2,1)}, u32[]{:S(2)}) copy-start(bf16[256,512]{1,0:T(8,128)(2,1)} %get-tuple-element.123) | copy-start | bytes 786436
  467.4 9.3 %copy-start.28 = (bf16[256,512]{1,0:T(8,128)(2,1)S(1)}, bf16[256,512]{1,0:T(8,128)(2,1)}, u32[]{:S(2)}) copy-start(bf16[256,512]{1,0:T(8,128)(2,1)} %get-tuple-element.124) | copy-start | bytes 786436
  467.4 10.7 %copy-start.33 = (bf16[256,512]{1,0:T(8,128)(2,1)S(1)}, bf16[256,512]{1,0:T(8,128)(2,1)}, u32[]{:S(2)}) copy-start(bf16[256,512]{1,0:T(8,128)(2,1)} %get-tuple-element.144) | copy-start | bytes 786436
  467.4 11.8 %copy-start.32 = (bf16[256,512]{1,0:T(8,128)(2,1)S(1)}, bf16[256,512]{1,0:T(8,128)(2,1)}, u32[]{:S(2)}) copy-start(bf16[256,512]{1,0:T(8,128)(2,1)} %get-tuple-element.145) | copy-start | bytes 786436
  467.4 23.4 %copy-start.31 = (bf16[256,512]{1,0:T(8,128)(2,1)S(1)}, bf16[256,512]{1,0:T(8,128)(2,1)}, u32[]{:S(2)}) copy-start(bf16[256,512]{1,0:T(8,128)(2,1)} %get-tuple-element.146) | copy-start | bytes 786436
  467.4 79.1 %all-to-all-start.5 = ((bf16[16,64,2240]{2,1,0:T(8,128)(2,1)}), bf16[16,64,2240]{2,1,0:T(8,128)(2,1)}, u32[]{:S(2)}, u32[]{:S(2)}) async-start(bf16[16,64,2240]{2,1,0:T(8,128)(2,1)} %add_convert_fusion), calls=%async_computation.7 | async-start | bytes 9437184 | tf_op jit(solution)/shard_map/all_to_all | solution.py:1013
  474.7 28.3 %copy-start.8 = (f32[256,512]{1,0:T(8,128)S(1)}, f32[256,512]{1,0:T(8,128)}, u32[]{:S(2)}) copy-start(f32[256,512]{1,0:T(8,128)} %get-tuple-element.143) | copy-start | bytes 1572868
  474.7 16.1 %collective-permute-start.14 = (bf16[256,512]{1,0:T(8,128)(2,1)S(1)}, bf16[256,512]{1,0:T(8,128)(2,1)S(1)}, u32[]{:S(2)}, u32[]{:S(2)}) collective-permute-start(bf16[256,512]{1,0:T(8,128)(2,1)S(1)} %copy-done.30), channel_id=1, source_target_pairs={{0,1},{1,2},{2,3},{3,0},{4,5},{5,6},{6,7},{7,4},{8,9},{9,10},{10,1... | collective-permute-start | bytes 786440 | tf_op jit(solution)/shard_map/ppermute | solution.py:708
  474.8 16.0 %collective-permute-start.15 = (bf16[256,512]{1,0:T(8,128)(2,1)S(1)}, bf16[256,512]{1,0:T(8,128)(2,1)S(1)}, u32[]{:S(2)}, u32[]{:S(2)}) collective-permute-start(bf16[256,512]{1,0:T(8,128)(2,1)S(1)} %copy-done.29), channel_id=1, source_target_pairs={{0,2},{1,3},{2,0},{3,1},{4,6},{5,7},{6,4},{7,5},{8,10},{9,11},{10,... | collective-permute-start | bytes 786440 | tf_op jit(solution)/shard_map/ppermute | solution.py:708
  476.7 15.1 %collective-permute-start.16 = (bf16[256,512]{1,0:T(8,128)(2,1)S(1)}, bf16[256,512]{1,0:T(8,128)(2,1)S(1)}, u32[]{:S(2)}, u32[]{:S(2)}) collective-permute-start(bf16[256,512]{1,0:T(8,128)(2,1)S(1)} %copy-done.28), channel_id=1, source_target_pairs={{0,3},{1,0},{2,1},{3,2},{4,7},{5,4},{6,5},{7,6},{8,11},{9,8},{10,9... | collective-permute-start | bytes 786440 | tf_op jit(solution)/shard_map/ppermute | solution.py:708
  478.1 22.8 %collective-permute-start.26 = (bf16[256,512]{1,0:T(8,128)(2,1)S(1)}, bf16[256,512]{1,0:T(8,128)(2,1)S(1)}, u32[]{:S(2)}, u32[]{:S(2)}) collective-permute-start(bf16[256,512]{1,0:T(8,128)(2,1)S(1)} %copy-done.33), channel_id=1, source_target_pairs={{0,1},{1,2},{2,3},{3,0},{4,5},{5,6},{6,7},{7,4},{8,9},{9,10},{10,1... | collective-permute-start | bytes 786440 | tf_op jit(solution)/shard_map/ppermute | solution.py:708
  479.2 21.7 %collective-permute-start.27 = (bf16[256,512]{1,0:T(8,128)(2,1)S(1)}, bf16[256,512]{1,0:T(8,128)(2,1)S(1)}, u32[]{:S(2)}, u32[]{:S(2)}) collective-permute-start(bf16[256,512]{1,0:T(8,128)(2,1)S(1)} %copy-done.32), channel_id=1, source_target_pairs={{0,2},{1,3},{2,0},{3,1},{4,6},{5,7},{6,4},{7,5},{8,10},{9,11},{10,... | collective-permute-start | bytes 786440 | tf_op jit(solution)/shard_map/ppermute | solution.py:708
  490.8 12.2 %collective-permute-start.28 = (bf16[256,512]{1,0:T(8,128)(2,1)S(1)}, bf16[256,512]{1,0:T(8,128)(2,1)S(1)}, u32[]{:S(2)}, u32[]{:S(2)}) collective-permute-start(bf16[256,512]{1,0:T(8,128)(2,1)S(1)} %copy-done.31), channel_id=1, source_target_pairs={{0,3},{1,0},{2,1},{3,2},{4,7},{5,4},{6,5},{7,6},{8,11},{9,8},{10,9... | collective-permute-start | bytes 786440 | tf_op jit(solution)/shard_map/ppermute | solution.py:708
  496.1 12.5 %collective-permute-start.17 = (bf16[256,512]{1,0:T(8,128)(2,1)}, bf16[256,512]{1,0:T(8,128)(2,1)S(1)}, u32[]{:S(2)}, u32[]{:S(2)}) collective-permute-start(bf16[256,512]{1,0:T(8,128)(2,1)} %routed.1.a0_ref), channel_id=1, source_target_pairs={{0,3},{1,0},{2,1},{3,2},{4,7},{5,4},{6,5},{7,6},{8,11},{9,8},{10,9... | collective-permute-start | bytes 786440 | tf_op jit(solution)/shard_map/ppermute | solution.py:708
  498.8 51.8 %collective-permute-start.18 = (bf16[256,512]{1,0:T(8,128)(2,1)}, bf16[256,512]{1,0:T(8,128)(2,1)S(1)}, u32[]{:S(2)}, u32[]{:S(2)}) collective-permute-start(bf16[256,512]{1,0:T(8,128)(2,1)} %routed.1.a0_ref), channel_id=1, source_target_pairs={{0,2},{1,3},{2,0},{3,1},{4,6},{5,7},{6,4},{7,5},{8,10},{9,11},{10,... | collective-permute-start | bytes 786440 | tf_op jit(solution)/shard_map/ppermute | solution.py:708
  500.9 52.8 %collective-permute-start.19 = (bf16[256,512]{1,0:T(8,128)(2,1)}, bf16[256,512]{1,0:T(8,128)(2,1)S(1)}, u32[]{:S(2)}, u32[]{:S(2)}) collective-permute-start(bf16[256,512]{1,0:T(8,128)(2,1)} %routed.1.a0_ref), channel_id=1, source_target_pairs={{0,1},{1,2},{2,3},{3,0},{4,5},{5,6},{6,7},{7,4},{8,9},{9,10},{10,1... | collective-permute-start | bytes 786440 | tf_op jit(solution)/shard_map/ppermute | solution.py:708
  503.1 58.3 %copy-start.6 = (bf16[256,512]{1,0:T(8,128)(2,1)}, bf16[256,512]{1,0:T(8,128)(2,1)S(1)}, u32[]{:S(2)}) copy-start(bf16[256,512]{1,0:T(8,128)(2,1)S(1)} %add_convert_fusion.1.a0_ref) | copy-start | bytes 786436
  503.2 52.4 %collective-permute-start.29 = (bf16[256,512]{1,0:T(8,128)(2,1)S(1)}, bf16[256,512]{1,0:T(8,128)(2,1)S(1)}, u32[]{:S(2)}, u32[]{:S(2)}) collective-permute-start(bf16[256,512]{1,0:T(8,128)(2,1)S(1)} %add_convert_fusion.1.a0_ref), channel_id=1, source_target_pairs={{0,3},{1,0},{2,1},{3,2},{4,7},{5,4},{6,5},{7,6},{8,11},{9,8},{10,9... | collective-permute-start | bytes 786440 | tf_op jit(solution)/shard_map/ppermute | solution.py:708
  504.6 56.8 %collective-permute-start.30 = (bf16[256,512]{1,0:T(8,128)(2,1)S(1)}, bf16[256,512]{1,0:T(8,128)(2,1)S(1)}, u32[]{:S(2)}, u32[]{:S(2)}) collective-permute-start(bf16[256,512]{1,0:T(8,128)(2,1)S(1)} %add_convert_fusion.1.a0_ref), channel_id=1, source_target_pairs={{0,2},{1,3},{2,0},{3,1},{4,6},{5,7},{6,4},{7,5},{8,10},{9,11},{10,... | collective-permute-start | bytes 786440 | tf_op jit(solution)/shard_map/ppermute | solution.py:708
  508.6 49.5 %copy-start.20 = (bf16[256,512]{1,0:T(8,128)(2,1)}, bf16[256,512]{1,0:T(8,128)(2,1)S(1)}, u32[]{:S(2)}) copy-start(bf16[256,512]{1,0:T(8,128)(2,1)S(1)} %collective-permute-done.17.a1_ref) | copy-start | bytes 786436
  508.6 52.8 %collective-permute-start.31 = (bf16[256,512]{1,0:T(8,128)(2,1)S(1)}, bf16[256,512]{1,0:T(8,128)(2,1)S(1)}, u32[]{:S(2)}, u32[]{:S(2)}) collective-permute-start(bf16[256,512]{1,0:T(8,128)(2,1)S(1)} %add_convert_fusion.1.a0_ref), channel_id=1, source_target_pairs={{0,1},{1,2},{2,3},{3,0},{4,5},{5,6},{6,7},{7,4},{8,9},{9,10},{10,1... | collective-permute-start | bytes 786440 | tf_op jit(solution)/shard_map/ppermute | solution.py:708
  550.6 7.5 %copy-start.21 = (bf16[256,512]{1,0:T(8,128)(2,1)}, bf16[256,512]{1,0:T(8,128)(2,1)S(1)}, u32[]{:S(2)}) copy-start(bf16[256,512]{1,0:T(8,128)(2,1)S(1)} %collective-permute-done.18.a2_ref) | copy-start | bytes 786436
  550.6 16.6 %collective-permute-start.33 = (f32[64,640]{1,0:T(8,128)}, f32[64,640]{1,0:T(8,128)S(1)}, u32[]{:S(2)}, u32[]{:S(2)}) collective-permute-start(f32[64,640]{1,0:T(8,128)} %get-tuple-element.149.own_ref), channel_id=1, source_target_pairs={{0,1},{1,2},{2,3},{3,0},{4,5},{5,6},{6,7},{7,4},{8,9},{9,10},{10,1... | collective-permute-start | bytes 491528 | tf_op jit(solution)/shard_map/ppermute | solution.py:708
  553.7 13.5 %collective-permute-start.34 = (f32[64,640]{1,0:T(8,128)}, f32[64,640]{1,0:T(8,128)S(1)}, u32[]{:S(2)}, u32[]{:S(2)}) collective-permute-start(f32[64,640]{1,0:T(8,128)} %get-tuple-element.149.own_ref), channel_id=1, source_target_pairs={{0,2},{1,3},{2,0},{3,1},{4,6},{5,7},{6,4},{7,5},{8,10},{9,11},{10,... | collective-permute-start | bytes 491528 | tf_op jit(solution)/shard_map/ppermute | solution.py:708
  555.6 11.6 %collective-permute-start.35 = (f32[64,640]{1,0:T(8,128)}, f32[64,640]{1,0:T(8,128)S(1)}, u32[]{:S(2)}, u32[]{:S(2)}) collective-permute-start(f32[64,640]{1,0:T(8,128)} %get-tuple-element.149.own_ref), channel_id=1, source_target_pairs={{0,3},{1,0},{2,1},{3,2},{4,7},{5,4},{6,5},{7,6},{8,11},{9,8},{10,9... | collective-permute-start | bytes 491528 | tf_op jit(solution)/shard_map/ppermute | solution.py:708
  (16 other events, 40.0 us)
Sparse Core Ops, SparseCore 0:
  13.4 76.2 all-gather.2
  92.0 53.7 all-gather.4
  242.1 50.0 reduce-scatter.3
  294.6 49.4 reduce-scatter.5
  382.6 92.6 reduce-scatter.7

commit v2 on v1

--- a/solution.py
+++ b/solution.py
@@ -447,28 +447,33 @@
     )(*first, *second)
 
 
+def slot_probs(t_ref, b_ref, index, width):
+    owners, capacity, _ = b_ref.shape
+    rows = owners * capacity
+    beside = b_ref[:, :, width:].reshape(rows, LANES).astype(F32)
+    lane = lax.broadcasted_iota(jnp.int32, (rows, LANES), 1)
+    expert = 2 * (lax.broadcasted_iota(jnp.int32, (rows, LANES), 0) // capacity) + index
+    spread = jnp.where(lane == expert + ROPE, beside[:, 0:1], 0.0) + jnp.where(
+        lane == expert, beside[:, 1:2], 0.0
+    )
+    return dot_nn(t_ref[...], spread.astype(BF16))
+
+
+def combine_first_kernel(t_ref, b_ref, shared_ref, sum_ref, probs_ref):
+    owners, capacity, _ = b_ref.shape
+    width = shared_ref.shape[1]
+    probs_ref[...] = slot_probs(t_ref, b_ref, 0, width)
+    sum_ref[...] = shared_ref[...] + dot_nn(t_ref[...], b_ref[:, :, :width].reshape(owners * capacity, width))
+
+
 def combine_kernel(
-    me_ref, t0_ref, t1_ref, b0_ref, b1_ref, shared_ref, own_ref, probs_ref, send1_ref, send2_ref, send3_ref
+    me_ref, t_ref, b_ref, sum_ref, first_probs_ref, own_ref, probs_ref, send1_ref, send2_ref, send3_ref
 ):
-    owners, capacity, _ = b0_ref.shape
+    owners, capacity, _ = b_ref.shape
     rows = owners * capacity
-    width = shared_ref.shape[1]
+    width = sum_ref.shape[1]
     piece = own_ref.shape[1]
-    me = me_ref[0]
-    t0, t1 = t0_ref[...], t1_ref[...]
-    lane = lax.broadcasted_iota(jnp.int32, (rows, LANES), 1)
-    owner = lax.broadcasted_iota(jnp.int32, (rows, LANES), 0) // capacity
-    spreads = []
-    for index, b_ref in ((0, b0_ref), (1, b1_ref)):
-        beside = b_ref[:, :, width:].reshape(rows, LANES).astype(F32)
-        expert = 2 * owner + index
-        spreads.append(
-            (
-                jnp.where(lane == expert + ROPE, beside[:, 0:1], 0.0)
-                + jnp.where(lane == expert, beside[:, 1:2], 0.0)
-            ).astype(BF16)
-        )
-    probs = dot_nn(t0, spreads[0]) + dot_nn(t1, spreads[1])
+    probs = first_probs_ref[...] + slot_probs(t_ref, b_ref, 1, width)
     probs = probs + pltpu.roll(probs, ROPE, 1)
     probs_ref[...] = probs
     high = probs.astype(BF16)
@@ -476,12 +481,8 @@
     short = lax.broadcasted_iota(jnp.int32, probs.shape, 1)
     message = jnp.where(short >= ROPE, high.astype(F32), low.astype(F32)).astype(BF16)
     for step, out_ref in enumerate((own_ref, send1_ref, send2_ref, send3_ref)):
-        place = block_at(me, step, width // piece, piece)
-        part = (
-            dot_nn(t0, b0_ref[:, :, place].reshape(rows, piece))
-            + dot_nn(t1, b1_ref[:, :, place].reshape(rows, piece))
-            + shared_ref[:, place]
-        )
+        place = block_at(me_ref[0], step, width // piece, piece)
+        part = sum_ref[:, place] + dot_nn(t_ref[...], b_ref[:, :, place].reshape(rows, piece))
         if step == 0:
             own_ref[...] = part
         else:
@@ -803,7 +804,6 @@
     )
     pack_two = jnp.concatenate([shared_gate, shared_up, shared_down.T], axis=1)
     one = lax.all_gather(pack_one, "expert", axis=0, tiled=True)
-    two = lax.all_gather(pack_two, "expert", axis=0, tiled=True)
 
     position = jnp.arange(tokens).astype(F32)
     exponent = jnp.arange(ROPE // 2).astype(F32) * (2.0 / ROPE)
@@ -826,8 +826,6 @@
         name="routing",
     )
 
-    cot_own = exchange(cot_out)
-    cot_before, cot_after = ring_first(cot_own)
     (
         own,
         send1,
@@ -861,14 +859,14 @@
             ((8, width), F32),
             ((8, LATENT), F32),
         ],
-        [after(me, cot_own), stream, one, segment_ids, segment_ids.T, cosine, sine],
+        [me, stream, one, segment_ids, segment_ids.T, cosine, sine],
         2 * tokens * width * outer,
         places=smem,
         name="attend",
     )
+    cot_own = exchange(after(cot_out, own))
     got = send_blocks([send1, send2, send3])
     attention = (own + got[0].astype(F32) + got[1].astype(F32) + got[2].astype(F32)).astype(BF16)
-    attention = after(attention, cot_before, cot_after)
     middle, mixed, x_out = run(
         dispatch_kernel,
         [
@@ -881,11 +879,25 @@
         places=smem,
         name="dispatch",
     )
-    x_in = exchange(x_out)
+    cot_before, cot_after = ring_first(after(cot_own, mixed))
+    x_in = exchange(after(x_out, cot_own))
     cots = ring_second(cot_own, cot_before, cot_after)
     x1s = x_in[:, :, width:]
     x1_before, x1_after = ring_first(x1s)
     x1s = [x_in] + ring_second(x1s, x1_before, x1_after)[1:]
+    gate_t = expert_gate.transpose(0, 2, 1)
+    up_t = expert_up.transpose(0, 2, 1)
+    chunk = owners // 2
+    back0, c0, hg0, gr0, ur0 = expert_back(
+        False, me, base, [x_in], cots, gate_t, up_t, expert_down, one, edge // LANES - 1, chunk // 2
+    )
+    out0 = expert_out(0, hg0, expert_down, owners, tensors, chunk)
+    two = lax.all_gather(after(pack_two, out0, x1_before, x1_after), "expert", axis=0, tiled=True)
+    back0 = exchange(back0)
+    back1, c1, hg1, gr1, ur1, x1 = expert_back(
+        True, me, after(base, hg0), x1s, cots, gate_t, up_t, expert_down, one, edge // LANES - 1, chunk // 2
+    )
+    back1 = exchange(after(back1, back0))
     router_block = one[:, queries + LATENT : edge]
     (
         shared_own,
@@ -906,36 +918,29 @@
             ((tokens, LANES), F32),
             ((width, 3 * hidden_columns), BF16),
         ],
-        [me, mixed, cot_low, two, router_block],
+        [after(me, hg1), mixed, cot_low, two, router_block],
         18 * tokens * width * hidden_columns,
         places=smem,
         name="shared",
     )
-    base = after(base, shared_back)
-
-    gate_t = expert_gate.transpose(0, 2, 1)
-    up_t = expert_up.transpose(0, 2, 1)
-    chunk = owners // 2
-    back0, c0, hg0, gr0, ur0 = expert_back(
-        False, me, base, [x_in], cots, gate_t, up_t, expert_down, one, edge // LANES - 1, chunk // 2
-    )
-    back0 = exchange(back0)
-    back1, c1, hg1, gr1, ur1, x1 = expert_back(
-        True, me, after(base, hg0), x1s, cots, gate_t, up_t, expert_down, one, edge // LANES - 1, chunk // 2
-    )
-    back1 = exchange(after(back1, back0))
+
     gr0 = after(gr0, back0)
     gate_grad, up_grad, down_grad = expert_grads(
         (x_in, c0, hg0, gr0, ur0), (x1, c1, hg1, gr1, ur1), tensors
     )
-    out0 = expert_out(0, hg0, expert_down, owners, tensors, chunk)
     out1 = expert_out(1, after(hg1, out0), expert_down, owners, tensors, chunk)
     out_rows = [
         lax.psum_scatter(out, "tensor", scatter_dimension=0, tiled=True).reshape(owners, 1, capacity, piece)
         for out in (out0, out1)
     ]
 
-    out_rows = exchange(after(jnp.concatenate(out_rows, axis=1), back1, gate_grad))
+    first_sum, first_probs = run(
+        combine_first_kernel,
+        [((tokens, width), F32), ((tokens, LANES), F32)],
+        [t0, back0, shared_back],
+        2 * tokens * rows * width,
+        name="combine_first",
+    )
     own, probs_own, send1, send2, send3 = run(
         combine_kernel,
         [
@@ -945,8 +950,8 @@
             ((tokens, piece + LANES), BF16),
             ((tokens, piece + LANES), BF16),
         ],
-        [after(me, out1, gate_grad), t0, t1, back0, back1, shared_back],
-        2 * tokens * rows * (width + piece),
+        [after(me, out1, gate_grad), t1, back1, first_sum, first_probs],
+        2 * tokens * rows * width,
         places=smem,
         name="combine",
     )
@@ -960,6 +965,8 @@
         + got[1][:, :piece].astype(F32)
         + got[2][:, :piece].astype(F32)
     ).astype(BF16)
+    mixed_sums = share_small(mixed_sum)
+    out_rows = exchange(after(jnp.concatenate(out_rows, axis=1), *mixed_sums[1:]))
     keep, passed, middle_grad, own, send1, send2, send3 = run(
         attend_back_kernel,
         [
@@ -972,12 +979,12 @@
             ((tokens, piece), BF16),
         ],
         [
-            after(me, out_rows),
+            me,
             core,
             stream,
             cotangent,
             middle,
-            *share_small(mixed_sum),
+            *mixed_sums,
             *got,
             probs_own,
             router_probs,
@@ -1008,7 +1015,7 @@
         out_places={0: pl.ANY, 1: pl.ANY},
         name="attend_back",
     )
-    paired = lax.ppermute(passed, "expert", [(i, i ^ 1) for i in range(owners)])
+    paired = lax.ppermute(after(passed, out_rows), "expert", [(i, i ^ 1) for i in range(owners)])
     paired = (keep.astype(F32) + paired.astype(F32)).astype(BF16)
     parts = lax.all_to_all(
         paired,
@@ -1017,26 +1024,6 @@
         concat_axis=0,
         tiled=True,
         axis_index_groups=[[2 * i + c for i in range(owners // 2)] for c in range(2)],
-    )
-    query_grad, late, output_grad, latent_up_grad, router_grad = run(
-        unpack_kernel,
-        [
-            (query_proj.shape, F32),
-            ((shard, edge - queries), F32),
-            ((shard, heads * VDIM), F32),
-            (latent_up.shape, F32),
-            (router_proj.shape, F32),
-        ],
-        [parts],
-        0,
-        name="unpack",
-    )
-    latent_down_grad, gain_grads = run(
-        late_kernel,
-        [(latent_down.shape, F32), ((8, LANES), F32)],
-        [late, *(shift(late, step) for step in range(1, tensors))],
-        0,
-        name="late",
     )
     got = send_blocks([send1, send2, send3])
     first_sum = (own + got[0].astype(F32) + got[1].astype(F32) + got[2].astype(F32)).astype(BF16)
@@ -1068,6 +1055,30 @@
     )
 
     shared_sum = shared_sum.astype(F32)
+    gate_sum = shared_sum[:, :hidden_columns]
+    up_sum = shared_sum[:, hidden_columns : 2 * hidden_columns]
+    down_sum = shared_sum[:, 2 * hidden_columns :]
+    parts = after(parts, stream_grad, result, gate_sum, up_sum, down_sum)
+    query_grad, late, output_grad, latent_up_grad, router_grad = run(
+        unpack_kernel,
+        [
+            (query_proj.shape, F32),
+            ((shard, edge - queries), F32),
+            ((shard, heads * VDIM), F32),
+            (latent_up.shape, F32),
+            (router_proj.shape, F32),
+        ],
+        [parts],
+        0,
+        name="unpack",
+    )
+    latent_down_grad, gain_grads = run(
+        late_kernel,
+        [(latent_down.shape, F32), ((8, LANES), F32)],
+        [late, *(shift(late, step) for step in range(1, tensors))],
+        0,
+        name="late",
+    )
     return (
         result,
         stream_grad,
@@ -1079,9 +1090,9 @@
         output_grad.T,
         gain_grads[1, :shard],
         router_grad,
-        shared_sum[:, :hidden_columns],
-        shared_sum[:, hidden_columns : 2 * hidden_columns],
-        shared_sum[:, 2 * hidden_columns :].T,
+        gate_sum,
+        up_sum,
+        down_sum.T,
         gate_grad.transpose(0, 2, 1),
         up_grad.transpose(0, 2, 1),
         down_grad,

time: 592 us -> 697 us (1.18)
  waiting for transfers between devices: 252 us -> 373 us
  blocking collectives: 40 us -> 0 us
  starting transfers between devices: 82.7 us -> 103 us
    reduce_scatter x2, waiting for transfers between devices: 0.04 us -> 55.7 us  [per_device(): lax.psum_scatter(out, 'tensor', scatter_dimension=0, tiled=True)]
    ppermute x35, waiting for transfers between devices: 102 us -> 153 us  [shift(): lax.ppermute(array, 'tensor', [(i, (i + step) % size) for i in range(size)])]
    reduce_scatter x1, waiting for transfers between devices: 0.01 us -> 47.1 us  [per_device(): lax.psum_scatter(after(shared_grads, own), 'expert', scatter_dimension=0,...]
    all_to_all x4 -> x5, waiting for transfers between devices: 79.7 us -> 38.1 us  [exchange(): lax.all_to_all(rows.reshape(shape[0], -1, shape[-1]), 'expert', split_axi...]
    all_to_all x1 -> x0, blocking collectives: 40 us -> none  [exchange(): lax.all_to_all(rows.reshape(shape[0], -1, shape[-1]), 'expert', split_axi...]
    all_to_all x1, waiting for transfers between devices: 37.9 us -> 0.01 us  [per_device(): lax.all_to_all(paired, 'expert', split_axis=0, concat_axis=0, tiled=True,...]
    all_gather x1, waiting for transfers between devices: 23.8 us -> 50 us  [per_device(): one = lax.all_gather(pack_one, 'expert', axis=0, tiled=True)]
    all_gather x1, waiting for transfers between devices: 0.01 us -> 20.4 us  [per_device(): lax.all_gather(after(pack_two, out0, x1_before, x1_after), 'expert', axis...]
  transfers between devices with their start and end apart: 46 -> 47, of which waited for: 26 -> 25; matrix products, arithmetic and copies ran while one was open for 5% -> 3% of each run, Pallas kernels for 26% -> 20%
where the time goes in v2:
time: 697 us; the launch traced here: 687 us
  waiting for transfers between devices  373 us (54%)
  Pallas kernels  156 us (22%)
  starting transfers between devices  103 us (15%)
  local copies, waits for them, and re-layouts  30.5 us (4%)
  between operations  14.8 us (2%)
  other arithmetic  9.42 us (1%)
    ppermute x35, waiting for transfers between devices, shift(): lax.ppermute(array, 'tensor', [(i, (i + step) % size) for i in range(size)])  153 us
    pallas_call x12, Pallas kernels, run(): pl.pallas_call(kernel, in_specs=in_specs, out_specs=out_specs, out_shape=...  92.7 us
    reduce_scatter x2, waiting for transfers between devices, per_device(): lax.psum_scatter(out, 'tensor', scatter_dimension=0, tiled=True)  55.7 us
    ppermute x35, starting transfers between devices, shift(): lax.ppermute(array, 'tensor', [(i, (i + step) % size) for i in range(size)])  52.4 us
    all_gather x1, waiting for transfers between devices, per_device(): one = lax.all_gather(pack_one, 'expert', axis=0, tiled=True)  50 us
    reduce_scatter x1, waiting for transfers between devices, per_device(): lax.psum_scatter(after(shared_grads, own), 'expert', scatter_dimension=0,...  47.1 us
    all_to_all x5, waiting for transfers between devices, exchange(): lax.all_to_all(rows.reshape(shape[0], -1, shape[-1]), 'expert', split_axi...  38.1 us
    all_to_all x5, starting transfers between devices, exchange(): lax.all_to_all(rows.reshape(shape[0], -1, shape[-1]), 'expert', split_axi...  37 us
  transfers between devices with their start and end apart: 47, of which 25 were waited for; matrix products, arithmetic and copies ran while one was open for 3% of the time, Pallas kernels for 20%

profile of v2, /device:TPU:0, one launch (start us, length us, event | category | flops | bytes accessed | tf_op | source)
XLA Modules:
  0.0 687.3 jit_solution(10823343812376901007)
XLA Ops:
  11.5 1.7 concatenate.18
  16.7 4.7 routing.1
  21.4 50.0 %all-gather.3.cloned.1.call-done.w_ref.refs_10_.refs_13_ = bf16[2048,2240]{1,0:T(8,128)(2,1)} async-done(((bf16[64,2240]{1,0:T(8,128)(2,1)}), bf16[2048,2240]{1,0:T(8,128)(2,1)}) %all-gather.3.cloned.1.call-update) | async-done | bytes 9175056 | tf_op jit(solution)/shard_map/all_gather | solution.py:806
  71.4 11.0 %attend.1 = (f32[256,512]{1,0:T(8,128)}, bf16[256,512]{1,0:T(8,128)(2,1)}, bf16[256,512]{1,0:T(8,128)(2,1)}, bf16[256,512]{1,0:T(8,128)(2,1)}, bf16[256,2048]{1,...) custom-call(s32[1]{0:T(128)} %bitcast.me_ref.refs_0_, ...), custom_call_target="tpu_custom_call" | custom-call | flops 201326592 | bytes 1627136 | tf_op jit(solution)/shard_map/attend/pallas_call | solution.py:81
  82.5 5.6 all-to-all-start
  88.1 1.6 collective-permute-start
  89.7 2.7 collective-permute-start.1
  93.8 4.0 collective-permute-done
  97.9 6.6 collective-permute-done.1
  104.6 2.4 collective-permute-start.3
  108.8 9.6 %collective-permute-done.3.a1_ref = bf16[256,512]{1,0:T(8,128)(2,1)S(1)} collective-permute-done((bf16[256,512]{1,0:T(8,128)(2,1)S(1)}, bf16[256,512]{1,0:T(8,128)(2,1)S(1)}, u32[]{:S(2)}, u32[]{:S(2)}) %collective-permute-start.3) | collective-permute-done | bytes 262176 | tf_op jit(solution)/shard_map/ppermute | solution.py:709
  118.4 3.6 collective-permute-done.5.a3_ref
  122.6 6.6 dispatch.1
  129.2 7.4 %all-to-all-start.1 = ((bf16[32,32,2560]{2,1,0:T(8,128)(2,1)}), bf16[32,32,2560]{2,1,0:T(8,128)(2,1)}, u32[]{:S(2)}, u32[]{:S(2)}) async-start(bf16[32,32,2560]{2,1,0:T(8,128)(2,1)} %get-tuple-element.104), calls=%async_computation.1 | async-start | bytes 10485760 | tf_op jit(solution)/shard_map/all_to_all | solution.py:737
  136.8 3.2 collective-permute-start.6
  140.0 45.7 %collective-permute-done.7.refs_6_.refs_9_ = bf16[32,2,32,512]{3,2,1,0:T(8,128)(2,1)S(1)} collective-permute-done((bf16[32,2,32,512]{3,2,1,0:T(8,128)(2,1)S(1)}, bf16[32,2,32,512]{3,2,1,0:T(8,128)(2,1)S(1)}, u32[]{:S(2)}, u32[]{:S(2)}) %collective-permute-start.7) | collective-permute-done | bytes 2097184 | tf_op jit(solution)/shard_map/ppermute | solution.py:709
  188.7 2.7 collective-permute-start.9
  192.3 20.6 %collective-permute-done.8 = bf16[16,2,32,512]{3,2,1,0:T(8,128)(2,1)S(1)} collective-permute-done((bf16[16,2,32,512]{3,2,1,0:T(8,128)(2,1)}, bf16[16,2,32,512]{3,2,1,0:T(8,128)(2,1)S(1)}, u32[]{:S(2)}, u32[]{:S(2)}) %collective-permute-start.8) | collective-permute-done | bytes 1048608 | tf_op jit(solution)/shard_map/ppermute | solution.py:709
  216.2 3.1 collective-permute-start.10
  219.3 16.3 %expert_back.2 = (bf16[32,32,2176]{2,1,0:T(8,128)(2,1)}, bf16[32,32,2048]{2,1,0:T(8,128)(2,1)}, bf16[1024,352]{1,0:T(8,128)(2,1)}, bf16[1024,352]{1,0:T(8,128)(2,1)}, bf16[1024,352]{1,0:T(8,128)(2,1)}) custom-call(s32[1]{0:T(128)} %bitcast.me_ref.refs_0_, s32[1]{0:T(128)} %bitcast.11.refs_1_, bf16[32,32,2560]{2,1,0:T(8,128)(2,1)} %all-to-all-done.1.refs_2_.x0_ref, ...), custom_call_target="tpu_custom_call" | custom-call | flops 73819750400 | bytes 25165824 | tf_op jit(solution)/shard_map/expert_back/pallas_call | solution.py:357
  235.6 5.5 expert_out.2
  241.1 2.5 collective-permute-done.11.refs_5_
  244.8 3.3 collective-permute-start.13
  248.1 7.2 %all-to-all-start.2 = ((bf16[32,32,2176]{2,1,0:T(8,128)(2,1)}), bf16[32,32,2176]{2,1,0:T(8,128)(2,1)}, u32[]{:S(2)}, u32[]{:S(2)}) async-start(bf16[32,32,2176]{2,1,0:T(8,128)(2,1)} %get-tuple-element.113), calls=%async_computation.4 | async-start | bytes 8912896 | tf_op jit(solution)/shard_map/all_to_all | solution.py:737
  257.9 16.8 %expert_back.3 = (bf16[32,32,2176]{2,1,0:T(8,128)(2,1)}, bf16[32,32,2048]{2,1,0:T(8,128)(2,1)}, bf16[1024,352]{1,0:T(8,128)(2,1)}, bf16[1024,352]{1,0:T(8,128)(2...) custom-call(s32[1]{0:T(128)} %bitcast.me_ref.refs_0_, s32[1]{0:T(128)} %bitcast.11.refs_1_, ...), custom_call_target="tpu_custom_call" | custom-call | flops 73819750400 | bytes 25165824 | tf_op jit(solution)/shard_map/expert_back/pallas_call | solution.py:357
  274.7 5.4 expert_out.3
  280.1 32.7 %all-to-all-done.2.b_ref = bf16[32,32,2176]{2,1,0:T(8,128)(2,1)} async-done(((bf16[32,32,2176]{2,1,0:T(8,128)(2,1)}), bf16[32,32,2176]{2,1,0:T(8,128)(2,1)}, u32[]{:S(2)}, u32[]{:S(2)}) %all-to-all-start.2) | async-done | bytes 4456480 | tf_op jit(solution)/shard_map/all_to_all | solution.py:737
  312.7 9.6 %all-to-all-start.3 = ((bf16[32,32,2176]{2,1,0:T(8,128)(2,1)}), bf16[32,32,2176]{2,1,0:T(8,128)(2,1)}, u32[]{:S(2)}, u32[]{:S(2)}) async-start(bf16[32,32,2176]{2,1,0:T(8,128)(2,1)} %get-tuple-element.123), calls=%async_computation.5 | async-start | bytes 8912896 | tf_op jit(solution)/shard_map/all_to_all | solution.py:737
  322.3 8.8 %reduce-scatter.8.cloned.1.call-start = ((), (), s32[]{:S(2)}) async-start(), calls=%async_computation.13 | async-start | bytes 9191424 | tf_op jit(solution)/shard_map/reduce_scatter | solution.py:959
  331.2 1.9 slice.75.router_ref
  333.1 19.4 %expert_grads.1 = (f32[2,352,2048]{2,1,0:T(8,128)}, f32[2,352,2048]{2,1,0:T(8,128)}, f32[2,352,2048]{2,1,0:T(8,128)}) custom-call(bf16[32,32,2560]{2,1,0:T(8,128)(2,1)} %all-to-all-done.1.refs_2_.x0_ref, bf16[32,32,2048]{2,1,0:T(8,128)(2,1)} %get-tuple-element.111.c0_ref, bf16[1024,352]{1,0:T(8,128)(2,1)} %get-tuple-element.107.hg_ref.hg0_ref, ...), custom_call_target="tpu_custom_call" | custom-call | flops 738197504 | bytes 4177920 | tf_op jit(solution)/shard_map/expert_grads/pallas_call | solution.py:436
  352.5 20.4 %all-gather.5.cloned.1.call-done.w_ref = bf16[2048,2112]{1,0:T(8,128)(2,1)} async-done(((bf16[64,2112]{1,0:T(8,128)(2,1)}), bf16[2048,2112]{1,0:T(8,128)(2,1)}) %all-gather.5.cloned.1.call-update) | async-done | bytes 8650768 | tf_op jit(solution)/shard_map/all_gather | solution.py:895
  373.0 16.5 %shared.1 = (f32[256,512]{1,0:T(8,128)}, bf16[256,512]{1,0:T(8,128)(2,1)}, bf16[256,512]{1,0:T(8,128)(2,1)}, bf16[256,512]{1,0:T(8,128)(2,1)}, f32[256,2048]{1,0...) custom-call(s32[1]{0:T(128)} %bitcast.me_ref.refs_0_, bf16[256,2048]{1,0:T(8,128)(2,1)} %get-tuple-element.105.mixed_ref, ...), custom_call_target="tpu_custom_call" | custom-call | flops 664377728 | bytes 2346189 | tf_op jit(solution)/shard_map/shared/pallas_call | solution.py:81
  389.5 6.8 combine_first.1
  396.3 5.6 combine.1
  404.3 3.4 collective-permute-start.15
  409.3 12.3 %collective-permute-done.14.r1_ref = bf16[256,640]{1,0:T(8,128)(2,1)S(1)} collective-permute-done((bf16[256,640]{1,0:T(8,128)(2,1)S(1)}, bf16[256,640]{1,0:T(8,128)(2,1)S(1)}, u32[]{:S(2)}, u32[]{:S(2)}) %collective-permute-start.14) | collective-permute-done | bytes 327712 | tf_op jit(solution)/shard_map/ppermute | solution.py:709
  421.5 15.5 %collective-permute-done.15.r2_ref = bf16[256,640]{1,0:T(8,128)(2,1)S(1)} collective-permute-done((bf16[256,640]{1,0:T(8,128)(2,1)S(1)}, bf16[256,640]{1,0:T(8,128)(2,1)S(1)}, u32[]{:S(2)}, u32[]{:S(2)}) %collective-permute-start.15) | collective-permute-done | bytes 327712 | tf_op jit(solution)/shard_map/ppermute | solution.py:709
  438.4 2.0 collective-permute-start.18
  442.9 54.5 %reduce-scatter.6.cloned.1.call-done = bf16[1,32,32,512]{3,2,1,0:T(8,128)(2,1)} async-done(((bf16[4,32,32,512]{3,2,1,0:T(8,128)(2,1)}), bf16[1,32,32,512]{3,2,1,0:T(8,128)(2,1)}) %reduce-scatter.6.cloned.1.call-update) | async-done | bytes 1048592 | tf_op jit(solution)/shard_map/reduce_scatter | solution.py:933
  497.4 1.7 pad_maximum_fusion
  499.2 1.6 copy.45
  500.8 7.3 %all-to-all-start.4 = ((bf16[32,64,512]{2,1,0:T(8,128)(2,1)}), bf16[32,64,512]{2,1,0:T(8,128)(2,1)S(1)}, u32[]{:S(2)}, u32[]{:S(2)}) async-start(bf16[32,64,512]{2,1,0:T(8,128)(2,1)} %bitcast.44), calls=%async_computation.6 | async-start | bytes 4194304 | tf_op jit(solution)/shard_map/all_to_all | solution.py:737
  508.1 23.5 %attend_back.1 = (bf16[16,64,2240]{2,1,0:T(8,128)(2,1)}, bf16[16,64,2240]{2,1,0:T(8,128)(2,1)}, f32[256,2048]{1,0:T(8,128)}, f32[256,512]{1,0:T(8,128)}, bf16[25...) custom-call(s32[1]{0:T(128)} %bitcast.me_ref.refs_0_, s32[1]{0:T(128)} %bitcast.21.core_ref, ...), custom_call_target="tpu_custom_call" | custom-call | flops 845571712 | bytes 3560244 | tf_op jit(solution)/shard_map/attend_back/pallas_call | solution.py:81
  531.6 5.4 all-to-all-done.4
  537.3 8.4 %collective-permute-done.32 = bf16[16,64,2240]{2,1,0:T(8,128)(2,1)S(1)} collective-permute-done((bf16[16,64,2240]{2,1,0:T(8,128)(2,1)}, bf16[16,64,2240]{2,1,0:T(8,128)(2,1)S(1)}, u32[]{:S(2)}, u32[]{:S(2)}) %collective-permute-start.32) | collective-permute-done | bytes 4587552 | tf_op jit(solution)/shard_map/ppermute | solution.py:1018
  545.6 6.0 add_convert_fusion
  551.6 4.7 all-to-all-start.5
  556.9 2.3 collective-permute-start.27
  562.7 9.9 %collective-permute-done.26 = bf16[256,512]{1,0:T(8,128)(2,1)S(1)} collective-permute-done((bf16[256,512]{1,0:T(8,128)(2,1)}, bf16[256,512]{1,0:T(8,128)(2,1)S(1)}, u32[]{:S(2)}, u32[]{:S(2)}) %collective-permute-start.26) | collective-permute-done | bytes 262176 | tf_op jit(solution)/shard_map/ppermute | solution.py:709
  573.7 2.8 collective-permute-start.29
  576.9 11.8 %collective-permute-done.20.r1_ref = bf16[256,512]{1,0:T(8,128)(2,1)S(1)} collective-permute-done((bf16[256,512]{1,0:T(8,128)(2,1)S(1)}, bf16[256,512]{1,0:T(8,128)(2,1)S(1)}, u32[]{:S(2)}, u32[]{:S(2)}) %collective-permute-start.20) | collective-permute-done | bytes 262176 | tf_op jit(solution)/shard_map/ppermute | solution.py:709
  589.6 3.7 routed.1.a0_ref
  593.3 3.1 collective-permute-start.23
  597.2 3.3 collective-permute-done.31.a3_ref
  601.3 5.1 stream.1
  608.2 3.3 result.1
  611.5 47.1 %reduce-scatter.8.cloned.1.call-done = bf16[64,2112]{1,0:T(8,128)(2,1)} async-done(((bf16[2048,2112]{1,0:T(8,128)(2,1)}), bf16[64,2112]{1,0:T(8,128)(2,1)}) %reduce-scatter.8.cloned.1.call-update) | async-done | bytes 270352 | tf_op jit(solution)/shard_map/reduce_scatter | solution.py:959
  658.7 1.8 fusion.1
  660.5 4.0 unpack.1
  666.0 2.7 collective-permute-start.34
  670.9 2.1 collective-permute-done.33.r1_ref
  673.0 1.8 collective-permute-done.34.r2_ref
  676.0 1.9 late.1
  (186 shorter events, 48.2 us)
Async XLA Ops:
  7.2 64.2 %all-gather.3.cloned.1.call-start = ((), (), s32[]{:S(2)}) async-start(), calls=%async_computation.9 | async-start | bytes 9732096 | tf_op jit(solution)/shard_map/all_gather | solution.py:806
  82.5 9.9 %copy-start.43 = (bf16[256,512]{1,0:T(8,128)(2,1)S(1)}, bf16[256,512]{1,0:T(8,128)(2,1)}, u32[]{:S(2)}) copy-start(bf16[256,512]{1,0:T(8,128)(2,1)} %get-tuple-element.96) | copy-start | bytes 786436
  82.5 22.0 %copy-start.10 = (f32[256,512]{1,0:T(8,128)S(1)}, f32[256,512]{1,0:T(8,128)}, u32[]{:S(2)}) copy-start(f32[256,512]{1,0:T(8,128)} %get-tuple-element.93) | copy-start | bytes 1572868
  82.5 46.7 %all-to-all-start = ((bf16[32,64,512]{2,1,0:T(8,128)(2,1)}), bf16[32,64,512]{2,1,0:T(8,128)(2,1)S(1)}, u32[]{:S(2)}, u32[]{:S(2)}) async-start(bf16[32,64,512]{2,1,0:T(8,128)(2,1)} %bitcast.49), calls=%async_computation | async-start | bytes 4194304 | tf_op jit(solution)/shard_map/all_to_all | solution.py:737
  88.1 9.8 %collective-permute-start = (bf16[256,512]{1,0:T(8,128)(2,1)S(1)}, bf16[256,512]{1,0:T(8,128)(2,1)S(1)}, u32[]{:S(2)}, u32[]{:S(2)}) collective-permute-start(bf16[256,512]{1,0:T(8,128)(2,1)S(1)} %copy-done.45), channel_id=1, source_target_pairs={{0,1},{1,2},{2,3},{3,0},{4,5},{5,6},{6,7},{7,4},{8,9},{9,10},{10,1... | collective-permute-start | bytes 786440 | tf_op jit(solution)/shard_map/ppermute | solution.py:709
  89.7 14.8 %collective-permute-start.1 = (bf16[256,512]{1,0:T(8,128)(2,1)S(1)}, bf16[256,512]{1,0:T(8,128)(2,1)S(1)}, u32[]{:S(2)}, u32[]{:S(2)}) collective-permute-start(bf16[256,512]{1,0:T(8,128)(2,1)S(1)} %copy-done.44), channel_id=1, source_target_pairs={{0,2},{1,3},{2,0},{3,1},{4,6},{5,7},{6,4},{7,5},{8,10},{9,11},{10,... | collective-permute-start | bytes 786440 | tf_op jit(solution)/shard_map/ppermute | solution.py:709
  92.4 12.1 %collective-permute-start.2 = (bf16[256,512]{1,0:T(8,128)(2,1)S(1)}, bf16[256,512]{1,0:T(8,128)(2,1)S(1)}, u32[]{:S(2)}, u32[]{:S(2)}) collective-permute-start(bf16[256,512]{1,0:T(8,128)(2,1)S(1)} %copy-done.43), channel_id=1, source_target_pairs={{0,3},{1,0},{2,1},{3,2},{4,7},{5,4},{6,5},{7,6},{8,11},{9,8},{10,9... | collective-permute-start | bytes 786440 | tf_op jit(solution)/shard_map/ppermute | solution.py:709
  104.6 17.3 %copy-start.8 = (bf16[256,512]{1,0:T(8,128)(2,1)}, bf16[256,512]{1,0:T(8,128)(2,1)S(1)}, u32[]{:S(2)}) copy-start(bf16[256,512]{1,0:T(8,128)(2,1)S(1)} %add_convert_fusion.3.a0_ref) | copy-start | bytes 786436
  104.6 13.7 %collective-permute-start.3 = (bf16[256,512]{1,0:T(8,128)(2,1)S(1)}, bf16[256,512]{1,0:T(8,128)(2,1)S(1)}, u32[]{:S(2)}, u32[]{:S(2)}) collective-permute-start(bf16[256,512]{1,0:T(8,128)(2,1)S(1)} %add_convert_fusion.3.a0_ref), channel_id=1, source_target_pairs={{0,3},{1,0},{2,1},{3,2},{4,7},{5,4},{6,5},{7,6},{8,11},{9,8},{10,9... | collective-permute-start | bytes 786440 | tf_op jit(solution)/shard_map/ppermute | solution.py:709
  107.0 11.4 %collective-permute-start.4 = (bf16[256,512]{1,0:T(8,128)(2,1)S(1)}, bf16[256,512]{1,0:T(8,128)(2,1)S(1)}, u32[]{:S(2)}, u32[]{:S(2)}) collective-permute-start(bf16[256,512]{1,0:T(8,128)(2,1)S(1)} %add_convert_fusion.3.a0_ref), channel_id=1, source_target_pairs={{0,2},{1,3},{2,0},{3,1},{4,6},{5,7},{6,4},{7,5},{8,10},{9,11},{10,... | collective-permute-start | bytes 786440 | tf_op jit(solution)/shard_map/ppermute | solution.py:709
  108.1 13.8 %collective-permute-start.5 = (bf16[256,512]{1,0:T(8,128)(2,1)S(1)}, bf16[256,512]{1,0:T(8,128)(2,1)S(1)}, u32[]{:S(2)}, u32[]{:S(2)}) collective-permute-start(bf16[256,512]{1,0:T(8,128)(2,1)S(1)} %add_convert_fusion.3.a0_ref), channel_id=1, source_target_pairs={{0,1},{1,2},{2,3},{3,0},{4,5},{5,6},{6,7},{7,4},{8,9},{9,10},{10,1... | collective-permute-start | bytes 786440 | tf_op jit(solution)/shard_map/ppermute | solution.py:709
  129.2 85.7 %all-to-all-start.1 = ((bf16[32,32,2560]{2,1,0:T(8,128)(2,1)}), bf16[32,32,2560]{2,1,0:T(8,128)(2,1)}, u32[]{:S(2)}, u32[]{:S(2)}) async-start(bf16[32,32,2560]{2,1,0:T(8,128)(2,1)} %get-tuple-element.104), calls=%async_computation.1 | async-start | bytes 10485760 | tf_op jit(solution)/shard_map/all_to_all | solution.py:737
  136.6 54.8 %copy-start.34 = (bf16[64,704]{1,0:T(8,128)(2,1)S(1)}, bf16[64,704]{1,0:T(8,128)(2,1)}, u32[]{:S(2)}) copy-start(bf16[64,704]{1,0:T(8,128)(2,1)} %param.29) | copy-start | bytes 270340
  136.6 54.8 %copy-start.35 = (bf16[64,704]{1,0:T(8,128)(2,1)S(1)}, bf16[64,704]{1,0:T(8,128)(2,1)}, u32[]{:S(2)}) copy-start(bf16[64,704]{1,0:T(8,128)(2,1)} %param.30) | copy-start | bytes 270340
  136.6 54.8 %copy-start.36 = (bf16[704,64]{0,1:T(8,128)(2,1)S(1)}, bf16[704,64]{0,1:T(8,128)(2,1)}, u32[]{:S(2)}) copy-start(bf16[704,64]{0,1:T(8,128)(2,1)} %param.31) | copy-start | bytes 270340
  136.6 236.3 %all-gather.5.cloned.1.call-start = ((), (), s32[]{:S(2)}) async-start(), calls=%async_computation.12 | async-start | bytes 9191424 | tf_op jit(solution)/shard_map/all_gather | solution.py:895
  136.7 49.0 %collective-permute-start.7 = (bf16[32,2,32,512]{3,2,1,0:T(8,128)(2,1)S(1)}, bf16[32,2,32,512]{3,2,1,0:T(8,128)(2,1)S(1)}, u32[]{:S(2)}, u32[]{:S(2)}) collective-permute-start(bf16[32,2,32,512]{3,2,1,0:T(8,128)(2,1)S(1)} %bitcast.45), channel_id=1, source_target_pairs={{0,1},{1,2},{2,3},{3,0},{4,5},{5,6},{6,7},{7,4},{8,9},{9,10},{10,1... | collective-permute-start | bytes 6291464 | tf_op jit(solution)/shard_map/ppermute | solution.py:709
  136.8 50.1 %collective-permute-start.6 = (bf16[32,2,32,512]{3,2,1,0:T(8,128)(2,1)S(1)}, bf16[32,2,32,512]{3,2,1,0:T(8,128)(2,1)S(1)}, u32[]{:S(2)}, u32[]{:S(2)}) collective-permute-start(bf16[32,2,32,512]{3,2,1,0:T(8,128)(2,1)S(1)} %bitcast.46), channel_id=1, source_target_pairs={{0,3},{1,0},{2,1},{3,2},{4,7},{5,4},{6,5},{7,6},{8,11},{9,8},{10,9... | collective-permute-start | bytes 6291464 | tf_op jit(solution)/shard_map/ppermute | solution.py:709
  186.9 26.0 %collective-permute-start.8 = (bf16[16,2,32,512]{3,2,1,0:T(8,128)(2,1)}, bf16[16,2,32,512]{3,2,1,0:T(8,128)(2,1)S(1)}, u32[]{:S(2)}, u32[]{:S(2)}) collective-permute-start(bf16[16,2,32,512]{3,2,1,0:T(8,128)(2,1)} %slice.70), channel_id=1, source_target_pairs={{0,1},{1,2},{2,3},{3,0},{4,5},{5,6},{6,7},{7,4},{8,9},{9,10},{10,1... | collective-permute-start | bytes 3145736 | tf_op jit(solution)/shard_map/ppermute | solution.py:709
  188.7 25.2 %collective-permute-start.9 = (bf16[16,2,32,512]{3,2,1,0:T(8,128)(2,1)S(1)}, bf16[16,2,32,512]{3,2,1,0:T(8,128)(2,1)S(1)}, u32[]{:S(2)}, u32[]{:S(2)}) collective-permute-start(bf16[16,2,32,512]{3,2,1,0:T(8,128)(2,1)S(1)} %slice.71), channel_id=1, source_target_pairs={{0,3},{1,0},{2,1},{3,2},{4,7},{5,4},{6,5},{7,6},{8,11},{9,8},{10,9... | collective-permute-start | bytes 3145736 | tf_op jit(solution)/shard_map/ppermute | solution.py:709
  216.2 24.9 %collective-permute-start.10 = (bf16[32,32,512]{2,1,0:T(8,128)(2,1)S(1)}, bf16[32,32,512]{2,1,0:T(8,128)(2,1)S(1)}, u32[]{:S(2)}, u32[]{:S(2)}) collective-permute-start(bf16[32,32,512]{2,1,0:T(8,128)(2,1)S(1)} %slice.72), channel_id=1, source_target_pairs={{0,3},{1,0},{2,1},{3,2},{4,7},{5,4},{6,5},{7,6},{8,11},{9,8},{10,9... | collective-permute-start | bytes 3145736 | tf_op jit(solution)/shard_map/ppermute | solution.py:709
  219.3 24.3 %collective-permute-start.11 = (bf16[32,32,512]{2,1,0:T(8,128)(2,1)S(1)}, bf16[32,32,512]{2,1,0:T(8,128)(2,1)S(1)}, u32[]{:S(2)}, u32[]{:S(2)}) collective-permute-start(bf16[32,32,512]{2,1,0:T(8,128)(2,1)S(1)} %slice.72), channel_id=1, source_target_pairs={{0,1},{1,2},{2,3},{3,0},{4,5},{5,6},{6,7},{7,4},{8,9},{9,10},{10,1... | collective-permute-start | bytes 3145736 | tf_op jit(solution)/shard_map/ppermute | solution.py:709
  243.7 199.2 %reduce-scatter.4.cloned.1.call-start = ((), (), s32[]{:S(2)}) async-start(), calls=%async_computation.10 | async-start | bytes 5242880 | tf_op jit(solution)/shard_map/reduce_scatter | solution.py:933
  244.6 12.2 %collective-permute-start.12 = (bf16[16,32,512]{2,1,0:T(8,128)(2,1)S(1)}, bf16[16,32,512]{2,1,0:T(8,128)(2,1)S(1)}, u32[]{:S(2)}, u32[]{:S(2)}) collective-permute-start(bf16[16,32,512]{2,1,0:T(8,128)(2,1)S(1)} %slice.73), channel_id=1, source_target_pairs={{0,1},{1,2},{2,3},{3,0},{4,5},{5,6},{6,7},{7,4},{8,9},{9,10},{10,1... | collective-permute-start | bytes 1572872 | tf_op jit(solution)/shard_map/ppermute | solution.py:709
  244.8 12.1 %collective-permute-start.13 = (bf16[16,32,512]{2,1,0:T(8,128)(2,1)S(1)}, bf16[16,32,512]{2,1,0:T(8,128)(2,1)S(1)}, u32[]{:S(2)}, u32[]{:S(2)}) collective-permute-start(bf16[16,32,512]{2,1,0:T(8,128)(2,1)S(1)} %slice.74), channel_id=1, source_target_pairs={{0,3},{1,0},{2,1},{3,2},{4,7},{5,4},{6,5},{7,6},{8,11},{9,8},{10,9... | collective-permute-start | bytes 1572872 | tf_op jit(solution)/shard_map/ppermute | solution.py:709
  248.1 64.7 %all-to-all-start.2 = ((bf16[32,32,2176]{2,1,0:T(8,128)(2,1)}), bf16[32,32,2176]{2,1,0:T(8,128)(2,1)}, u32[]{:S(2)}, u32[]{:S(2)}) async-start(bf16[32,32,2176]{2,1,0:T(8,128)(2,1)} %get-tuple-element.113), calls=%async_computation.4 | async-start | bytes 8912896 | tf_op jit(solution)/shard_map/all_to_all | solution.py:737
  255.3 242.1 %reduce-scatter.6.cloned.1.call-start = ((), (), s32[]{:S(2)}) async-start(), calls=%async_computation.11 | async-start | bytes 5242880 | tf_op jit(solution)/shard_map/reduce_scatter | solution.py:933
  312.7 83.5 %all-to-all-start.3 = ((bf16[32,32,2176]{2,1,0:T(8,128)(2,1)}), bf16[32,32,2176]{2,1,0:T(8,128)(2,1)}, u32[]{:S(2)}, u32[]{:S(2)}) async-start(bf16[32,32,2176]{2,1,0:T(8,128)(2,1)} %get-tuple-element.123), calls=%async_computation.5 | async-start | bytes 8912896 | tf_op jit(solution)/shard_map/all_to_all | solution.py:737
  322.3 336.3 %reduce-scatter.8.cloned.1.call-start = ((), (), s32[]{:S(2)}) async-start(), calls=%async_computation.13 | async-start | bytes 9191424 | tf_op jit(solution)/shard_map/reduce_scatter | solution.py:959
  401.9 35.2 %copy-start.11 = (f32[256,512]{1,0:T(8,128)S(1)}, f32[256,512]{1,0:T(8,128)}, u32[]{:S(2)}) copy-start(f32[256,512]{1,0:T(8,128)} %get-tuple-element.130) | copy-start | bytes 1572868
  402.8 18.7 %collective-permute-start.14 = (bf16[256,640]{1,0:T(8,128)(2,1)S(1)}, bf16[256,640]{1,0:T(8,128)(2,1)S(1)}, u32[]{:S(2)}, u32[]{:S(2)}) collective-permute-start(bf16[256,640]{1,0:T(8,128)(2,1)S(1)} %copy-done.39), channel_id=1, source_target_pairs={{0,1},{1,2},{2,3},{3,0},{4,5},{5,6},{6,7},{7,4},{8,9},{9,10},{10,1... | collective-permute-start | bytes 983048 | tf_op jit(solution)/shard_map/ppermute | solution.py:709
  404.3 32.7 %collective-permute-start.15 = (bf16[256,640]{1,0:T(8,128)(2,1)S(1)}, bf16[256,640]{1,0:T(8,128)(2,1)S(1)}, u32[]{:S(2)}, u32[]{:S(2)}) collective-permute-start(bf16[256,640]{1,0:T(8,128)(2,1)S(1)} %copy-done.38), channel_id=1, source_target_pairs={{0,2},{1,3},{2,0},{3,1},{4,6},{5,7},{6,4},{7,5},{8,10},{9,11},{10,... | collective-permute-start | bytes 983048 | tf_op jit(solution)/shard_map/ppermute | solution.py:709
  407.7 29.3 %collective-permute-start.16 = (bf16[256,640]{1,0:T(8,128)(2,1)S(1)}, bf16[256,640]{1,0:T(8,128)(2,1)S(1)}, u32[]{:S(2)}, u32[]{:S(2)}) collective-permute-start(bf16[256,640]{1,0:T(8,128)(2,1)S(1)} %copy-done.37), channel_id=1, source_target_pairs={{0,3},{1,0},{2,1},{3,2},{4,7},{5,4},{6,5},{7,6},{8,11},{9,8},{10,9... | collective-permute-start | bytes 983048 | tf_op jit(solution)/shard_map/ppermute | solution.py:709
  421.5 79.3 %copy-start.3 = (bf16[256,640]{1,0:T(8,128)(2,1)}, bf16[256,640]{1,0:T(8,128)(2,1)S(1)}, u32[]{:S(2)}) copy-start(bf16[256,640]{1,0:T(8,128)(2,1)S(1)} %collective-permute-done.14.r1_ref) | copy-start | bytes 983044
  437.0 63.8 %copy-start.4 = (bf16[256,640]{1,0:T(8,128)(2,1)}, bf16[256,640]{1,0:T(8,128)(2,1)S(1)}, u32[]{:S(2)}) copy-start(bf16[256,640]{1,0:T(8,128)(2,1)S(1)} %collective-permute-done.15.r2_ref) | copy-start | bytes 983044
  437.0 63.8 %copy-start.5 = (bf16[256,640]{1,0:T(8,128)(2,1)}, bf16[256,640]{1,0:T(8,128)(2,1)S(1)}, u32[]{:S(2)}) copy-start(bf16[256,640]{1,0:T(8,128)(2,1)S(1)} %collective-permute-done.16.r3_ref) | copy-start | bytes 983044
  437.2 63.6 %copy-start.6 = (bf16[256,512]{1,0:T(8,128)(2,1)}, bf16[256,512]{1,0:T(8,128)(2,1)S(1)}, u32[]{:S(2)}) copy-start(bf16[256,512]{1,0:T(8,128)(2,1)S(1)} %add_convert_fusion.2.a0_ref) | copy-start | bytes 786436
  437.2 62.0 %collective-permute-start.17 = (bf16[256,512]{1,0:T(8,128)(2,1)S(1)}, bf16[256,512]{1,0:T(8,128)(2,1)S(1)}, u32[]{:S(2)}, u32[]{:S(2)}) collective-permute-start(bf16[256,512]{1,0:T(8,128)(2,1)S(1)} %add_convert_fusion.2.a0_ref), channel_id=1, source_target_pairs={{0,3},{1,0},{2,1},{3,2},{4,7},{5,4},{6,5},{7,6},{8,11},{9,8},{10,9... | collective-permute-start | bytes 786440 | tf_op jit(solution)/shard_map/ppermute | solution.py:709
  438.4 60.8 %collective-permute-start.18 = (bf16[256,512]{1,0:T(8,128)(2,1)S(1)}, bf16[256,512]{1,0:T(8,128)(2,1)S(1)}, u32[]{:S(2)}, u32[]{:S(2)}) collective-permute-start(bf16[256,512]{1,0:T(8,128)(2,1)S(1)} %add_convert_fusion.2.a0_ref), channel_id=1, source_target_pairs={{0,2},{1,3},{2,0},{3,1},{4,6},{5,7},{6,4},{7,5},{8,10},{9,11},{10,... | collective-permute-start | bytes 786440 | tf_op jit(solution)/shard_map/ppermute | solution.py:709
  440.4 58.8 %collective-permute-start.19 = (bf16[256,512]{1,0:T(8,128)(2,1)S(1)}, bf16[256,512]{1,0:T(8,128)(2,1)S(1)}, u32[]{:S(2)}, u32[]{:S(2)}) collective-permute-start(bf16[256,512]{1,0:T(8,128)(2,1)S(1)} %add_convert_fusion.2.a0_ref), channel_id=1, source_target_pairs={{0,1},{1,2},{2,3},{3,0},{4,5},{5,6},{6,7},{7,4},{8,9},{9,10},{10,1... | collective-permute-start | bytes 786440 | tf_op jit(solution)/shard_map/ppermute | solution.py:709
  500.8 36.2 %all-to-all-start.4 = ((bf16[32,64,512]{2,1,0:T(8,128)(2,1)}), bf16[32,64,512]{2,1,0:T(8,128)(2,1)S(1)}, u32[]{:S(2)}, u32[]{:S(2)}) async-start(bf16[32,64,512]{2,1,0:T(8,128)(2,1)} %bitcast.44), calls=%async_computation.6 | async-start | bytes 4194304 | tf_op jit(solution)/shard_map/all_to_all | solution.py:737
  537.0 14.6 %copy-start = (bf16[32,64,512]{2,1,0:T(8,128)(2,1)}, bf16[32,64,512]{2,1,0:T(8,128)(2,1)S(1)}, u32[]{:S(2)}) copy-start(bf16[32,64,512]{2,1,0:T(8,128)(2,1)S(1)} %all-to-all-done.4) | copy-start | bytes 6291460
  537.0 8.6 %collective-permute-start.32 = (bf16[16,64,2240]{2,1,0:T(8,128)(2,1)}, bf16[16,64,2240]{2,1,0:T(8,128)(2,1)S(1)}, u32[]{:S(2)}, u32[]{:S(2)}) collective-permute-start(bf16[16,64,2240]{2,1,0:T(8,128)(2,1)} %get-tuple-element.157), channel_id=1, source_target_pairs={{0,4},{4,0},{8,12},{12,8},{16,20},{20,16},{24,28},{28,24},{32,36},... | collective-permute-start | bytes 13762568 | tf_op jit(solution)/shard_map/ppermute | solution.py:1018
  551.6 9.6 %copy-start.41 = (bf16[256,512]{1,0:T(8,128)(2,1)S(1)}, bf16[256,512]{1,0:T(8,128)(2,1)}, u32[]{:S(2)}) copy-start(bf16[256,512]{1,0:T(8,128)(2,1)} %get-tuple-element.137) | copy-start | bytes 786436
  551.6 21.0 %copy-start.40 = (bf16[256,512]{1,0:T(8,128)(2,1)S(1)}, bf16[256,512]{1,0:T(8,128)(2,1)}, u32[]{:S(2)}) copy-start(bf16[256,512]{1,0:T(8,128)(2,1)} %get-tuple-element.138) | copy-start | bytes 786436
  551.6 21.9 %copy-start.9 = (f32[256,512]{1,0:T(8,128)S(1)}, f32[256,512]{1,0:T(8,128)}, u32[]{:S(2)}) copy-start(f32[256,512]{1,0:T(8,128)} %get-tuple-element.151) | copy-start | bytes 1572868
  551.6 108.9 %all-to-all-start.5 = ((bf16[16,64,2240]{2,1,0:T(8,128)(2,1)}), bf16[16,64,2240]{2,1,0:T(8,128)(2,1)}, u32[]{:S(2)}, u32[]{:S(2)}) async-start(bf16[16,64,2240]{2,1,0:T(8,128)(2,1)} %add_convert_fusion), calls=%async_computation.7 | async-start | bytes 9437184 | tf_op jit(solution)/shard_map/all_to_all | solution.py:1020
  556.3 16.3 %collective-permute-start.26 = (bf16[256,512]{1,0:T(8,128)(2,1)}, bf16[256,512]{1,0:T(8,128)(2,1)S(1)}, u32[]{:S(2)}, u32[]{:S(2)}) collective-permute-start(bf16[256,512]{1,0:T(8,128)(2,1)} %get-tuple-element.152), channel_id=1, source_target_pairs={{0,1},{1,2},{2,3},{3,0},{4,5},{5,6},{6,7},{7,4},{8,9},{9,10},{10,1... | collective-permute-start | bytes 786440 | tf_op jit(solution)/shard_map/ppermute | solution.py:709
  556.9 15.7 %collective-permute-start.27 = (bf16[256,512]{1,0:T(8,128)(2,1)}, bf16[256,512]{1,0:T(8,128)(2,1)S(1)}, u32[]{:S(2)}, u32[]{:S(2)}) collective-permute-start(bf16[256,512]{1,0:T(8,128)(2,1)} %get-tuple-element.153), channel_id=1, source_target_pairs={{0,2},{1,3},{2,0},{3,1},{4,6},{5,7},{6,4},{7,5},{8,10},{9,11},{10,... | collective-permute-start | bytes 786440 | tf_op jit(solution)/shard_map/ppermute | solution.py:709
  559.2 14.3 %collective-permute-start.28 = (bf16[256,512]{1,0:T(8,128)(2,1)}, bf16[256,512]{1,0:T(8,128)(2,1)S(1)}, u32[]{:S(2)}, u32[]{:S(2)}) collective-permute-start(bf16[256,512]{1,0:T(8,128)(2,1)} %get-tuple-element.154), channel_id=1, source_target_pairs={{0,3},{1,0},{2,1},{3,2},{4,7},{5,4},{6,5},{7,6},{8,11},{9,8},{10,9... | collective-permute-start | bytes 786440 | tf_op jit(solution)/shard_map/ppermute | solution.py:709
  560.7 28.0 %collective-permute-start.20 = (bf16[256,512]{1,0:T(8,128)(2,1)S(1)}, bf16[256,512]{1,0:T(8,128)(2,1)S(1)}, u32[]{:S(2)}, u32[]{:S(2)}) collective-permute-start(bf16[256,512]{1,0:T(8,128)(2,1)S(1)} %copy-done.42), channel_id=1, source_target_pairs={{0,1},{1,2},{2,3},{3,0},{4,5},{5,6},{6,7},{7,4},{8,9},{9,10},{10,1... | collective-permute-start | bytes 786440 | tf_op jit(solution)/shard_map/ppermute | solution.py:709
  561.2 27.5 %collective-permute-start.21 = (bf16[256,512]{1,0:T(8,128)(2,1)S(1)}, bf16[256,512]{1,0:T(8,128)(2,1)S(1)}, u32[]{:S(2)}, u32[]{:S(2)}) collective-permute-start(bf16[256,512]{1,0:T(8,128)(2,1)S(1)} %copy-done.41), channel_id=1, source_target_pairs={{0,2},{1,3},{2,0},{3,1},{4,6},{5,7},{6,4},{7,5},{8,10},{9,11},{10,... | collective-permute-start | bytes 786440 | tf_op jit(solution)/shard_map/ppermute | solution.py:709
  572.6 16.1 %collective-permute-start.22 = (bf16[256,512]{1,0:T(8,128)(2,1)S(1)}, bf16[256,512]{1,0:T(8,128)(2,1)S(1)}, u32[]{:S(2)}, u32[]{:S(2)}) collective-permute-start(bf16[256,512]{1,0:T(8,128)(2,1)S(1)} %copy-done.40), channel_id=1, source_target_pairs={{0,3},{1,0},{2,1},{3,2},{4,7},{5,4},{6,5},{7,6},{8,11},{9,8},{10,9... | collective-permute-start | bytes 786440 | tf_op jit(solution)/shard_map/ppermute | solution.py:709
  573.7 26.9 %copy-start.7 = (bf16[256,512]{1,0:T(8,128)(2,1)}, bf16[256,512]{1,0:T(8,128)(2,1)S(1)}, u32[]{:S(2)}) copy-start(bf16[256,512]{1,0:T(8,128)(2,1)S(1)} %add_convert_fusion.1.a0_ref) | copy-start | bytes 786436
  573.7 22.7 %collective-permute-start.29 = (bf16[256,512]{1,0:T(8,128)(2,1)S(1)}, bf16[256,512]{1,0:T(8,128)(2,1)S(1)}, u32[]{:S(2)}, u32[]{:S(2)}) collective-permute-start(bf16[256,512]{1,0:T(8,128)(2,1)S(1)} %add_convert_fusion.1.a0_ref), channel_id=1, source_target_pairs={{0,3},{1,0},{2,1},{3,2},{4,7},{5,4},{6,5},{7,6},{8,11},{9,8},{10,9... | collective-permute-start | bytes 786440 | tf_op jit(solution)/shard_map/ppermute | solution.py:709
  576.5 20.7 %collective-permute-start.30 = (bf16[256,512]{1,0:T(8,128)(2,1)S(1)}, bf16[256,512]{1,0:T(8,128)(2,1)S(1)}, u32[]{:S(2)}, u32[]{:S(2)}) collective-permute-start(bf16[256,512]{1,0:T(8,128)(2,1)S(1)} %add_convert_fusion.1.a0_ref), channel_id=1, source_target_pairs={{0,2},{1,3},{2,0},{3,1},{4,6},{5,7},{6,4},{7,5},{8,10},{9,11},{10,... | collective-permute-start | bytes 786440 | tf_op jit(solution)/shard_map/ppermute | solution.py:709
  588.7 11.9 %collective-permute-start.31 = (bf16[256,512]{1,0:T(8,128)(2,1)S(1)}, bf16[256,512]{1,0:T(8,128)(2,1)S(1)}, u32[]{:S(2)}, u32[]{:S(2)}) collective-permute-start(bf16[256,512]{1,0:T(8,128)(2,1)S(1)} %add_convert_fusion.1.a0_ref), channel_id=1, source_target_pairs={{0,1},{1,2},{2,3},{3,0},{4,5},{5,6},{6,7},{7,4},{8,9},{9,10},{10,1... | collective-permute-start | bytes 786440 | tf_op jit(solution)/shard_map/ppermute | solution.py:709
  593.3 13.1 %collective-permute-start.23 = (bf16[256,512]{1,0:T(8,128)(2,1)}, bf16[256,512]{1,0:T(8,128)(2,1)S(1)}, u32[]{:S(2)}, u32[]{:S(2)}) collective-permute-start(bf16[256,512]{1,0:T(8,128)(2,1)} %routed.1.a0_ref), channel_id=1, source_target_pairs={{0,3},{1,0},{2,1},{3,2},{4,7},{5,4},{6,5},{7,6},{8,11},{9,8},{10,9... | collective-permute-start | bytes 786440 | tf_op jit(solution)/shard_map/ppermute | solution.py:709
  596.4 10.0 %collective-permute-start.24 = (bf16[256,512]{1,0:T(8,128)(2,1)}, bf16[256,512]{1,0:T(8,128)(2,1)S(1)}, u32[]{:S(2)}, u32[]{:S(2)}) collective-permute-start(bf16[256,512]{1,0:T(8,128)(2,1)} %routed.1.a0_ref), channel_id=1, source_target_pairs={{0,2},{1,3},{2,0},{3,1},{4,6},{5,7},{6,4},{7,5},{8,10},{9,11},{10,... | collective-permute-start | bytes 786440 | tf_op jit(solution)/shard_map/ppermute | solution.py:709
  596.4 11.1 %collective-permute-start.25 = (bf16[256,512]{1,0:T(8,128)(2,1)}, bf16[256,512]{1,0:T(8,128)(2,1)S(1)}, u32[]{:S(2)}, u32[]{:S(2)}) collective-permute-start(bf16[256,512]{1,0:T(8,128)(2,1)} %routed.1.a0_ref), channel_id=1, source_target_pairs={{0,1},{1,2},{2,3},{3,0},{4,5},{5,6},{6,7},{7,4},{8,9},{9,10},{10,1... | collective-permute-start | bytes 786440 | tf_op jit(solution)/shard_map/ppermute | solution.py:709
  658.7 11.5 %copy-start.2 = (bf16[64,2112]{1,0:T(8,128)(2,1)S(1)}, bf16[64,2112]{1,0:T(8,128)(2,1)}, u32[]{:S(2)}) copy-start(bf16[64,2112]{1,0:T(8,128)(2,1)} %reduce-scatter.8.cloned.1.call-done) | copy-start | bytes 811012
  664.5 8.5 %collective-permute-start.33 = (f32[64,640]{1,0:T(8,128)}, f32[64,640]{1,0:T(8,128)S(1)}, u32[]{:S(2)}, u32[]{:S(2)}) collective-permute-start(f32[64,640]{1,0:T(8,128)} %get-tuple-element.161.own_ref), channel_id=1, source_target_pairs={{0,1},{1,2},{2,3},{3,0},{4,5},{5,6},{6,7},{7,4},{8,9},{9,10},{10,1... | collective-permute-start | bytes 491528 | tf_op jit(solution)/shard_map/ppermute | solution.py:709
  666.0 8.7 %collective-permute-start.34 = (f32[64,640]{1,0:T(8,128)}, f32[64,640]{1,0:T(8,128)S(1)}, u32[]{:S(2)}, u32[]{:S(2)}) collective-permute-start(f32[64,640]{1,0:T(8,128)} %get-tuple-element.161.own_ref), channel_id=1, source_target_pairs={{0,2},{1,3},{2,0},{3,1},{4,6},{5,7},{6,4},{7,5},{8,10},{9,11},{10,... | collective-permute-start | bytes 491528 | tf_op jit(solution)/shard_map/ppermute | solution.py:709
  668.7 6.0 collective-permute-start.35
  (29 other events, 79.1 us)
Sparse Core Ops, SparseCore 0:
  13.4 57.9 all-gather.2
  243.8 129.1 all-gather.4
  375.4 67.4 reduce-scatter.3
  445.3 52.1 reduce-scatter.5
  501.1 157.5 reduce-scatter.7

commit v3 on v2

--- a/solution.py
+++ b/solution.py
@@ -804,6 +804,7 @@
     )
     pack_two = jnp.concatenate([shared_gate, shared_up, shared_down.T], axis=1)
     one = lax.all_gather(pack_one, "expert", axis=0, tiled=True)
+    two = lax.all_gather(pack_two, "expert", axis=0, tiled=True)
 
     position = jnp.arange(tokens).astype(F32)
     exponent = jnp.arange(ROPE // 2).astype(F32) * (2.0 / ROPE)
@@ -826,6 +827,8 @@
         name="routing",
     )
 
+    cot_own = exchange(cot_out)
+    cot_before, cot_after = ring_first(cot_own)
     (
         own,
         send1,
@@ -859,14 +862,14 @@
             ((8, width), F32),
             ((8, LATENT), F32),
         ],
-        [me, stream, one, segment_ids, segment_ids.T, cosine, sine],
+        [after(me, cot_own), stream, one, segment_ids, segment_ids.T, cosine, sine],
         2 * tokens * width * outer,
         places=smem,
         name="attend",
     )
-    cot_own = exchange(after(cot_out, own))
     got = send_blocks([send1, send2, send3])
     attention = (own + got[0].astype(F32) + got[1].astype(F32) + got[2].astype(F32)).astype(BF16)
+    attention = after(attention, cot_before, cot_after)
     middle, mixed, x_out = run(
         dispatch_kernel,
         [
@@ -879,25 +882,11 @@
         places=smem,
         name="dispatch",
     )
-    cot_before, cot_after = ring_first(after(cot_own, mixed))
-    x_in = exchange(after(x_out, cot_own))
+    x_in = exchange(x_out)
     cots = ring_second(cot_own, cot_before, cot_after)
     x1s = x_in[:, :, width:]
     x1_before, x1_after = ring_first(x1s)
     x1s = [x_in] + ring_second(x1s, x1_before, x1_after)[1:]
-    gate_t = expert_gate.transpose(0, 2, 1)
-    up_t = expert_up.transpose(0, 2, 1)
-    chunk = owners // 2
-    back0, c0, hg0, gr0, ur0 = expert_back(
-        False, me, base, [x_in], cots, gate_t, up_t, expert_down, one, edge // LANES - 1, chunk // 2
-    )
-    out0 = expert_out(0, hg0, expert_down, owners, tensors, chunk)
-    two = lax.all_gather(after(pack_two, out0, x1_before, x1_after), "expert", axis=0, tiled=True)
-    back0 = exchange(back0)
-    back1, c1, hg1, gr1, ur1, x1 = expert_back(
-        True, me, after(base, hg0), x1s, cots, gate_t, up_t, expert_down, one, edge // LANES - 1, chunk // 2
-    )
-    back1 = exchange(after(back1, back0))
     router_block = one[:, queries + LATENT : edge]
     (
         shared_own,
@@ -918,16 +907,29 @@
             ((tokens, LANES), F32),
             ((width, 3 * hidden_columns), BF16),
         ],
-        [after(me, hg1), mixed, cot_low, two, router_block],
+        [me, mixed, cot_low, two, router_block],
         18 * tokens * width * hidden_columns,
         places=smem,
         name="shared",
     )
-
+    base = after(base, shared_back)
+
+    gate_t = expert_gate.transpose(0, 2, 1)
+    up_t = expert_up.transpose(0, 2, 1)
+    chunk = owners // 2
+    back0, c0, hg0, gr0, ur0 = expert_back(
+        False, me, base, [x_in], cots, gate_t, up_t, expert_down, one, edge // LANES - 1, chunk // 2
+    )
+    back0 = exchange(back0)
+    back1, c1, hg1, gr1, ur1, x1 = expert_back(
+        True, me, after(base, hg0), x1s, cots, gate_t, up_t, expert_down, one, edge // LANES - 1, chunk // 2
+    )
+    back1 = exchange(after(back1, back0))
     gr0 = after(gr0, back0)
     gate_grad, up_grad, down_grad = expert_grads(
         (x_in, c0, hg0, gr0, ur0), (x1, c1, hg1, gr1, ur1), tensors
     )
+    out0 = expert_out(0, hg0, expert_down, owners, tensors, chunk)
     out1 = expert_out(1, after(hg1, out0), expert_down, owners, tensors, chunk)
     out_rows = [
         lax.psum_scatter(out, "tensor", scatter_dimension=0, tiled=True).reshape(owners, 1, capacity, piece)
@@ -956,6 +958,7 @@
         name="combine",
     )
     got = send_blocks([send1, send2, send3])
+    out_rows = exchange(after(jnp.concatenate(out_rows, axis=1), own))
     shared_sum = lax.psum_scatter(
         after(shared_grads, own), "expert", scatter_dimension=0, tiled=True
     )
@@ -965,8 +968,6 @@
         + got[1][:, :piece].astype(F32)
         + got[2][:, :piece].astype(F32)
     ).astype(BF16)
-    mixed_sums = share_small(mixed_sum)
-    out_rows = exchange(after(jnp.concatenate(out_rows, axis=1), *mixed_sums[1:]))
     keep, passed, middle_grad, own, send1, send2, send3 = run(
         attend_back_kernel,
         [
@@ -984,7 +985,7 @@
             stream,
             cotangent,
             middle,
-            *mixed_sums,
+            *share_small(mixed_sum),
             *got,
             probs_own,
             router_probs,

time: 697 us -> 583 us (0.84)
  waiting for transfers between devices: 373 us -> 234 us
  blocking collectives: 0 us -> 40 us
  starting transfers between devices: 103 us -> 87.1 us
    reduce_scatter x2, waiting for transfers between devices: 55.7 us -> 0.04 us  [per_device(): lax.psum_scatter(out, 'tensor', scatter_dimension=0, tiled=True)]
    reduce_scatter x1, waiting for transfers between devices: 47.1 us -> 0.01 us  [per_device(): lax.psum_scatter(after(shared_grads, own), 'expert', scatter_dimension=0,...]
    all_to_all x0 -> x1, blocking collectives: none -> 40 us  [exchange(): lax.all_to_all(rows.reshape(shape[0], -1, shape[-1]), 'expert', split_axi...]
    ppermute x35, waiting for transfers between devices: 153 us -> 118 us  [shift(): lax.ppermute(array, 'tensor', [(i, (i + step) % size) for i in range(size)])]
    all_to_all x5 -> x4, waiting for transfers between devices: 38.1 us -> 68.4 us  [exchange(): lax.all_to_all(rows.reshape(shape[0], -1, shape[-1]), 'expert', split_axi...]
    all_gather x1, waiting for transfers between devices: 50 us -> 23.8 us  [per_device(): one = lax.all_gather(pack_one, 'expert', axis=0, tiled=True)]
    all_gather x1, waiting for transfers between devices: 20.4 us -> 0.01 us  [per_device(): two = lax.all_gather(pack_two, 'expert', axis=0, tiled=True)]
    all_to_all x1, waiting for transfers between devices: 0.01 us -> 15.2 us  [per_device(): lax.all_to_all(paired, 'expert', split_axis=0, concat_axis=0, tiled=True,...]
  transfers between devices with their start and end apart: 47 -> 46, of which waited for: 25 -> 27; matrix products, arithmetic and copies ran while one was open for 3% -> 5% of each run, Pallas kernels for 20% -> 26%
where the time goes in v3:
time: 583 us; the launch traced here: 573 us
  waiting for transfers between devices  234 us (40%)
  Pallas kernels  155 us (27%)
  starting transfers between devices  87.1 us (15%)
  blocking collectives  40 us (7%)
  local copies, waits for them, and re-layouts  30.9 us (5%)
  between operations  14.7 us (3%)
  other arithmetic  11.7 us (2%)
    ppermute x35, waiting for transfers between devices, shift(): lax.ppermute(array, 'tensor', [(i, (i + step) % size) for i in range(size)])  118 us
    pallas_call x12, Pallas kernels, run(): pl.pallas_call(kernel, in_specs=in_specs, out_specs=out_specs, out_shape=...  91.7 us
    all_to_all x4, waiting for transfers between devices, exchange(): lax.all_to_all(rows.reshape(shape[0], -1, shape[-1]), 'expert', split_axi...  68.4 us
    ppermute x35, starting transfers between devices, shift(): lax.ppermute(array, 'tensor', [(i, (i + step) % size) for i in range(size)])  52.7 us
    all_to_all x1, blocking collectives, exchange(): lax.all_to_all(rows.reshape(shape[0], -1, shape[-1]), 'expert', split_axi...  40 us
    pallas_call x2, Pallas kernels, expert_back(): pl.pallas_call(functools.partial(expert_back_kernel, split), grid=(owners...  32.9 us
    all_to_all x4, starting transfers between devices, exchange(): lax.all_to_all(rows.reshape(shape[0], -1, shape[-1]), 'expert', split_axi...  26.6 us
    all_gather x1, waiting for transfers between devices, per_device(): one = lax.all_gather(pack_one, 'expert', axis=0, tiled=True)  23.8 us
  transfers between devices with their start and end apart: 46, of which 27 were waited for; matrix products, arithmetic and copies ran while one was open for 5% of the time, Pallas kernels for 26%

profile of v3, /device:TPU:0, one launch (start us, length us, event | category | flops | bytes accessed | tf_op | source)
XLA Modules:
  0.0 572.8 jit_solution(12079324928756828255)
XLA Ops:
  13.3 1.8 concatenate.20
  15.2 4.7 routing.1
  19.9 40.0 %all_to_all.30 = bf16[32,64,512]{2,1,0:T(8,128)(2,1)S(1)} all-to-all(bf16[32,64,512]{2,1,0:T(8,128)(2,1)} %bitcast.49), channel_id=1, replica_groups=mesh['expert'=32,'tensor'=4] {'expert'}, dimensions={0} | all-to-all | bytes 4194304 | tf_op jit(solution)/shard_map/all_to_all | solution.py:737
  61.1 2.1 collective-permute-start.4
  65.9 23.8 %all-gather.3.cloned.1.call-done.w_ref.refs_10_.refs_13_ = bf16[2048,2240]{1,0:T(8,128)(2,1)} async-done(((bf16[64,2240]{1,0:T(8,128)(2,1)}), bf16[2048,2240]{1,0:T(8,128)(2,1)}) %all-gather.3.cloned.1.call-update) | async-done | bytes 9175056 | tf_op jit(solution)/shard_map/all_gather | solution.py:806
  89.7 11.1 %attend.1 = (f32[256,512]{1,0:T(8,128)}, bf16[256,512]{1,0:T(8,128)(2,1)}, bf16[256,512]{1,0:T(8,128)(2,1)}, bf16[256,512]{1,0:T(8,128)(2,1)}, bf16[256,2048]{1,...) custom-call(s32[1]{0:T(128)} %bitcast.me_ref.refs_0_, ...), custom_call_target="tpu_custom_call" | custom-call | flops 201326592 | bytes 1627136 | tf_op jit(solution)/shard_map/attend/pallas_call | solution.py:81
  102.3 2.7 collective-permute-start.1
  106.5 7.7 %collective-permute-done = bf16[256,512]{1,0:T(8,128)(2,1)S(1)} collective-permute-done((bf16[256,512]{1,0:T(8,128)(2,1)}, bf16[256,512]{1,0:T(8,128)(2,1)S(1)}, u32[]{:S(2)}, u32[]{:S(2)}) %collective-permute-start) | collective-permute-done | bytes 262176 | tf_op jit(solution)/shard_map/ppermute | solution.py:709
  114.2 6.7 %collective-permute-done.1 = bf16[256,512]{1,0:T(8,128)(2,1)S(1)} collective-permute-done((bf16[256,512]{1,0:T(8,128)(2,1)}, bf16[256,512]{1,0:T(8,128)(2,1)S(1)}, u32[]{:S(2)}, u32[]{:S(2)}) %collective-permute-start.1) | collective-permute-done | bytes 262176 | tf_op jit(solution)/shard_map/ppermute | solution.py:709
  122.1 2.0 collective-permute-start.5
  125.5 5.8 %collective-permute-done.5.a1_ref = bf16[256,512]{1,0:T(8,128)(2,1)S(1)} collective-permute-done((bf16[256,512]{1,0:T(8,128)(2,1)S(1)}, bf16[256,512]{1,0:T(8,128)(2,1)S(1)}, u32[]{:S(2)}, u32[]{:S(2)}) %collective-permute-start.5) | collective-permute-done | bytes 262176 | tf_op jit(solution)/shard_map/ppermute | solution.py:709
  131.4 3.4 collective-permute-done.6.a2_ref
  134.8 3.1 collective-permute-done.7.a3_ref
  138.6 6.7 %dispatch.1 = (f32[256,2048]{1,0:T(8,128)}, bf16[256,2048]{1,0:T(8,128)(2,1)}, bf16[32,32,2560]{2,1,0:T(8,128)(2,1)}) custom-call(s32[1]{0:T(128)} %bitcast.me_ref.refs_0_, bf16[256,2048]{1,0:T(8,128)(2,1)} %stream_ref.7, bf16[256,512]{1,0:T(8,128)(2,1)} %copy-done.8, bf16[256,512]{1,0:T(8,128)(2,1)} %copy-done.18, bf16[256,512]{1,0:T(8,128)(2,1)} %copy-done.19, ...), custom_call_target="tpu_custom_call" | custom-call | flops 134217728 | bytes 1159987 | tf_op jit(solution)/shard_map/dispatch/pallas_call | solution.py:81
  145.3 4.9 all-to-all-start.1
  150.2 2.3 slice.71
  153.8 3.3 collective-permute-start.9
  157.1 22.0 %collective-permute-done.8 = bf16[16,2,32,512]{3,2,1,0:T(8,128)(2,1)S(1)} collective-permute-done((bf16[16,2,32,512]{3,2,1,0:T(8,128)(2,1)}, bf16[16,2,32,512]{3,2,1,0:T(8,128)(2,1)S(1)}, u32[]{:S(2)}, u32[]{:S(2)}) %collective-permute-start.8) | collective-permute-done | bytes 1048608 | tf_op jit(solution)/shard_map/ppermute | solution.py:709
  181.0 1.9 slice.70.router_ref
  182.9 16.5 %shared.1 = (f32[256,512]{1,0:T(8,128)}, bf16[256,512]{1,0:T(8,128)(2,1)}, bf16[256,512]{1,0:T(8,128)(2,1)}, bf16[256,512]{1,0:T(8,128)(2,1)}, f32[256,2048]{1,0...) custom-call(s32[1]{0:T(128)} %bitcast.me_ref.refs_0_, bf16[256,2048]{1,0:T(8,128)(2,1)} %get-tuple-element.102.mixed_ref, ...), custom_call_target="tpu_custom_call" | custom-call | flops 664377728 | bytes 2346189 | tf_op jit(solution)/shard_map/shared/pallas_call | solution.py:81
  199.4 15.9 %all-to-all-done.1.refs_2_.x0_ref = bf16[32,32,2560]{2,1,0:T(8,128)(2,1)} async-done(((bf16[32,32,2560]{2,1,0:T(8,128)(2,1)}), bf16[32,32,2560]{2,1,0:T(8,128)(2,1)}, u32[]{:S(2)}, u32[]{:S(2)}) %all-to-all-start.1) | async-done | bytes 5242912 | tf_op jit(solution)/shard_map/all_to_all | solution.py:737
  216.6 3.6 collective-permute-start.10
  220.2 16.3 %expert_back.2 = (bf16[32,32,2176]{2,1,0:T(8,128)(2,1)}, bf16[32,32,2048]{2,1,0:T(8,128)(2,1)}, bf16[1024,352]{1,0:T(8,128)(2,1)}, bf16[1024,352]{1,0:T(8,128)(2,1)}, bf16[1024,352]{1,0:T(8,128)(2,1)}) custom-call(s32[1]{0:T(128)} %bitcast.me_ref.refs_0_, s32[1]{0:T(128)} %bitcast.13.refs_1_, bf16[32,32,2560]{2,1,0:T(8,128)(2,1)} %all-to-all-done.1.refs_2_.x0_ref, ...), custom_call_target="tpu_custom_call" | custom-call | flops 73819750400 | bytes 25165824 | tf_op jit(solution)/shard_map/expert_back/pallas_call | solution.py:357
  236.5 5.4 expert_out.2
  244.1 3.1 collective-permute-start.13
  247.2 8.4 %all-to-all-start.2 = ((bf16[32,32,2176]{2,1,0:T(8,128)(2,1)}), bf16[32,32,2176]{2,1,0:T(8,128)(2,1)}, u32[]{:S(2)}, u32[]{:S(2)}) async-start(bf16[32,32,2176]{2,1,0:T(8,128)(2,1)} %get-tuple-element.113), calls=%async_computation.4 | async-start | bytes 8912896 | tf_op jit(solution)/shard_map/all_to_all | solution.py:737
  255.6 5.9 %collective-permute-done.12 = bf16[16,32,512]{2,1,0:T(8,128)(2,1)S(1)} collective-permute-done((bf16[16,32,512]{2,1,0:T(8,128)(2,1)S(1)}, bf16[16,32,512]{2,1,0:T(8,128)(2,1)S(1)}, u32[]{:S(2)}, u32[]{:S(2)}) %collective-permute-start.12) | collective-permute-done | bytes 524320 | tf_op jit(solution)/shard_map/ppermute | solution.py:709
  261.5 4.7 collective-permute-done.13
  267.2 16.7 %expert_back.3 = (bf16[32,32,2176]{2,1,0:T(8,128)(2,1)}, bf16[32,32,2048]{2,1,0:T(8,128)(2,1)}, bf16[1024,352]{1,0:T(8,128)(2,1)}, bf16[1024,352]{1,0:T(8,128)(2...) custom-call(s32[1]{0:T(128)} %bitcast.me_ref.refs_0_, s32[1]{0:T(128)} %bitcast.13.refs_1_, ...), custom_call_target="tpu_custom_call" | custom-call | flops 73819750400 | bytes 25165824 | tf_op jit(solution)/shard_map/expert_back/pallas_call | solution.py:357
  283.9 5.4 expert_out.3
  289.3 22.4 %all-to-all-done.2.b_ref = bf16[32,32,2176]{2,1,0:T(8,128)(2,1)} async-done(((bf16[32,32,2176]{2,1,0:T(8,128)(2,1)}), bf16[32,32,2176]{2,1,0:T(8,128)(2,1)}, u32[]{:S(2)}, u32[]{:S(2)}) %all-to-all-start.2) | async-done | bytes 4456480 | tf_op jit(solution)/shard_map/all_to_all | solution.py:737
  311.7 6.6 %all-to-all-start.3 = ((bf16[32,32,2176]{2,1,0:T(8,128)(2,1)}), bf16[32,32,2176]{2,1,0:T(8,128)(2,1)}, u32[]{:S(2)}, u32[]{:S(2)}) async-start(bf16[32,32,2176]{2,1,0:T(8,128)(2,1)} %get-tuple-element.123), calls=%async_computation.5 | async-start | bytes 8912896 | tf_op jit(solution)/shard_map/all_to_all | solution.py:737
  318.5 19.4 %expert_grads.1 = (f32[2,352,2048]{2,1,0:T(8,128)}, f32[2,352,2048]{2,1,0:T(8,128)}, f32[2,352,2048]{2,1,0:T(8,128)}) custom-call(bf16[32,32,2560]{2,1,0:T(8,128)(2,1)} %all-to-all-done.1.refs_2_.x0_ref, bf16[32,32,2048]{2,1,0:T(8,128)(2,1)} %get-tuple-element.111.c0_ref, bf16[1024,352]{1,0:T(8,128)(2,1)} %get-tuple-element.107.hg_ref.hg0_ref, ...), custom_call_target="tpu_custom_call" | custom-call | flops 738197504 | bytes 4177920 | tf_op jit(solution)/shard_map/expert_grads/pallas_call | solution.py:436
  337.9 6.1 %combine_first.1 = (f32[256,2048]{1,0:T(8,128)}, f32[256,128]{1,0:T(8,128)}) custom-call(bf16[256,1024]{1,0:T(8,128)(2,1)} %get-tuple-element.99.t0_ref.t_ref, bf16[32,32,2176]{2,1,0:T(8,128)(2,1)} %all-to-all-done.2.b_ref, f32[256,2048]{1,0:T(8,128)} %get-tuple-element.104.shared_ref), custom_call_target="tpu_custom_call" | custom-call | flops 107374184 | bytes 930611 | tf_op jit(solution)/shard_map/combine_first/pallas_call | solution.py:81
  344.0 30.2 %all-to-all-done.3.b_ref = bf16[32,32,2176]{2,1,0:T(8,128)(2,1)} async-done(((bf16[32,32,2176]{2,1,0:T(8,128)(2,1)}), bf16[32,32,2176]{2,1,0:T(8,128)(2,1)}, u32[]{:S(2)}, u32[]{:S(2)}) %all-to-all-start.3) | async-done | bytes 4456480 | tf_op jit(solution)/shard_map/all_to_all | solution.py:737
  374.2 5.5 combine.1
  383.0 6.7 %all-to-all-start.4 = ((bf16[32,64,512]{2,1,0:T(8,128)(2,1)}), bf16[32,64,512]{2,1,0:T(8,128)(2,1)S(1)}, u32[]{:S(2)}, u32[]{:S(2)}) async-start(bf16[32,64,512]{2,1,0:T(8,128)(2,1)} %bitcast.44), calls=%async_computation.6 | async-start | bytes 4194304 | tf_op jit(solution)/shard_map/all_to_all | solution.py:737
  393.1 15.1 %collective-permute-done.20.r1_ref = bf16[256,640]{1,0:T(8,128)(2,1)S(1)} collective-permute-done((bf16[256,640]{1,0:T(8,128)(2,1)}, bf16[256,640]{1,0:T(8,128)(2,1)S(1)}, u32[]{:S(2)}, u32[]{:S(2)}) %collective-permute-start.20) | collective-permute-done | bytes 327712 | tf_op jit(solution)/shard_map/ppermute | solution.py:709
  410.1 2.2 collective-permute-start.23
  413.5 9.8 %collective-permute-done.23.a1_ref = bf16[256,512]{1,0:T(8,128)(2,1)} collective-permute-done((bf16[256,512]{1,0:T(8,128)(2,1)S(1)}, bf16[256,512]{1,0:T(8,128)(2,1)}, u32[]{:S(2)}, u32[]{:S(2)}) %collective-permute-start.23) | collective-permute-done | bytes 262176 | tf_op jit(solution)/shard_map/ppermute | solution.py:709
  423.2 3.8 collective-permute-done.25.a3_ref
  427.0 23.3 %attend_back.1 = (bf16[16,64,2240]{2,1,0:T(8,128)(2,1)}, bf16[16,64,2240]{2,1,0:T(8,128)(2,1)}, f32[256,2048]{1,0:T(8,128)}, f32[256,512]{1,0:T(8,128)}, bf16[25...) custom-call(s32[1]{0:T(128)} %bitcast.me_ref.refs_0_, s32[1]{0:T(128)} %bitcast.21.core_ref, ...), custom_call_target="tpu_custom_call" | custom-call | flops 845571712 | bytes 3560244 | tf_op jit(solution)/shard_map/attend_back/pallas_call | solution.py:81
  450.5 8.1 %collective-permute-done.32 = bf16[16,64,2240]{2,1,0:T(8,128)(2,1)S(1)} collective-permute-done((bf16[16,64,2240]{2,1,0:T(8,128)(2,1)}, bf16[16,64,2240]{2,1,0:T(8,128)(2,1)S(1)}, u32[]{:S(2)}, u32[]{:S(2)}) %collective-permute-start.32) | collective-permute-done | bytes 4587552 | tf_op jit(solution)/shard_map/ppermute | solution.py:1019
  458.6 6.0 %add_convert_fusion = bf16[16,64,2240]{2,1,0:T(8,128)(2,1)} fusion(bf16[16,64,2240]{2,1,0:T(8,128)(2,1)S(1)} %collective-permute-done.32, bf16[16,64,2240]{2,1,0:T(8,128)(2,1)} %get-tuple-element.151), kind=kLoop, calls=%fused_computation | loop fusion | flops 9175040 | bytes 13762560 | tf_op jit(solution)/shard_map/convert_element_type | solution.py:1020
  464.6 7.3 %all-to-all-start.5 = ((bf16[16,64,2240]{2,1,0:T(8,128)(2,1)}), bf16[16,64,2240]{2,1,0:T(8,128)(2,1)}, u32[]{:S(2)}, u32[]{:S(2)}) async-start(bf16[16,64,2240]{2,1,0:T(8,128)(2,1)} %add_convert_fusion), calls=%async_computation.7 | async-start | bytes 9437184 | tf_op jit(solution)/shard_map/all_to_all | solution.py:1021
  472.0 1.8 collective-permute-start.27
  476.3 2.2 collective-permute-start.15
  478.5 9.7 %collective-permute-done.26 = bf16[256,512]{1,0:T(8,128)(2,1)S(1)} collective-permute-done((bf16[256,512]{1,0:T(8,128)(2,1)}, bf16[256,512]{1,0:T(8,128)(2,1)S(1)}, u32[]{:S(2)}, u32[]{:S(2)}) %collective-permute-start.26) | collective-permute-done | bytes 262176 | tf_op jit(solution)/shard_map/ppermute | solution.py:709
  489.3 5.7 collective-permute-start.29
  494.9 7.3 %collective-permute-done.14.r1_ref = bf16[256,512]{1,0:T(8,128)(2,1)S(1)} collective-permute-done((bf16[256,512]{1,0:T(8,128)(2,1)S(1)}, bf16[256,512]{1,0:T(8,128)(2,1)S(1)}, u32[]{:S(2)}, u32[]{:S(2)}) %collective-permute-start.14) | collective-permute-done | bytes 262176 | tf_op jit(solution)/shard_map/ppermute | solution.py:709
  503.1 3.6 routed.1.a0_ref
  506.7 3.1 collective-permute-start.17
  511.5 5.0 stream.1
  517.2 2.9 collective-permute-done.18.a2_ref
  520.2 2.5 collective-permute-done.19.a3_ref
  523.4 3.3 result.1
  526.7 1.8 fusion.1
  528.5 15.2 %all-to-all-done.5.parts_ref = bf16[16,64,2240]{2,1,0:T(8,128)(2,1)} async-done(((bf16[16,64,2240]{2,1,0:T(8,128)(2,1)}), bf16[16,64,2240]{2,1,0:T(8,128)(2,1)}, u32[]{:S(2)}, u32[]{:S(2)}) %all-to-all-start.5) | async-done | bytes 4587552 | tf_op jit(solution)/shard_map/all_to_all | solution.py:1021
  543.8 4.0 unpack.1
  547.8 2.9 collective-permute-start.33
  550.6 1.8 collective-permute-start.34
  552.4 2.6 collective-permute-start.35
  555.8 4.4 collective-permute-done.34.r2_ref
  561.5 1.9 late.1
  (157 shorter events, 46.4 us)
Async XLA Ops:
  7.2 82.5 %all-gather.3.cloned.1.call-start = ((), (), s32[]{:S(2)}) async-start(), calls=%async_computation.9 | async-start | bytes 9732096 | tf_op jit(solution)/shard_map/all_gather | solution.py:806
  13.3 169.6 %all-gather.5.cloned.1.call-start = ((), (), s32[]{:S(2)}) async-start(), calls=%async_computation.10 | async-start | bytes 9191424 | tf_op jit(solution)/shard_map/all_gather | solution.py:807
  15.2 50.0 %copy-start.27 = (s32[1,256]{1,0:T(1,128)S(1)}, s32[1,256]{1,0:T(1,128)}, u32[]{:S(2)}) copy-start(s32[1,256]{1,0:T(1,128)} %seg_row_ref.1) | copy-start | bytes 3076
  59.9 40.8 %copy-start.1 = (bf16[32,64,512]{2,1,0:T(8,128)(2,1)}, bf16[32,64,512]{2,1,0:T(8,128)(2,1)S(1)}, u32[]{:S(2)}) copy-start(bf16[32,64,512]{2,1,0:T(8,128)(2,1)S(1)} %all_to_all.30) | copy-start | bytes 6291460
  59.9 62.1 %collective-permute-start.3 = (bf16[32,2,32,512]{3,2,1,0:T(8,128)(2,1)S(1)}, bf16[32,2,32,512]{3,2,1,0:T(8,128)(2,1)}, u32[]{:S(2)}, u32[]{:S(2)}) collective-permute-start(bf16[32,2,32,512]{3,2,1,0:T(8,128)(2,1)S(1)} %bitcast.45), channel_id=1, source_target_pairs={{0,1},{1,2},{2,3},{3,0},{4,5},{5,6},{6,7},{7,4},{8,9},{9,10},{10,1... | collective-permute-start | bytes 6291464 | tf_op jit(solution)/shard_map/ppermute | solution.py:709
  61.1 61.0 %collective-permute-start.4 = (bf16[32,2,32,512]{3,2,1,0:T(8,128)(2,1)S(1)}, bf16[32,2,32,512]{3,2,1,0:T(8,128)(2,1)}, u32[]{:S(2)}, u32[]{:S(2)}) collective-permute-start(bf16[32,2,32,512]{3,2,1,0:T(8,128)(2,1)S(1)} %bitcast.46), channel_id=1, source_target_pairs={{0,3},{1,0},{2,1},{3,2},{4,7},{5,4},{6,5},{7,6},{8,11},{9,8},{10,9... | collective-permute-start | bytes 6291464 | tf_op jit(solution)/shard_map/ppermute | solution.py:709
  100.8 13.4 %collective-permute-start = (bf16[256,512]{1,0:T(8,128)(2,1)}, bf16[256,512]{1,0:T(8,128)(2,1)S(1)}, u32[]{:S(2)}, u32[]{:S(2)}) collective-permute-start(bf16[256,512]{1,0:T(8,128)(2,1)} %get-tuple-element.94), channel_id=1, source_target_pairs={{0,1},{1,2},{2,3},{3,0},{4,5},{5,6},{6,7},{7,4},{8,9},{9,10},{10,1... | collective-permute-start | bytes 786440 | tf_op jit(solution)/shard_map/ppermute | solution.py:709
  102.3 18.5 %collective-permute-start.1 = (bf16[256,512]{1,0:T(8,128)(2,1)}, bf16[256,512]{1,0:T(8,128)(2,1)S(1)}, u32[]{:S(2)}, u32[]{:S(2)}) collective-permute-start(bf16[256,512]{1,0:T(8,128)(2,1)} %get-tuple-element.95), channel_id=1, source_target_pairs={{0,2},{1,3},{2,0},{3,1},{4,6},{5,7},{6,4},{7,5},{8,10},{9,11},{10,... | collective-permute-start | bytes 786440 | tf_op jit(solution)/shard_map/ppermute | solution.py:709
  105.1 15.8 %collective-permute-start.2 = (bf16[256,512]{1,0:T(8,128)(2,1)}, bf16[256,512]{1,0:T(8,128)(2,1)S(1)}, u32[]{:S(2)}, u32[]{:S(2)}) collective-permute-start(bf16[256,512]{1,0:T(8,128)(2,1)} %get-tuple-element.96), channel_id=1, source_target_pairs={{0,3},{1,0},{2,1},{3,2},{4,7},{5,4},{6,5},{7,6},{8,11},{9,8},{10,9... | collective-permute-start | bytes 786440 | tf_op jit(solution)/shard_map/ppermute | solution.py:709
  122.0 15.8 %copy-start.8 = (bf16[256,512]{1,0:T(8,128)(2,1)}, bf16[256,512]{1,0:T(8,128)(2,1)S(1)}, u32[]{:S(2)}) copy-start(bf16[256,512]{1,0:T(8,128)(2,1)S(1)} %add_convert_fusion.3.a0_ref) | copy-start | bytes 786436
  122.1 9.3 %collective-permute-start.5 = (bf16[256,512]{1,0:T(8,128)(2,1)S(1)}, bf16[256,512]{1,0:T(8,128)(2,1)S(1)}, u32[]{:S(2)}, u32[]{:S(2)}) collective-permute-start(bf16[256,512]{1,0:T(8,128)(2,1)S(1)} %add_convert_fusion.3.a0_ref), channel_id=1, source_target_pairs={{0,3},{1,0},{2,1},{3,2},{4,7},{5,4},{6,5},{7,6},{8,11},{9,8},{10,9... | collective-permute-start | bytes 786440 | tf_op jit(solution)/shard_map/ppermute | solution.py:709
  124.0 10.8 %collective-permute-start.6 = (bf16[256,512]{1,0:T(8,128)(2,1)S(1)}, bf16[256,512]{1,0:T(8,128)(2,1)S(1)}, u32[]{:S(2)}, u32[]{:S(2)}) collective-permute-start(bf16[256,512]{1,0:T(8,128)(2,1)S(1)} %add_convert_fusion.3.a0_ref), channel_id=1, source_target_pairs={{0,2},{1,3},{2,0},{3,1},{4,6},{5,7},{6,4},{7,5},{8,10},{9,11},{10,... | collective-permute-start | bytes 786440 | tf_op jit(solution)/shard_map/ppermute | solution.py:709
  124.6 13.2 %collective-permute-start.7 = (bf16[256,512]{1,0:T(8,128)(2,1)S(1)}, bf16[256,512]{1,0:T(8,128)(2,1)S(1)}, u32[]{:S(2)}, u32[]{:S(2)}) collective-permute-start(bf16[256,512]{1,0:T(8,128)(2,1)S(1)} %add_convert_fusion.3.a0_ref), channel_id=1, source_target_pairs={{0,1},{1,2},{2,3},{3,0},{4,5},{5,6},{6,7},{7,4},{8,9},{9,10},{10,1... | collective-permute-start | bytes 786440 | tf_op jit(solution)/shard_map/ppermute | solution.py:709
  131.4 6.5 %copy-start.18 = (bf16[256,512]{1,0:T(8,128)(2,1)}, bf16[256,512]{1,0:T(8,128)(2,1)S(1)}, u32[]{:S(2)}) copy-start(bf16[256,512]{1,0:T(8,128)(2,1)S(1)} %collective-permute-done.5.a1_ref) | copy-start | bytes 786436
  145.3 69.9 %all-to-all-start.1 = ((bf16[32,32,2560]{2,1,0:T(8,128)(2,1)}), bf16[32,32,2560]{2,1,0:T(8,128)(2,1)}, u32[]{:S(2)}, u32[]{:S(2)}) async-start(bf16[32,32,2560]{2,1,0:T(8,128)(2,1)} %get-tuple-element.106), calls=%async_computation.1 | async-start | bytes 10485760 | tf_op jit(solution)/shard_map/all_to_all | solution.py:737
  150.2 229.5 %reduce-scatter.4.cloned.1.call-start = ((), (), s32[]{:S(2)}) async-start(), calls=%async_computation.11 | async-start | bytes 5242880 | tf_op jit(solution)/shard_map/reduce_scatter | solution.py:935
  152.5 26.6 %collective-permute-start.8 = (bf16[16,2,32,512]{3,2,1,0:T(8,128)(2,1)}, bf16[16,2,32,512]{3,2,1,0:T(8,128)(2,1)S(1)}, u32[]{:S(2)}, u32[]{:S(2)}) collective-permute-start(bf16[16,2,32,512]{3,2,1,0:T(8,128)(2,1)} %slice.71), channel_id=1, source_target_pairs={{0,1},{1,2},{2,3},{3,0},{4,5},{5,6},{6,7},{7,4},{8,9},{9,10},{10,1... | collective-permute-start | bytes 3145736 | tf_op jit(solution)/shard_map/ppermute | solution.py:709
  153.8 25.7 %collective-permute-start.9 = (bf16[16,2,32,512]{3,2,1,0:T(8,128)(2,1)S(1)}, bf16[16,2,32,512]{3,2,1,0:T(8,128)(2,1)S(1)}, u32[]{:S(2)}, u32[]{:S(2)}) collective-permute-start(bf16[16,2,32,512]{3,2,1,0:T(8,128)(2,1)S(1)} %slice.72), channel_id=1, source_target_pairs={{0,3},{1,0},{2,1},{3,2},{4,7},{5,4},{6,5},{7,6},{8,11},{9,8},{10,9... | collective-permute-start | bytes 3145736 | tf_op jit(solution)/shard_map/ppermute | solution.py:709
  216.5 26.1 %collective-permute-start.11 = (bf16[32,32,512]{2,1,0:T(8,128)(2,1)S(1)}, bf16[32,32,512]{2,1,0:T(8,128)(2,1)S(1)}, u32[]{:S(2)}, u32[]{:S(2)}) collective-permute-start(bf16[32,32,512]{2,1,0:T(8,128)(2,1)S(1)} %slice.73), channel_id=1, source_target_pairs={{0,1},{1,2},{2,3},{3,0},{4,5},{5,6},{6,7},{7,4},{8,9},{9,10},{10,1... | collective-permute-start | bytes 3145736 | tf_op jit(solution)/shard_map/ppermute | solution.py:709
  216.6 26.1 %collective-permute-start.10 = (bf16[32,32,512]{2,1,0:T(8,128)(2,1)S(1)}, bf16[32,32,512]{2,1,0:T(8,128)(2,1)}, u32[]{:S(2)}, u32[]{:S(2)}) collective-permute-start(bf16[32,32,512]{2,1,0:T(8,128)(2,1)S(1)} %slice.73), channel_id=1, source_target_pairs={{0,3},{1,0},{2,1},{3,2},{4,7},{5,4},{6,5},{7,6},{8,11},{9,8},{10,9... | collective-permute-start | bytes 3145736 | tf_op jit(solution)/shard_map/ppermute | solution.py:709
  242.6 4.6 copy-start.17
  242.6 18.8 %collective-permute-start.12 = (bf16[16,32,512]{2,1,0:T(8,128)(2,1)S(1)}, bf16[16,32,512]{2,1,0:T(8,128)(2,1)S(1)}, u32[]{:S(2)}, u32[]{:S(2)}) collective-permute-start(bf16[16,32,512]{2,1,0:T(8,128)(2,1)S(1)} %slice.74), channel_id=1, source_target_pairs={{0,1},{1,2},{2,3},{3,0},{4,5},{5,6},{6,7},{7,4},{8,9},{9,10},{10,1... | collective-permute-start | bytes 1572872 | tf_op jit(solution)/shard_map/ppermute | solution.py:709
  244.1 22.1 %collective-permute-start.13 = (bf16[16,32,512]{2,1,0:T(8,128)(2,1)S(1)}, bf16[16,32,512]{2,1,0:T(8,128)(2,1)S(1)}, u32[]{:S(2)}, u32[]{:S(2)}) collective-permute-start(bf16[16,32,512]{2,1,0:T(8,128)(2,1)S(1)} %slice.75), channel_id=1, source_target_pairs={{0,3},{1,0},{2,1},{3,2},{4,7},{5,4},{6,5},{7,6},{8,11},{9,8},{10,9... | collective-permute-start | bytes 1572872 | tf_op jit(solution)/shard_map/ppermute | solution.py:709
  247.2 64.5 %all-to-all-start.2 = ((bf16[32,32,2176]{2,1,0:T(8,128)(2,1)}), bf16[32,32,2176]{2,1,0:T(8,128)(2,1)}, u32[]{:S(2)}, u32[]{:S(2)}) async-start(bf16[32,32,2176]{2,1,0:T(8,128)(2,1)} %get-tuple-element.113), calls=%async_computation.4 | async-start | bytes 8912896 | tf_op jit(solution)/shard_map/all_to_all | solution.py:737
  255.6 124.1 %reduce-scatter.6.cloned.1.call-start = ((), (), s32[]{:S(2)}) async-start(), calls=%async_computation.12 | async-start | bytes 5242880 | tf_op jit(solution)/shard_map/reduce_scatter | solution.py:935
  311.7 62.5 %all-to-all-start.3 = ((bf16[32,32,2176]{2,1,0:T(8,128)(2,1)}), bf16[32,32,2176]{2,1,0:T(8,128)(2,1)}, u32[]{:S(2)}, u32[]{:S(2)}) async-start(bf16[32,32,2176]{2,1,0:T(8,128)(2,1)} %get-tuple-element.123), calls=%async_computation.5 | async-start | bytes 8912896 | tf_op jit(solution)/shard_map/all_to_all | solution.py:737
  318.3 208.4 %reduce-scatter.8.cloned.1.call-start = ((), (), s32[]{:S(2)}) async-start(), calls=%async_computation.13 | async-start | bytes 9191424 | tf_op jit(solution)/shard_map/reduce_scatter | solution.py:962
  381.5 9.9 %copy-start.28 = (bf16[256,640]{1,0:T(8,128)(2,1)S(1)}, bf16[256,640]{1,0:T(8,128)(2,1)}, u32[]{:S(2)}) copy-start(bf16[256,640]{1,0:T(8,128)(2,1)} %get-tuple-element.134) | copy-start | bytes 983044
  383.0 67.3 %all-to-all-start.4 = ((bf16[32,64,512]{2,1,0:T(8,128)(2,1)}), bf16[32,64,512]{2,1,0:T(8,128)(2,1)S(1)}, u32[]{:S(2)}, u32[]{:S(2)}) async-start(bf16[32,64,512]{2,1,0:T(8,128)(2,1)} %bitcast.44), calls=%async_computation.6 | async-start | bytes 4194304 | tf_op jit(solution)/shard_map/all_to_all | solution.py:737
  389.8 18.4 %collective-permute-start.20 = (bf16[256,640]{1,0:T(8,128)(2,1)}, bf16[256,640]{1,0:T(8,128)(2,1)S(1)}, u32[]{:S(2)}, u32[]{:S(2)}) collective-permute-start(bf16[256,640]{1,0:T(8,128)(2,1)} %get-tuple-element.132), channel_id=1, source_target_pairs={{0,1},{1,2},{2,3},{3,0},{4,5},{5,6},{6,7},{7,4},{8,9},{9,10},{10,1... | collective-permute-start | bytes 983048 | tf_op jit(solution)/shard_map/ppermute | solution.py:709
  389.9 18.3 %collective-permute-start.21 = (bf16[256,640]{1,0:T(8,128)(2,1)}, bf16[256,640]{1,0:T(8,128)(2,1)S(1)}, u32[]{:S(2)}, u32[]{:S(2)}) collective-permute-start(bf16[256,640]{1,0:T(8,128)(2,1)} %get-tuple-element.133), channel_id=1, source_target_pairs={{0,2},{1,3},{2,0},{3,1},{4,6},{5,7},{6,4},{7,5},{8,10},{9,11},{10,... | collective-permute-start | bytes 983048 | tf_op jit(solution)/shard_map/ppermute | solution.py:709
  391.3 17.5 %collective-permute-start.22 = (bf16[256,640]{1,0:T(8,128)(2,1)S(1)}, bf16[256,640]{1,0:T(8,128)(2,1)S(1)}, u32[]{:S(2)}, u32[]{:S(2)}) collective-permute-start(bf16[256,640]{1,0:T(8,128)(2,1)S(1)} %copy-done.28), channel_id=1, source_target_pairs={{0,3},{1,0},{2,1},{3,2},{4,7},{5,4},{6,5},{7,6},{8,11},{9,8},{10,9... | collective-permute-start | bytes 983048 | tf_op jit(solution)/shard_map/ppermute | solution.py:709
  408.2 18.8 %copy-start.3 = (bf16[256,640]{1,0:T(8,128)(2,1)}, bf16[256,640]{1,0:T(8,128)(2,1)S(1)}, u32[]{:S(2)}) copy-start(bf16[256,640]{1,0:T(8,128)(2,1)S(1)} %collective-permute-done.20.r1_ref) | copy-start | bytes 983044
  408.2 18.8 %copy-start.4 = (bf16[256,640]{1,0:T(8,128)(2,1)}, bf16[256,640]{1,0:T(8,128)(2,1)S(1)}, u32[]{:S(2)}) copy-start(bf16[256,640]{1,0:T(8,128)(2,1)S(1)} %collective-permute-done.21.r2_ref) | copy-start | bytes 983044
  408.8 18.2 %copy-start.5 = (bf16[256,640]{1,0:T(8,128)(2,1)}, bf16[256,640]{1,0:T(8,128)(2,1)S(1)}, u32[]{:S(2)}) copy-start(bf16[256,640]{1,0:T(8,128)(2,1)S(1)} %collective-permute-done.22.r3_ref) | copy-start | bytes 983044
  410.1 16.9 %copy-start.6 = (bf16[256,512]{1,0:T(8,128)(2,1)}, bf16[256,512]{1,0:T(8,128)(2,1)S(1)}, u32[]{:S(2)}) copy-start(bf16[256,512]{1,0:T(8,128)(2,1)S(1)} %add_convert_fusion.2.a0_ref) | copy-start | bytes 786436
  410.1 13.1 %collective-permute-start.23 = (bf16[256,512]{1,0:T(8,128)(2,1)S(1)}, bf16[256,512]{1,0:T(8,128)(2,1)}, u32[]{:S(2)}, u32[]{:S(2)}) collective-permute-start(bf16[256,512]{1,0:T(8,128)(2,1)S(1)} %add_convert_fusion.2.a0_ref), channel_id=1, source_target_pairs={{0,3},{1,0},{2,1},{3,2},{4,7},{5,4},{6,5},{7,6},{8,11},{9,8},{10,9... | collective-permute-start | bytes 786440 | tf_op jit(solution)/shard_map/ppermute | solution.py:709
  412.3 10.9 %collective-permute-start.24 = (bf16[256,512]{1,0:T(8,128)(2,1)S(1)}, bf16[256,512]{1,0:T(8,128)(2,1)}, u32[]{:S(2)}, u32[]{:S(2)}) collective-permute-start(bf16[256,512]{1,0:T(8,128)(2,1)S(1)} %add_convert_fusion.2.a0_ref), channel_id=1, source_target_pairs={{0,2},{1,3},{2,0},{3,1},{4,6},{5,7},{6,4},{7,5},{8,10},{9,11},{10,... | collective-permute-start | bytes 786440 | tf_op jit(solution)/shard_map/ppermute | solution.py:709
  412.5 14.5 %collective-permute-start.25 = (bf16[256,512]{1,0:T(8,128)(2,1)S(1)}, bf16[256,512]{1,0:T(8,128)(2,1)}, u32[]{:S(2)}, u32[]{:S(2)}) collective-permute-start(bf16[256,512]{1,0:T(8,128)(2,1)S(1)} %add_convert_fusion.2.a0_ref), channel_id=1, source_target_pairs={{0,1},{1,2},{2,3},{3,0},{4,5},{5,6},{6,7},{7,4},{8,9},{9,10},{10,1... | collective-permute-start | bytes 786440 | tf_op jit(solution)/shard_map/ppermute | solution.py:709
  450.4 14.2 %copy-start = (bf16[32,64,512]{2,1,0:T(8,128)(2,1)}, bf16[32,64,512]{2,1,0:T(8,128)(2,1)S(1)}, u32[]{:S(2)}) copy-start(bf16[32,64,512]{2,1,0:T(8,128)(2,1)S(1)} %all-to-all-done.4) | copy-start | bytes 6291460
  450.4 8.2 %collective-permute-start.32 = (bf16[16,64,2240]{2,1,0:T(8,128)(2,1)}, bf16[16,64,2240]{2,1,0:T(8,128)(2,1)S(1)}, u32[]{:S(2)}, u32[]{:S(2)}) collective-permute-start(bf16[16,64,2240]{2,1,0:T(8,128)(2,1)} %get-tuple-element.153), channel_id=1, source_target_pairs={{0,4},{4,0},{8,12},{12,8},{16,20},{20,16},{24,28},{28,24},{32,36},... | collective-permute-start | bytes 13762568 | tf_op jit(solution)/shard_map/ppermute | solution.py:1019
  464.6 10.6 %copy-start.31 = (bf16[256,512]{1,0:T(8,128)(2,1)S(1)}, bf16[256,512]{1,0:T(8,128)(2,1)}, u32[]{:S(2)}) copy-start(bf16[256,512]{1,0:T(8,128)(2,1)} %get-tuple-element.129) | copy-start | bytes 786436
  464.6 11.7 %copy-start.30 = (bf16[256,512]{1,0:T(8,128)(2,1)S(1)}, bf16[256,512]{1,0:T(8,128)(2,1)}, u32[]{:S(2)}) copy-start(bf16[256,512]{1,0:T(8,128)(2,1)} %get-tuple-element.130) | copy-start | bytes 786436
  464.6 23.6 %copy-start.29 = (bf16[256,512]{1,0:T(8,128)(2,1)S(1)}, bf16[256,512]{1,0:T(8,128)(2,1)}, u32[]{:S(2)}) copy-start(bf16[256,512]{1,0:T(8,128)(2,1)} %get-tuple-element.131) | copy-start | bytes 786436
  464.6 24.5 %copy-start.9 = (f32[256,512]{1,0:T(8,128)S(1)}, f32[256,512]{1,0:T(8,128)}, u32[]{:S(2)}) copy-start(f32[256,512]{1,0:T(8,128)} %get-tuple-element.147) | copy-start | bytes 1572868
  464.6 79.1 %all-to-all-start.5 = ((bf16[16,64,2240]{2,1,0:T(8,128)(2,1)}), bf16[16,64,2240]{2,1,0:T(8,128)(2,1)}, u32[]{:S(2)}, u32[]{:S(2)}) async-start(bf16[16,64,2240]{2,1,0:T(8,128)(2,1)} %add_convert_fusion), calls=%async_computation.7 | async-start | bytes 9437184 | tf_op jit(solution)/shard_map/all_to_all | solution.py:1021
  471.9 16.3 %collective-permute-start.26 = (bf16[256,512]{1,0:T(8,128)(2,1)}, bf16[256,512]{1,0:T(8,128)(2,1)S(1)}, u32[]{:S(2)}, u32[]{:S(2)}) collective-permute-start(bf16[256,512]{1,0:T(8,128)(2,1)} %get-tuple-element.148), channel_id=1, source_target_pairs={{0,1},{1,2},{2,3},{3,0},{4,5},{5,6},{6,7},{7,4},{8,9},{9,10},{10,1... | collective-permute-start | bytes 786440 | tf_op jit(solution)/shard_map/ppermute | solution.py:709
  472.0 16.2 %collective-permute-start.27 = (bf16[256,512]{1,0:T(8,128)(2,1)}, bf16[256,512]{1,0:T(8,128)(2,1)S(1)}, u32[]{:S(2)}, u32[]{:S(2)}) collective-permute-start(bf16[256,512]{1,0:T(8,128)(2,1)} %get-tuple-element.149), channel_id=1, source_target_pairs={{0,2},{1,3},{2,0},{3,1},{4,6},{5,7},{6,4},{7,5},{8,10},{9,11},{10,... | collective-permute-start | bytes 786440 | tf_op jit(solution)/shard_map/ppermute | solution.py:709
  473.8 15.3 %collective-permute-start.28 = (bf16[256,512]{1,0:T(8,128)(2,1)}, bf16[256,512]{1,0:T(8,128)(2,1)S(1)}, u32[]{:S(2)}, u32[]{:S(2)}) collective-permute-start(bf16[256,512]{1,0:T(8,128)(2,1)} %get-tuple-element.150), channel_id=1, source_target_pairs={{0,3},{1,0},{2,1},{3,2},{4,7},{5,4},{6,5},{7,6},{8,11},{9,8},{10,9... | collective-permute-start | bytes 786440 | tf_op jit(solution)/shard_map/ppermute | solution.py:709
  475.2 27.0 %collective-permute-start.14 = (bf16[256,512]{1,0:T(8,128)(2,1)S(1)}, bf16[256,512]{1,0:T(8,128)(2,1)S(1)}, u32[]{:S(2)}, u32[]{:S(2)}) collective-permute-start(bf16[256,512]{1,0:T(8,128)(2,1)S(1)} %copy-done.31), channel_id=1, source_target_pairs={{0,1},{1,2},{2,3},{3,0},{4,5},{5,6},{6,7},{7,4},{8,9},{9,10},{10,1... | collective-permute-start | bytes 786440 | tf_op jit(solution)/shard_map/ppermute | solution.py:709
  476.3 25.9 %collective-permute-start.15 = (bf16[256,512]{1,0:T(8,128)(2,1)S(1)}, bf16[256,512]{1,0:T(8,128)(2,1)S(1)}, u32[]{:S(2)}, u32[]{:S(2)}) collective-permute-start(bf16[256,512]{1,0:T(8,128)(2,1)S(1)} %copy-done.30), channel_id=1, source_target_pairs={{0,2},{1,3},{2,0},{3,1},{4,6},{5,7},{6,4},{7,5},{8,10},{9,11},{10,... | collective-permute-start | bytes 786440 | tf_op jit(solution)/shard_map/ppermute | solution.py:709
  488.2 14.0 %collective-permute-start.16 = (bf16[256,512]{1,0:T(8,128)(2,1)S(1)}, bf16[256,512]{1,0:T(8,128)(2,1)S(1)}, u32[]{:S(2)}, u32[]{:S(2)}) collective-permute-start(bf16[256,512]{1,0:T(8,128)(2,1)S(1)} %copy-done.29), channel_id=1, source_target_pairs={{0,3},{1,0},{2,1},{3,2},{4,7},{5,4},{6,5},{7,6},{8,11},{9,8},{10,9... | collective-permute-start | bytes 786440 | tf_op jit(solution)/shard_map/ppermute | solution.py:709
  489.3 21.5 %copy-start.7 = (bf16[256,512]{1,0:T(8,128)(2,1)}, bf16[256,512]{1,0:T(8,128)(2,1)S(1)}, u32[]{:S(2)}) copy-start(bf16[256,512]{1,0:T(8,128)(2,1)S(1)} %add_convert_fusion.1.a0_ref) | copy-start | bytes 786436
  489.3 20.6 %collective-permute-start.29 = (bf16[256,512]{1,0:T(8,128)(2,1)S(1)}, bf16[256,512]{1,0:T(8,128)(2,1)S(1)}, u32[]{:S(2)}, u32[]{:S(2)}) collective-permute-start(bf16[256,512]{1,0:T(8,128)(2,1)S(1)} %add_convert_fusion.1.a0_ref), channel_id=1, source_target_pairs={{0,3},{1,0},{2,1},{3,2},{4,7},{5,4},{6,5},{7,6},{8,11},{9,8},{10,9... | collective-permute-start | bytes 786440 | tf_op jit(solution)/shard_map/ppermute | solution.py:709
  494.9 15.8 %collective-permute-start.30 = (bf16[256,512]{1,0:T(8,128)(2,1)S(1)}, bf16[256,512]{1,0:T(8,128)(2,1)S(1)}, u32[]{:S(2)}, u32[]{:S(2)}) collective-permute-start(bf16[256,512]{1,0:T(8,128)(2,1)S(1)} %add_convert_fusion.1.a0_ref), channel_id=1, source_target_pairs={{0,2},{1,3},{2,0},{3,1},{4,6},{5,7},{6,4},{7,5},{8,10},{9,11},{10,... | collective-permute-start | bytes 786440 | tf_op jit(solution)/shard_map/ppermute | solution.py:709
  502.2 8.5 %collective-permute-start.31 = (bf16[256,512]{1,0:T(8,128)(2,1)S(1)}, bf16[256,512]{1,0:T(8,128)(2,1)S(1)}, u32[]{:S(2)}, u32[]{:S(2)}) collective-permute-start(bf16[256,512]{1,0:T(8,128)(2,1)S(1)} %add_convert_fusion.1.a0_ref), channel_id=1, source_target_pairs={{0,1},{1,2},{2,3},{3,0},{4,5},{5,6},{6,7},{7,4},{8,9},{9,10},{10,1... | collective-permute-start | bytes 786440 | tf_op jit(solution)/shard_map/ppermute | solution.py:709
  506.7 10.5 %collective-permute-start.17 = (bf16[256,512]{1,0:T(8,128)(2,1)}, bf16[256,512]{1,0:T(8,128)(2,1)S(1)}, u32[]{:S(2)}, u32[]{:S(2)}) collective-permute-start(bf16[256,512]{1,0:T(8,128)(2,1)} %routed.1.a0_ref), channel_id=1, source_target_pairs={{0,3},{1,0},{2,1},{3,2},{4,7},{5,4},{6,5},{7,6},{8,11},{9,8},{10,9... | collective-permute-start | bytes 786440 | tf_op jit(solution)/shard_map/ppermute | solution.py:709
  509.9 10.3 %collective-permute-start.18 = (bf16[256,512]{1,0:T(8,128)(2,1)}, bf16[256,512]{1,0:T(8,128)(2,1)S(1)}, u32[]{:S(2)}, u32[]{:S(2)}) collective-permute-start(bf16[256,512]{1,0:T(8,128)(2,1)} %routed.1.a0_ref), channel_id=1, source_target_pairs={{0,2},{1,3},{2,0},{3,1},{4,6},{5,7},{6,4},{7,5},{8,10},{9,11},{10,... | collective-permute-start | bytes 786440 | tf_op jit(solution)/shard_map/ppermute | solution.py:709
  509.9 12.8 %collective-permute-start.19 = (bf16[256,512]{1,0:T(8,128)(2,1)}, bf16[256,512]{1,0:T(8,128)(2,1)S(1)}, u32[]{:S(2)}, u32[]{:S(2)}) collective-permute-start(bf16[256,512]{1,0:T(8,128)(2,1)} %routed.1.a0_ref), channel_id=1, source_target_pairs={{0,1},{1,2},{2,3},{3,0},{4,5},{5,6},{6,7},{7,4},{8,9},{9,10},{10,1... | collective-permute-start | bytes 786440 | tf_op jit(solution)/shard_map/ppermute | solution.py:709
  517.2 5.4 copy-start.21
  526.7 28.4 %copy-start.2 = (bf16[64,2112]{1,0:T(8,128)(2,1)S(1)}, bf16[64,2112]{1,0:T(8,128)(2,1)}, u32[]{:S(2)}) copy-start(bf16[64,2112]{1,0:T(8,128)(2,1)} %reduce-scatter.8.cloned.1.call-done) | copy-start | bytes 811012
  547.8 8.0 %collective-permute-start.33 = (f32[64,640]{1,0:T(8,128)}, f32[64,640]{1,0:T(8,128)S(1)}, u32[]{:S(2)}, u32[]{:S(2)}) collective-permute-start(f32[64,640]{1,0:T(8,128)} %get-tuple-element.157.own_ref), channel_id=1, source_target_pairs={{0,1},{1,2},{2,3},{3,0},{4,5},{5,6},{6,7},{7,4},{8,9},{9,10},{10,1... | collective-permute-start | bytes 491528 | tf_op jit(solution)/shard_map/ppermute | solution.py:709
  550.6 9.5 %collective-permute-start.34 = (f32[64,640]{1,0:T(8,128)}, f32[64,640]{1,0:T(8,128)S(1)}, u32[]{:S(2)}, u32[]{:S(2)}) collective-permute-start(f32[64,640]{1,0:T(8,128)} %get-tuple-element.157.own_ref), channel_id=1, source_target_pairs={{0,2},{1,3},{2,0},{3,1},{4,6},{5,7},{6,4},{7,5},{8,10},{9,11},{10,... | collective-permute-start | bytes 491528 | tf_op jit(solution)/shard_map/ppermute | solution.py:709
  552.4 7.7 %collective-permute-start.35 = (f32[64,640]{1,0:T(8,128)}, f32[64,640]{1,0:T(8,128)S(1)}, u32[]{:S(2)}, u32[]{:S(2)}) collective-permute-start(f32[64,640]{1,0:T(8,128)} %get-tuple-element.157.own_ref), channel_id=1, source_target_pairs={{0,3},{1,0},{2,1},{3,2},{4,7},{5,4},{6,5},{7,6},{8,11},{9,8},{10,9... | collective-permute-start | bytes 491528 | tf_op jit(solution)/shard_map/ppermute | solution.py:709
  (14 other events, 18.7 us)
Sparse Core Ops, SparseCore 0:
  13.4 76.2 all-gather.2
  92.5 53.7 all-gather.4
  242.0 50.0 reduce-scatter.3
  294.5 49.4 reduce-scatter.5
  379.8 92.6 reduce-scatter.7

commit v4 on v3

--- a/solution.py
+++ b/solution.py
@@ -645,14 +645,54 @@
     second.wait()
 
 
-def unpack_kernel(parts_ref, query_ref, late_ref, output_ref, up_ref, router_ref):
+def pair_kernel(at_ref, keep_ref, got_ref, along_z_ref, *along_x_refs):
+    side = len(along_x_refs)
+    cut = along_x_refs[0].shape[2]
+
+    def part(index, columns):
+        return (keep_ref[index, :, columns].astype(F32) + got_ref[index, :, columns].astype(F32)).astype(BF16)
+
+    for z in range(side):
+        for x in range(side):
+            along_z_ref[z, x] = part(x * side + z, slice(cut, None))
+    for step, out_ref in enumerate(along_x_refs):
+        peer = lax.rem(at_ref[0] + step, side)
+        for other in range(side):
+            out_ref[other] = part(peer * side + other, slice(0, cut))
+
+
+def cross_kernel(group, at_ref, *refs):
+    parts, out_refs = refs[:-4], refs[-4:]
+    for step, out_ref in enumerate(out_refs):
+        peer = lax.rem(at_ref[1 - group] + step, len(out_refs))
+        if len(parts) == 1:
+            rows = [parts[0][source, peer] for source in range(parts[0].shape[0])]
+        else:
+            rows = [r_ref[peer] for r_ref in parts]
+        total = rows[0].astype(F32)
+        for row in rows[1:]:
+            total = total + row.astype(F32)
+        out_ref[...] = total.astype(out_ref.dtype)
+
+
+def unpack_kernel(*refs):
+    query_ref, late_ref, output_ref, up_ref, router_ref, total_ref = refs[-6:]
     heads = up_ref.shape[1] // (2 * NOPE)
     short = up_ref.shape[0]
     nope = heads * NOPE
     queries = nope + heads * ROPE
     edge = queries + LATENT + LANES
     outer = edge + heads * VDIM
-    total = jnp.sum(parts_ref[...].astype(F32), axis=0)
+    start = 0
+    for group in range(2):
+        parts = refs[4 * group : 4 * group + 4]
+        width = parts[0].shape[1]
+        total = parts[0][...]
+        for r_ref in parts[1:]:
+            total = total + r_ref[...].astype(F32)
+        total_ref[:, start : start + width] = total
+        start += width
+    total = total_ref[...]
     for head in range(heads):
         start = head * (NOPE + ROPE)
         query_ref[:, start : start + NOPE] = total[:, head * NOPE : (head + 1) * NOPE]
@@ -1017,15 +1057,52 @@
         name="attend_back",
     )
     paired = lax.ppermute(after(passed, out_rows), "expert", [(i, i ^ 1) for i in range(owners)])
-    paired = (keep.astype(F32) + paired.astype(F32)).astype(BF16)
-    parts = lax.all_to_all(
-        paired,
+    side = 4
+    chip = lax.axis_index("expert") // 2
+    at = jnp.stack([chip // side, lax.rem(chip, side)]).astype(jnp.int32)
+    columns = outer + 2 * NOPE + experts
+    cut = columns // 2 // LANES * LANES + LANES
+
+    def along(group, array, step):
+        def target(i):
+            x, z, core = i // (2 * side), i // 2 % side, i % 2
+            if group == 0:
+                x = (x + step) % side
+            else:
+                z = (z + step) % side
+            return (x * side + z) * 2 + core
+
+        return lax.ppermute(array, "expert", [(i, target(i)) for i in range(owners)])
+
+    widths = [cut, columns - cut]
+    along_z, *along_x = run(
+        pair_kernel,
+        [((side, side, shard, widths[1]), BF16)] + [((side, shard, cut), BF16)] * side,
+        [at, keep, paired],
+        0,
+        places=smem,
+        name="pair",
+    )
+    came_z = lax.all_to_all(
+        along_z.reshape(side, side * shard, widths[1]),
         "expert",
         split_axis=0,
         concat_axis=0,
         tiled=True,
-        axis_index_groups=[[2 * i + c for i in range(owners // 2)] for c in range(2)],
-    )
+        axis_index_groups=[[(x * side + z) * 2 + c for z in range(side)] for x in range(side) for c in range(2)],
+    ).reshape(along_z.shape)
+    came_x = [along_x[0]] + [along(0, along_x[step], step) for step in range(1, side)]
+    parts = []
+    for group, came in enumerate((came_x, [came_z])):
+        crossed = run(
+            functools.partial(cross_kernel, group),
+            [((shard, widths[group]), F32)] + [((shard, widths[group]), BF16)] * (side - 1),
+            [at, *came],
+            0,
+            places=smem,
+            name="cross",
+        )
+        parts += [crossed[0]] + [along(1 - group, crossed[step], step) for step in range(1, side)]
     got = send_blocks([send1, send2, send3])
     first_sum = (own + got[0].astype(F32) + got[1].astype(F32) + got[2].astype(F32)).astype(BF16)
     (stream_grad,) = run(
@@ -1059,7 +1136,7 @@
     gate_sum = shared_sum[:, :hidden_columns]
     up_sum = shared_sum[:, hidden_columns : 2 * hidden_columns]
     down_sum = shared_sum[:, 2 * hidden_columns :]
-    parts = after(parts, stream_grad, result, gate_sum, up_sum, down_sum)
+    parts[0] = after(parts[0], stream_grad, result, gate_sum, up_sum, down_sum)
     query_grad, late, output_grad, latent_up_grad, router_grad = run(
         unpack_kernel,
         [
@@ -1069,8 +1146,9 @@
             (latent_up.shape, F32),
             (router_proj.shape, F32),
         ],
-        [parts],
+        parts,
         0,
+        scratch=[pltpu.VMEM((shard, columns), F32)],
         name="unpack",
     )
     latent_down_grad, gain_grads = run(

time: 583 us -> 590 us (1.012)
  waiting for transfers between devices: 234 us -> 221 us
  Pallas kernels: 155 us -> 165 us
  starting transfers between devices: 87.1 us -> 95.8 us
    ppermute x0 -> x9, starting transfers between devices: none -> 17.3 us  [along(): lax.ppermute(array, 'expert', [(i, target(i)) for i in range(owners)])]
    all_to_all x1, waiting for transfers between devices: 15.2 us -> 0.01 us  [per_device(): lax.all_to_all(along_z.reshape(side, side * shard, widths[1]), 'expert',...]
    pallas_call x12 -> x15, Pallas kernels: 91.7 us -> 102 us  [run(): pl.pallas_call(kernel, in_specs=in_specs, out_specs=out_specs, out_shape=...]
    ppermute x35, starting transfers between devices: 52.7 us -> 46.6 us  [shift(): lax.ppermute(array, 'tensor', [(i, (i + step) % size) for i in range(size)])]
    convert_element_type x1 -> x0, other arithmetic: 6.03 us -> none  [per_device(): paired = (keep.astype(F32) + paired.astype(F32)).astype(BF16)]
  transfers between devices with their start and end apart: 46 -> 55, of which waited for: 27 -> 29; matrix products, arithmetic and copies ran while one was open for 5% -> 5% of each run, Pallas kernels for 26% -> 28%
where the time goes in v4:
time: 590 us; the launch traced here: 581 us
  waiting for transfers between devices  221 us (37%)
  Pallas kernels  165 us (28%)
  starting transfers between devices  95.8 us (16%)
  blocking collectives  39.6 us (7%)
  local copies, waits for them, and re-layouts  36.8 us (6%)
  between operations  14.7 us (2%)
  other arithmetic  7.48 us (1%)
    ppermute x35, waiting for transfers between devices, shift(): lax.ppermute(array, 'tensor', [(i, (i + step) % size) for i in range(size)])  120 us
    pallas_call x15, Pallas kernels, run(): pl.pallas_call(kernel, in_specs=in_specs, out_specs=out_specs, out_shape=...  102 us
    all_to_all x4, waiting for transfers between devices, exchange(): lax.all_to_all(rows.reshape(shape[0], -1, shape[-1]), 'expert', split_axi...  68.3 us
    ppermute x35, starting transfers between devices, shift(): lax.ppermute(array, 'tensor', [(i, (i + step) % size) for i in range(size)])  46.6 us
    all_to_all x1, blocking collectives, exchange(): lax.all_to_all(rows.reshape(shape[0], -1, shape[-1]), 'expert', split_axi...  39.6 us
    pallas_call x2, Pallas kernels, expert_back(): pl.pallas_call(functools.partial(expert_back_kernel, split), grid=(owners...  33 us
    all_to_all x4, starting transfers between devices, exchange(): lax.all_to_all(rows.reshape(shape[0], -1, shape[-1]), 'expert', split_axi...  26.7 us
    all_gather x1, waiting for transfers between devices, per_device(): one = lax.all_gather(pack_one, 'expert', axis=0, tiled=True)  24.3 us
  transfers between devices with their start and end apart: 55, of which 29 were waited for; matrix products, arithmetic and copies ran while one was open for 5% of the time, Pallas kernels for 28%

profile of v4, /device:TPU:0, one launch (start us, length us, event | category | flops | bytes accessed | tf_op | source)
XLA Modules:
  0.0 580.5 jit_solution(7214724098144168818)
XLA Ops:
  15.2 4.7 routing.1
  19.9 39.6 %all_to_all.30 = bf16[32,64,512]{2,1,0:T(8,128)(2,1)S(1)} all-to-all(bf16[32,64,512]{2,1,0:T(8,128)(2,1)} %bitcast.55), channel_id=1, replica_groups=mesh['expert'=32,'tensor'=4] {'expert'}, dimensions={0} | all-to-all | bytes 4194304 | tf_op jit(solution)/shard_map/all_to_all | solution.py:777
  65.6 24.3 %all-gather.3.cloned.1.call-done.w_ref.refs_10_.refs_13_ = bf16[2048,2240]{1,0:T(8,128)(2,1)} async-done(((bf16[64,2240]{1,0:T(8,128)(2,1)}), bf16[2048,2240]{1,0:T(8,128)(2,1)}) %all-gather.3.cloned.1.call-update) | async-done | bytes 9175056 | tf_op jit(solution)/shard_map/all_gather | solution.py:846
  89.8 11.2 %attend.1 = (f32[256,512]{1,0:T(8,128)}, bf16[256,512]{1,0:T(8,128)(2,1)}, bf16[256,512]{1,0:T(8,128)(2,1)}, bf16[256,512]{1,0:T(8,128)(2,1)}, bf16[256,2048]{1,...) custom-call(s32[1]{0:T(128)} %bitcast.me_ref.refs_0_, ...), custom_call_target="tpu_custom_call" | custom-call | flops 201326592 | bytes 1627136 | tf_op jit(solution)/shard_map/attend/pallas_call | solution.py:81
  102.6 2.7 collective-permute-start.1
  106.8 7.4 %collective-permute-done = bf16[256,512]{1,0:T(8,128)(2,1)S(1)} collective-permute-done((bf16[256,512]{1,0:T(8,128)(2,1)}, bf16[256,512]{1,0:T(8,128)(2,1)S(1)}, u32[]{:S(2)}, u32[]{:S(2)}) %collective-permute-start) | collective-permute-done | bytes 262176 | tf_op jit(solution)/shard_map/ppermute | solution.py:749
  114.2 6.8 %collective-permute-done.1 = bf16[256,512]{1,0:T(8,128)(2,1)S(1)} collective-permute-done((bf16[256,512]{1,0:T(8,128)(2,1)}, bf16[256,512]{1,0:T(8,128)(2,1)S(1)}, u32[]{:S(2)}, u32[]{:S(2)}) %collective-permute-start.1) | collective-permute-done | bytes 262176 | tf_op jit(solution)/shard_map/ppermute | solution.py:749
  122.2 1.9 collective-permute-start.5
  125.6 8.9 %collective-permute-done.5.a1_ref = bf16[256,512]{1,0:T(8,128)(2,1)S(1)} collective-permute-done((bf16[256,512]{1,0:T(8,128)(2,1)S(1)}, bf16[256,512]{1,0:T(8,128)(2,1)S(1)}, u32[]{:S(2)}, u32[]{:S(2)}) %collective-permute-start.5) | collective-permute-done | bytes 262176 | tf_op jit(solution)/shard_map/ppermute | solution.py:749
  134.8 3.4 collective-permute-done.7.a3_ref
  138.9 6.7 %dispatch.1 = (f32[256,2048]{1,0:T(8,128)}, bf16[256,2048]{1,0:T(8,128)(2,1)}, bf16[32,32,2560]{2,1,0:T(8,128)(2,1)}) custom-call(s32[1]{0:T(128)} %bitcast.me_ref.refs_0_, bf16[256,2048]{1,0:T(8,128)(2,1)} %stream_ref.7, bf16[256,512]{1,0:T(8,128)(2,1)} %copy-done.8, bf16[256,512]{1,0:T(8,128)(2,1)} %copy-done.17, bf16[256,512]{1,0:T(8,128)(2,1)} %copy-done.18, ...), custom_call_target="tpu_custom_call" | custom-call | flops 134217728 | bytes 1159987 | tf_op jit(solution)/shard_map/dispatch/pallas_call | solution.py:81
  145.6 4.9 all-to-all-start.1
  150.6 2.3 slice.71
  154.2 3.3 collective-permute-start.9
  157.5 22.0 %collective-permute-done.8 = bf16[16,2,32,512]{3,2,1,0:T(8,128)(2,1)S(1)} collective-permute-done((bf16[16,2,32,512]{3,2,1,0:T(8,128)(2,1)}, bf16[16,2,32,512]{3,2,1,0:T(8,128)(2,1)S(1)}, u32[]{:S(2)}, u32[]{:S(2)}) %collective-permute-start.8) | collective-permute-done | bytes 1048608 | tf_op jit(solution)/shard_map/ppermute | solution.py:749
  183.2 16.5 %shared.1 = (f32[256,512]{1,0:T(8,128)}, bf16[256,512]{1,0:T(8,128)(2,1)}, bf16[256,512]{1,0:T(8,128)(2,1)}, bf16[256,512]{1,0:T(8,128)(2,1)}, f32[256,2048]{1,0...) custom-call(s32[1]{0:T(128)} %bitcast.me_ref.refs_0_, bf16[256,2048]{1,0:T(8,128)(2,1)} %get-tuple-element.115.mixed_ref, ...), custom_call_target="tpu_custom_call" | custom-call | flops 664377728 | bytes 2346189 | tf_op jit(solution)/shard_map/shared/pallas_call | solution.py:81
  199.7 15.9 %all-to-all-done.1.refs_2_.x0_ref = bf16[32,32,2560]{2,1,0:T(8,128)(2,1)} async-done(((bf16[32,32,2560]{2,1,0:T(8,128)(2,1)}), bf16[32,32,2560]{2,1,0:T(8,128)(2,1)}, u32[]{:S(2)}, u32[]{:S(2)}) %all-to-all-start.1) | async-done | bytes 5242912 | tf_op jit(solution)/shard_map/all_to_all | solution.py:777
  216.9 3.6 collective-permute-start.10
  220.6 16.3 %expert_back.2 = (bf16[32,32,2176]{2,1,0:T(8,128)(2,1)}, bf16[32,32,2048]{2,1,0:T(8,128)(2,1)}, bf16[1024,352]{1,0:T(8,128)(2,1)}, bf16[1024,352]{1,0:T(8,128)(2,1)}, bf16[1024,352]{1,0:T(8,128)(2,1)}) custom-call(s32[1]{0:T(128)} %bitcast.me_ref.refs_0_, s32[1]{0:T(128)} %bitcast.13.refs_1_, bf16[32,32,2560]{2,1,0:T(8,128)(2,1)} %all-to-all-done.1.refs_2_.x0_ref, ...), custom_call_target="tpu_custom_call" | custom-call | flops 73819750400 | bytes 25165824 | tf_op jit(solution)/shard_map/expert_back/pallas_call | solution.py:357
  236.9 5.3 expert_out.2
  244.4 3.1 collective-permute-start.13
  247.5 8.4 %all-to-all-start.2 = ((bf16[32,32,2176]{2,1,0:T(8,128)(2,1)}), bf16[32,32,2176]{2,1,0:T(8,128)(2,1)}, u32[]{:S(2)}, u32[]{:S(2)}) async-start(bf16[32,32,2176]{2,1,0:T(8,128)(2,1)} %get-tuple-element.126), calls=%async_computation.4 | async-start | bytes 8912896 | tf_op jit(solution)/shard_map/all_to_all | solution.py:777
  256.0 5.9 %collective-permute-done.12 = bf16[16,32,512]{2,1,0:T(8,128)(2,1)S(1)} collective-permute-done((bf16[16,32,512]{2,1,0:T(8,128)(2,1)S(1)}, bf16[16,32,512]{2,1,0:T(8,128)(2,1)S(1)}, u32[]{:S(2)}, u32[]{:S(2)}) %collective-permute-start.12) | collective-permute-done | bytes 524320 | tf_op jit(solution)/shard_map/ppermute | solution.py:749
  261.9 4.7 collective-permute-done.13
  267.6 16.7 %expert_back.3 = (bf16[32,32,2176]{2,1,0:T(8,128)(2,1)}, bf16[32,32,2048]{2,1,0:T(8,128)(2,1)}, bf16[1024,352]{1,0:T(8,128)(2,1)}, bf16[1024,352]{1,0:T(8,128)(2...) custom-call(s32[1]{0:T(128)} %bitcast.me_ref.refs_0_, s32[1]{0:T(128)} %bitcast.13.refs_1_, ...), custom_call_target="tpu_custom_call" | custom-call | flops 73819750400 | bytes 25165824 | tf_op jit(solution)/shard_map/expert_back/pallas_call | solution.py:357
  284.3 5.4 expert_out.3
  289.7 22.3 %all-to-all-done.2.b_ref = bf16[32,32,2176]{2,1,0:T(8,128)(2,1)} async-done(((bf16[32,32,2176]{2,1,0:T(8,128)(2,1)}), bf16[32,32,2176]{2,1,0:T(8,128)(2,1)}, u32[]{:S(2)}, u32[]{:S(2)}) %all-to-all-start.2) | async-done | bytes 4456480 | tf_op jit(solution)/shard_map/all_to_all | solution.py:777
  312.0 6.6 %all-to-all-start.3 = ((bf16[32,32,2176]{2,1,0:T(8,128)(2,1)}), bf16[32,32,2176]{2,1,0:T(8,128)(2,1)}, u32[]{:S(2)}, u32[]{:S(2)}) async-start(bf16[32,32,2176]{2,1,0:T(8,128)(2,1)} %get-tuple-element.136), calls=%async_computation.5 | async-start | bytes 8912896 | tf_op jit(solution)/shard_map/all_to_all | solution.py:777
  318.8 19.4 %expert_grads.1 = (f32[2,352,2048]{2,1,0:T(8,128)}, f32[2,352,2048]{2,1,0:T(8,128)}, f32[2,352,2048]{2,1,0:T(8,128)}) custom-call(bf16[32,32,2560]{2,1,0:T(8,128)(2,1)} %all-to-all-done.1.refs_2_.x0_ref, bf16[32,32,2048]{2,1,0:T(8,128)(2,1)} %get-tuple-element.124.c0_ref, bf16[1024,352]{1,0:T(8,128)(2,1)} %get-tuple-element.120.hg_ref.hg0_ref, ...), custom_call_target="tpu_custom_call" | custom-call | flops 738197504 | bytes 4177920 | tf_op jit(solution)/shard_map/expert_grads/pallas_call | solution.py:436
  338.2 6.1 %combine_first.1 = (f32[256,2048]{1,0:T(8,128)}, f32[256,128]{1,0:T(8,128)}) custom-call(bf16[256,1024]{1,0:T(8,128)(2,1)} %get-tuple-element.112.t0_ref.t_ref, bf16[32,32,2176]{2,1,0:T(8,128)(2,1)} %all-to-all-done.2.b_ref, f32[256,2048]{1,0:T(8,128)} %get-tuple-element.117.shared_ref), custom_call_target="tpu_custom_call" | custom-call | flops 107374184 | bytes 930611 | tf_op jit(solution)/shard_map/combine_first/pallas_call | solution.py:81
  344.3 30.2 %all-to-all-done.3.b_ref = bf16[32,32,2176]{2,1,0:T(8,128)(2,1)} async-done(((bf16[32,32,2176]{2,1,0:T(8,128)(2,1)}), bf16[32,32,2176]{2,1,0:T(8,128)(2,1)}, u32[]{:S(2)}, u32[]{:S(2)}) %all-to-all-start.3) | async-done | bytes 4456480 | tf_op jit(solution)/shard_map/all_to_all | solution.py:777
  374.5 5.5 combine.1
  383.3 6.9 %all-to-all-start.4 = ((bf16[32,64,512]{2,1,0:T(8,128)(2,1)}), bf16[32,64,512]{2,1,0:T(8,128)(2,1)S(1)}, u32[]{:S(2)}, u32[]{:S(2)}) async-start(bf16[32,64,512]{2,1,0:T(8,128)(2,1)} %bitcast.49), calls=%async_computation.6 | async-start | bytes 4194304 | tf_op jit(solution)/shard_map/all_to_all | solution.py:777
  393.5 15.1 %collective-permute-done.20.r1_ref = bf16[256,640]{1,0:T(8,128)(2,1)S(1)} collective-permute-done((bf16[256,640]{1,0:T(8,128)(2,1)}, bf16[256,640]{1,0:T(8,128)(2,1)S(1)}, u32[]{:S(2)}, u32[]{:S(2)}) %collective-permute-start.20) | collective-permute-done | bytes 327712 | tf_op jit(solution)/shard_map/ppermute | solution.py:749
  410.5 2.2 collective-permute-start.23
  413.9 9.8 %collective-permute-done.23.a1_ref = bf16[256,512]{1,0:T(8,128)(2,1)} collective-permute-done((bf16[256,512]{1,0:T(8,128)(2,1)S(1)}, bf16[256,512]{1,0:T(8,128)(2,1)}, u32[]{:S(2)}, u32[]{:S(2)}) %collective-permute-start.23) | collective-permute-done | bytes 262176 | tf_op jit(solution)/shard_map/ppermute | solution.py:749
  423.6 3.8 collective-permute-done.25.a3_ref
  427.4 23.2 %attend_back.1 = (bf16[16,64,2240]{2,1,0:T(8,128)(2,1)}, bf16[16,64,2240]{2,1,0:T(8,128)(2,1)}, f32[256,2048]{1,0:T(8,128)}, f32[256,512]{1,0:T(8,128)}, bf16[25...) custom-call(s32[1]{0:T(128)} %bitcast.me_ref.refs_0_, s32[1]{0:T(128)} %bitcast.21.core_ref, ...), custom_call_target="tpu_custom_call" | custom-call | flops 845571712 | bytes 3560244 | tf_op jit(solution)/shard_map/attend_back/pallas_call | solution.py:81
  451.6 7.4 %collective-permute-done.32.got_ref = bf16[16,64,2240]{2,1,0:T(8,128)(2,1)} collective-permute-done((bf16[16,64,2240]{2,1,0:T(8,128)(2,1)}, bf16[16,64,2240]{2,1,0:T(8,128)(2,1)}, u32[]{:S(2)}, u32[]{:S(2)}) %collective-permute-start.32) | collective-permute-done | bytes 4587552 | tf_op jit(solution)/shard_map/ppermute | solution.py:1059
  459.0 6.5 %pair.1 = (bf16[4,4,64,1088]{3,2,1,0:T(8,128)(2,1)}, bf16[4,64,1152]{2,1,0:T(8,128)(2,1)}, bf16[4,64,1152]{2,1,0:T(8,128)(2,1)}, bf16[4,64,1152]{2,1,0:T(8,128)(2,1)}, bf16[4,64,1152]{2,1,0:T(8,128)(2,1)}) custom-call(s32[2]{0:T(128)} %pad_add_fusion.at_ref, bf16[16,64,2240]{2,1,0:T(8,128)(2,1)} %get-tuple-element.164.keep_ref, ...), custom_call_target="tpu_custom_call" | custom-call | bytes 1376256 | tf_op jit(solution)/shard_map/pair/pallas_call | solution.py:81
  465.5 4.2 copy.58
  469.7 4.6 all-to-all-start.5
  475.1 3.9 collective-permute-start.27
  480.9 3.8 collective-permute-done.14.r1_ref
  484.7 3.1 collective-permute-start.34
  487.8 7.0 %collective-permute-done.26 = bf16[256,512]{1,0:T(8,128)(2,1)S(1)} collective-permute-done((bf16[256,512]{1,0:T(8,128)(2,1)}, bf16[256,512]{1,0:T(8,128)(2,1)S(1)}, u32[]{:S(2)}, u32[]{:S(2)}) %collective-permute-start.26) | collective-permute-done | bytes 262176 | tf_op jit(solution)/shard_map/ppermute | solution.py:749
  494.9 2.9 collective-permute-start.35
  499.0 7.4 %collective-permute-done.15.r2_ref = bf16[256,512]{1,0:T(8,128)(2,1)S(1)} collective-permute-done((bf16[256,512]{1,0:T(8,128)(2,1)}, bf16[256,512]{1,0:T(8,128)(2,1)S(1)}, u32[]{:S(2)}, u32[]{:S(2)}) %collective-permute-start.15) | collective-permute-done | bytes 262176 | tf_op jit(solution)/shard_map/ppermute | solution.py:749
  509.4 2.0 collective-permute-start.30
  511.4 3.6 routed.1.a0_ref
  515.8 3.2 collective-permute-start.17
  520.0 2.6 cross.2
  522.6 2.2 collective-permute-start.36
  524.8 6.5 %collective-permute-done.31.a3_ref = bf16[256,512]{1,0:T(8,128)(2,1)S(1)} collective-permute-done((bf16[256,512]{1,0:T(8,128)(2,1)S(1)}, bf16[256,512]{1,0:T(8,128)(2,1)S(1)}, u32[]{:S(2)}, u32[]{:S(2)}) %collective-permute-start.31) | collective-permute-done | bytes 262176 | tf_op jit(solution)/shard_map/ppermute | solution.py:749
  532.0 5.0 stream.1
  537.0 3.4 result.1
  541.5 2.6 copy.59
  544.1 2.6 cross.3
  546.7 2.3 collective-permute-start.39
  550.7 2.6 collective-permute-start.41
  556.9 2.3 unpack.1
  559.2 2.1 collective-permute-start.43
  561.3 2.6 collective-permute-start.44
  564.6 3.1 collective-permute-done.42.r1_ref
  (184 shorter events, 63.5 us)
Async XLA Ops:
  7.2 82.6 %all-gather.3.cloned.1.call-start = ((), (), s32[]{:S(2)}) async-start(), calls=%async_computation.9 | async-start | bytes 9732096 | tf_op jit(solution)/shard_map/all_gather | solution.py:846
  13.3 169.9 %all-gather.5.cloned.1.call-start = ((), (), s32[]{:S(2)}) async-start(), calls=%async_computation.10 | async-start | bytes 9191424 | tf_op jit(solution)/shard_map/all_gather | solution.py:847
  19.9 44.9 %copy-start.29 = (s32[1,256]{1,0:T(1,128)S(1)}, s32[1,256]{1,0:T(1,128)}, u32[]{:S(2)}) copy-start(s32[1,256]{1,0:T(1,128)} %seg_row_ref.1) | copy-start | bytes 3076
  59.5 41.6 %copy-start.1 = (bf16[32,64,512]{2,1,0:T(8,128)(2,1)}, bf16[32,64,512]{2,1,0:T(8,128)(2,1)S(1)}, u32[]{:S(2)}) copy-start(bf16[32,64,512]{2,1,0:T(8,128)(2,1)S(1)} %all_to_all.30) | copy-start | bytes 6291460
  59.5 62.7 %collective-permute-start.3 = (bf16[32,2,32,512]{3,2,1,0:T(8,128)(2,1)S(1)}, bf16[32,2,32,512]{3,2,1,0:T(8,128)(2,1)}, u32[]{:S(2)}, u32[]{:S(2)}) collective-permute-start(bf16[32,2,32,512]{3,2,1,0:T(8,128)(2,1)S(1)} %bitcast.51), channel_id=1, source_target_pairs={{0,1},{1,2},{2,3},{3,0},{4,5},{5,6},{6,7},{7,4},{8,9},{9,10},{10,1... | collective-permute-start | bytes 6291464 | tf_op jit(solution)/shard_map/ppermute | solution.py:749
  61.1 61.1 %collective-permute-start.4 = (bf16[32,2,32,512]{3,2,1,0:T(8,128)(2,1)S(1)}, bf16[32,2,32,512]{3,2,1,0:T(8,128)(2,1)}, u32[]{:S(2)}, u32[]{:S(2)}) collective-permute-start(bf16[32,2,32,512]{3,2,1,0:T(8,128)(2,1)S(1)} %bitcast.52), channel_id=1, source_target_pairs={{0,3},{1,0},{2,1},{3,2},{4,7},{5,4},{6,5},{7,6},{8,11},{9,8},{10,9... | collective-permute-start | bytes 6291464 | tf_op jit(solution)/shard_map/ppermute | solution.py:749
  101.1 13.1 %collective-permute-start = (bf16[256,512]{1,0:T(8,128)(2,1)}, bf16[256,512]{1,0:T(8,128)(2,1)S(1)}, u32[]{:S(2)}, u32[]{:S(2)}) collective-permute-start(bf16[256,512]{1,0:T(8,128)(2,1)} %get-tuple-element.107), channel_id=1, source_target_pairs={{0,1},{1,2},{2,3},{3,0},{4,5},{5,6},{6,7},{7,4},{8,9},{9,10},{10,1... | collective-permute-start | bytes 786440 | tf_op jit(solution)/shard_map/ppermute | solution.py:749
  102.6 18.3 %collective-permute-start.1 = (bf16[256,512]{1,0:T(8,128)(2,1)}, bf16[256,512]{1,0:T(8,128)(2,1)S(1)}, u32[]{:S(2)}, u32[]{:S(2)}) collective-permute-start(bf16[256,512]{1,0:T(8,128)(2,1)} %get-tuple-element.108), channel_id=1, source_target_pairs={{0,2},{1,3},{2,0},{3,1},{4,6},{5,7},{6,4},{7,5},{8,10},{9,11},{10,... | collective-permute-start | bytes 786440 | tf_op jit(solution)/shard_map/ppermute | solution.py:749
  105.3 15.6 %collective-permute-start.2 = (bf16[256,512]{1,0:T(8,128)(2,1)}, bf16[256,512]{1,0:T(8,128)(2,1)S(1)}, u32[]{:S(2)}, u32[]{:S(2)}) collective-permute-start(bf16[256,512]{1,0:T(8,128)(2,1)} %get-tuple-element.109), channel_id=1, source_target_pairs={{0,3},{1,0},{2,1},{3,2},{4,7},{5,4},{6,5},{7,6},{8,11},{9,8},{10,9... | collective-permute-start | bytes 786440 | tf_op jit(solution)/shard_map/ppermute | solution.py:749
  122.1 16.1 %copy-start.8 = (bf16[256,512]{1,0:T(8,128)(2,1)}, bf16[256,512]{1,0:T(8,128)(2,1)S(1)}, u32[]{:S(2)}) copy-start(bf16[256,512]{1,0:T(8,128)(2,1)S(1)} %add_convert_fusion.2.a0_ref) | copy-start | bytes 786436
  122.2 12.3 %collective-permute-start.5 = (bf16[256,512]{1,0:T(8,128)(2,1)S(1)}, bf16[256,512]{1,0:T(8,128)(2,1)S(1)}, u32[]{:S(2)}, u32[]{:S(2)}) collective-permute-start(bf16[256,512]{1,0:T(8,128)(2,1)S(1)} %add_convert_fusion.2.a0_ref), channel_id=1, source_target_pairs={{0,3},{1,0},{2,1},{3,2},{4,7},{5,4},{6,5},{7,6},{8,11},{9,8},{10,9... | collective-permute-start | bytes 786440 | tf_op jit(solution)/shard_map/ppermute | solution.py:749
  124.0 10.8 %collective-permute-start.6 = (bf16[256,512]{1,0:T(8,128)(2,1)S(1)}, bf16[256,512]{1,0:T(8,128)(2,1)S(1)}, u32[]{:S(2)}, u32[]{:S(2)}) collective-permute-start(bf16[256,512]{1,0:T(8,128)(2,1)S(1)} %add_convert_fusion.2.a0_ref), channel_id=1, source_target_pairs={{0,2},{1,3},{2,0},{3,1},{4,6},{5,7},{6,4},{7,5},{8,10},{9,11},{10,... | collective-permute-start | bytes 786440 | tf_op jit(solution)/shard_map/ppermute | solution.py:749
  124.8 13.4 %collective-permute-start.7 = (bf16[256,512]{1,0:T(8,128)(2,1)S(1)}, bf16[256,512]{1,0:T(8,128)(2,1)S(1)}, u32[]{:S(2)}, u32[]{:S(2)}) collective-permute-start(bf16[256,512]{1,0:T(8,128)(2,1)S(1)} %add_convert_fusion.2.a0_ref), channel_id=1, source_target_pairs={{0,1},{1,2},{2,3},{3,0},{4,5},{5,6},{6,7},{7,4},{8,9},{9,10},{10,1... | collective-permute-start | bytes 786440 | tf_op jit(solution)/shard_map/ppermute | solution.py:749
  145.6 69.9 %all-to-all-start.1 = ((bf16[32,32,2560]{2,1,0:T(8,128)(2,1)}), bf16[32,32,2560]{2,1,0:T(8,128)(2,1)}, u32[]{:S(2)}, u32[]{:S(2)}) async-start(bf16[32,32,2560]{2,1,0:T(8,128)(2,1)} %get-tuple-element.119), calls=%async_computation.1 | async-start | bytes 10485760 | tf_op jit(solution)/shard_map/all_to_all | solution.py:777
  150.5 229.5 %reduce-scatter.4.cloned.1.call-start = ((), (), s32[]{:S(2)}) async-start(), calls=%async_computation.11 | async-start | bytes 5242880 | tf_op jit(solution)/shard_map/reduce_scatter | solution.py:975
  152.9 26.6 %collective-permute-start.8 = (bf16[16,2,32,512]{3,2,1,0:T(8,128)(2,1)}, bf16[16,2,32,512]{3,2,1,0:T(8,128)(2,1)S(1)}, u32[]{:S(2)}, u32[]{:S(2)}) collective-permute-start(bf16[16,2,32,512]{3,2,1,0:T(8,128)(2,1)} %slice.71), channel_id=1, source_target_pairs={{0,1},{1,2},{2,3},{3,0},{4,5},{5,6},{6,7},{7,4},{8,9},{9,10},{10,1... | collective-permute-start | bytes 3145736 | tf_op jit(solution)/shard_map/ppermute | solution.py:749
  154.2 25.7 %collective-permute-start.9 = (bf16[16,2,32,512]{3,2,1,0:T(8,128)(2,1)S(1)}, bf16[16,2,32,512]{3,2,1,0:T(8,128)(2,1)S(1)}, u32[]{:S(2)}, u32[]{:S(2)}) collective-permute-start(bf16[16,2,32,512]{3,2,1,0:T(8,128)(2,1)S(1)} %slice.72), channel_id=1, source_target_pairs={{0,3},{1,0},{2,1},{3,2},{4,7},{5,4},{6,5},{7,6},{8,11},{9,8},{10,9... | collective-permute-start | bytes 3145736 | tf_op jit(solution)/shard_map/ppermute | solution.py:749
  216.9 26.1 %collective-permute-start.11 = (bf16[32,32,512]{2,1,0:T(8,128)(2,1)S(1)}, bf16[32,32,512]{2,1,0:T(8,128)(2,1)S(1)}, u32[]{:S(2)}, u32[]{:S(2)}) collective-permute-start(bf16[32,32,512]{2,1,0:T(8,128)(2,1)S(1)} %slice.73), channel_id=1, source_target_pairs={{0,1},{1,2},{2,3},{3,0},{4,5},{5,6},{6,7},{7,4},{8,9},{9,10},{10,1... | collective-permute-start | bytes 3145736 | tf_op jit(solution)/shard_map/ppermute | solution.py:749
  216.9 26.1 %collective-permute-start.10 = (bf16[32,32,512]{2,1,0:T(8,128)(2,1)S(1)}, bf16[32,32,512]{2,1,0:T(8,128)(2,1)}, u32[]{:S(2)}, u32[]{:S(2)}) collective-permute-start(bf16[32,32,512]{2,1,0:T(8,128)(2,1)S(1)} %slice.73), channel_id=1, source_target_pairs={{0,3},{1,0},{2,1},{3,2},{4,7},{5,4},{6,5},{7,6},{8,11},{9,8},{10,9... | collective-permute-start | bytes 3145736 | tf_op jit(solution)/shard_map/ppermute | solution.py:749
  243.0 18.9 %collective-permute-start.12 = (bf16[16,32,512]{2,1,0:T(8,128)(2,1)S(1)}, bf16[16,32,512]{2,1,0:T(8,128)(2,1)S(1)}, u32[]{:S(2)}, u32[]{:S(2)}) collective-permute-start(bf16[16,32,512]{2,1,0:T(8,128)(2,1)S(1)} %slice.74), channel_id=1, source_target_pairs={{0,1},{1,2},{2,3},{3,0},{4,5},{5,6},{6,7},{7,4},{8,9},{9,10},{10,1... | collective-permute-start | bytes 1572872 | tf_op jit(solution)/shard_map/ppermute | solution.py:749
  244.4 22.2 %collective-permute-start.13 = (bf16[16,32,512]{2,1,0:T(8,128)(2,1)S(1)}, bf16[16,32,512]{2,1,0:T(8,128)(2,1)S(1)}, u32[]{:S(2)}, u32[]{:S(2)}) collective-permute-start(bf16[16,32,512]{2,1,0:T(8,128)(2,1)S(1)} %slice.75), channel_id=1, source_target_pairs={{0,3},{1,0},{2,1},{3,2},{4,7},{5,4},{6,5},{7,6},{8,11},{9,8},{10,9... | collective-permute-start | bytes 1572872 | tf_op jit(solution)/shard_map/ppermute | solution.py:749
  247.5 64.5 %all-to-all-start.2 = ((bf16[32,32,2176]{2,1,0:T(8,128)(2,1)}), bf16[32,32,2176]{2,1,0:T(8,128)(2,1)}, u32[]{:S(2)}, u32[]{:S(2)}) async-start(bf16[32,32,2176]{2,1,0:T(8,128)(2,1)} %get-tuple-element.126), calls=%async_computation.4 | async-start | bytes 8912896 | tf_op jit(solution)/shard_map/all_to_all | solution.py:777
  255.9 124.1 %reduce-scatter.6.cloned.1.call-start = ((), (), s32[]{:S(2)}) async-start(), calls=%async_computation.12 | async-start | bytes 5242880 | tf_op jit(solution)/shard_map/reduce_scatter | solution.py:975
  312.0 62.5 %all-to-all-start.3 = ((bf16[32,32,2176]{2,1,0:T(8,128)(2,1)}), bf16[32,32,2176]{2,1,0:T(8,128)(2,1)}, u32[]{:S(2)}, u32[]{:S(2)}) async-start(bf16[32,32,2176]{2,1,0:T(8,128)(2,1)} %get-tuple-element.136), calls=%async_computation.5 | async-start | bytes 8912896 | tf_op jit(solution)/shard_map/all_to_all | solution.py:777
  318.6 234.7 %reduce-scatter.8.cloned.1.call-start = ((), (), s32[]{:S(2)}) async-start(), calls=%async_computation.13 | async-start | bytes 9191424 | tf_op jit(solution)/shard_map/reduce_scatter | solution.py:1002
  383.3 67.3 %all-to-all-start.4 = ((bf16[32,64,512]{2,1,0:T(8,128)(2,1)}), bf16[32,64,512]{2,1,0:T(8,128)(2,1)S(1)}, u32[]{:S(2)}, u32[]{:S(2)}) async-start(bf16[32,64,512]{2,1,0:T(8,128)(2,1)} %bitcast.49), calls=%async_computation.6 | async-start | bytes 4194304 | tf_op jit(solution)/shard_map/all_to_all | solution.py:777
  390.2 18.4 %collective-permute-start.20 = (bf16[256,640]{1,0:T(8,128)(2,1)}, bf16[256,640]{1,0:T(8,128)(2,1)S(1)}, u32[]{:S(2)}, u32[]{:S(2)}) collective-permute-start(bf16[256,640]{1,0:T(8,128)(2,1)} %get-tuple-element.145), channel_id=1, source_target_pairs={{0,1},{1,2},{2,3},{3,0},{4,5},{5,6},{6,7},{7,4},{8,9},{9,10},{10,1... | collective-permute-start | bytes 983048 | tf_op jit(solution)/shard_map/ppermute | solution.py:749
  390.3 18.3 %collective-permute-start.21 = (bf16[256,640]{1,0:T(8,128)(2,1)}, bf16[256,640]{1,0:T(8,128)(2,1)S(1)}, u32[]{:S(2)}, u32[]{:S(2)}) collective-permute-start(bf16[256,640]{1,0:T(8,128)(2,1)} %get-tuple-element.146), channel_id=1, source_target_pairs={{0,2},{1,3},{2,0},{3,1},{4,6},{5,7},{6,4},{7,5},{8,10},{9,11},{10,... | collective-permute-start | bytes 983048 | tf_op jit(solution)/shard_map/ppermute | solution.py:749
  391.7 17.5 %collective-permute-start.22 = (bf16[256,640]{1,0:T(8,128)(2,1)S(1)}, bf16[256,640]{1,0:T(8,128)(2,1)S(1)}, u32[]{:S(2)}, u32[]{:S(2)}) collective-permute-start(bf16[256,640]{1,0:T(8,128)(2,1)S(1)} %copy-done.30), channel_id=1, source_target_pairs={{0,3},{1,0},{2,1},{3,2},{4,7},{5,4},{6,5},{7,6},{8,11},{9,8},{10,9... | collective-permute-start | bytes 983048 | tf_op jit(solution)/shard_map/ppermute | solution.py:749
  408.6 18.8 %copy-start.3 = (bf16[256,640]{1,0:T(8,128)(2,1)}, bf16[256,640]{1,0:T(8,128)(2,1)S(1)}, u32[]{:S(2)}) copy-start(bf16[256,640]{1,0:T(8,128)(2,1)S(1)} %collective-permute-done.20.r1_ref) | copy-start | bytes 983044
  408.6 18.8 %copy-start.4 = (bf16[256,640]{1,0:T(8,128)(2,1)}, bf16[256,640]{1,0:T(8,128)(2,1)S(1)}, u32[]{:S(2)}) copy-start(bf16[256,640]{1,0:T(8,128)(2,1)S(1)} %collective-permute-done.21.r2_ref) | copy-start | bytes 983044
  409.2 18.2 %copy-start.5 = (bf16[256,640]{1,0:T(8,128)(2,1)}, bf16[256,640]{1,0:T(8,128)(2,1)S(1)}, u32[]{:S(2)}) copy-start(bf16[256,640]{1,0:T(8,128)(2,1)S(1)} %collective-permute-done.22.r3_ref) | copy-start | bytes 983044
  410.5 16.9 %copy-start.6 = (bf16[256,512]{1,0:T(8,128)(2,1)}, bf16[256,512]{1,0:T(8,128)(2,1)S(1)}, u32[]{:S(2)}) copy-start(bf16[256,512]{1,0:T(8,128)(2,1)S(1)} %add_convert_fusion.1.a0_ref) | copy-start | bytes 786436
  410.5 13.1 %collective-permute-start.23 = (bf16[256,512]{1,0:T(8,128)(2,1)S(1)}, bf16[256,512]{1,0:T(8,128)(2,1)}, u32[]{:S(2)}, u32[]{:S(2)}) collective-permute-start(bf16[256,512]{1,0:T(8,128)(2,1)S(1)} %add_convert_fusion.1.a0_ref), channel_id=1, source_target_pairs={{0,3},{1,0},{2,1},{3,2},{4,7},{5,4},{6,5},{7,6},{8,11},{9,8},{10,9... | collective-permute-start | bytes 786440 | tf_op jit(solution)/shard_map/ppermute | solution.py:749
  412.7 10.9 %collective-permute-start.24 = (bf16[256,512]{1,0:T(8,128)(2,1)S(1)}, bf16[256,512]{1,0:T(8,128)(2,1)}, u32[]{:S(2)}, u32[]{:S(2)}) collective-permute-start(bf16[256,512]{1,0:T(8,128)(2,1)S(1)} %add_convert_fusion.1.a0_ref), channel_id=1, source_target_pairs={{0,2},{1,3},{2,0},{3,1},{4,6},{5,7},{6,4},{7,5},{8,10},{9,11},{10,... | collective-permute-start | bytes 786440 | tf_op jit(solution)/shard_map/ppermute | solution.py:749
  412.9 14.5 %collective-permute-start.25 = (bf16[256,512]{1,0:T(8,128)(2,1)S(1)}, bf16[256,512]{1,0:T(8,128)(2,1)}, u32[]{:S(2)}, u32[]{:S(2)}) collective-permute-start(bf16[256,512]{1,0:T(8,128)(2,1)S(1)} %add_convert_fusion.1.a0_ref), channel_id=1, source_target_pairs={{0,1},{1,2},{2,3},{3,0},{4,5},{5,6},{6,7},{7,4},{8,9},{9,10},{10,1... | collective-permute-start | bytes 786440 | tf_op jit(solution)/shard_map/ppermute | solution.py:749
  450.7 8.3 %collective-permute-start.32 = (bf16[16,64,2240]{2,1,0:T(8,128)(2,1)}, bf16[16,64,2240]{2,1,0:T(8,128)(2,1)}, u32[]{:S(2)}, u32[]{:S(2)}) collective-permute-start(bf16[16,64,2240]{2,1,0:T(8,128)(2,1)} %get-tuple-element.166), channel_id=1, source_target_pairs={{0,4},{4,0},{8,12},{12,8},{16,20},{20,16},{24,28},{28,24},{32,36},... | collective-permute-start | bytes 13762568 | tf_op jit(solution)/shard_map/ppermute | solution.py:1059
  469.7 71.8 %all-to-all-start.5 = ((bf16[4,256,1088]{1,2,0:T(8,128)(2,1)}), bf16[4,256,1088]{1,2,0:T(8,128)(2,1)S(1)}, u32[]{:S(2)}, u32[]{:S(2)}) async-start(bf16[4,256,1088]{1,2,0:T(8,128)(2,1)} %copy.58), calls=%async_computation.8 | async-start | bytes 4456448 | tf_op jit(solution)/shard_map/all_to_all | solution.py:1086
  474.3 10.4 %collective-permute-start.14 = (bf16[256,512]{1,0:T(8,128)(2,1)S(1)}, bf16[256,512]{1,0:T(8,128)(2,1)S(1)}, u32[]{:S(2)}, u32[]{:S(2)}) collective-permute-start(bf16[256,512]{1,0:T(8,128)(2,1)S(1)} %copy-done.31), channel_id=1, source_target_pairs={{0,1},{1,2},{2,3},{3,0},{4,5},{5,6},{6,7},{7,4},{8,9},{9,10},{10,1... | collective-permute-start | bytes 786440 | tf_op jit(solution)/shard_map/ppermute | solution.py:749
  474.3 20.5 %collective-permute-start.26 = (bf16[256,512]{1,0:T(8,128)(2,1)}, bf16[256,512]{1,0:T(8,128)(2,1)S(1)}, u32[]{:S(2)}, u32[]{:S(2)}) collective-permute-start(bf16[256,512]{1,0:T(8,128)(2,1)} %get-tuple-element.161), channel_id=1, source_target_pairs={{0,1},{1,2},{2,3},{3,0},{4,5},{5,6},{6,7},{7,4},{8,9},{9,10},{10,1... | collective-permute-start | bytes 786440 | tf_op jit(solution)/shard_map/ppermute | solution.py:749
  475.1 22.7 %collective-permute-start.27 = (bf16[256,512]{1,0:T(8,128)(2,1)}, bf16[256,512]{1,0:T(8,128)(2,1)S(1)}, u32[]{:S(2)}, u32[]{:S(2)}) collective-permute-start(bf16[256,512]{1,0:T(8,128)(2,1)} %get-tuple-element.162), channel_id=1, source_target_pairs={{0,2},{1,3},{2,0},{3,1},{4,6},{5,7},{6,4},{7,5},{8,10},{9,11},{10,... | collective-permute-start | bytes 786440 | tf_op jit(solution)/shard_map/ppermute | solution.py:749
  479.0 18.7 %collective-permute-start.28 = (bf16[256,512]{1,0:T(8,128)(2,1)}, bf16[256,512]{1,0:T(8,128)(2,1)S(1)}, u32[]{:S(2)}, u32[]{:S(2)}) collective-permute-start(bf16[256,512]{1,0:T(8,128)(2,1)} %get-tuple-element.163), channel_id=1, source_target_pairs={{0,3},{1,0},{2,1},{3,2},{4,7},{5,4},{6,5},{7,6},{8,11},{9,8},{10,9... | collective-permute-start | bytes 786440 | tf_op jit(solution)/shard_map/ppermute | solution.py:749
  479.4 36.4 %collective-permute-start.33 = (bf16[4,64,1152]{2,1,0:T(8,128)(2,1)}, bf16[4,64,1152]{2,1,0:T(8,128)(2,1)S(1)}, u32[]{:S(2)}, u32[]{:S(2)}) collective-permute-start(bf16[4,64,1152]{2,1,0:T(8,128)(2,1)} %get-tuple-element.168), channel_id=1, source_target_pairs={{0,32},{4,36},{8,40},{12,44},{16,48},{20,52},{24,56},{28,60},{32,6... | collective-permute-start | bytes 1769480 | tf_op jit(solution)/shard_map/ppermute | solution.py:1075
  484.7 26.7 %copy-start.12 = (bf16[256,512]{1,0:T(8,128)(2,1)}, bf16[256,512]{1,0:T(8,128)(2,1)S(1)}, u32[]{:S(2)}) copy-start(bf16[256,512]{1,0:T(8,128)(2,1)S(1)} %collective-permute-done.14.r1_ref) | copy-start | bytes 786436
  484.7 34.3 %collective-permute-start.34 = (bf16[4,64,1152]{2,1,0:T(8,128)(2,1)}, bf16[4,64,1152]{2,1,0:T(8,128)(2,1)S(1)}, u32[]{:S(2)}, u32[]{:S(2)}) collective-permute-start(bf16[4,64,1152]{2,1,0:T(8,128)(2,1)} %get-tuple-element.169), channel_id=1, source_target_pairs={{0,64},{4,68},{8,72},{12,76},{16,80},{20,84},{24,88},{28,92},{32,9... | collective-permute-start | bytes 1769480 | tf_op jit(solution)/shard_map/ppermute | solution.py:1075
  494.9 24.2 %collective-permute-start.35 = (bf16[4,64,1152]{2,1,0:T(8,128)(2,1)}, bf16[4,64,1152]{2,1,0:T(8,128)(2,1)}, u32[]{:S(2)}, u32[]{:S(2)}) collective-permute-start(bf16[4,64,1152]{2,1,0:T(8,128)(2,1)} %get-tuple-element.170), channel_id=1, source_target_pairs={{0,96},{4,100},{8,104},{12,108},{16,112},{20,116},{24,120},{28,124... | collective-permute-start | bytes 1769480 | tf_op jit(solution)/shard_map/ppermute | solution.py:1075
  497.7 8.7 %collective-permute-start.15 = (bf16[256,512]{1,0:T(8,128)(2,1)}, bf16[256,512]{1,0:T(8,128)(2,1)S(1)}, u32[]{:S(2)}, u32[]{:S(2)}) collective-permute-start(bf16[256,512]{1,0:T(8,128)(2,1)} %get-tuple-element.143), channel_id=1, source_target_pairs={{0,2},{1,3},{2,0},{3,1},{4,6},{5,7},{6,4},{7,5},{8,10},{9,11},{10,... | collective-permute-start | bytes 786440 | tf_op jit(solution)/shard_map/ppermute | solution.py:749
  497.8 10.9 %collective-permute-start.16 = (bf16[256,512]{1,0:T(8,128)(2,1)}, bf16[256,512]{1,0:T(8,128)(2,1)S(1)}, u32[]{:S(2)}, u32[]{:S(2)}) collective-permute-start(bf16[256,512]{1,0:T(8,128)(2,1)} %get-tuple-element.144), channel_id=1, source_target_pairs={{0,3},{1,0},{2,1},{3,2},{4,7},{5,4},{6,5},{7,6},{8,11},{9,8},{10,9... | collective-permute-start | bytes 786440 | tf_op jit(solution)/shard_map/ppermute | solution.py:749
  499.0 16.7 %copy-start.7 = (bf16[256,512]{1,0:T(8,128)(2,1)}, bf16[256,512]{1,0:T(8,128)(2,1)S(1)}, u32[]{:S(2)}) copy-start(bf16[256,512]{1,0:T(8,128)(2,1)S(1)} %add_convert_fusion.a0_ref) | copy-start | bytes 786436
  506.4 9.4 %collective-permute-start.29 = (bf16[256,512]{1,0:T(8,128)(2,1)S(1)}, bf16[256,512]{1,0:T(8,128)(2,1)}, u32[]{:S(2)}, u32[]{:S(2)}) collective-permute-start(bf16[256,512]{1,0:T(8,128)(2,1)S(1)} %add_convert_fusion.a0_ref), channel_id=1, source_target_pairs={{0,3},{1,0},{2,1},{3,2},{4,7},{5,4},{6,5},{7,6},{8,11},{9,8},{10,9... | collective-permute-start | bytes 786440 | tf_op jit(solution)/shard_map/ppermute | solution.py:749
  509.4 13.2 %collective-permute-start.30 = (bf16[256,512]{1,0:T(8,128)(2,1)S(1)}, bf16[256,512]{1,0:T(8,128)(2,1)}, u32[]{:S(2)}, u32[]{:S(2)}) collective-permute-start(bf16[256,512]{1,0:T(8,128)(2,1)S(1)} %add_convert_fusion.a0_ref), channel_id=1, source_target_pairs={{0,2},{1,3},{2,0},{3,1},{4,6},{5,7},{6,4},{7,5},{8,10},{9,11},{10,... | collective-permute-start | bytes 786440 | tf_op jit(solution)/shard_map/ppermute | solution.py:749
  515.8 15.5 %collective-permute-start.31 = (bf16[256,512]{1,0:T(8,128)(2,1)S(1)}, bf16[256,512]{1,0:T(8,128)(2,1)S(1)}, u32[]{:S(2)}, u32[]{:S(2)}) collective-permute-start(bf16[256,512]{1,0:T(8,128)(2,1)S(1)} %add_convert_fusion.a0_ref), channel_id=1, source_target_pairs={{0,1},{1,2},{2,3},{3,0},{4,5},{5,6},{6,7},{7,4},{8,9},{9,10},{10,1... | collective-permute-start | bytes 786440 | tf_op jit(solution)/shard_map/ppermute | solution.py:749
  515.8 21.2 %collective-permute-start.17 = (bf16[256,512]{1,0:T(8,128)(2,1)}, bf16[256,512]{1,0:T(8,128)(2,1)}, u32[]{:S(2)}, u32[]{:S(2)}) collective-permute-start(bf16[256,512]{1,0:T(8,128)(2,1)} %routed.1.a0_ref), channel_id=1, source_target_pairs={{0,3},{1,0},{2,1},{3,2},{4,7},{5,4},{6,5},{7,6},{8,11},{9,8},{10,9... | collective-permute-start | bytes 786440 | tf_op jit(solution)/shard_map/ppermute | solution.py:749
  519.0 18.0 %collective-permute-start.18 = (bf16[256,512]{1,0:T(8,128)(2,1)}, bf16[256,512]{1,0:T(8,128)(2,1)}, u32[]{:S(2)}, u32[]{:S(2)}) collective-permute-start(bf16[256,512]{1,0:T(8,128)(2,1)} %routed.1.a0_ref), channel_id=1, source_target_pairs={{0,2},{1,3},{2,0},{3,1},{4,6},{5,7},{6,4},{7,5},{8,10},{9,11},{10,... | collective-permute-start | bytes 786440 | tf_op jit(solution)/shard_map/ppermute | solution.py:749
  519.0 18.0 %collective-permute-start.19 = (bf16[256,512]{1,0:T(8,128)(2,1)}, bf16[256,512]{1,0:T(8,128)(2,1)}, u32[]{:S(2)}, u32[]{:S(2)}) collective-permute-start(bf16[256,512]{1,0:T(8,128)(2,1)} %routed.1.a0_ref), channel_id=1, source_target_pairs={{0,1},{1,2},{2,3},{3,0},{4,5},{5,6},{6,7},{7,4},{8,9},{9,10},{10,1... | collective-permute-start | bytes 786440 | tf_op jit(solution)/shard_map/ppermute | solution.py:749
  522.6 28.1 %collective-permute-start.36 = (bf16[64,1152]{1,0:T(8,128)(2,1)}, bf16[64,1152]{1,0:T(8,128)(2,1)S(1)}, u32[]{:S(2)}, u32[]{:S(2)}) collective-permute-start(bf16[64,1152]{1,0:T(8,128)(2,1)} %get-tuple-element.175), channel_id=1, source_target_pairs={{0,8},{4,12},{8,16},{12,20},{16,24},{20,28},{24,0},{28,4},{32,40},... | collective-permute-start | bytes 442376 | tf_op jit(solution)/shard_map/ppermute | solution.py:1075
  540.4 14.7 %collective-permute-start.37 = (bf16[64,1152]{1,0:T(8,128)(2,1)S(1)}, bf16[64,1152]{1,0:T(8,128)(2,1)S(1)}, u32[]{:S(2)}, u32[]{:S(2)}) collective-permute-start(bf16[64,1152]{1,0:T(8,128)(2,1)S(1)} %copy-done.33), channel_id=1, source_target_pairs={{0,16},{4,20},{8,24},{12,28},{16,0},{20,4},{24,8},{28,12},{32,48},... | collective-permute-start | bytes 442376 | tf_op jit(solution)/shard_map/ppermute | solution.py:1075
  540.4 14.7 %collective-permute-start.38 = (bf16[64,1152]{1,0:T(8,128)(2,1)S(1)}, bf16[64,1152]{1,0:T(8,128)(2,1)S(1)}, u32[]{:S(2)}, u32[]{:S(2)}) collective-permute-start(bf16[64,1152]{1,0:T(8,128)(2,1)S(1)} %copy-done.32), channel_id=1, source_target_pairs={{0,24},{4,28},{8,0},{12,4},{16,8},{20,12},{24,16},{28,20},{32,56},... | collective-permute-start | bytes 442376 | tf_op jit(solution)/shard_map/ppermute | solution.py:1075
  546.7 8.4 %collective-permute-start.39 = (bf16[64,1088]{1,0:T(8,128)(2,1)}, bf16[64,1088]{1,0:T(8,128)(2,1)S(1)}, u32[]{:S(2)}, u32[]{:S(2)}) collective-permute-start(bf16[64,1088]{1,0:T(8,128)(2,1)} %get-tuple-element.180), channel_id=1, source_target_pairs={{0,32},{4,36},{8,40},{12,44},{16,48},{20,52},{24,56},{28,60},{32,6... | collective-permute-start | bytes 417800 | tf_op jit(solution)/shard_map/ppermute | solution.py:1075
  549.0 6.9 %collective-permute-start.40 = (bf16[64,1088]{1,0:T(8,128)(2,1)}, bf16[64,1088]{1,0:T(8,128)(2,1)S(1)}, u32[]{:S(2)}, u32[]{:S(2)}) collective-permute-start(bf16[64,1088]{1,0:T(8,128)(2,1)} %get-tuple-element.181), channel_id=1, source_target_pairs={{0,64},{4,68},{8,72},{12,76},{16,80},{20,84},{24,88},{28,92},{32,9... | collective-permute-start | bytes 417800 | tf_op jit(solution)/shard_map/ppermute | solution.py:1075
  550.7 5.6 collective-permute-start.41
  559.2 8.5 %collective-permute-start.42 = (f32[64,640]{1,0:T(8,128)}, f32[64,640]{1,0:T(8,128)S(1)}, u32[]{:S(2)}, u32[]{:S(2)}) collective-permute-start(f32[64,640]{1,0:T(8,128)} %get-tuple-element.183.own_ref), channel_id=1, source_target_pairs={{0,1},{1,2},{2,3},{3,0},{4,5},{5,6},{6,7},{7,4},{8,9},{9,10},{10,1... | collective-permute-start | bytes 491528 | tf_op jit(solution)/shard_map/ppermute | solution.py:749
  559.2 8.5 %collective-permute-start.43 = (f32[64,640]{1,0:T(8,128)}, f32[64,640]{1,0:T(8,128)S(1)}, u32[]{:S(2)}, u32[]{:S(2)}) collective-permute-start(f32[64,640]{1,0:T(8,128)} %get-tuple-element.183.own_ref), channel_id=1, source_target_pairs={{0,2},{1,3},{2,0},{3,1},{4,6},{5,7},{6,4},{7,5},{8,10},{9,11},{10,... | collective-permute-start | bytes 491528 | tf_op jit(solution)/shard_map/ppermute | solution.py:749
  561.3 7.2 %collective-permute-start.44 = (f32[64,640]{1,0:T(8,128)}, f32[64,640]{1,0:T(8,128)S(1)}, u32[]{:S(2)}, u32[]{:S(2)}) collective-permute-start(f32[64,640]{1,0:T(8,128)} %get-tuple-element.183.own_ref), channel_id=1, source_target_pairs={{0,3},{1,0},{2,1},{3,2},{4,7},{5,4},{6,5},{7,6},{8,11},{9,8},{10,9... | collective-permute-start | bytes 491528 | tf_op jit(solution)/shard_map/ppermute | solution.py:749
  (25 other events, 79.6 us)
Sparse Core Ops, SparseCore 0:
  13.4 76.3 all-gather.2
  92.6 53.7 all-gather.4
  242.3 50.1 reduce-scatter.3
  294.9 49.3 reduce-scatter.5
  380.1 92.6 reduce-scatter.7

commit v5 on v4

--- a/solution.py
+++ b/solution.py
@@ -93,7 +93,7 @@
     )(*args)
 
 
-def routing_kernel(me_ref, ids_ref, cot_ref, t0_ref, t1_ref, low_ref, out_ref):
+def routing_kernel(me_ref, ids_ref, cot_ref, t0_ref, t1_ref, s0_ref, s1_ref, low_ref, out_ref):
     choices, tokens = ids_ref.shape
     owners, local, capacity, piece = out_ref.shape
     experts = owners * local
@@ -114,7 +114,7 @@
     low_ref[...] = low
     mine = cot_ref[:, block_at(me_ref[0], 0, cot_ref.shape[1] // piece, piece)].astype(BF16)
     slot = (lax.broadcasted_iota(jnp.int32, (tokens, rows), 1) % capacity).astype(F32)
-    for index, t_ref in ((0, t0_ref), (1, t1_ref)):
+    for index, (t_ref, s_ref) in enumerate(((t0_ref, s0_ref), (t1_ref, s1_ref))):
         spread = jnp.where(
             lax.broadcasted_iota(jnp.int32, (experts, rows), 0)
             == lax.broadcasted_iota(jnp.int32, (experts, rows), 1) // capacity * local + index,
@@ -124,7 +124,9 @@
         wanted = dot_tn(place, spread)
         matrix = jnp.where(wanted == slot, 1.0, 0.0).astype(BF16)
         t_ref[...] = matrix
-        out_ref[:, index] = dot_tn(matrix, mine).astype(BF16).reshape(owners, capacity, piece)
+        by_slot = matrix.T
+        s_ref[...] = by_slot
+        out_ref[:, index] = dot_nn(by_slot, mine).astype(BF16).reshape(owners, capacity, piece)
 
 
 def attend_kernel(
@@ -214,7 +216,7 @@
 
 
 def dispatch_kernel(
-    me_ref, stream_ref, a0_ref, a1_ref, a2_ref, a3_ref, gains_ref, t0_ref, t1_ref, middle_ref, mixed_ref, out_ref
+    me_ref, stream_ref, a0_ref, a1_ref, a2_ref, a3_ref, gains_ref, s0_ref, s1_ref, middle_ref, mixed_ref, out_ref
 ):
     piece = a0_ref.shape[1]
     width = stream_ref.shape[1]
@@ -227,8 +229,8 @@
     mixed = (middle * inverse_rms(middle) * gains_ref[1:2, :]).astype(BF16)
     mixed_ref[...] = mixed
     mine = mixed_ref[:, block_at(me_ref[0], 0, count, piece)]
-    out_ref[:, :, width:] = dot_tn(t1_ref[...], mine).astype(BF16).reshape(owners, capacity, piece)
-    out_ref[:, :, :width] = dot_tn(t0_ref[...], mixed).astype(BF16).reshape(owners, capacity, width)
+    out_ref[:, :, width:] = dot_nn(s1_ref[...], mine).astype(BF16).reshape(owners, capacity, piece)
+    out_ref[:, :, :width] = dot_nn(s0_ref[...], mixed).astype(BF16).reshape(owners, capacity, width)
 
 
 def shared_kernel(
@@ -505,16 +507,16 @@
     r3_ref,
     probs_own_ref,
     router_probs_ref,
-    w_ref,
+    w_in,
     router_ref,
     mixed_ref,
-    normed_ref,
-    query_ref,
-    expanded_ref,
+    normed_in,
+    query_in,
+    expanded_in,
     key_ref,
     latent_ref,
-    compressed_ref,
-    probs_ref,
+    compressed_in,
+    probs_in,
     attended_ref,
     gains_ref,
     latent_gain_ref,
@@ -530,7 +532,14 @@
     scr_ref,
     low_ref,
     wide_ref,
+    w_ref,
+    normed_ref,
+    query_ref,
+    expanded_ref,
+    compressed_ref,
+    probs_ref,
     sems,
+    in_sems,
 ):
     heads, tokens, _ = probs_ref.shape
     width = stream_ref.shape[1]
@@ -544,6 +553,18 @@
     short = LATENT // owners
     count = width // piece
     me = me_ref[0]
+    copies = []
+    for source, target in (
+        (w_in.at[:, edge : outer + 2 * NOPE], w_ref.at[:, edge:]),
+        (probs_in, probs_ref),
+        (expanded_in, expanded_ref),
+        (query_in, query_ref),
+        (compressed_in, compressed_ref),
+        (w_in.at[:, :edge], w_ref.at[:, :edge]),
+        (normed_in, normed_ref),
+    ):
+        copies.append(pltpu.make_async_copy(source, target, in_sems.at[len(copies)]))
+        copies[-1].start()
     probs_grad = probs_own_ref[...]
     for r_ref in (r1_ref, r2_ref, r3_ref):
         other = r_ref[:, piece:].astype(F32)
@@ -562,7 +583,14 @@
     middle_grad = cot_ref[...] + norm_grad
     middle_grad_ref[...] = middle_grad
     middle_low = middle_grad.astype(BF16)
+    core = core_ref[0]
+    router_grad = dot_tn(mixed_ref[...], logits_low)
+    scr_ref[:, outer + 2 * NOPE :] = pltpu.roll(router_grad, ROPE, 1).astype(BF16)
+    scr_ref[:, edge:outer] = dot_tn(middle_low, attended_ref[...]).astype(BF16)
+    copies[0].wait()
     attended_grad = dot_nn(middle_low, w_ref[:, edge:outer]).astype(BF16)
+    for copy in copies[1:5]:
+        copy.wait()
     scale = (NOPE + ROPE) ** (-0.5)
     key_low = key_ref[...]
     key_odd = pltpu.roll(key_low.astype(F32), ROPE, 1).astype(BF16)
@@ -609,6 +637,15 @@
     key_grad = jnp.where(lane < ROPE, key_even_grad + pltpu.roll(key_odd_grad, ROPE, 1), 0.0)
     key_grad = rotated(key_grad, cos_ref[:, :LANES], -sin_ref[:, :LANES])
     low_ref[:, queries + LATENT : edge] = jnp.where(lane < ROPE, key_grad, 0.0).astype(BF16)
+    halves = scr_ref.reshape(owners // 2, 2, shard, scr_ref.shape[1])
+    outgoing = [
+        pltpu.make_async_copy(halves.at[:, 1 - core, :, edge:], pass_ref.at[:, :, edge:], sems.at[0]),
+        pltpu.make_async_copy(halves.at[:, core, :, edge:], keep_ref.at[:, :, edge:], sems.at[1]),
+    ]
+    for copy in outgoing:
+        copy.start()
+    for copy in copies[5:]:
+        copy.wait()
     low = low_ref[...]
     for step, out_ref in enumerate((own_ref, send1_ref, send2_ref, send3_ref)):
         place = block_at(me, step, count, piece)
@@ -631,18 +668,15 @@
     )
     grads4[:, :, queries + LATENT : edge] = key_columns.astype(BF16)
     grads4[:, :short, queries + LATENT : edge] = (key_columns[:, :short] + latent_columns).astype(BF16)
-    scr_ref[:, edge:outer] = dot_tn(middle_low, attended_ref[...]).astype(BF16)
     scr_ref[:, :queries] = dot_tn(normed_ref[...], low[:, :queries]).astype(BF16)
-    router_grad = dot_tn(mixed_ref[...], logits_low)
-    scr_ref[:, outer + 2 * NOPE :] = router_grad[:, ROPE:].astype(BF16)
-    halves = scr_ref.reshape(owners // 2, 2, shard, scr_ref.shape[1])
-    core = core_ref[0]
-    first = pltpu.make_async_copy(halves.at[:, 1 - core], pass_ref, sems.at[0])
-    second = pltpu.make_async_copy(halves.at[:, core], keep_ref, sems.at[1])
-    first.start()
-    second.start()
-    first.wait()
-    second.wait()
+    outgoing += [
+        pltpu.make_async_copy(halves.at[:, 1 - core, :, :edge], pass_ref.at[:, :, :edge], sems.at[2]),
+        pltpu.make_async_copy(halves.at[:, core, :, :edge], keep_ref.at[:, :, :edge], sems.at[3]),
+    ]
+    for copy in outgoing[2:]:
+        copy.start()
+    for copy in outgoing:
+        copy.wait()
 
 
 def pair_kernel(at_ref, keep_ref, got_ref, along_z_ref, *along_x_refs):
@@ -704,11 +738,13 @@
         ]
     late_ref[...] = total[:, queries:edge]
     output_ref[...] = total[:, edge:outer]
-    router_ref[...] = total[:, outer + 2 * NOPE :]
+    router_ref[...] = total[:, outer + 2 * NOPE : outer + 2 * NOPE + ROPE]
 
 
 def late_kernel(own_ref, r1_ref, r2_ref, r3_ref, down_ref, gains_ref):
-    total = own_ref[...] + r1_ref[...] + r2_ref[...] + r3_ref[...]
+    total = own_ref[...]
+    for r_ref in (r1_ref, r2_ref, r3_ref):
+        total = total + r_ref[...].astype(F32)
     down_ref[...] = total[:, : down_ref.shape[1]]
     columns = total[:, LATENT:]
     columns = jnp.concatenate([columns, jnp.zeros(columns.shape, F32)], axis=0)
@@ -853,11 +889,13 @@
     sine = jnp.sin(angles)
     sine = jnp.tile(jnp.concatenate([-sine, sine], axis=1), (1, heads))
 
-    t0, t1, cot_low, cot_out = run(
+    t0, t1, s0, s1, cot_low, cot_out = run(
         routing_kernel,
         [
             ((tokens, rows), BF16),
             ((tokens, rows), BF16),
+            ((rows, tokens), BF16),
+            ((rows, tokens), BF16),
             ((tokens, width), BF16),
             ((owners, local, capacity, piece), BF16),
         ],
@@ -917,7 +955,7 @@
             ((tokens, width), BF16),
             ((owners, capacity, width + piece), BF16),
         ],
-        [me, stream, *share_small(attention), gain_rows, t0, t1],
+        [me, stream, *share_small(attention), gain_rows, s0, s1],
         2 * tokens * rows * (width + piece),
         places=smem,
         name="dispatch",
@@ -1011,8 +1049,8 @@
     keep, passed, middle_grad, own, send1, send2, send3 = run(
         attend_back_kernel,
         [
-            ((owners // 2, shard, outer + 2 * NOPE + experts), BF16),
-            ((owners // 2, shard, outer + 2 * NOPE + experts), BF16),
+            ((owners // 2, shard, outer + 2 * NOPE + LANES), BF16),
+            ((owners // 2, shard, outer + 2 * NOPE + LANES), BF16),
             ((tokens, width), F32),
             ((tokens, piece), F32),
             ((tokens, piece), BF16),
@@ -1047,12 +1085,19 @@
         ],
         2 * tokens * width * (3 * edge + 2 * outer),
         scratch=[
-            pltpu.VMEM((width, outer + 2 * NOPE + experts), BF16),
+            pltpu.VMEM((width, outer + 2 * NOPE + LANES), BF16),
             pltpu.VMEM((tokens, edge), BF16),
             pltpu.VMEM((tokens, width), F32),
-            pltpu.SemaphoreType.DMA((2,)),
+            pltpu.VMEM((width, outer + 2 * NOPE), BF16),
+            pltpu.VMEM(normed.shape, BF16),
+            pltpu.VMEM(query.shape, BF16),
+            pltpu.VMEM(expanded.shape, BF16),
+            pltpu.VMEM(compressed.shape, F32),
+            pltpu.VMEM(probs.shape, F32),
+            pltpu.SemaphoreType.DMA((4,)),
+            pltpu.SemaphoreType.DMA((7,)),
         ],
-        places={0: pltpu.SMEM, 1: pltpu.SMEM},
+        places={0: pltpu.SMEM, 1: pltpu.SMEM} | {i: pl.ANY for i in (14, 17, 18, 19, 22, 23)},
         out_places={0: pl.ANY, 1: pl.ANY},
         name="attend_back",
     )
@@ -1060,8 +1105,8 @@
     side = 4
     chip = lax.axis_index("expert") // 2
     at = jnp.stack([chip // side, lax.rem(chip, side)]).astype(jnp.int32)
-    columns = outer + 2 * NOPE + experts
-    cut = columns // 2 // LANES * LANES + LANES
+    columns = outer + 2 * NOPE + LANES
+    cut = columns // 2
 
     def along(group, array, step):
         def target(i):
@@ -1108,7 +1153,7 @@
     (stream_grad,) = run(
         stream_kernel,
         [((tokens, width), F32)],
-        [me, middle_grad, stream, gain_rows, *share_small(first_sum)],
+        [after(me, parts[0], parts[4]), middle_grad, stream, gain_rows, *share_small(first_sum)],
         0,
         scratch=[pltpu.VMEM((tokens, width), F32)],
         places=smem,
@@ -1126,7 +1171,7 @@
     (result,) = run(
         result_kernel,
         [((tokens, width), F32)],
-        [me, middle, *share_small(branch)],
+        [after(me, parts[0], parts[4]), middle, *share_small(branch)],
         0,
         places=smem,
         name="result",
@@ -1154,7 +1199,7 @@
     latent_down_grad, gain_grads = run(
         late_kernel,
         [(latent_down.shape, F32), ((8, LANES), F32)],
-        [late, *(shift(late, step) for step in range(1, tensors))],
+        [late, *(shift(late.astype(BF16), step) for step in range(1, tensors))],
         0,
         name="late",
     )

time: 590 us -> 576 us (0.976)
  starting transfers between devices: 95.8 us -> 89.4 us
  local copies, waits for them, and re-layouts: 36.8 us -> 30.8 us
  transfers between devices with their start and end apart: 55 -> 55, of which waited for: 29 -> 28; matrix products, arithmetic and copies ran while one was open for 5% -> 4% of each run, Pallas kernels for 28% -> 28%
where the time goes in v5:
time: 576 us; the launch traced here: 567 us
  waiting for transfers between devices  223 us (39%)
  Pallas kernels  161 us (28%)
  starting transfers between devices  89.4 us (16%)
  blocking collectives  39.7 us (7%)
  local copies, waits for them, and re-layouts  30.8 us (5%)
  between operations  14.8 us (3%)
  other arithmetic  8.38 us (1%)
    ppermute x35, waiting for transfers between devices, shift(): lax.ppermute(array, 'tensor', [(i, (i + step) % size) for i in range(size)])  121 us
    pallas_call x15, Pallas kernels, run(): pl.pallas_call(kernel, in_specs=in_specs, out_specs=out_specs, out_shape=...  97.7 us
    all_to_all x4, waiting for transfers between devices, exchange(): lax.all_to_all(rows.reshape(shape[0], -1, shape[-1]), 'expert', split_axi...  68.4 us
    ppermute x35, starting transfers between devices, shift(): lax.ppermute(array, 'tensor', [(i, (i + step) % size) for i in range(size)])  42.7 us
    all_to_all x1, blocking collectives, exchange(): lax.all_to_all(rows.reshape(shape[0], -1, shape[-1]), 'expert', split_axi...  39.7 us
    pallas_call x2, Pallas kernels, expert_back(): pl.pallas_call(functools.partial(expert_back_kernel, split), grid=(owners...  32.9 us
    all_to_all x4, starting transfers between devices, exchange(): lax.all_to_all(rows.reshape(shape[0], -1, shape[-1]), 'expert', split_axi...  26.7 us
    all_gather x1, waiting for transfers between devices, per_device(): one = lax.all_gather(pack_one, 'expert', axis=0, tiled=True)  24.1 us
  transfers between devices with their start and end apart: 55, of which 28 were waited for; matrix products, arithmetic and copies ran while one was open for 4% of the time, Pallas kernels for 28%

profile of v5, /device:TPU:0, one launch (start us, length us, event | category | flops | bytes accessed | tf_op | source)
XLA Modules:
  0.0 566.9 jit_solution(1622010652079081386)
XLA Ops:
  13.3 1.9 concatenate.20
  15.2 4.8 routing.1
  20.0 39.7 %all_to_all.30 = bf16[32,64,512]{2,1,0:T(8,128)(2,1)S(1)} all-to-all(bf16[32,64,512]{2,1,0:T(8,128)(2,1)} %bitcast.55), channel_id=1, replica_groups=mesh['expert'=32,'tensor'=4] {'expert'}, dimensions={0} | all-to-all | bytes 4194304 | tf_op jit(solution)/shard_map/all_to_all | solution.py:813
  59.8 1.8 collective-permute-start.3
  65.9 24.1 %all-gather.3.cloned.1.call-done.w_ref.refs_10_.refs_13_.w_in = bf16[2048,2240]{1,0:T(8,128)(2,1)} async-done(((bf16[64,2240]{1,0:T(8,128)(2,1)}), bf16[2048,2240]{1,0:T(8,128)(2,1)}) %all-gather.3.cloned.1.call-update) | async-done | bytes 9175056 | tf_op jit(solution)/shard_map/all_gather | solution.py:882
  89.9 11.0 %attend.1 = (f32[256,512]{1,0:T(8,128)}, bf16[256,512]{1,0:T(8,128)(2,1)}, bf16[256,512]{1,0:T(8,128)(2,1)}, bf16[256,512]{1,0:T(8,128)(2,1)}, bf16[256,2048]{1,...) custom-call(s32[1]{0:T(128)} %bitcast.me_ref.refs_0_, ...), custom_call_target="tpu_custom_call" | custom-call | flops 201326592 | bytes 1627136 | tf_op jit(solution)/shard_map/attend/pallas_call | solution.py:81
  102.5 2.7 collective-permute-start.1
  106.7 7.7 %collective-permute-done = bf16[256,512]{1,0:T(8,128)(2,1)S(1)} collective-permute-done((bf16[256,512]{1,0:T(8,128)(2,1)}, bf16[256,512]{1,0:T(8,128)(2,1)S(1)}, u32[]{:S(2)}, u32[]{:S(2)}) %collective-permute-start) | collective-permute-done | bytes 262176 | tf_op jit(solution)/shard_map/ppermute | solution.py:785
  114.4 6.6 %collective-permute-done.1 = bf16[256,512]{1,0:T(8,128)(2,1)S(1)} collective-permute-done((bf16[256,512]{1,0:T(8,128)(2,1)}, bf16[256,512]{1,0:T(8,128)(2,1)S(1)}, u32[]{:S(2)}, u32[]{:S(2)}) %collective-permute-start.1) | collective-permute-done | bytes 262176 | tf_op jit(solution)/shard_map/ppermute | solution.py:785
  122.2 1.9 collective-permute-start.5
  125.7 8.7 %collective-permute-done.5.a1_ref = bf16[256,512]{1,0:T(8,128)(2,1)S(1)} collective-permute-done((bf16[256,512]{1,0:T(8,128)(2,1)S(1)}, bf16[256,512]{1,0:T(8,128)(2,1)S(1)}, u32[]{:S(2)}, u32[]{:S(2)}) %collective-permute-start.5) | collective-permute-done | bytes 262176 | tf_op jit(solution)/shard_map/ppermute | solution.py:785
  134.9 3.2 collective-permute-done.7.a3_ref
  138.8 6.7 %dispatch.1 = (f32[256,2048]{1,0:T(8,128)}, bf16[256,2048]{1,0:T(8,128)(2,1)}, bf16[32,32,2560]{2,1,0:T(8,128)(2,1)}) custom-call(s32[1]{0:T(128)} %bitcast.me_ref.refs_0_, bf16[256,2048]{1,0:T(8,128)(2,1)} %stream_ref.7, bf16[256,512]{1,0:T(8,128)(2,1)} %copy-done.9, bf16[256,512]{1,0:T(8,128)(2,1)} %copy-done.18, bf16[256,512]{1,0:T(8,128)(2,1)} %copy-done.19, ...), custom_call_target="tpu_custom_call" | custom-call | flops 134217728 | bytes 1159987 | tf_op jit(solution)/shard_map/dispatch/pallas_call | solution.py:81
  145.5 4.9 all-to-all-start.1
  150.4 2.3 slice.71
  154.0 3.3 collective-permute-start.9
  157.3 22.0 %collective-permute-done.8 = bf16[16,2,32,512]{3,2,1,0:T(8,128)(2,1)S(1)} collective-permute-done((bf16[16,2,32,512]{3,2,1,0:T(8,128)(2,1)}, bf16[16,2,32,512]{3,2,1,0:T(8,128)(2,1)S(1)}, u32[]{:S(2)}, u32[]{:S(2)}) %collective-permute-start.8) | collective-permute-done | bytes 1048608 | tf_op jit(solution)/shard_map/ppermute | solution.py:785
  181.2 1.9 slice.70.router_ref
  183.0 16.6 %shared.1 = (f32[256,512]{1,0:T(8,128)}, bf16[256,512]{1,0:T(8,128)(2,1)}, bf16[256,512]{1,0:T(8,128)(2,1)}, bf16[256,512]{1,0:T(8,128)(2,1)}, f32[256,2048]{1,0...) custom-call(s32[1]{0:T(128)} %bitcast.me_ref.refs_0_, bf16[256,2048]{1,0:T(8,128)(2,1)} %get-tuple-element.118.mixed_ref, ...), custom_call_target="tpu_custom_call" | custom-call | flops 664377728 | bytes 2346189 | tf_op jit(solution)/shard_map/shared/pallas_call | solution.py:81
  199.6 15.8 %all-to-all-done.1.refs_2_.x0_ref = bf16[32,32,2560]{2,1,0:T(8,128)(2,1)} async-done(((bf16[32,32,2560]{2,1,0:T(8,128)(2,1)}), bf16[32,32,2560]{2,1,0:T(8,128)(2,1)}, u32[]{:S(2)}, u32[]{:S(2)}) %all-to-all-start.1) | async-done | bytes 5242912 | tf_op jit(solution)/shard_map/all_to_all | solution.py:813
  216.8 3.6 collective-permute-start.10
  220.4 16.3 %expert_back.2 = (bf16[32,32,2176]{2,1,0:T(8,128)(2,1)}, bf16[32,32,2048]{2,1,0:T(8,128)(2,1)}, bf16[1024,352]{1,0:T(8,128)(2,1)}, bf16[1024,352]{1,0:T(8,128)(2,1)}, bf16[1024,352]{1,0:T(8,128)(2,1)}) custom-call(s32[1]{0:T(128)} %bitcast.me_ref.refs_0_, s32[1]{0:T(128)} %bitcast.16.refs_1_, bf16[32,32,2560]{2,1,0:T(8,128)(2,1)} %all-to-all-done.1.refs_2_.x0_ref, ...), custom_call_target="tpu_custom_call" | custom-call | flops 73819750400 | bytes 25165824 | tf_op jit(solution)/shard_map/expert_back/pallas_call | solution.py:359
  236.7 5.4 expert_out.2
  244.3 3.1 collective-permute-start.13
  247.4 8.4 %all-to-all-start.2 = ((bf16[32,32,2176]{2,1,0:T(8,128)(2,1)}), bf16[32,32,2176]{2,1,0:T(8,128)(2,1)}, u32[]{:S(2)}, u32[]{:S(2)}) async-start(bf16[32,32,2176]{2,1,0:T(8,128)(2,1)} %get-tuple-element.129), calls=%async_computation.2 | async-start | bytes 8912896 | tf_op jit(solution)/shard_map/all_to_all | solution.py:813
  255.8 5.9 %collective-permute-done.12 = bf16[16,32,512]{2,1,0:T(8,128)(2,1)S(1)} collective-permute-done((bf16[16,32,512]{2,1,0:T(8,128)(2,1)S(1)}, bf16[16,32,512]{2,1,0:T(8,128)(2,1)S(1)}, u32[]{:S(2)}, u32[]{:S(2)}) %collective-permute-start.12) | collective-permute-done | bytes 524320 | tf_op jit(solution)/shard_map/ppermute | solution.py:785
  261.7 4.7 collective-permute-done.13
  267.5 16.6 %expert_back.3 = (bf16[32,32,2176]{2,1,0:T(8,128)(2,1)}, bf16[32,32,2048]{2,1,0:T(8,128)(2,1)}, bf16[1024,352]{1,0:T(8,128)(2,1)}, bf16[1024,352]{1,0:T(8,128)(2...) custom-call(s32[1]{0:T(128)} %bitcast.me_ref.refs_0_, s32[1]{0:T(128)} %bitcast.16.refs_1_, ...), custom_call_target="tpu_custom_call" | custom-call | flops 73819750400 | bytes 25165824 | tf_op jit(solution)/shard_map/expert_back/pallas_call | solution.py:359
  284.1 5.4 expert_out.3
  289.5 22.4 %all-to-all-done.2.b_ref = bf16[32,32,2176]{2,1,0:T(8,128)(2,1)} async-done(((bf16[32,32,2176]{2,1,0:T(8,128)(2,1)}), bf16[32,32,2176]{2,1,0:T(8,128)(2,1)}, u32[]{:S(2)}, u32[]{:S(2)}) %all-to-all-start.2) | async-done | bytes 4456480 | tf_op jit(solution)/shard_map/all_to_all | solution.py:813
  311.9 6.6 %all-to-all-start.3 = ((bf16[32,32,2176]{2,1,0:T(8,128)(2,1)}), bf16[32,32,2176]{2,1,0:T(8,128)(2,1)}, u32[]{:S(2)}, u32[]{:S(2)}) async-start(bf16[32,32,2176]{2,1,0:T(8,128)(2,1)} %get-tuple-element.140), calls=%async_computation.3 | async-start | bytes 8912896 | tf_op jit(solution)/shard_map/all_to_all | solution.py:813
  318.7 19.4 %expert_grads.1 = (f32[2,352,2048]{2,1,0:T(8,128)}, f32[2,352,2048]{2,1,0:T(8,128)}, f32[2,352,2048]{2,1,0:T(8,128)}) custom-call(bf16[32,32,2560]{2,1,0:T(8,128)(2,1)} %all-to-all-done.1.refs_2_.x0_ref, bf16[32,32,2048]{2,1,0:T(8,128)(2,1)} %get-tuple-element.127.c0_ref, bf16[1024,352]{1,0:T(8,128)(2,1)} %get-tuple-element.123.hg_ref.hg0_ref, ...), custom_call_target="tpu_custom_call" | custom-call | flops 738197504 | bytes 4177920 | tf_op jit(solution)/shard_map/expert_grads/pallas_call | solution.py:438
  338.1 6.1 %combine_first.1 = (f32[256,2048]{1,0:T(8,128)}, f32[256,128]{1,0:T(8,128)}) custom-call(bf16[256,1024]{1,0:T(8,128)(2,1)} %get-tuple-element.141.t_ref.t0_ref, bf16[32,32,2176]{2,1,0:T(8,128)(2,1)} %all-to-all-done.2.b_ref, f32[256,2048]{1,0:T(8,128)} %get-tuple-element.120.shared_ref), custom_call_target="tpu_custom_call" | custom-call | flops 107374184 | bytes 930611 | tf_op jit(solution)/shard_map/combine_first/pallas_call | solution.py:81
  344.2 30.2 %all-to-all-done.3.b_ref = bf16[32,32,2176]{2,1,0:T(8,128)(2,1)} async-done(((bf16[32,32,2176]{2,1,0:T(8,128)(2,1)}), bf16[32,32,2176]{2,1,0:T(8,128)(2,1)}, u32[]{:S(2)}, u32[]{:S(2)}) %all-to-all-start.3) | async-done | bytes 4456480 | tf_op jit(solution)/shard_map/all_to_all | solution.py:813
  374.4 5.5 combine.1
  383.2 6.9 %all-to-all-start.4 = ((bf16[32,64,512]{2,1,0:T(8,128)(2,1)}), bf16[32,64,512]{2,1,0:T(8,128)(2,1)S(1)}, u32[]{:S(2)}, u32[]{:S(2)}) async-start(bf16[32,64,512]{2,1,0:T(8,128)(2,1)} %bitcast.49), calls=%async_computation.6 | async-start | bytes 4194304 | tf_op jit(solution)/shard_map/all_to_all | solution.py:813
  391.7 1.8 collective-permute-start.16
  393.4 15.1 %collective-permute-done.14.r1_ref = bf16[256,640]{1,0:T(8,128)(2,1)S(1)} collective-permute-done((bf16[256,640]{1,0:T(8,128)(2,1)}, bf16[256,640]{1,0:T(8,128)(2,1)S(1)}, u32[]{:S(2)}, u32[]{:S(2)}) %collective-permute-start.14) | collective-permute-done | bytes 327712 | tf_op jit(solution)/shard_map/ppermute | solution.py:785
  410.4 2.2 collective-permute-start.17
  413.8 9.8 %collective-permute-done.17.a1_ref = bf16[256,512]{1,0:T(8,128)(2,1)} collective-permute-done((bf16[256,512]{1,0:T(8,128)(2,1)S(1)}, bf16[256,512]{1,0:T(8,128)(2,1)}, u32[]{:S(2)}, u32[]{:S(2)}) %collective-permute-start.17) | collective-permute-done | bytes 262176 | tf_op jit(solution)/shard_map/ppermute | solution.py:785
  423.6 3.8 collective-permute-done.19.a3_ref
  427.4 19.4 %attend_back.1 = (bf16[16,64,2304]{2,1,0:T(8,128)(2,1)}, bf16[16,64,2304]{2,1,0:T(8,128)(2,1)}, f32[256,2048]{1,0:T(8,128)}, f32[256,512]{1,0:T(8,128)}, bf16[25...) custom-call(s32[1]{0:T(128)} %bitcast.me_ref.refs_0_, s32[1]{0:T(128)} %bitcast.3.core_ref, ...), custom_call_target="tpu_custom_call" | custom-call | flops 845571712 | bytes 3586458 | tf_op jit(solution)/shard_map/attend_back/pallas_call | solution.py:81
  447.7 7.4 %collective-permute-done.20.got_ref = bf16[16,64,2304]{2,1,0:T(8,128)(2,1)} collective-permute-done((bf16[16,64,2304]{2,1,0:T(8,128)(2,1)}, bf16[16,64,2304]{2,1,0:T(8,128)(2,1)}, u32[]{:S(2)}, u32[]{:S(2)}) %collective-permute-start.20) | collective-permute-done | bytes 4718624 | tf_op jit(solution)/shard_map/ppermute | solution.py:1104
  455.1 6.4 %pair.1 = (bf16[4,4,64,1152]{3,2,1,0:T(8,128)(2,1)}, bf16[4,64,1152]{2,1,0:T(8,128)(2,1)}, bf16[4,64,1152]{2,1,0:T(8,128)(2,1)}, bf16[4,64,1152]{2,1,0:T(8,128)(2,1)}, bf16[4,64,1152]{2,1,0:T(8,128)(2,1)}) custom-call(s32[2]{0:T(128)} %pad_add_fusion.at_ref, bf16[16,64,2304]{2,1,0:T(8,128)(2,1)} %get-tuple-element.159.keep_ref, ...), custom_call_target="tpu_custom_call" | custom-call | bytes 1415578 | tf_op jit(solution)/shard_map/pair/pallas_call | solution.py:81
  461.5 4.5 all-to-all-start.5
  470.4 2.2 collective-permute-start.31
  472.5 9.5 %collective-permute-done.24.r1_ref = bf16[256,512]{1,0:T(8,128)(2,1)S(1)} collective-permute-done((bf16[256,512]{1,0:T(8,128)(2,1)S(1)}, bf16[256,512]{1,0:T(8,128)(2,1)S(1)}, u32[]{:S(2)}, u32[]{:S(2)}) %collective-permute-start.24) | collective-permute-done | bytes 262176 | tf_op jit(solution)/shard_map/ppermute | solution.py:785
  483.5 2.7 collective-permute-start.22
  487.7 3.7 routed.1.a0_ref
  492.3 9.4 %collective-permute-done.32 = bf16[256,512]{1,0:T(8,128)(2,1)S(1)} collective-permute-done((bf16[256,512]{1,0:T(8,128)(2,1)}, bf16[256,512]{1,0:T(8,128)(2,1)S(1)}, u32[]{:S(2)}, u32[]{:S(2)}) %collective-permute-start.32) | collective-permute-done | bytes 262176 | tf_op jit(solution)/shard_map/ppermute | solution.py:785
  501.8 5.6 collective-permute-done.27.a1_ref
  509.3 2.6 collective-permute-start.33
  512.9 2.6 cross.2
  515.5 1.8 collective-permute-start.36
  518.6 2.6 cross.3
  521.2 2.5 collective-permute-done.29.a3_ref
  523.8 3.1 collective-permute-start.37
  526.9 3.3 result.1
  532.7 5.0 stream.1
  537.8 2.1 collective-permute-start.41
  539.8 1.8 fusion.1
  541.7 2.1 collective-permute-done.41.refs_7_
  544.5 2.3 unpack.1
  548.2 2.1 collective-permute-start.43
  (191 shorter events, 60.9 us)
Async XLA Ops:
  7.2 82.7 %all-gather.3.cloned.1.call-start = ((), (), s32[]{:S(2)}) async-start(), calls=%async_computation.9 | async-start | bytes 9732096 | tf_op jit(solution)/shard_map/all_gather | solution.py:882
  13.3 169.8 %all-gather.5.cloned.1.call-start = ((), (), s32[]{:S(2)}) async-start(), calls=%async_computation.10 | async-start | bytes 9191424 | tf_op jit(solution)/shard_map/all_gather | solution.py:883
  20.0 45.0 %copy-start.31 = (s32[1,256]{1,0:T(1,128)S(1)}, s32[1,256]{1,0:T(1,128)}, u32[]{:S(2)}) copy-start(s32[1,256]{1,0:T(1,128)} %seg_row_ref.1) | copy-start | bytes 3076
  59.8 41.2 %copy-start.2 = (bf16[32,64,512]{2,1,0:T(8,128)(2,1)}, bf16[32,64,512]{2,1,0:T(8,128)(2,1)S(1)}, u32[]{:S(2)}) copy-start(bf16[32,64,512]{2,1,0:T(8,128)(2,1)S(1)} %all_to_all.30) | copy-start | bytes 6291460
  59.8 62.4 %collective-permute-start.3 = (bf16[32,2,32,512]{3,2,1,0:T(8,128)(2,1)S(1)}, bf16[32,2,32,512]{3,2,1,0:T(8,128)(2,1)}, u32[]{:S(2)}, u32[]{:S(2)}) collective-permute-start(bf16[32,2,32,512]{3,2,1,0:T(8,128)(2,1)S(1)} %bitcast.51), channel_id=1, source_target_pairs={{0,1},{1,2},{2,3},{3,0},{4,5},{5,6},{6,7},{7,4},{8,9},{9,10},{10,1... | collective-permute-start | bytes 6291464 | tf_op jit(solution)/shard_map/ppermute | solution.py:785
  61.6 60.6 %collective-permute-start.4 = (bf16[32,2,32,512]{3,2,1,0:T(8,128)(2,1)S(1)}, bf16[32,2,32,512]{3,2,1,0:T(8,128)(2,1)}, u32[]{:S(2)}, u32[]{:S(2)}) collective-permute-start(bf16[32,2,32,512]{3,2,1,0:T(8,128)(2,1)S(1)} %bitcast.52), channel_id=1, source_target_pairs={{0,3},{1,0},{2,1},{3,2},{4,7},{5,4},{6,5},{7,6},{8,11},{9,8},{10,9... | collective-permute-start | bytes 6291464 | tf_op jit(solution)/shard_map/ppermute | solution.py:785
  100.9 13.5 %collective-permute-start = (bf16[256,512]{1,0:T(8,128)(2,1)}, bf16[256,512]{1,0:T(8,128)(2,1)S(1)}, u32[]{:S(2)}, u32[]{:S(2)}) collective-permute-start(bf16[256,512]{1,0:T(8,128)(2,1)} %get-tuple-element.110), channel_id=1, source_target_pairs={{0,1},{1,2},{2,3},{3,0},{4,5},{5,6},{6,7},{7,4},{8,9},{9,10},{10,1... | collective-permute-start | bytes 786440 | tf_op jit(solution)/shard_map/ppermute | solution.py:785
  102.5 18.5 %collective-permute-start.1 = (bf16[256,512]{1,0:T(8,128)(2,1)}, bf16[256,512]{1,0:T(8,128)(2,1)S(1)}, u32[]{:S(2)}, u32[]{:S(2)}) collective-permute-start(bf16[256,512]{1,0:T(8,128)(2,1)} %get-tuple-element.111), channel_id=1, source_target_pairs={{0,2},{1,3},{2,0},{3,1},{4,6},{5,7},{6,4},{7,5},{8,10},{9,11},{10,... | collective-permute-start | bytes 786440 | tf_op jit(solution)/shard_map/ppermute | solution.py:785
  105.2 15.8 %collective-permute-start.2 = (bf16[256,512]{1,0:T(8,128)(2,1)}, bf16[256,512]{1,0:T(8,128)(2,1)S(1)}, u32[]{:S(2)}, u32[]{:S(2)}) collective-permute-start(bf16[256,512]{1,0:T(8,128)(2,1)} %get-tuple-element.112), channel_id=1, source_target_pairs={{0,3},{1,0},{2,1},{3,2},{4,7},{5,4},{6,5},{7,6},{8,11},{9,8},{10,9... | collective-permute-start | bytes 786440 | tf_op jit(solution)/shard_map/ppermute | solution.py:785
  122.2 15.9 %copy-start.9 = (bf16[256,512]{1,0:T(8,128)(2,1)}, bf16[256,512]{1,0:T(8,128)(2,1)S(1)}, u32[]{:S(2)}) copy-start(bf16[256,512]{1,0:T(8,128)(2,1)S(1)} %add_convert_fusion.2.a0_ref) | copy-start | bytes 786436
  122.2 12.2 %collective-permute-start.5 = (bf16[256,512]{1,0:T(8,128)(2,1)S(1)}, bf16[256,512]{1,0:T(8,128)(2,1)S(1)}, u32[]{:S(2)}, u32[]{:S(2)}) collective-permute-start(bf16[256,512]{1,0:T(8,128)(2,1)S(1)} %add_convert_fusion.2.a0_ref), channel_id=1, source_target_pairs={{0,3},{1,0},{2,1},{3,2},{4,7},{5,4},{6,5},{7,6},{8,11},{9,8},{10,9... | collective-permute-start | bytes 786440 | tf_op jit(solution)/shard_map/ppermute | solution.py:785
  124.1 10.8 %collective-permute-start.6 = (bf16[256,512]{1,0:T(8,128)(2,1)S(1)}, bf16[256,512]{1,0:T(8,128)(2,1)S(1)}, u32[]{:S(2)}, u32[]{:S(2)}) collective-permute-start(bf16[256,512]{1,0:T(8,128)(2,1)S(1)} %add_convert_fusion.2.a0_ref), channel_id=1, source_target_pairs={{0,2},{1,3},{2,0},{3,1},{4,6},{5,7},{6,4},{7,5},{8,10},{9,11},{10,... | collective-permute-start | bytes 786440 | tf_op jit(solution)/shard_map/ppermute | solution.py:785
  124.9 13.2 %collective-permute-start.7 = (bf16[256,512]{1,0:T(8,128)(2,1)S(1)}, bf16[256,512]{1,0:T(8,128)(2,1)S(1)}, u32[]{:S(2)}, u32[]{:S(2)}) collective-permute-start(bf16[256,512]{1,0:T(8,128)(2,1)S(1)} %add_convert_fusion.2.a0_ref), channel_id=1, source_target_pairs={{0,1},{1,2},{2,3},{3,0},{4,5},{5,6},{6,7},{7,4},{8,9},{9,10},{10,1... | collective-permute-start | bytes 786440 | tf_op jit(solution)/shard_map/ppermute | solution.py:785
  145.5 70.0 %all-to-all-start.1 = ((bf16[32,32,2560]{2,1,0:T(8,128)(2,1)}), bf16[32,32,2560]{2,1,0:T(8,128)(2,1)}, u32[]{:S(2)}, u32[]{:S(2)}) async-start(bf16[32,32,2560]{2,1,0:T(8,128)(2,1)} %get-tuple-element.122), calls=%async_computation.1 | async-start | bytes 10485760 | tf_op jit(solution)/shard_map/all_to_all | solution.py:813
  150.4 229.5 %reduce-scatter.4.cloned.1.call-start = ((), (), s32[]{:S(2)}) async-start(), calls=%async_computation.11 | async-start | bytes 5242880 | tf_op jit(solution)/shard_map/reduce_scatter | solution.py:1013
  152.7 26.6 %collective-permute-start.8 = (bf16[16,2,32,512]{3,2,1,0:T(8,128)(2,1)}, bf16[16,2,32,512]{3,2,1,0:T(8,128)(2,1)S(1)}, u32[]{:S(2)}, u32[]{:S(2)}) collective-permute-start(bf16[16,2,32,512]{3,2,1,0:T(8,128)(2,1)} %slice.71), channel_id=1, source_target_pairs={{0,1},{1,2},{2,3},{3,0},{4,5},{5,6},{6,7},{7,4},{8,9},{9,10},{10,1... | collective-permute-start | bytes 3145736 | tf_op jit(solution)/shard_map/ppermute | solution.py:785
  154.0 25.7 %collective-permute-start.9 = (bf16[16,2,32,512]{3,2,1,0:T(8,128)(2,1)S(1)}, bf16[16,2,32,512]{3,2,1,0:T(8,128)(2,1)S(1)}, u32[]{:S(2)}, u32[]{:S(2)}) collective-permute-start(bf16[16,2,32,512]{3,2,1,0:T(8,128)(2,1)S(1)} %slice.72), channel_id=1, source_target_pairs={{0,3},{1,0},{2,1},{3,2},{4,7},{5,4},{6,5},{7,6},{8,11},{9,8},{10,9... | collective-permute-start | bytes 3145736 | tf_op jit(solution)/shard_map/ppermute | solution.py:785
  216.7 26.1 %collective-permute-start.11 = (bf16[32,32,512]{2,1,0:T(8,128)(2,1)S(1)}, bf16[32,32,512]{2,1,0:T(8,128)(2,1)S(1)}, u32[]{:S(2)}, u32[]{:S(2)}) collective-permute-start(bf16[32,32,512]{2,1,0:T(8,128)(2,1)S(1)} %slice.73), channel_id=1, source_target_pairs={{0,1},{1,2},{2,3},{3,0},{4,5},{5,6},{6,7},{7,4},{8,9},{9,10},{10,1... | collective-permute-start | bytes 3145736 | tf_op jit(solution)/shard_map/ppermute | solution.py:785
  216.8 26.1 %collective-permute-start.10 = (bf16[32,32,512]{2,1,0:T(8,128)(2,1)S(1)}, bf16[32,32,512]{2,1,0:T(8,128)(2,1)}, u32[]{:S(2)}, u32[]{:S(2)}) collective-permute-start(bf16[32,32,512]{2,1,0:T(8,128)(2,1)S(1)} %slice.73), channel_id=1, source_target_pairs={{0,3},{1,0},{2,1},{3,2},{4,7},{5,4},{6,5},{7,6},{8,11},{9,8},{10,9... | collective-permute-start | bytes 3145736 | tf_op jit(solution)/shard_map/ppermute | solution.py:785
  242.8 18.9 %collective-permute-start.12 = (bf16[16,32,512]{2,1,0:T(8,128)(2,1)S(1)}, bf16[16,32,512]{2,1,0:T(8,128)(2,1)S(1)}, u32[]{:S(2)}, u32[]{:S(2)}) collective-permute-start(bf16[16,32,512]{2,1,0:T(8,128)(2,1)S(1)} %slice.74), channel_id=1, source_target_pairs={{0,1},{1,2},{2,3},{3,0},{4,5},{5,6},{6,7},{7,4},{8,9},{9,10},{10,1... | collective-permute-start | bytes 1572872 | tf_op jit(solution)/shard_map/ppermute | solution.py:785
  244.3 22.1 %collective-permute-start.13 = (bf16[16,32,512]{2,1,0:T(8,128)(2,1)S(1)}, bf16[16,32,512]{2,1,0:T(8,128)(2,1)S(1)}, u32[]{:S(2)}, u32[]{:S(2)}) collective-permute-start(bf16[16,32,512]{2,1,0:T(8,128)(2,1)S(1)} %slice.75), channel_id=1, source_target_pairs={{0,3},{1,0},{2,1},{3,2},{4,7},{5,4},{6,5},{7,6},{8,11},{9,8},{10,9... | collective-permute-start | bytes 1572872 | tf_op jit(solution)/shard_map/ppermute | solution.py:785
  247.4 64.5 %all-to-all-start.2 = ((bf16[32,32,2176]{2,1,0:T(8,128)(2,1)}), bf16[32,32,2176]{2,1,0:T(8,128)(2,1)}, u32[]{:S(2)}, u32[]{:S(2)}) async-start(bf16[32,32,2176]{2,1,0:T(8,128)(2,1)} %get-tuple-element.129), calls=%async_computation.2 | async-start | bytes 8912896 | tf_op jit(solution)/shard_map/all_to_all | solution.py:813
  255.8 124.2 %reduce-scatter.6.cloned.1.call-start = ((), (), s32[]{:S(2)}) async-start(), calls=%async_computation.12 | async-start | bytes 5242880 | tf_op jit(solution)/shard_map/reduce_scatter | solution.py:1013
  311.9 62.5 %all-to-all-start.3 = ((bf16[32,32,2176]{2,1,0:T(8,128)(2,1)}), bf16[32,32,2176]{2,1,0:T(8,128)(2,1)}, u32[]{:S(2)}, u32[]{:S(2)}) async-start(bf16[32,32,2176]{2,1,0:T(8,128)(2,1)} %get-tuple-element.140), calls=%async_computation.3 | async-start | bytes 8912896 | tf_op jit(solution)/shard_map/all_to_all | solution.py:813
  318.5 221.3 %reduce-scatter.8.cloned.1.call-start = ((), (), s32[]{:S(2)}) async-start(), calls=%async_computation.13 | async-start | bytes 9191424 | tf_op jit(solution)/shard_map/reduce_scatter | solution.py:1040
  383.2 63.5 %all-to-all-start.4 = ((bf16[32,64,512]{2,1,0:T(8,128)(2,1)}), bf16[32,64,512]{2,1,0:T(8,128)(2,1)S(1)}, u32[]{:S(2)}, u32[]{:S(2)}) async-start(bf16[32,64,512]{2,1,0:T(8,128)(2,1)} %bitcast.49), calls=%async_computation.6 | async-start | bytes 4194304 | tf_op jit(solution)/shard_map/all_to_all | solution.py:813
  390.1 18.4 %collective-permute-start.14 = (bf16[256,640]{1,0:T(8,128)(2,1)}, bf16[256,640]{1,0:T(8,128)(2,1)S(1)}, u32[]{:S(2)}, u32[]{:S(2)}) collective-permute-start(bf16[256,640]{1,0:T(8,128)(2,1)} %get-tuple-element.145), channel_id=1, source_target_pairs={{0,1},{1,2},{2,3},{3,0},{4,5},{5,6},{6,7},{7,4},{8,9},{9,10},{10,1... | collective-permute-start | bytes 983048 | tf_op jit(solution)/shard_map/ppermute | solution.py:785
  390.2 18.3 %collective-permute-start.15 = (bf16[256,640]{1,0:T(8,128)(2,1)}, bf16[256,640]{1,0:T(8,128)(2,1)S(1)}, u32[]{:S(2)}, u32[]{:S(2)}) collective-permute-start(bf16[256,640]{1,0:T(8,128)(2,1)} %get-tuple-element.146), channel_id=1, source_target_pairs={{0,2},{1,3},{2,0},{3,1},{4,6},{5,7},{6,4},{7,5},{8,10},{9,11},{10,... | collective-permute-start | bytes 983048 | tf_op jit(solution)/shard_map/ppermute | solution.py:785
  391.7 17.5 %collective-permute-start.16 = (bf16[256,640]{1,0:T(8,128)(2,1)S(1)}, bf16[256,640]{1,0:T(8,128)(2,1)S(1)}, u32[]{:S(2)}, u32[]{:S(2)}) collective-permute-start(bf16[256,640]{1,0:T(8,128)(2,1)S(1)} %copy-done.32), channel_id=1, source_target_pairs={{0,3},{1,0},{2,1},{3,2},{4,7},{5,4},{6,5},{7,6},{8,11},{9,8},{10,9... | collective-permute-start | bytes 983048 | tf_op jit(solution)/shard_map/ppermute | solution.py:785
  408.5 18.8 %copy-start.4 = (bf16[256,640]{1,0:T(8,128)(2,1)}, bf16[256,640]{1,0:T(8,128)(2,1)S(1)}, u32[]{:S(2)}) copy-start(bf16[256,640]{1,0:T(8,128)(2,1)S(1)} %collective-permute-done.14.r1_ref) | copy-start | bytes 983044
  408.5 18.8 %copy-start.5 = (bf16[256,640]{1,0:T(8,128)(2,1)}, bf16[256,640]{1,0:T(8,128)(2,1)S(1)}, u32[]{:S(2)}) copy-start(bf16[256,640]{1,0:T(8,128)(2,1)S(1)} %collective-permute-done.15.r2_ref) | copy-start | bytes 983044
  409.1 18.2 %copy-start.6 = (bf16[256,640]{1,0:T(8,128)(2,1)}, bf16[256,640]{1,0:T(8,128)(2,1)S(1)}, u32[]{:S(2)}) copy-start(bf16[256,640]{1,0:T(8,128)(2,1)S(1)} %collective-permute-done.16.r3_ref) | copy-start | bytes 983044
  410.4 16.9 %copy-start.7 = (bf16[256,512]{1,0:T(8,128)(2,1)}, bf16[256,512]{1,0:T(8,128)(2,1)S(1)}, u32[]{:S(2)}) copy-start(bf16[256,512]{1,0:T(8,128)(2,1)S(1)} %add_convert_fusion.1.a0_ref) | copy-start | bytes 786436
  410.4 13.1 %collective-permute-start.17 = (bf16[256,512]{1,0:T(8,128)(2,1)S(1)}, bf16[256,512]{1,0:T(8,128)(2,1)}, u32[]{:S(2)}, u32[]{:S(2)}) collective-permute-start(bf16[256,512]{1,0:T(8,128)(2,1)S(1)} %add_convert_fusion.1.a0_ref), channel_id=1, source_target_pairs={{0,3},{1,0},{2,1},{3,2},{4,7},{5,4},{6,5},{7,6},{8,11},{9,8},{10,9... | collective-permute-start | bytes 786440 | tf_op jit(solution)/shard_map/ppermute | solution.py:785
  412.6 10.9 %collective-permute-start.18 = (bf16[256,512]{1,0:T(8,128)(2,1)S(1)}, bf16[256,512]{1,0:T(8,128)(2,1)}, u32[]{:S(2)}, u32[]{:S(2)}) collective-permute-start(bf16[256,512]{1,0:T(8,128)(2,1)S(1)} %add_convert_fusion.1.a0_ref), channel_id=1, source_target_pairs={{0,2},{1,3},{2,0},{3,1},{4,6},{5,7},{6,4},{7,5},{8,10},{9,11},{10,... | collective-permute-start | bytes 786440 | tf_op jit(solution)/shard_map/ppermute | solution.py:785
  412.8 14.5 %collective-permute-start.19 = (bf16[256,512]{1,0:T(8,128)(2,1)S(1)}, bf16[256,512]{1,0:T(8,128)(2,1)}, u32[]{:S(2)}, u32[]{:S(2)}) collective-permute-start(bf16[256,512]{1,0:T(8,128)(2,1)S(1)} %add_convert_fusion.1.a0_ref), channel_id=1, source_target_pairs={{0,1},{1,2},{2,3},{3,0},{4,5},{5,6},{6,7},{7,4},{8,9},{9,10},{10,1... | collective-permute-start | bytes 786440 | tf_op jit(solution)/shard_map/ppermute | solution.py:785
  446.8 14.8 %copy-start.1 = (bf16[32,64,512]{2,1,0:T(8,128)(2,1)}, bf16[32,64,512]{2,1,0:T(8,128)(2,1)S(1)}, u32[]{:S(2)}) copy-start(bf16[32,64,512]{2,1,0:T(8,128)(2,1)S(1)} %all-to-all-done.4) | copy-start | bytes 6291460
  446.8 8.3 %collective-permute-start.20 = (bf16[16,64,2304]{2,1,0:T(8,128)(2,1)}, bf16[16,64,2304]{2,1,0:T(8,128)(2,1)}, u32[]{:S(2)}, u32[]{:S(2)}) collective-permute-start(bf16[16,64,2304]{2,1,0:T(8,128)(2,1)} %get-tuple-element.162), channel_id=1, source_target_pairs={{0,4},{4,0},{8,12},{12,8},{16,20},{20,16},{24,28},{28,24},{32,36},... | collective-permute-start | bytes 14155784 | tf_op jit(solution)/shard_map/ppermute | solution.py:1104
  461.5 55.7 %all-to-all-start.5 = ((bf16[4,256,1152]{2,1,0:T(8,128)(2,1)}), bf16[4,256,1152]{2,1,0:T(8,128)(2,1)S(1)}, u32[]{:S(2)}, u32[]{:S(2)}) async-start(bf16[4,256,1152]{2,1,0:T(8,128)(2,1)} %bitcast.50), calls=%async_computation.7 | async-start | bytes 4718592 | tf_op jit(solution)/shard_map/all_to_all | solution.py:1131
  466.1 16.0 %collective-permute-start.24 = (bf16[256,512]{1,0:T(8,128)(2,1)S(1)}, bf16[256,512]{1,0:T(8,128)(2,1)S(1)}, u32[]{:S(2)}, u32[]{:S(2)}) collective-permute-start(bf16[256,512]{1,0:T(8,128)(2,1)S(1)} %copy-done.33), channel_id=1, source_target_pairs={{0,1},{1,2},{2,3},{3,0},{4,5},{5,6},{6,7},{7,4},{8,9},{9,10},{10,1... | collective-permute-start | bytes 786440 | tf_op jit(solution)/shard_map/ppermute | solution.py:785
  466.1 17.5 %collective-permute-start.25 = (bf16[256,512]{1,0:T(8,128)(2,1)}, bf16[256,512]{1,0:T(8,128)(2,1)S(1)}, u32[]{:S(2)}, u32[]{:S(2)}) collective-permute-start(bf16[256,512]{1,0:T(8,128)(2,1)} %get-tuple-element.173), channel_id=1, source_target_pairs={{0,2},{1,3},{2,0},{3,1},{4,6},{5,7},{6,4},{7,5},{8,10},{9,11},{10,... | collective-permute-start | bytes 786440 | tf_op jit(solution)/shard_map/ppermute | solution.py:785
  467.7 18.6 %collective-permute-start.26 = (bf16[256,512]{1,0:T(8,128)(2,1)}, bf16[256,512]{1,0:T(8,128)(2,1)S(1)}, u32[]{:S(2)}, u32[]{:S(2)}) collective-permute-start(bf16[256,512]{1,0:T(8,128)(2,1)} %get-tuple-element.174), channel_id=1, source_target_pairs={{0,3},{1,0},{2,1},{3,2},{4,7},{5,4},{6,5},{7,6},{8,11},{9,8},{10,9... | collective-permute-start | bytes 786440 | tf_op jit(solution)/shard_map/ppermute | solution.py:785
  469.3 23.0 %collective-permute-start.30 = (bf16[256,512]{1,0:T(8,128)(2,1)}, bf16[256,512]{1,0:T(8,128)(2,1)}, u32[]{:S(2)}, u32[]{:S(2)}) collective-permute-start(bf16[256,512]{1,0:T(8,128)(2,1)} %get-tuple-element.177), channel_id=1, source_target_pairs={{0,1},{1,2},{2,3},{3,0},{4,5},{5,6},{6,7},{7,4},{8,9},{9,10},{10,1... | collective-permute-start | bytes 786440 | tf_op jit(solution)/shard_map/ppermute | solution.py:785
  470.4 21.9 %collective-permute-start.31 = (bf16[256,512]{1,0:T(8,128)(2,1)}, bf16[256,512]{1,0:T(8,128)(2,1)}, u32[]{:S(2)}, u32[]{:S(2)}) collective-permute-start(bf16[256,512]{1,0:T(8,128)(2,1)} %get-tuple-element.178), channel_id=1, source_target_pairs={{0,2},{1,3},{2,0},{3,1},{4,6},{5,7},{6,4},{7,5},{8,10},{9,11},{10,... | collective-permute-start | bytes 786440 | tf_op jit(solution)/shard_map/ppermute | solution.py:785
  482.1 27.2 %collective-permute-start.21 = (bf16[4,64,1152]{2,1,0:T(8,128)(2,1)}, bf16[4,64,1152]{2,1,0:T(8,128)(2,1)S(1)}, u32[]{:S(2)}, u32[]{:S(2)}) collective-permute-start(bf16[4,64,1152]{2,1,0:T(8,128)(2,1)} %get-tuple-element.164), channel_id=1, source_target_pairs={{0,32},{4,36},{8,40},{12,44},{16,48},{20,52},{24,56},{28,60},{32,6... | collective-permute-start | bytes 1769480 | tf_op jit(solution)/shard_map/ppermute | solution.py:1120
  483.5 28.4 %collective-permute-start.22 = (bf16[4,64,1152]{2,1,0:T(8,128)(2,1)}, bf16[4,64,1152]{2,1,0:T(8,128)(2,1)}, u32[]{:S(2)}, u32[]{:S(2)}) collective-permute-start(bf16[4,64,1152]{2,1,0:T(8,128)(2,1)} %get-tuple-element.165), channel_id=1, source_target_pairs={{0,64},{4,68},{8,72},{12,76},{16,80},{20,84},{24,88},{28,92},{32,9... | collective-permute-start | bytes 1769480 | tf_op jit(solution)/shard_map/ppermute | solution.py:1120
  486.2 25.7 %collective-permute-start.23 = (bf16[4,64,1152]{2,1,0:T(8,128)(2,1)}, bf16[4,64,1152]{2,1,0:T(8,128)(2,1)}, u32[]{:S(2)}, u32[]{:S(2)}) collective-permute-start(bf16[4,64,1152]{2,1,0:T(8,128)(2,1)} %get-tuple-element.166), channel_id=1, source_target_pairs={{0,96},{4,100},{8,104},{12,108},{16,112},{20,116},{24,120},{28,124... | collective-permute-start | bytes 1769480 | tf_op jit(solution)/shard_map/ppermute | solution.py:1120
  487.7 20.4 %copy-start.11 = (f32[256,512]{1,0:T(8,128)S(1)}, f32[256,512]{1,0:T(8,128)}, u32[]{:S(2)}) copy-start(f32[256,512]{1,0:T(8,128)} %get-tuple-element.176) | copy-start | bytes 1572868
  492.3 9.5 %collective-permute-start.32 = (bf16[256,512]{1,0:T(8,128)(2,1)}, bf16[256,512]{1,0:T(8,128)(2,1)S(1)}, u32[]{:S(2)}, u32[]{:S(2)}) collective-permute-start(bf16[256,512]{1,0:T(8,128)(2,1)} %get-tuple-element.179), channel_id=1, source_target_pairs={{0,3},{1,0},{2,1},{3,2},{4,7},{5,4},{6,5},{7,6},{8,11},{9,8},{10,9... | collective-permute-start | bytes 786440 | tf_op jit(solution)/shard_map/ppermute | solution.py:785
  492.3 15.1 %collective-permute-start.27 = (bf16[256,512]{1,0:T(8,128)(2,1)}, bf16[256,512]{1,0:T(8,128)(2,1)S(1)}, u32[]{:S(2)}, u32[]{:S(2)}) collective-permute-start(bf16[256,512]{1,0:T(8,128)(2,1)} %routed.1.a0_ref), channel_id=1, source_target_pairs={{0,3},{1,0},{2,1},{3,2},{4,7},{5,4},{6,5},{7,6},{8,11},{9,8},{10,9... | collective-permute-start | bytes 786440 | tf_op jit(solution)/shard_map/ppermute | solution.py:785
  501.8 13.7 %collective-permute-start.28 = (bf16[256,512]{1,0:T(8,128)(2,1)}, bf16[256,512]{1,0:T(8,128)(2,1)}, u32[]{:S(2)}, u32[]{:S(2)}) collective-permute-start(bf16[256,512]{1,0:T(8,128)(2,1)} %routed.1.a0_ref), channel_id=1, source_target_pairs={{0,2},{1,3},{2,0},{3,1},{4,6},{5,7},{6,4},{7,5},{8,10},{9,11},{10,... | collective-permute-start | bytes 786440 | tf_op jit(solution)/shard_map/ppermute | solution.py:785
  507.4 16.4 %collective-permute-start.29 = (bf16[256,512]{1,0:T(8,128)(2,1)}, bf16[256,512]{1,0:T(8,128)(2,1)}, u32[]{:S(2)}, u32[]{:S(2)}) collective-permute-start(bf16[256,512]{1,0:T(8,128)(2,1)} %routed.1.a0_ref), channel_id=1, source_target_pairs={{0,1},{1,2},{2,3},{3,0},{4,5},{5,6},{6,7},{7,4},{8,9},{9,10},{10,1... | collective-permute-start | bytes 786440 | tf_op jit(solution)/shard_map/ppermute | solution.py:785
  509.3 20.9 %collective-permute-start.33 = (bf16[256,512]{1,0:T(8,128)(2,1)S(1)}, bf16[256,512]{1,0:T(8,128)(2,1)S(1)}, u32[]{:S(2)}, u32[]{:S(2)}) collective-permute-start(bf16[256,512]{1,0:T(8,128)(2,1)S(1)} %add_convert_fusion.a0_ref), channel_id=1, source_target_pairs={{0,3},{1,0},{2,1},{3,2},{4,7},{5,4},{6,5},{7,6},{8,11},{9,8},{10,9... | collective-permute-start | bytes 786440 | tf_op jit(solution)/shard_map/ppermute | solution.py:785
  511.9 19.6 %collective-permute-start.34 = (bf16[256,512]{1,0:T(8,128)(2,1)S(1)}, bf16[256,512]{1,0:T(8,128)(2,1)}, u32[]{:S(2)}, u32[]{:S(2)}) collective-permute-start(bf16[256,512]{1,0:T(8,128)(2,1)S(1)} %add_convert_fusion.a0_ref), channel_id=1, source_target_pairs={{0,2},{1,3},{2,0},{3,1},{4,6},{5,7},{6,4},{7,5},{8,10},{9,11},{10,... | collective-permute-start | bytes 786440 | tf_op jit(solution)/shard_map/ppermute | solution.py:785
  511.9 19.6 %collective-permute-start.35 = (bf16[256,512]{1,0:T(8,128)(2,1)S(1)}, bf16[256,512]{1,0:T(8,128)(2,1)}, u32[]{:S(2)}, u32[]{:S(2)}) collective-permute-start(bf16[256,512]{1,0:T(8,128)(2,1)S(1)} %add_convert_fusion.a0_ref), channel_id=1, source_target_pairs={{0,1},{1,2},{2,3},{3,0},{4,5},{5,6},{6,7},{7,4},{8,9},{9,10},{10,1... | collective-permute-start | bytes 786440 | tf_op jit(solution)/shard_map/ppermute | solution.py:785
  515.5 22.3 %collective-permute-start.36 = (bf16[64,1152]{1,0:T(8,128)(2,1)}, bf16[64,1152]{1,0:T(8,128)(2,1)S(1)}, u32[]{:S(2)}, u32[]{:S(2)}) collective-permute-start(bf16[64,1152]{1,0:T(8,128)(2,1)} %get-tuple-element.183), channel_id=1, source_target_pairs={{0,8},{4,12},{8,16},{12,20},{16,24},{20,28},{24,0},{28,4},{32,40},... | collective-permute-start | bytes 442376 | tf_op jit(solution)/shard_map/ppermute | solution.py:1120
  523.8 17.9 %collective-permute-start.37 = (bf16[64,1152]{1,0:T(8,128)(2,1)}, bf16[64,1152]{1,0:T(8,128)(2,1)S(1)}, u32[]{:S(2)}, u32[]{:S(2)}) collective-permute-start(bf16[64,1152]{1,0:T(8,128)(2,1)} %get-tuple-element.184), channel_id=1, source_target_pairs={{0,16},{4,20},{8,24},{12,28},{16,0},{20,4},{24,8},{28,12},{32,48},... | collective-permute-start | bytes 442376 | tf_op jit(solution)/shard_map/ppermute | solution.py:1120
  530.2 11.4 %collective-permute-start.38 = (bf16[64,1152]{1,0:T(8,128)(2,1)S(1)}, bf16[64,1152]{1,0:T(8,128)(2,1)S(1)}, u32[]{:S(2)}, u32[]{:S(2)}) collective-permute-start(bf16[64,1152]{1,0:T(8,128)(2,1)S(1)} %copy-done.34), channel_id=1, source_target_pairs={{0,24},{4,28},{8,0},{12,4},{16,8},{20,12},{24,16},{28,20},{32,56},... | collective-permute-start | bytes 442376 | tf_op jit(solution)/shard_map/ppermute | solution.py:1120
  531.5 10.2 %collective-permute-start.39 = (bf16[64,1152]{1,0:T(8,128)(2,1)S(1)}, bf16[64,1152]{1,0:T(8,128)(2,1)S(1)}, u32[]{:S(2)}, u32[]{:S(2)}) collective-permute-start(bf16[64,1152]{1,0:T(8,128)(2,1)S(1)} %copy-done.37), channel_id=1, source_target_pairs={{0,32},{4,36},{8,40},{12,44},{16,48},{20,52},{24,56},{28,60},{32,6... | collective-permute-start | bytes 442376 | tf_op jit(solution)/shard_map/ppermute | solution.py:1120
  531.5 10.2 %collective-permute-start.40 = (bf16[64,1152]{1,0:T(8,128)(2,1)S(1)}, bf16[64,1152]{1,0:T(8,128)(2,1)S(1)}, u32[]{:S(2)}, u32[]{:S(2)}) collective-permute-start(bf16[64,1152]{1,0:T(8,128)(2,1)S(1)} %copy-done.36), channel_id=1, source_target_pairs={{0,64},{4,68},{8,72},{12,76},{16,80},{20,84},{24,88},{28,92},{32,9... | collective-permute-start | bytes 442376 | tf_op jit(solution)/shard_map/ppermute | solution.py:1120
  537.8 6.0 %collective-permute-start.41 = (bf16[64,1152]{1,0:T(8,128)(2,1)S(1)}, bf16[64,1152]{1,0:T(8,128)(2,1)S(1)}, u32[]{:S(2)}, u32[]{:S(2)}) collective-permute-start(bf16[64,1152]{1,0:T(8,128)(2,1)S(1)} %copy-done.35), channel_id=1, source_target_pairs={{0,96},{4,100},{8,104},{12,108},{16,112},{20,116},{24,120},{28,124... | collective-permute-start | bytes 442376 | tf_op jit(solution)/shard_map/ppermute | solution.py:1120
  547.7 5.7 %collective-permute-start.42 = (bf16[64,640]{1,0:T(8,128)(2,1)S(1)}, bf16[64,640]{1,0:T(8,128)(2,1)S(1)}, u32[]{:S(2)}, u32[]{:S(2)}) collective-permute-start(bf16[64,640]{1,0:T(8,128)(2,1)S(1)} %convert_element_type.87), channel_id=1, source_target_pairs={{0,1},{1,2},{2,3},{3,0},{4,5},{5,6},{6,7},{7,4},{8,9},{9,10},{10,1... | collective-permute-start | bytes 245768 | tf_op jit(solution)/shard_map/ppermute | solution.py:785
  548.2 6.0 %collective-permute-start.43 = (bf16[64,640]{1,0:T(8,128)(2,1)S(1)}, bf16[64,640]{1,0:T(8,128)(2,1)S(1)}, u32[]{:S(2)}, u32[]{:S(2)}) collective-permute-start(bf16[64,640]{1,0:T(8,128)(2,1)S(1)} %convert_element_type.87), channel_id=1, source_target_pairs={{0,2},{1,3},{2,0},{3,1},{4,6},{5,7},{6,4},{7,5},{8,10},{9,11},{10,... | collective-permute-start | bytes 245768 | tf_op jit(solution)/shard_map/ppermute | solution.py:785
  550.3 4.8 collective-permute-start.44
  (29 other events, 114.3 us)
Sparse Core Ops, SparseCore 0:
  13.4 76.4 all-gather.2
  92.2 53.7 all-gather.4
  242.2 50.0 reduce-scatter.3
  294.8 49.4 reduce-scatter.5
  380.0 93.0 reduce-scatter.7

commit v6 on v5

--- a/solution.py
+++ b/solution.py
@@ -91,6 +91,37 @@
         ),
         name=name,
     )(*args)
+
+
+def pack_kernel(
+    first_ref, second_ref, latent_gain_ref, query_ref, down_ref, router_ref, output_ref, up_ref, out_ref
+):
+    shard = query_ref.shape[0]
+    short = up_ref.shape[0]
+    heads = up_ref.shape[1] // (2 * NOPE)
+    nope = heads * NOPE
+    queries = nope + heads * ROPE
+    edge = queries + LATENT + LANES
+    outer = edge + output_ref.shape[1]
+    for head in range(heads):
+        start = head * (NOPE + ROPE)
+        out_ref[:, head * NOPE : (head + 1) * NOPE] = query_ref[:, start : start + NOPE]
+        out_ref[:, nope + head * ROPE : nope + (head + 1) * ROPE] = query_ref[
+            :, start + NOPE : start + NOPE + ROPE
+        ]
+        out_ref[head * short : (head + 1) * short, outer : outer + 2 * NOPE] = up_ref[
+            :, head * 2 * NOPE : (head + 1) * 2 * NOPE
+        ]
+    out_ref[:, queries : queries + LATENT + ROPE] = down_ref[...]
+    out_ref[:, queries + LATENT + ROPE : edge] = router_ref[...]
+    out_ref[:, edge:outer] = output_ref[...]
+    sub = lax.broadcasted_iota(jnp.int32, (LANES, LANES), 0)
+    lane = lax.broadcasted_iota(jnp.int32, (LANES, LANES), 1)
+    rows = jnp.zeros((LANES, LANES), F32)
+    for index, g_ref in enumerate((first_ref, second_ref, latent_gain_ref)):
+        gain = jnp.concatenate([g_ref[...].astype(F32), jnp.zeros((1, LANES - shard), F32)], axis=1)
+        rows = jnp.where((sub == index) & (lane < shard), gain, rows)
+    out_ref[:, outer + 2 * NOPE :] = rows.T[:shard, : out_ref.shape[1] - outer - 2 * NOPE].astype(BF16)
 
 
 def routing_kernel(me_ref, ids_ref, cot_ref, t0_ref, t1_ref, s0_ref, s1_ref, low_ref, out_ref):
@@ -856,27 +887,21 @@
     core = lax.rem(lax.axis_index("expert"), 2).astype(jnp.int32).reshape(1)
     smem = {0: pltpu.SMEM}
 
-    gains = jnp.concatenate(
+    (pack_one,) = run(
+        pack_kernel,
+        [((shard, outer + 2 * NOPE + ROPE), BF16)],
         [
-            first_gain[:, None],
-            second_gain[:, None],
-            jnp.pad(latent_gain, (0, shard - short))[:, None],
-            jnp.zeros((shard, ROPE - 3), BF16),
-        ],
-        axis=1,
-    )
-    by_head = query_proj.reshape(shard, heads, NOPE + ROPE)
-    pack_one = jnp.concatenate(
-        [
-            by_head[:, :, :NOPE].reshape(shard, nope),
-            by_head[:, :, NOPE:].reshape(shard, heads * ROPE),
+            first_gain.reshape(1, shard),
+            second_gain.reshape(1, shard),
+            jnp.pad(latent_gain, (0, shard - short)).reshape(1, shard),
+            query_proj,
             latent_down,
             router_proj,
             output_proj.T,
-            latent_up.reshape(short, heads, 2 * NOPE).transpose(1, 0, 2).reshape(shard, 2 * NOPE),
-            gains,
+            latent_up,
         ],
-        axis=1,
+        0,
+        name="pack",
     )
     pack_two = jnp.concatenate([shared_gate, shared_up, shared_down.T], axis=1)
     one = lax.all_gather(pack_one, "expert", axis=0, tiled=True)
@@ -1014,6 +1039,8 @@
         for out in (out0, out1)
     ]
 
+    out_cat = jnp.concatenate(out_rows, axis=1)
+    shared_got = send_blocks([after(shared1, back0), shared2, shared3])
     first_sum, first_probs = run(
         combine_first_kernel,
         [((tokens, width), F32), ((tokens, LANES), F32)],
@@ -1030,13 +1057,13 @@
             ((tokens, piece + LANES), BF16),
             ((tokens, piece + LANES), BF16),
         ],
-        [after(me, out1, gate_grad), t1, back1, first_sum, first_probs],
+        [after(me, out_cat, gate_grad, *shared_got), t1, back1, first_sum, first_probs],
         2 * tokens * rows * width,
         places=smem,
         name="combine",
     )
     got = send_blocks([send1, send2, send3])
-    out_rows = exchange(after(jnp.concatenate(out_rows, axis=1), own))
+    out_rows = exchange(after(out_cat, own))
     shared_sum = lax.psum_scatter(
         after(shared_grads, own), "expert", scatter_dimension=0, tiled=True
     )
@@ -1148,40 +1175,11 @@
             name="cross",
         )
         parts += [crossed[0]] + [along(1 - group, crossed[step], step) for step in range(1, side)]
-    got = send_blocks([send1, send2, send3])
-    first_sum = (own + got[0].astype(F32) + got[1].astype(F32) + got[2].astype(F32)).astype(BF16)
-    (stream_grad,) = run(
-        stream_kernel,
-        [((tokens, width), F32)],
-        [after(me, parts[0], parts[4]), middle_grad, stream, gain_rows, *share_small(first_sum)],
-        0,
-        scratch=[pltpu.VMEM((tokens, width), F32)],
-        places=smem,
-        name="stream",
-    )
-
-    got = send_blocks([shared1, shared2, shared3])
-    (branch,) = run(
-        routed_kernel,
-        [((tokens, piece), BF16)],
-        [t0, t1, out_rows, shared_own, *got],
-        4 * tokens * rows * piece,
-        name="routed",
-    )
-    (result,) = run(
-        result_kernel,
-        [((tokens, width), F32)],
-        [after(me, parts[0], parts[4]), middle, *share_small(branch)],
-        0,
-        places=smem,
-        name="result",
-    )
-
     shared_sum = shared_sum.astype(F32)
     gate_sum = shared_sum[:, :hidden_columns]
     up_sum = shared_sum[:, hidden_columns : 2 * hidden_columns]
     down_sum = shared_sum[:, 2 * hidden_columns :]
-    parts[0] = after(parts[0], stream_grad, result, gate_sum, up_sum, down_sum)
+    parts[0] = after(parts[0], gate_sum, up_sum, down_sum)
     query_grad, late, output_grad, latent_up_grad, router_grad = run(
         unpack_kernel,
         [
@@ -1196,6 +1194,34 @@
         scratch=[pltpu.VMEM((shard, columns), F32)],
         name="unpack",
     )
+    got = send_blocks([send1, send2, send3])
+    first_sum = (own + got[0].astype(F32) + got[1].astype(F32) + got[2].astype(F32)).astype(BF16)
+    (stream_grad,) = run(
+        stream_kernel,
+        [((tokens, width), F32)],
+        [after(me, late), middle_grad, stream, gain_rows, *share_small(first_sum)],
+        0,
+        scratch=[pltpu.VMEM((tokens, width), F32)],
+        places=smem,
+        name="stream",
+    )
+
+    (branch,) = run(
+        routed_kernel,
+        [((tokens, piece), BF16)],
+        [t0, t1, out_rows, shared_own, *shared_got],
+        4 * tokens * rows * piece,
+        name="routed",
+    )
+    (result,) = run(
+        result_kernel,
+        [((tokens, width), F32)],
+        [after(me, late), middle, *share_small(branch)],
+        0,
+        places=smem,
+        name="result",
+    )
+
     latent_down_grad, gain_grads = run(
         late_kernel,
         [(latent_down.shape, F32), ((8, LANES), F32)],

time: 576 us -> 570 us (0.990)
  waiting for transfers between devices: 223 us -> 213 us
  starting transfers between devices: 89.4 us -> 96.2 us
    ppermute x35, waiting for transfers between devices: 121 us -> 103 us  [shift(): lax.ppermute(array, 'tensor', [(i, (i + step) % size) for i in range(size)])]
    all_to_all x4, waiting for transfers between devices: 68.4 us -> 55.4 us  [exchange(): lax.all_to_all(rows.reshape(shape[0], -1, shape[-1]), 'expert', split_axi...]
    ppermute x9, waiting for transfers between devices: 2.1 us -> 14.4 us  [along(): lax.ppermute(array, 'expert', [(i, target(i)) for i in range(owners)])]
    reduce_scatter x2, waiting for transfers between devices: 0.04 us -> 8.98 us  [per_device(): lax.psum_scatter(out, 'tensor', scatter_dimension=0, tiled=True)]
    pallas_call x15 -> x16, Pallas kernels: 97.7 us -> 99.6 us  [run(): pl.pallas_call(kernel, in_specs=in_specs, out_specs=out_specs, out_shape=...]
  transfers between devices with their start and end apart: 55 -> 55, of which waited for: 28 -> 25; matrix products, arithmetic and copies ran while one was open for 4% -> 4% of each run, Pallas kernels for 28% -> 27%
where the time goes in v6:
time: 570 us; the launch traced here: 561 us
  waiting for transfers between devices  213 us (37%)
  Pallas kernels  162 us (28%)
  starting transfers between devices  96.2 us (17%)
  blocking collectives  40.2 us (7%)
  local copies, waits for them, and re-layouts  25.8 us (5%)
  between operations  14.8 us (3%)
  other arithmetic  8.41 us (1%)
    ppermute x35, waiting for transfers between devices, shift(): lax.ppermute(array, 'tensor', [(i, (i + step) % size) for i in range(size)])  103 us
    pallas_call x16, Pallas kernels, run(): pl.pallas_call(kernel, in_specs=in_specs, out_specs=out_specs, out_shape=...  99.6 us
    all_to_all x4, waiting for transfers between devices, exchange(): lax.all_to_all(rows.reshape(shape[0], -1, shape[-1]), 'expert', split_axi...  55.4 us
    ppermute x35, starting transfers between devices, shift(): lax.ppermute(array, 'tensor', [(i, (i + step) % size) for i in range(size)])  46.6 us
    all_to_all x1, blocking collectives, exchange(): lax.all_to_all(rows.reshape(shape[0], -1, shape[-1]), 'expert', split_axi...  40.2 us
    pallas_call x2, Pallas kernels, expert_back(): pl.pallas_call(functools.partial(expert_back_kernel, split), grid=(owners...  32.9 us
    all_to_all x4, starting transfers between devices, exchange(): lax.all_to_all(rows.reshape(shape[0], -1, shape[-1]), 'expert', split_axi...  26.8 us
    all_gather x1, waiting for transfers between devices, per_device(): one = lax.all_gather(pack_one, 'expert', axis=0, tiled=True)  23.7 us
  transfers between devices with their start and end apart: 55, of which 25 were waited for; matrix products, arithmetic and copies ran while one was open for 4% of the time, Pallas kernels for 27%

profile of v6, /device:TPU:0, one launch (start us, length us, event | category | flops | bytes accessed | tf_op | source)
XLA Modules:
  0.0 561.1 jit_solution(15404853679467046141)
XLA Ops:
  8.4 1.8 pack.1
  10.3 1.8 concatenate.16
  12.2 4.8 routing.1
  17.0 40.2 %all_to_all.30 = bf16[32,64,512]{2,1,0:T(8,128)(2,1)S(1)} all-to-all(bf16[32,64,512]{2,1,0:T(8,128)(2,1)} %bitcast.44), channel_id=1, replica_groups=mesh['expert'=32,'tensor'=4] {'expert'}, dimensions={0} | all-to-all | bytes 4194304 | tf_op jit(solution)/shard_map/all_to_all | solution.py:844
  63.2 23.7 %all-gather.3.cloned.1.call-done.w_ref.refs_10_.refs_13_.w_in = bf16[2048,2240]{1,0:T(8,128)(2,1)} async-done(((bf16[64,2240]{1,0:T(8,128)(2,1)}), bf16[2048,2240]{1,0:T(8,128)(2,1)}) %all-gather.3.cloned.1.call-update) | async-done | bytes 9175056 | tf_op jit(solution)/shard_map/all_gather | solution.py:907
  86.9 11.2 %attend.1 = (f32[256,512]{1,0:T(8,128)}, bf16[256,512]{1,0:T(8,128)(2,1)}, bf16[256,512]{1,0:T(8,128)(2,1)}, bf16[256,512]{1,0:T(8,128)(2,1)}, bf16[256,2048]{1,...) custom-call(s32[1]{0:T(128)} %bitcast.me_ref.refs_0_, ...), custom_call_target="tpu_custom_call" | custom-call | flops 201326592 | bytes 1627136 | tf_op jit(solution)/shard_map/attend/pallas_call | solution.py:81
  99.6 2.7 collective-permute-start.1
  103.8 7.5 %collective-permute-done = bf16[256,512]{1,0:T(8,128)(2,1)S(1)} collective-permute-done((bf16[256,512]{1,0:T(8,128)(2,1)}, bf16[256,512]{1,0:T(8,128)(2,1)S(1)}, u32[]{:S(2)}, u32[]{:S(2)}) %collective-permute-start) | collective-permute-done | bytes 262176 | tf_op jit(solution)/shard_map/ppermute | solution.py:816
  111.3 6.8 %collective-permute-done.1 = bf16[256,512]{1,0:T(8,128)(2,1)S(1)} collective-permute-done((bf16[256,512]{1,0:T(8,128)(2,1)}, bf16[256,512]{1,0:T(8,128)(2,1)S(1)}, u32[]{:S(2)}, u32[]{:S(2)}) %collective-permute-start.1) | collective-permute-done | bytes 262176 | tf_op jit(solution)/shard_map/ppermute | solution.py:816
  119.3 1.8 collective-permute-start.5
  122.8 5.8 %collective-permute-done.5.a1_ref = bf16[256,512]{1,0:T(8,128)(2,1)S(1)} collective-permute-done((bf16[256,512]{1,0:T(8,128)(2,1)S(1)}, bf16[256,512]{1,0:T(8,128)(2,1)S(1)}, u32[]{:S(2)}, u32[]{:S(2)}) %collective-permute-start.5) | collective-permute-done | bytes 262176 | tf_op jit(solution)/shard_map/ppermute | solution.py:816
  128.6 3.3 collective-permute-done.6.a2_ref
  131.9 3.0 collective-permute-done.7.a3_ref
  135.6 6.7 %dispatch.1 = (f32[256,2048]{1,0:T(8,128)}, bf16[256,2048]{1,0:T(8,128)(2,1)}, bf16[32,32,2560]{2,1,0:T(8,128)(2,1)}) custom-call(s32[1]{0:T(128)} %bitcast.me_ref.refs_0_, bf16[256,2048]{1,0:T(8,128)(2,1)} %stream_ref.7, bf16[256,512]{1,0:T(8,128)(2,1)} %copy-done.9, bf16[256,512]{1,0:T(8,128)(2,1)} %copy-done.19, bf16[256,512]{1,0:T(8,128)(2,1)} %copy-done.20, ...), custom_call_target="tpu_custom_call" | custom-call | flops 134217728 | bytes 1159987 | tf_op jit(solution)/shard_map/dispatch/pallas_call | solution.py:81
  142.3 4.9 all-to-all-start.1
  147.3 2.3 slice.61
  150.9 3.3 collective-permute-start.9
  154.2 22.0 %collective-permute-done.8 = bf16[16,2,32,512]{3,2,1,0:T(8,128)(2,1)S(1)} collective-permute-done((bf16[16,2,32,512]{3,2,1,0:T(8,128)(2,1)}, bf16[16,2,32,512]{3,2,1,0:T(8,128)(2,1)S(1)}, u32[]{:S(2)}, u32[]{:S(2)}) %collective-permute-start.8) | collective-permute-done | bytes 1048608 | tf_op jit(solution)/shard_map/ppermute | solution.py:816
  178.0 1.9 slice.60.router_ref
  179.9 16.6 %shared.1 = (f32[256,512]{1,0:T(8,128)}, bf16[256,512]{1,0:T(8,128)(2,1)}, bf16[256,512]{1,0:T(8,128)(2,1)}, bf16[256,512]{1,0:T(8,128)(2,1)}, f32[256,2048]{1,0...) custom-call(s32[1]{0:T(128)} %bitcast.me_ref.refs_0_, bf16[256,2048]{1,0:T(8,128)(2,1)} %get-tuple-element.119.mixed_ref, ...), custom_call_target="tpu_custom_call" | custom-call | flops 664377728 | bytes 2346189 | tf_op jit(solution)/shard_map/shared/pallas_call | solution.py:81
  196.5 15.8 %all-to-all-done.1.refs_2_.x0_ref = bf16[32,32,2560]{2,1,0:T(8,128)(2,1)} async-done(((bf16[32,32,2560]{2,1,0:T(8,128)(2,1)}), bf16[32,32,2560]{2,1,0:T(8,128)(2,1)}, u32[]{:S(2)}, u32[]{:S(2)}) %all-to-all-start.1) | async-done | bytes 5242912 | tf_op jit(solution)/shard_map/all_to_all | solution.py:844
  213.7 3.6 collective-permute-start.10
  217.3 16.3 %expert_back.2 = (bf16[32,32,2176]{2,1,0:T(8,128)(2,1)}, bf16[32,32,2048]{2,1,0:T(8,128)(2,1)}, bf16[1024,352]{1,0:T(8,128)(2,1)}, bf16[1024,352]{1,0:T(8,128)(2,1)}, bf16[1024,352]{1,0:T(8,128)(2,1)}) custom-call(s32[1]{0:T(128)} %bitcast.me_ref.refs_0_, s32[1]{0:T(128)} %bitcast.14.refs_1_, bf16[32,32,2560]{2,1,0:T(8,128)(2,1)} %all-to-all-done.1.refs_2_.x0_ref, ...), custom_call_target="tpu_custom_call" | custom-call | flops 73819750400 | bytes 25165824 | tf_op jit(solution)/shard_map/expert_back/pallas_call | solution.py:390
  233.6 5.3 expert_out.2
  241.1 3.1 collective-permute-start.13
  244.2 8.4 %all-to-all-start.2 = ((bf16[32,32,2176]{2,1,0:T(8,128)(2,1)}), bf16[32,32,2176]{2,1,0:T(8,128)(2,1)}, u32[]{:S(2)}, u32[]{:S(2)}) async-start(bf16[32,32,2176]{2,1,0:T(8,128)(2,1)} %get-tuple-element.130), calls=%async_computation.4 | async-start | bytes 8912896 | tf_op jit(solution)/shard_map/all_to_all | solution.py:844
  252.7 5.9 %collective-permute-done.12 = bf16[16,32,512]{2,1,0:T(8,128)(2,1)S(1)} collective-permute-done((bf16[16,32,512]{2,1,0:T(8,128)(2,1)S(1)}, bf16[16,32,512]{2,1,0:T(8,128)(2,1)S(1)}, u32[]{:S(2)}, u32[]{:S(2)}) %collective-permute-start.12) | collective-permute-done | bytes 524320 | tf_op jit(solution)/shard_map/ppermute | solution.py:816
  258.6 4.7 collective-permute-done.13
  264.3 16.6 %expert_back.3 = (bf16[32,32,2176]{2,1,0:T(8,128)(2,1)}, bf16[32,32,2048]{2,1,0:T(8,128)(2,1)}, bf16[1024,352]{1,0:T(8,128)(2,1)}, bf16[1024,352]{1,0:T(8,128)(2...) custom-call(s32[1]{0:T(128)} %bitcast.me_ref.refs_0_, s32[1]{0:T(128)} %bitcast.14.refs_1_, ...), custom_call_target="tpu_custom_call" | custom-call | flops 73819750400 | bytes 25165824 | tf_op jit(solution)/shard_map/expert_back/pallas_call | solution.py:390
  281.0 5.3 expert_out.3
  286.3 22.4 %all-to-all-done.2.b_ref = bf16[32,32,2176]{2,1,0:T(8,128)(2,1)} async-done(((bf16[32,32,2176]{2,1,0:T(8,128)(2,1)}), bf16[32,32,2176]{2,1,0:T(8,128)(2,1)}, u32[]{:S(2)}, u32[]{:S(2)}) %all-to-all-start.2) | async-done | bytes 4456480 | tf_op jit(solution)/shard_map/all_to_all | solution.py:844
  308.7 6.7 %all-to-all-start.3 = ((bf16[32,32,2176]{2,1,0:T(8,128)(2,1)}), bf16[32,32,2176]{2,1,0:T(8,128)(2,1)}, u32[]{:S(2)}, u32[]{:S(2)}) async-start(bf16[32,32,2176]{2,1,0:T(8,128)(2,1)} %get-tuple-element.145), calls=%async_computation.5 | async-start | bytes 8912896 | tf_op jit(solution)/shard_map/all_to_all | solution.py:844
  317.9 6.1 %combine_first.1 = (f32[256,2048]{1,0:T(8,128)}, f32[256,128]{1,0:T(8,128)}) custom-call(bf16[256,1024]{1,0:T(8,128)(2,1)} %get-tuple-element.146.t_ref.t0_ref, bf16[32,32,2176]{2,1,0:T(8,128)(2,1)} %all-to-all-done.2.b_ref, f32[256,2048]{1,0:T(8,128)} %get-tuple-element.121.shared_ref), custom_call_target="tpu_custom_call" | custom-call | flops 107374184 | bytes 930611 | tf_op jit(solution)/shard_map/combine_first/pallas_call | solution.py:81
  324.0 19.3 %expert_grads.1 = (f32[2,352,2048]{2,1,0:T(8,128)}, f32[2,352,2048]{2,1,0:T(8,128)}, f32[2,352,2048]{2,1,0:T(8,128)}) custom-call(bf16[32,32,2560]{2,1,0:T(8,128)(2,1)} %all-to-all-done.1.refs_2_.x0_ref, bf16[32,32,2048]{2,1,0:T(8,128)(2,1)} %get-tuple-element.128.c0_ref, bf16[1024,352]{1,0:T(8,128)(2,1)} %get-tuple-element.124.hg_ref.hg0_ref, ...), custom_call_target="tpu_custom_call" | custom-call | flops 738197504 | bytes 4177920 | tf_op jit(solution)/shard_map/expert_grads/pallas_call | solution.py:469
  343.3 9.0 %reduce-scatter.6.cloned.1.call-done = bf16[1,32,32,512]{3,2,1,0:T(8,128)(2,1)} async-done(((bf16[4,32,32,512]{3,2,1,0:T(8,128)(2,1)}), bf16[1,32,32,512]{3,2,1,0:T(8,128)(2,1)}) %reduce-scatter.6.cloned.1.call-update) | async-done | bytes 1048592 | tf_op jit(solution)/shard_map/reduce_scatter | solution.py:1038
  354.1 17.3 %all-to-all-done.3.b_ref = bf16[32,32,2176]{2,1,0:T(8,128)(2,1)} async-done(((bf16[32,32,2176]{2,1,0:T(8,128)(2,1)}), bf16[32,32,2176]{2,1,0:T(8,128)(2,1)}, u32[]{:S(2)}, u32[]{:S(2)}) %all-to-all-start.3) | async-done | bytes 4456480 | tf_op jit(solution)/shard_map/all_to_all | solution.py:844
  371.4 5.5 combine.1
  378.3 6.8 %all-to-all-start.4 = ((bf16[32,64,512]{2,1,0:T(8,128)(2,1)}), bf16[32,64,512]{2,1,0:T(8,128)(2,1)S(1)}, u32[]{:S(2)}, u32[]{:S(2)}) async-start(bf16[32,64,512]{2,1,0:T(8,128)(2,1)} %bitcast.38), calls=%async_computation.6 | async-start | bytes 4194304 | tf_op jit(solution)/shard_map/all_to_all | solution.py:844
  388.5 15.1 %collective-permute-done.17.r1_ref = bf16[256,640]{1,0:T(8,128)(2,1)S(1)} collective-permute-done((bf16[256,640]{1,0:T(8,128)(2,1)}, bf16[256,640]{1,0:T(8,128)(2,1)S(1)}, u32[]{:S(2)}, u32[]{:S(2)}) %collective-permute-start.17) | collective-permute-done | bytes 327712 | tf_op jit(solution)/shard_map/ppermute | solution.py:816
  405.5 2.2 collective-permute-start.20
  408.9 9.7 %collective-permute-done.20.a1_ref = bf16[256,512]{1,0:T(8,128)(2,1)} collective-permute-done((bf16[256,512]{1,0:T(8,128)(2,1)S(1)}, bf16[256,512]{1,0:T(8,128)(2,1)}, u32[]{:S(2)}, u32[]{:S(2)}) %collective-permute-start.20) | collective-permute-done | bytes 262176 | tf_op jit(solution)/shard_map/ppermute | solution.py:816
  418.6 3.8 collective-permute-done.22.a3_ref
  422.4 19.3 %attend_back.1 = (bf16[16,64,2304]{2,1,0:T(8,128)(2,1)}, bf16[16,64,2304]{2,1,0:T(8,128)(2,1)}, f32[256,2048]{1,0:T(8,128)}, f32[256,512]{1,0:T(8,128)}, bf16[25...) custom-call(s32[1]{0:T(128)} %bitcast.me_ref.refs_0_, s32[1]{0:T(128)} %bitcast.3.core_ref, ...), custom_call_target="tpu_custom_call" | custom-call | flops 845571712 | bytes 3586458 | tf_op jit(solution)/shard_map/attend_back/pallas_call | solution.py:81
  442.6 7.4 %collective-permute-done.23.got_ref = bf16[16,64,2304]{2,1,0:T(8,128)(2,1)} collective-permute-done((bf16[16,64,2304]{2,1,0:T(8,128)(2,1)}, bf16[16,64,2304]{2,1,0:T(8,128)(2,1)}, u32[]{:S(2)}, u32[]{:S(2)}) %collective-permute-start.23) | collective-permute-done | bytes 4718624 | tf_op jit(solution)/shard_map/ppermute | solution.py:1131
  450.1 6.4 %pair.1 = (bf16[4,4,64,1152]{3,2,1,0:T(8,128)(2,1)}, bf16[4,64,1152]{2,1,0:T(8,128)(2,1)}, bf16[4,64,1152]{2,1,0:T(8,128)(2,1)}, bf16[4,64,1152]{2,1,0:T(8,128)(2,1)}, bf16[4,64,1152]{2,1,0:T(8,128)(2,1)}) custom-call(s32[2]{0:T(128)} %pad_add_fusion.at_ref, bf16[16,64,2304]{2,1,0:T(8,128)(2,1)} %get-tuple-element.164.keep_ref, ...), custom_call_target="tpu_custom_call" | custom-call | bytes 1415578 | tf_op jit(solution)/shard_map/pair/pallas_call | solution.py:81
  456.5 4.5 all-to-all-start.5
  465.9 2.8 collective-permute-start.25
  468.7 7.3 %collective-permute-done.36 = bf16[256,512]{1,0:T(8,128)(2,1)S(1)} collective-permute-done((bf16[256,512]{1,0:T(8,128)(2,1)}, bf16[256,512]{1,0:T(8,128)(2,1)S(1)}, u32[]{:S(2)}, u32[]{:S(2)}) %collective-permute-start.36) | collective-permute-done | bytes 262176 | tf_op jit(solution)/shard_map/ppermute | solution.py:816
  476.1 2.8 collective-permute-start.26
  481.4 13.1 %collective-permute-done.25.refs_2_ = bf16[4,64,1152]{2,1,0:T(8,128)(2,1)} collective-permute-done((bf16[4,64,1152]{2,1,0:T(8,128)(2,1)}, bf16[4,64,1152]{2,1,0:T(8,128)(2,1)}, u32[]{:S(2)}, u32[]{:S(2)}) %collective-permute-start.25) | collective-permute-done | bytes 589856 | tf_op jit(solution)/shard_map/ppermute | solution.py:1147
  494.5 2.6 cross.2
  498.7 2.7 collective-permute-start.28
  504.1 2.6 cross.3
  506.7 1.9 collective-permute-start.30
  508.7 1.9 collective-permute-start.31
  512.0 3.6 routed.1.a0_ref
  516.6 1.9 collective-permute-start.34
  519.7 2.2 collective-permute-start.40
  524.6 2.3 unpack.1
  528.5 3.4 collective-permute-start.43
  531.8 3.0 collective-permute-done.35.a3_ref
  536.1 3.3 result.1
  539.4 3.5 collective-permute-done.41.a3_ref
  543.7 5.0 stream.1
  (185 shorter events, 61.5 us)
Async XLA Ops:
  7.2 79.7 %all-gather.3.cloned.1.call-start = ((), (), s32[]{:S(2)}) async-start(), calls=%async_computation.9 | async-start | bytes 9732096 | tf_op jit(solution)/shard_map/all_gather | solution.py:907
  10.3 169.7 %all-gather.5.cloned.1.call-start = ((), (), s32[]{:S(2)}) async-start(), calls=%async_computation.10 | async-start | bytes 9191424 | tf_op jit(solution)/shard_map/all_gather | solution.py:908
  17.0 45.4 %copy-start.34 = (s32[1,256]{1,0:T(1,128)S(1)}, s32[1,256]{1,0:T(1,128)}, u32[]{:S(2)}) copy-start(s32[1,256]{1,0:T(1,128)} %seg_row_ref.1) | copy-start | bytes 3076
  57.2 40.9 %copy-start.2 = (bf16[32,64,512]{2,1,0:T(8,128)(2,1)}, bf16[32,64,512]{2,1,0:T(8,128)(2,1)S(1)}, u32[]{:S(2)}) copy-start(bf16[32,64,512]{2,1,0:T(8,128)(2,1)S(1)} %all_to_all.30) | copy-start | bytes 6291460
  57.2 62.1 %collective-permute-start.3 = (bf16[32,2,32,512]{3,2,1,0:T(8,128)(2,1)S(1)}, bf16[32,2,32,512]{3,2,1,0:T(8,128)(2,1)}, u32[]{:S(2)}, u32[]{:S(2)}) collective-permute-start(bf16[32,2,32,512]{3,2,1,0:T(8,128)(2,1)S(1)} %bitcast.40), channel_id=1, source_target_pairs={{0,1},{1,2},{2,3},{3,0},{4,5},{5,6},{6,7},{7,4},{8,9},{9,10},{10,1... | collective-permute-start | bytes 6291464 | tf_op jit(solution)/shard_map/ppermute | solution.py:816
  58.7 60.6 %collective-permute-start.4 = (bf16[32,2,32,512]{3,2,1,0:T(8,128)(2,1)S(1)}, bf16[32,2,32,512]{3,2,1,0:T(8,128)(2,1)}, u32[]{:S(2)}, u32[]{:S(2)}) collective-permute-start(bf16[32,2,32,512]{3,2,1,0:T(8,128)(2,1)S(1)} %bitcast.41), channel_id=1, source_target_pairs={{0,3},{1,0},{2,1},{3,2},{4,7},{5,4},{6,5},{7,6},{8,11},{9,8},{10,9... | collective-permute-start | bytes 6291464 | tf_op jit(solution)/shard_map/ppermute | solution.py:816
  98.1 13.2 %collective-permute-start = (bf16[256,512]{1,0:T(8,128)(2,1)}, bf16[256,512]{1,0:T(8,128)(2,1)S(1)}, u32[]{:S(2)}, u32[]{:S(2)}) collective-permute-start(bf16[256,512]{1,0:T(8,128)(2,1)} %get-tuple-element.111), channel_id=1, source_target_pairs={{0,1},{1,2},{2,3},{3,0},{4,5},{5,6},{6,7},{7,4},{8,9},{9,10},{10,1... | collective-permute-start | bytes 786440 | tf_op jit(solution)/shard_map/ppermute | solution.py:816
  99.6 18.5 %collective-permute-start.1 = (bf16[256,512]{1,0:T(8,128)(2,1)}, bf16[256,512]{1,0:T(8,128)(2,1)S(1)}, u32[]{:S(2)}, u32[]{:S(2)}) collective-permute-start(bf16[256,512]{1,0:T(8,128)(2,1)} %get-tuple-element.112), channel_id=1, source_target_pairs={{0,2},{1,3},{2,0},{3,1},{4,6},{5,7},{6,4},{7,5},{8,10},{9,11},{10,... | collective-permute-start | bytes 786440 | tf_op jit(solution)/shard_map/ppermute | solution.py:816
  102.4 15.7 %collective-permute-start.2 = (bf16[256,512]{1,0:T(8,128)(2,1)}, bf16[256,512]{1,0:T(8,128)(2,1)S(1)}, u32[]{:S(2)}, u32[]{:S(2)}) collective-permute-start(bf16[256,512]{1,0:T(8,128)(2,1)} %get-tuple-element.113), channel_id=1, source_target_pairs={{0,3},{1,0},{2,1},{3,2},{4,7},{5,4},{6,5},{7,6},{8,11},{9,8},{10,9... | collective-permute-start | bytes 786440 | tf_op jit(solution)/shard_map/ppermute | solution.py:816
  119.3 9.3 %collective-permute-start.5 = (bf16[256,512]{1,0:T(8,128)(2,1)S(1)}, bf16[256,512]{1,0:T(8,128)(2,1)S(1)}, u32[]{:S(2)}, u32[]{:S(2)}) collective-permute-start(bf16[256,512]{1,0:T(8,128)(2,1)S(1)} %add_convert_fusion.2.a0_ref), channel_id=1, source_target_pairs={{0,3},{1,0},{2,1},{3,2},{4,7},{5,4},{6,5},{7,6},{8,11},{9,8},{10,9... | collective-permute-start | bytes 786440 | tf_op jit(solution)/shard_map/ppermute | solution.py:816
  121.2 10.7 %collective-permute-start.6 = (bf16[256,512]{1,0:T(8,128)(2,1)S(1)}, bf16[256,512]{1,0:T(8,128)(2,1)S(1)}, u32[]{:S(2)}, u32[]{:S(2)}) collective-permute-start(bf16[256,512]{1,0:T(8,128)(2,1)S(1)} %add_convert_fusion.2.a0_ref), channel_id=1, source_target_pairs={{0,2},{1,3},{2,0},{3,1},{4,6},{5,7},{6,4},{7,5},{8,10},{9,11},{10,... | collective-permute-start | bytes 786440 | tf_op jit(solution)/shard_map/ppermute | solution.py:816
  122.0 12.9 %collective-permute-start.7 = (bf16[256,512]{1,0:T(8,128)(2,1)S(1)}, bf16[256,512]{1,0:T(8,128)(2,1)S(1)}, u32[]{:S(2)}, u32[]{:S(2)}) collective-permute-start(bf16[256,512]{1,0:T(8,128)(2,1)S(1)} %add_convert_fusion.2.a0_ref), channel_id=1, source_target_pairs={{0,1},{1,2},{2,3},{3,0},{4,5},{5,6},{6,7},{7,4},{8,9},{9,10},{10,1... | collective-permute-start | bytes 786440 | tf_op jit(solution)/shard_map/ppermute | solution.py:816
  142.3 69.9 %all-to-all-start.1 = ((bf16[32,32,2560]{2,1,0:T(8,128)(2,1)}), bf16[32,32,2560]{2,1,0:T(8,128)(2,1)}, u32[]{:S(2)}, u32[]{:S(2)}) async-start(bf16[32,32,2560]{2,1,0:T(8,128)(2,1)} %get-tuple-element.123), calls=%async_computation.1 | async-start | bytes 10485760 | tf_op jit(solution)/shard_map/all_to_all | solution.py:844
  147.2 196.1 %reduce-scatter.4.cloned.1.call-start = ((), (), s32[]{:S(2)}) async-start(), calls=%async_computation.11 | async-start | bytes 5242880 | tf_op jit(solution)/shard_map/reduce_scatter | solution.py:1038
  149.6 26.6 %collective-permute-start.8 = (bf16[16,2,32,512]{3,2,1,0:T(8,128)(2,1)}, bf16[16,2,32,512]{3,2,1,0:T(8,128)(2,1)S(1)}, u32[]{:S(2)}, u32[]{:S(2)}) collective-permute-start(bf16[16,2,32,512]{3,2,1,0:T(8,128)(2,1)} %slice.61), channel_id=1, source_target_pairs={{0,1},{1,2},{2,3},{3,0},{4,5},{5,6},{6,7},{7,4},{8,9},{9,10},{10,1... | collective-permute-start | bytes 3145736 | tf_op jit(solution)/shard_map/ppermute | solution.py:816
  150.9 25.7 %collective-permute-start.9 = (bf16[16,2,32,512]{3,2,1,0:T(8,128)(2,1)S(1)}, bf16[16,2,32,512]{3,2,1,0:T(8,128)(2,1)S(1)}, u32[]{:S(2)}, u32[]{:S(2)}) collective-permute-start(bf16[16,2,32,512]{3,2,1,0:T(8,128)(2,1)S(1)} %slice.62), channel_id=1, source_target_pairs={{0,3},{1,0},{2,1},{3,2},{4,7},{5,4},{6,5},{7,6},{8,11},{9,8},{10,9... | collective-permute-start | bytes 3145736 | tf_op jit(solution)/shard_map/ppermute | solution.py:816
  213.6 26.1 %collective-permute-start.11 = (bf16[32,32,512]{2,1,0:T(8,128)(2,1)S(1)}, bf16[32,32,512]{2,1,0:T(8,128)(2,1)S(1)}, u32[]{:S(2)}, u32[]{:S(2)}) collective-permute-start(bf16[32,32,512]{2,1,0:T(8,128)(2,1)S(1)} %slice.63), channel_id=1, source_target_pairs={{0,1},{1,2},{2,3},{3,0},{4,5},{5,6},{6,7},{7,4},{8,9},{9,10},{10,1... | collective-permute-start | bytes 3145736 | tf_op jit(solution)/shard_map/ppermute | solution.py:816
  213.7 26.1 %collective-permute-start.10 = (bf16[32,32,512]{2,1,0:T(8,128)(2,1)S(1)}, bf16[32,32,512]{2,1,0:T(8,128)(2,1)}, u32[]{:S(2)}, u32[]{:S(2)}) collective-permute-start(bf16[32,32,512]{2,1,0:T(8,128)(2,1)S(1)} %slice.63), channel_id=1, source_target_pairs={{0,3},{1,0},{2,1},{3,2},{4,7},{5,4},{6,5},{7,6},{8,11},{9,8},{10,9... | collective-permute-start | bytes 3145736 | tf_op jit(solution)/shard_map/ppermute | solution.py:816
  239.7 18.9 %collective-permute-start.12 = (bf16[16,32,512]{2,1,0:T(8,128)(2,1)S(1)}, bf16[16,32,512]{2,1,0:T(8,128)(2,1)S(1)}, u32[]{:S(2)}, u32[]{:S(2)}) collective-permute-start(bf16[16,32,512]{2,1,0:T(8,128)(2,1)S(1)} %slice.64), channel_id=1, source_target_pairs={{0,1},{1,2},{2,3},{3,0},{4,5},{5,6},{6,7},{7,4},{8,9},{9,10},{10,1... | collective-permute-start | bytes 1572872 | tf_op jit(solution)/shard_map/ppermute | solution.py:816
  241.1 22.1 %collective-permute-start.13 = (bf16[16,32,512]{2,1,0:T(8,128)(2,1)S(1)}, bf16[16,32,512]{2,1,0:T(8,128)(2,1)S(1)}, u32[]{:S(2)}, u32[]{:S(2)}) collective-permute-start(bf16[16,32,512]{2,1,0:T(8,128)(2,1)S(1)} %slice.65), channel_id=1, source_target_pairs={{0,3},{1,0},{2,1},{3,2},{4,7},{5,4},{6,5},{7,6},{8,11},{9,8},{10,9... | collective-permute-start | bytes 1572872 | tf_op jit(solution)/shard_map/ppermute | solution.py:816
  244.2 64.5 %all-to-all-start.2 = ((bf16[32,32,2176]{2,1,0:T(8,128)(2,1)}), bf16[32,32,2176]{2,1,0:T(8,128)(2,1)}, u32[]{:S(2)}, u32[]{:S(2)}) async-start(bf16[32,32,2176]{2,1,0:T(8,128)(2,1)} %get-tuple-element.130), calls=%async_computation.4 | async-start | bytes 8912896 | tf_op jit(solution)/shard_map/all_to_all | solution.py:844
  252.6 99.7 %reduce-scatter.6.cloned.1.call-start = ((), (), s32[]{:S(2)}) async-start(), calls=%async_computation.12 | async-start | bytes 5242880 | tf_op jit(solution)/shard_map/reduce_scatter | solution.py:1038
  308.7 62.6 %all-to-all-start.3 = ((bf16[32,32,2176]{2,1,0:T(8,128)(2,1)}), bf16[32,32,2176]{2,1,0:T(8,128)(2,1)}, u32[]{:S(2)}, u32[]{:S(2)}) async-start(bf16[32,32,2176]{2,1,0:T(8,128)(2,1)} %get-tuple-element.145), calls=%async_computation.5 | async-start | bytes 8912896 | tf_op jit(solution)/shard_map/all_to_all | solution.py:844
  315.5 207.2 %reduce-scatter.8.cloned.1.call-start = ((), (), s32[]{:S(2)}) async-start(), calls=%async_computation.13 | async-start | bytes 9191424 | tf_op jit(solution)/shard_map/reduce_scatter | solution.py:1067
  315.5 38.5 %collective-permute-start.15 = (bf16[256,512]{1,0:T(8,128)(2,1)}, bf16[256,512]{1,0:T(8,128)(2,1)S(1)}, u32[]{:S(2)}, u32[]{:S(2)}) collective-permute-start(bf16[256,512]{1,0:T(8,128)(2,1)} %get-tuple-element.140), channel_id=1, source_target_pairs={{0,2},{1,3},{2,0},{3,1},{4,6},{5,7},{6,4},{7,5},{8,10},{9,11},{10,... | collective-permute-start | bytes 786440 | tf_op jit(solution)/shard_map/ppermute | solution.py:816
  315.6 38.4 %collective-permute-start.16 = (bf16[256,512]{1,0:T(8,128)(2,1)S(1)}, bf16[256,512]{1,0:T(8,128)(2,1)S(1)}, u32[]{:S(2)}, u32[]{:S(2)}) collective-permute-start(bf16[256,512]{1,0:T(8,128)(2,1)S(1)} %copy-done.37), channel_id=1, source_target_pairs={{0,3},{1,0},{2,1},{3,2},{4,7},{5,4},{6,5},{7,6},{8,11},{9,8},{10,9... | collective-permute-start | bytes 786440 | tf_op jit(solution)/shard_map/ppermute | solution.py:816
  317.4 36.7 %collective-permute-start.14 = (bf16[256,512]{1,0:T(8,128)(2,1)S(1)}, bf16[256,512]{1,0:T(8,128)(2,1)S(1)}, u32[]{:S(2)}, u32[]{:S(2)}) collective-permute-start(bf16[256,512]{1,0:T(8,128)(2,1)S(1)} %copy-done.36), channel_id=1, source_target_pairs={{0,1},{1,2},{2,3},{3,0},{4,5},{5,6},{6,7},{7,4},{8,9},{9,10},{10,1... | collective-permute-start | bytes 786440 | tf_op jit(solution)/shard_map/ppermute | solution.py:816
  354.0 22.8 %copy-start.12 = (bf16[256,512]{1,0:T(8,128)(2,1)}, bf16[256,512]{1,0:T(8,128)(2,1)S(1)}, u32[]{:S(2)}) copy-start(bf16[256,512]{1,0:T(8,128)(2,1)S(1)} %collective-permute-done.15.r2_ref) | copy-start | bytes 786436
  354.1 22.8 %copy-start.13 = (bf16[256,512]{1,0:T(8,128)(2,1)}, bf16[256,512]{1,0:T(8,128)(2,1)S(1)}, u32[]{:S(2)}) copy-start(bf16[256,512]{1,0:T(8,128)(2,1)S(1)} %collective-permute-done.16.r3_ref) | copy-start | bytes 786436
  354.1 22.8 %copy-start.14 = (bf16[256,512]{1,0:T(8,128)(2,1)}, bf16[256,512]{1,0:T(8,128)(2,1)S(1)}, u32[]{:S(2)}) copy-start(bf16[256,512]{1,0:T(8,128)(2,1)S(1)} %collective-permute-done.14.r1_ref) | copy-start | bytes 786436
  378.3 63.4 %all-to-all-start.4 = ((bf16[32,64,512]{2,1,0:T(8,128)(2,1)}), bf16[32,64,512]{2,1,0:T(8,128)(2,1)S(1)}, u32[]{:S(2)}, u32[]{:S(2)}) async-start(bf16[32,64,512]{2,1,0:T(8,128)(2,1)} %bitcast.38), calls=%async_computation.6 | async-start | bytes 4194304 | tf_op jit(solution)/shard_map/all_to_all | solution.py:844
  385.2 18.4 %collective-permute-start.17 = (bf16[256,640]{1,0:T(8,128)(2,1)}, bf16[256,640]{1,0:T(8,128)(2,1)S(1)}, u32[]{:S(2)}, u32[]{:S(2)}) collective-permute-start(bf16[256,640]{1,0:T(8,128)(2,1)} %get-tuple-element.150), channel_id=1, source_target_pairs={{0,1},{1,2},{2,3},{3,0},{4,5},{5,6},{6,7},{7,4},{8,9},{9,10},{10,1... | collective-permute-start | bytes 983048 | tf_op jit(solution)/shard_map/ppermute | solution.py:816
  385.3 18.3 %collective-permute-start.18 = (bf16[256,640]{1,0:T(8,128)(2,1)}, bf16[256,640]{1,0:T(8,128)(2,1)S(1)}, u32[]{:S(2)}, u32[]{:S(2)}) collective-permute-start(bf16[256,640]{1,0:T(8,128)(2,1)} %get-tuple-element.151), channel_id=1, source_target_pairs={{0,2},{1,3},{2,0},{3,1},{4,6},{5,7},{6,4},{7,5},{8,10},{9,11},{10,... | collective-permute-start | bytes 983048 | tf_op jit(solution)/shard_map/ppermute | solution.py:816
  386.7 17.5 %collective-permute-start.19 = (bf16[256,640]{1,0:T(8,128)(2,1)S(1)}, bf16[256,640]{1,0:T(8,128)(2,1)S(1)}, u32[]{:S(2)}, u32[]{:S(2)}) collective-permute-start(bf16[256,640]{1,0:T(8,128)(2,1)S(1)} %copy-done.35), channel_id=1, source_target_pairs={{0,3},{1,0},{2,1},{3,2},{4,7},{5,4},{6,5},{7,6},{8,11},{9,8},{10,9... | collective-permute-start | bytes 983048 | tf_op jit(solution)/shard_map/ppermute | solution.py:816
  403.6 18.8 %copy-start.4 = (bf16[256,640]{1,0:T(8,128)(2,1)}, bf16[256,640]{1,0:T(8,128)(2,1)S(1)}, u32[]{:S(2)}) copy-start(bf16[256,640]{1,0:T(8,128)(2,1)S(1)} %collective-permute-done.17.r1_ref) | copy-start | bytes 983044
  403.6 18.8 %copy-start.5 = (bf16[256,640]{1,0:T(8,128)(2,1)}, bf16[256,640]{1,0:T(8,128)(2,1)S(1)}, u32[]{:S(2)}) copy-start(bf16[256,640]{1,0:T(8,128)(2,1)S(1)} %collective-permute-done.18.r2_ref) | copy-start | bytes 983044
  404.2 18.2 %copy-start.6 = (bf16[256,640]{1,0:T(8,128)(2,1)}, bf16[256,640]{1,0:T(8,128)(2,1)S(1)}, u32[]{:S(2)}) copy-start(bf16[256,640]{1,0:T(8,128)(2,1)S(1)} %collective-permute-done.19.r3_ref) | copy-start | bytes 983044
  405.5 13.1 %collective-permute-start.20 = (bf16[256,512]{1,0:T(8,128)(2,1)S(1)}, bf16[256,512]{1,0:T(8,128)(2,1)}, u32[]{:S(2)}, u32[]{:S(2)}) collective-permute-start(bf16[256,512]{1,0:T(8,128)(2,1)S(1)} %add_convert_fusion.1.a0_ref), channel_id=1, source_target_pairs={{0,3},{1,0},{2,1},{3,2},{4,7},{5,4},{6,5},{7,6},{8,11},{9,8},{10,9... | collective-permute-start | bytes 786440 | tf_op jit(solution)/shard_map/ppermute | solution.py:816
  407.7 10.9 %collective-permute-start.21 = (bf16[256,512]{1,0:T(8,128)(2,1)S(1)}, bf16[256,512]{1,0:T(8,128)(2,1)}, u32[]{:S(2)}, u32[]{:S(2)}) collective-permute-start(bf16[256,512]{1,0:T(8,128)(2,1)S(1)} %add_convert_fusion.1.a0_ref), channel_id=1, source_target_pairs={{0,2},{1,3},{2,0},{3,1},{4,6},{5,7},{6,4},{7,5},{8,10},{9,11},{10,... | collective-permute-start | bytes 786440 | tf_op jit(solution)/shard_map/ppermute | solution.py:816
  407.9 14.5 %collective-permute-start.22 = (bf16[256,512]{1,0:T(8,128)(2,1)S(1)}, bf16[256,512]{1,0:T(8,128)(2,1)}, u32[]{:S(2)}, u32[]{:S(2)}) collective-permute-start(bf16[256,512]{1,0:T(8,128)(2,1)S(1)} %add_convert_fusion.1.a0_ref), channel_id=1, source_target_pairs={{0,1},{1,2},{2,3},{3,0},{4,5},{5,6},{6,7},{7,4},{8,9},{9,10},{10,1... | collective-permute-start | bytes 786440 | tf_op jit(solution)/shard_map/ppermute | solution.py:816
  441.7 8.3 %collective-permute-start.23 = (bf16[16,64,2304]{2,1,0:T(8,128)(2,1)}, bf16[16,64,2304]{2,1,0:T(8,128)(2,1)}, u32[]{:S(2)}, u32[]{:S(2)}) collective-permute-start(bf16[16,64,2304]{2,1,0:T(8,128)(2,1)} %get-tuple-element.167), channel_id=1, source_target_pairs={{0,4},{4,0},{8,12},{12,8},{16,20},{20,16},{24,28},{28,24},{32,36},... | collective-permute-start | bytes 14155784 | tf_op jit(solution)/shard_map/ppermute | solution.py:1131
  456.5 46.2 %all-to-all-start.5 = ((bf16[4,256,1152]{2,1,0:T(8,128)(2,1)}), bf16[4,256,1152]{2,1,0:T(8,128)(2,1)S(1)}, u32[]{:S(2)}, u32[]{:S(2)}) async-start(bf16[4,256,1152]{2,1,0:T(8,128)(2,1)} %bitcast.39), calls=%async_computation.8 | async-start | bytes 4718592 | tf_op jit(solution)/shard_map/all_to_all | solution.py:1158
  461.0 15.1 %collective-permute-start.36 = (bf16[256,512]{1,0:T(8,128)(2,1)}, bf16[256,512]{1,0:T(8,128)(2,1)S(1)}, u32[]{:S(2)}, u32[]{:S(2)}) collective-permute-start(bf16[256,512]{1,0:T(8,128)(2,1)} %get-tuple-element.189), channel_id=1, source_target_pairs={{0,1},{1,2},{2,3},{3,0},{4,5},{5,6},{6,7},{7,4},{8,9},{9,10},{10,1... | collective-permute-start | bytes 786440 | tf_op jit(solution)/shard_map/ppermute | solution.py:816
  461.0 17.9 %collective-permute-start.37 = (bf16[256,512]{1,0:T(8,128)(2,1)S(1)}, bf16[256,512]{1,0:T(8,128)(2,1)S(1)}, u32[]{:S(2)}, u32[]{:S(2)}) collective-permute-start(bf16[256,512]{1,0:T(8,128)(2,1)S(1)} %copy-done.39), channel_id=1, source_target_pairs={{0,2},{1,3},{2,0},{3,1},{4,6},{5,7},{6,4},{7,5},{8,10},{9,11},{10,... | collective-permute-start | bytes 786440 | tf_op jit(solution)/shard_map/ppermute | solution.py:816
  462.5 16.4 %collective-permute-start.38 = (bf16[256,512]{1,0:T(8,128)(2,1)S(1)}, bf16[256,512]{1,0:T(8,128)(2,1)S(1)}, u32[]{:S(2)}, u32[]{:S(2)}) collective-permute-start(bf16[256,512]{1,0:T(8,128)(2,1)S(1)} %copy-done.38), channel_id=1, source_target_pairs={{0,3},{1,0},{2,1},{3,2},{4,7},{5,4},{6,5},{7,6},{8,11},{9,8},{10,9... | collective-permute-start | bytes 786440 | tf_op jit(solution)/shard_map/ppermute | solution.py:816
  464.3 17.1 %collective-permute-start.24 = (bf16[4,64,1152]{2,1,0:T(8,128)(2,1)}, bf16[4,64,1152]{2,1,0:T(8,128)(2,1)S(1)}, u32[]{:S(2)}, u32[]{:S(2)}) collective-permute-start(bf16[4,64,1152]{2,1,0:T(8,128)(2,1)} %get-tuple-element.169), channel_id=1, source_target_pairs={{0,32},{4,36},{8,40},{12,44},{16,48},{20,52},{24,56},{28,60},{32,6... | collective-permute-start | bytes 1769480 | tf_op jit(solution)/shard_map/ppermute | solution.py:1147
  465.9 28.6 %collective-permute-start.25 = (bf16[4,64,1152]{2,1,0:T(8,128)(2,1)}, bf16[4,64,1152]{2,1,0:T(8,128)(2,1)}, u32[]{:S(2)}, u32[]{:S(2)}) collective-permute-start(bf16[4,64,1152]{2,1,0:T(8,128)(2,1)} %get-tuple-element.170), channel_id=1, source_target_pairs={{0,64},{4,68},{8,72},{12,76},{16,80},{20,84},{24,88},{28,92},{32,9... | collective-permute-start | bytes 1769480 | tf_op jit(solution)/shard_map/ppermute | solution.py:1147
  476.1 18.4 %collective-permute-start.26 = (bf16[4,64,1152]{2,1,0:T(8,128)(2,1)}, bf16[4,64,1152]{2,1,0:T(8,128)(2,1)}, u32[]{:S(2)}, u32[]{:S(2)}) collective-permute-start(bf16[4,64,1152]{2,1,0:T(8,128)(2,1)} %get-tuple-element.171), channel_id=1, source_target_pairs={{0,96},{4,100},{8,104},{12,108},{16,112},{20,116},{24,120},{28,124... | collective-permute-start | bytes 1769480 | tf_op jit(solution)/shard_map/ppermute | solution.py:1147
  480.0 41.9 %copy-start.8 = (bf16[256,512]{1,0:T(8,128)(2,1)}, bf16[256,512]{1,0:T(8,128)(2,1)S(1)}, u32[]{:S(2)}) copy-start(bf16[256,512]{1,0:T(8,128)(2,1)S(1)} %add_convert_fusion.a0_ref) | copy-start | bytes 786436
  480.0 28.6 %collective-permute-start.39 = (bf16[256,512]{1,0:T(8,128)(2,1)S(1)}, bf16[256,512]{1,0:T(8,128)(2,1)S(1)}, u32[]{:S(2)}, u32[]{:S(2)}) collective-permute-start(bf16[256,512]{1,0:T(8,128)(2,1)S(1)} %add_convert_fusion.a0_ref), channel_id=1, source_target_pairs={{0,3},{1,0},{2,1},{3,2},{4,7},{5,4},{6,5},{7,6},{8,11},{9,8},{10,9... | collective-permute-start | bytes 786440 | tf_op jit(solution)/shard_map/ppermute | solution.py:816
  497.1 13.4 %collective-permute-start.27 = (bf16[64,1152]{1,0:T(8,128)(2,1)}, bf16[64,1152]{1,0:T(8,128)(2,1)S(1)}, u32[]{:S(2)}, u32[]{:S(2)}) collective-permute-start(bf16[64,1152]{1,0:T(8,128)(2,1)} %get-tuple-element.176), channel_id=1, source_target_pairs={{0,8},{4,12},{8,16},{12,20},{16,24},{20,28},{24,0},{28,4},{32,40},... | collective-permute-start | bytes 442376 | tf_op jit(solution)/shard_map/ppermute | solution.py:1147
  498.7 16.9 %collective-permute-start.28 = (bf16[64,1152]{1,0:T(8,128)(2,1)}, bf16[64,1152]{1,0:T(8,128)(2,1)S(1)}, u32[]{:S(2)}, u32[]{:S(2)}) collective-permute-start(bf16[64,1152]{1,0:T(8,128)(2,1)} %get-tuple-element.177), channel_id=1, source_target_pairs={{0,16},{4,20},{8,24},{12,28},{16,0},{20,4},{24,8},{28,12},{32,48},... | collective-permute-start | bytes 442376 | tf_op jit(solution)/shard_map/ppermute | solution.py:1147
  501.4 15.2 %collective-permute-start.29 = (bf16[64,1152]{1,0:T(8,128)(2,1)}, bf16[64,1152]{1,0:T(8,128)(2,1)S(1)}, u32[]{:S(2)}, u32[]{:S(2)}) collective-permute-start(bf16[64,1152]{1,0:T(8,128)(2,1)} %get-tuple-element.178), channel_id=1, source_target_pairs={{0,24},{4,28},{8,0},{12,4},{16,8},{20,12},{24,16},{28,20},{32,56},... | collective-permute-start | bytes 442376 | tf_op jit(solution)/shard_map/ppermute | solution.py:1147
  506.7 11.8 %collective-permute-start.30 = (bf16[64,1152]{1,0:T(8,128)(2,1)}, bf16[64,1152]{1,0:T(8,128)(2,1)S(1)}, u32[]{:S(2)}, u32[]{:S(2)}) collective-permute-start(bf16[64,1152]{1,0:T(8,128)(2,1)} %get-tuple-element.181), channel_id=1, source_target_pairs={{0,32},{4,36},{8,40},{12,44},{16,48},{20,52},{24,56},{28,60},{32,6... | collective-permute-start | bytes 442376 | tf_op jit(solution)/shard_map/ppermute | solution.py:1147
  508.7 11.0 %collective-permute-start.31 = (bf16[64,1152]{1,0:T(8,128)(2,1)}, bf16[64,1152]{1,0:T(8,128)(2,1)S(1)}, u32[]{:S(2)}, u32[]{:S(2)}) collective-permute-start(bf16[64,1152]{1,0:T(8,128)(2,1)} %get-tuple-element.182), channel_id=1, source_target_pairs={{0,64},{4,68},{8,72},{12,76},{16,80},{20,84},{24,88},{28,92},{32,9... | collective-permute-start | bytes 442376 | tf_op jit(solution)/shard_map/ppermute | solution.py:1147
  510.6 11.3 %collective-permute-start.32 = (bf16[64,1152]{1,0:T(8,128)(2,1)}, bf16[64,1152]{1,0:T(8,128)(2,1)S(1)}, u32[]{:S(2)}, u32[]{:S(2)}) collective-permute-start(bf16[64,1152]{1,0:T(8,128)(2,1)} %get-tuple-element.183), channel_id=1, source_target_pairs={{0,96},{4,100},{8,104},{12,108},{16,112},{20,116},{24,120},{28,124... | collective-permute-start | bytes 442376 | tf_op jit(solution)/shard_map/ppermute | solution.py:1147
  515.6 12.2 %collective-permute-start.33 = (bf16[256,512]{1,0:T(8,128)(2,1)}, bf16[256,512]{1,0:T(8,128)(2,1)S(1)}, u32[]{:S(2)}, u32[]{:S(2)}) collective-permute-start(bf16[256,512]{1,0:T(8,128)(2,1)} %routed.1.a0_ref), channel_id=1, source_target_pairs={{0,3},{1,0},{2,1},{3,2},{4,7},{5,4},{6,5},{7,6},{8,11},{9,8},{10,9... | collective-permute-start | bytes 786440 | tf_op jit(solution)/shard_map/ppermute | solution.py:816
  516.6 11.9 %collective-permute-start.34 = (bf16[256,512]{1,0:T(8,128)(2,1)}, bf16[256,512]{1,0:T(8,128)(2,1)S(1)}, u32[]{:S(2)}, u32[]{:S(2)}) collective-permute-start(bf16[256,512]{1,0:T(8,128)(2,1)} %routed.1.a0_ref), channel_id=1, source_target_pairs={{0,2},{1,3},{2,0},{3,1},{4,6},{5,7},{6,4},{7,5},{8,10},{9,11},{10,... | collective-permute-start | bytes 786440 | tf_op jit(solution)/shard_map/ppermute | solution.py:816
  518.6 16.3 %collective-permute-start.35 = (bf16[256,512]{1,0:T(8,128)(2,1)}, bf16[256,512]{1,0:T(8,128)(2,1)S(1)}, u32[]{:S(2)}, u32[]{:S(2)}) collective-permute-start(bf16[256,512]{1,0:T(8,128)(2,1)} %routed.1.a0_ref), channel_id=1, source_target_pairs={{0,1},{1,2},{2,3},{3,0},{4,5},{5,6},{6,7},{7,4},{8,9},{9,10},{10,1... | collective-permute-start | bytes 786440 | tf_op jit(solution)/shard_map/ppermute | solution.py:816
  519.7 19.7 %collective-permute-start.40 = (bf16[256,512]{1,0:T(8,128)(2,1)S(1)}, bf16[256,512]{1,0:T(8,128)(2,1)S(1)}, u32[]{:S(2)}, u32[]{:S(2)}) collective-permute-start(bf16[256,512]{1,0:T(8,128)(2,1)S(1)} %add_convert_fusion.a0_ref), channel_id=1, source_target_pairs={{0,2},{1,3},{2,0},{3,1},{4,6},{5,7},{6,4},{7,5},{8,10},{9,11},{10,... | collective-permute-start | bytes 786440 | tf_op jit(solution)/shard_map/ppermute | solution.py:816
  521.9 21.1 %collective-permute-start.41 = (bf16[256,512]{1,0:T(8,128)(2,1)S(1)}, bf16[256,512]{1,0:T(8,128)(2,1)S(1)}, u32[]{:S(2)}, u32[]{:S(2)}) collective-permute-start(bf16[256,512]{1,0:T(8,128)(2,1)S(1)} %add_convert_fusion.a0_ref), channel_id=1, source_target_pairs={{0,1},{1,2},{2,3},{3,0},{4,5},{5,6},{6,7},{7,4},{8,9},{9,10},{10,1... | collective-permute-start | bytes 786440 | tf_op jit(solution)/shard_map/ppermute | solution.py:816
  527.9 20.8 %collective-permute-start.42 = (bf16[64,640]{1,0:T(8,128)(2,1)S(1)}, bf16[64,640]{1,0:T(8,128)(2,1)S(1)}, u32[]{:S(2)}, u32[]{:S(2)}) collective-permute-start(bf16[64,640]{1,0:T(8,128)(2,1)S(1)} %convert_element_type.87), channel_id=1, source_target_pairs={{0,1},{1,2},{2,3},{3,0},{4,5},{5,6},{6,7},{7,4},{8,9},{9,10},{10,1... | collective-permute-start | bytes 245768 | tf_op jit(solution)/shard_map/ppermute | solution.py:816
  528.5 20.2 %collective-permute-start.43 = (bf16[64,640]{1,0:T(8,128)(2,1)S(1)}, bf16[64,640]{1,0:T(8,128)(2,1)S(1)}, u32[]{:S(2)}, u32[]{:S(2)}) collective-permute-start(bf16[64,640]{1,0:T(8,128)(2,1)S(1)} %convert_element_type.87), channel_id=1, source_target_pairs={{0,2},{1,3},{2,0},{3,1},{4,6},{5,7},{6,4},{7,5},{8,10},{9,11},{10,... | collective-permute-start | bytes 245768 | tf_op jit(solution)/shard_map/ppermute | solution.py:816
  534.9 13.8 %collective-permute-start.44 = (bf16[64,640]{1,0:T(8,128)(2,1)S(1)}, bf16[64,640]{1,0:T(8,128)(2,1)S(1)}, u32[]{:S(2)}, u32[]{:S(2)}) collective-permute-start(bf16[64,640]{1,0:T(8,128)(2,1)S(1)} %convert_element_type.87), channel_id=1, source_target_pairs={{0,3},{1,0},{2,1},{3,2},{4,7},{5,4},{6,5},{7,6},{8,11},{9,8},{10,9... | collective-permute-start | bytes 245768 | tf_op jit(solution)/shard_map/ppermute | solution.py:816
  (31 other events, 183.0 us)
Sparse Core Ops, SparseCore 0:
  10.8 76.0 all-gather.2
  89.2 53.7 all-gather.4
  239.1 50.0 reduce-scatter.3
  291.6 60.6 reduce-scatter.5
  377.0 93.5 reduce-scatter.7

commit v7 on v6

--- a/solution.py
+++ b/solution.py
@@ -1164,22 +1164,43 @@
         axis_index_groups=[[(x * side + z) * 2 + c for z in range(side)] for x in range(side) for c in range(2)],
     ).reshape(along_z.shape)
     came_x = [along_x[0]] + [along(0, along_x[step], step) for step in range(1, side)]
+    got = send_blocks([send1, send2, send3])
+    first_sum = (own + got[0].astype(F32) + got[1].astype(F32) + got[2].astype(F32)).astype(BF16)
+    streams = share_small(first_sum)
+    (branch,) = run(
+        routed_kernel,
+        [((tokens, piece), BF16)],
+        [t0, t1, out_rows, shared_own, *shared_got],
+        4 * tokens * rows * piece,
+        name="routed",
+    )
+    at_last = after(at, branch, *streams[1:])
     parts = []
     for group, came in enumerate((came_x, [came_z])):
         crossed = run(
             functools.partial(cross_kernel, group),
             [((shard, widths[group]), F32)] + [((shard, widths[group]), BF16)] * (side - 1),
-            [at, *came],
+            [at_last, *came],
             0,
             places=smem,
             name="cross",
         )
         parts += [crossed[0]] + [along(1 - group, crossed[step], step) for step in range(1, side)]
+    (stream_grad,) = run(
+        stream_kernel,
+        [((tokens, width), F32)],
+        [after(me, parts[0], parts[4]), middle_grad, stream, gain_rows, *streams],
+        0,
+        scratch=[pltpu.VMEM((tokens, width), F32)],
+        places=smem,
+        name="stream",
+    )
+
     shared_sum = shared_sum.astype(F32)
     gate_sum = shared_sum[:, :hidden_columns]
     up_sum = shared_sum[:, hidden_columns : 2 * hidden_columns]
     down_sum = shared_sum[:, 2 * hidden_columns :]
-    parts[0] = after(parts[0], gate_sum, up_sum, down_sum)
+    parts[0] = after(parts[0], stream_grad, gate_sum, up_sum, down_sum)
     query_grad, late, output_grad, latent_up_grad, router_grad = run(
         unpack_kernel,
         [
@@ -1193,25 +1214,6 @@
         0,
         scratch=[pltpu.VMEM((shard, columns), F32)],
         name="unpack",
-    )
-    got = send_blocks([send1, send2, send3])
-    first_sum = (own + got[0].astype(F32) + got[1].astype(F32) + got[2].astype(F32)).astype(BF16)
-    (stream_grad,) = run(
-        stream_kernel,
-        [((tokens, width), F32)],
-        [after(me, late), middle_grad, stream, gain_rows, *share_small(first_sum)],
-        0,
-        scratch=[pltpu.VMEM((tokens, width), F32)],
-        places=smem,
-        name="stream",
-    )
-
-    (branch,) = run(
-        routed_kernel,
-        [((tokens, piece), BF16)],
-        [t0, t1, out_rows, shared_own, *shared_got],
-        4 * tokens * rows * piece,
-        name="routed",
     )
     (result,) = run(
         result_kernel,

time: 570 us -> 568 us (level)
    ppermute x9, waiting for transfers between devices: 14.4 us -> 2.22 us  [along(): lax.ppermute(array, 'expert', [(i, target(i)) for i in range(owners)])]
    ppermute x35, waiting for transfers between devices: 103 us -> 110 us  [shift(): lax.ppermute(array, 'tensor', [(i, (i + step) % size) for i in range(size)])]
where the time goes in v7:
time: 568 us; the launch traced here: 560 us
  waiting for transfers between devices  208 us (37%)
  Pallas kernels  162 us (29%)
  starting transfers between devices  98.2 us (17%)
  blocking collectives  40.2 us (7%)
  local copies, waits for them, and re-layouts  28 us (5%)
  between operations  14.8 us (3%)
  other arithmetic  8.38 us (1%)
    ppermute x35, waiting for transfers between devices, shift(): lax.ppermute(array, 'tensor', [(i, (i + step) % size) for i in range(size)])  110 us
    pallas_call x16, Pallas kernels, run(): pl.pallas_call(kernel, in_specs=in_specs, out_specs=out_specs, out_shape=...  99.5 us
    all_to_all x4, waiting for transfers between devices, exchange(): lax.all_to_all(rows.reshape(shape[0], -1, shape[-1]), 'expert', split_axi...  55.5 us
    ppermute x35, starting transfers between devices, shift(): lax.ppermute(array, 'tensor', [(i, (i + step) % size) for i in range(size)])  44 us
    all_to_all x1, blocking collectives, exchange(): lax.all_to_all(rows.reshape(shape[0], -1, shape[-1]), 'expert', split_axi...  40.2 us
    pallas_call x2, Pallas kernels, expert_back(): pl.pallas_call(functools.partial(expert_back_kernel, split), grid=(owners...  32.9 us
    all_to_all x4, starting transfers between devices, exchange(): lax.all_to_all(rows.reshape(shape[0], -1, shape[-1]), 'expert', split_axi...  26.9 us
    all_gather x1, waiting for transfers between devices, per_device(): one = lax.all_gather(pack_one, 'expert', axis=0, tiled=True)  23.7 us
  transfers between devices with their start and end apart: 55, of which 25 were waited for; matrix products, arithmetic and copies ran while one was open for 4% of the time, Pallas kernels for 27%

profile of v7, /device:TPU:0, one launch (start us, length us, event | category | flops | bytes accessed | tf_op | source)
XLA Modules:
  0.0 559.7 jit_solution(2151433921868632821)
XLA Ops:
  8.4 1.8 pack.1
  10.3 1.9 concatenate.16
  12.2 4.8 routing.1
  17.0 40.2 %all_to_all.30 = bf16[32,64,512]{2,1,0:T(8,128)(2,1)S(1)} all-to-all(bf16[32,64,512]{2,1,0:T(8,128)(2,1)} %bitcast.44), channel_id=1, replica_groups=mesh['expert'=32,'tensor'=4] {'expert'}, dimensions={0} | all-to-all | bytes 4194304 | tf_op jit(solution)/shard_map/all_to_all | solution.py:844
  63.2 23.7 %all-gather.3.cloned.1.call-done.w_ref.refs_10_.refs_13_.w_in = bf16[2048,2240]{1,0:T(8,128)(2,1)} async-done(((bf16[64,2240]{1,0:T(8,128)(2,1)}), bf16[2048,2240]{1,0:T(8,128)(2,1)}) %all-gather.3.cloned.1.call-update) | async-done | bytes 9175056 | tf_op jit(solution)/shard_map/all_gather | solution.py:907
  87.0 11.0 %attend.1 = (f32[256,512]{1,0:T(8,128)}, bf16[256,512]{1,0:T(8,128)(2,1)}, bf16[256,512]{1,0:T(8,128)(2,1)}, bf16[256,512]{1,0:T(8,128)(2,1)}, bf16[256,2048]{1,...) custom-call(s32[1]{0:T(128)} %bitcast.me_ref.refs_0_, ...), custom_call_target="tpu_custom_call" | custom-call | flops 201326592 | bytes 1627136 | tf_op jit(solution)/shard_map/attend/pallas_call | solution.py:81
  99.6 2.7 collective-permute-start.1
  103.7 7.7 %collective-permute-done = bf16[256,512]{1,0:T(8,128)(2,1)S(1)} collective-permute-done((bf16[256,512]{1,0:T(8,128)(2,1)}, bf16[256,512]{1,0:T(8,128)(2,1)S(1)}, u32[]{:S(2)}, u32[]{:S(2)}) %collective-permute-start) | collective-permute-done | bytes 262176 | tf_op jit(solution)/shard_map/ppermute | solution.py:816
  111.4 6.8 %collective-permute-done.1 = bf16[256,512]{1,0:T(8,128)(2,1)S(1)} collective-permute-done((bf16[256,512]{1,0:T(8,128)(2,1)}, bf16[256,512]{1,0:T(8,128)(2,1)S(1)}, u32[]{:S(2)}, u32[]{:S(2)}) %collective-permute-start.1) | collective-permute-done | bytes 262176 | tf_op jit(solution)/shard_map/ppermute | solution.py:816
  119.4 1.8 collective-permute-start.5
  122.9 5.8 %collective-permute-done.5.a1_ref = bf16[256,512]{1,0:T(8,128)(2,1)S(1)} collective-permute-done((bf16[256,512]{1,0:T(8,128)(2,1)S(1)}, bf16[256,512]{1,0:T(8,128)(2,1)S(1)}, u32[]{:S(2)}, u32[]{:S(2)}) %collective-permute-start.5) | collective-permute-done | bytes 262176 | tf_op jit(solution)/shard_map/ppermute | solution.py:816
  128.7 3.3 collective-permute-done.6.a2_ref
  132.0 3.0 collective-permute-done.7.a3_ref
  135.7 6.7 %dispatch.1 = (f32[256,2048]{1,0:T(8,128)}, bf16[256,2048]{1,0:T(8,128)(2,1)}, bf16[32,32,2560]{2,1,0:T(8,128)(2,1)}) custom-call(s32[1]{0:T(128)} %bitcast.me_ref.refs_0_, bf16[256,2048]{1,0:T(8,128)(2,1)} %stream_ref.7, bf16[256,512]{1,0:T(8,128)(2,1)} %copy-done.9, bf16[256,512]{1,0:T(8,128)(2,1)} %copy-done.20, bf16[256,512]{1,0:T(8,128)(2,1)} %copy-done.21, ...), custom_call_target="tpu_custom_call" | custom-call | flops 134217728 | bytes 1159987 | tf_op jit(solution)/shard_map/dispatch/pallas_call | solution.py:81
  142.4 4.9 all-to-all-start.1
  147.3 2.3 slice.61
  150.9 3.3 collective-permute-start.9
  154.2 22.0 %collective-permute-done.8 = bf16[16,2,32,512]{3,2,1,0:T(8,128)(2,1)S(1)} collective-permute-done((bf16[16,2,32,512]{3,2,1,0:T(8,128)(2,1)}, bf16[16,2,32,512]{3,2,1,0:T(8,128)(2,1)S(1)}, u32[]{:S(2)}, u32[]{:S(2)}) %collective-permute-start.8) | collective-permute-done | bytes 1048608 | tf_op jit(solution)/shard_map/ppermute | solution.py:816
  178.1 1.9 slice.60.router_ref
  179.9 16.6 %shared.1 = (f32[256,512]{1,0:T(8,128)}, bf16[256,512]{1,0:T(8,128)(2,1)}, bf16[256,512]{1,0:T(8,128)(2,1)}, bf16[256,512]{1,0:T(8,128)(2,1)}, f32[256,2048]{1,0...) custom-call(s32[1]{0:T(128)} %bitcast.me_ref.refs_0_, bf16[256,2048]{1,0:T(8,128)(2,1)} %get-tuple-element.122.mixed_ref, ...), custom_call_target="tpu_custom_call" | custom-call | flops 664377728 | bytes 2346189 | tf_op jit(solution)/shard_map/shared/pallas_call | solution.py:81
  196.5 15.8 %all-to-all-done.1.refs_2_.x0_ref = bf16[32,32,2560]{2,1,0:T(8,128)(2,1)} async-done(((bf16[32,32,2560]{2,1,0:T(8,128)(2,1)}), bf16[32,32,2560]{2,1,0:T(8,128)(2,1)}, u32[]{:S(2)}, u32[]{:S(2)}) %all-to-all-start.1) | async-done | bytes 5242912 | tf_op jit(solution)/shard_map/all_to_all | solution.py:844
  213.7 3.6 collective-permute-start.10
  217.3 16.3 %expert_back.2 = (bf16[32,32,2176]{2,1,0:T(8,128)(2,1)}, bf16[32,32,2048]{2,1,0:T(8,128)(2,1)}, bf16[1024,352]{1,0:T(8,128)(2,1)}, bf16[1024,352]{1,0:T(8,128)(2,1)}, bf16[1024,352]{1,0:T(8,128)(2,1)}) custom-call(s32[1]{0:T(128)} %bitcast.me_ref.refs_0_, s32[1]{0:T(128)} %bitcast.4.refs_1_, bf16[32,32,2560]{2,1,0:T(8,128)(2,1)} %all-to-all-done.1.refs_2_.x0_ref, ...), custom_call_target="tpu_custom_call" | custom-call | flops 73819750400 | bytes 25165824 | tf_op jit(solution)/shard_map/expert_back/pallas_call | solution.py:390
  233.6 5.4 expert_out.2
  241.1 3.1 collective-permute-start.13
  244.3 8.4 %all-to-all-start.2 = ((bf16[32,32,2176]{2,1,0:T(8,128)(2,1)}), bf16[32,32,2176]{2,1,0:T(8,128)(2,1)}, u32[]{:S(2)}, u32[]{:S(2)}) async-start(bf16[32,32,2176]{2,1,0:T(8,128)(2,1)} %get-tuple-element.133), calls=%async_computation.4 | async-start | bytes 8912896 | tf_op jit(solution)/shard_map/all_to_all | solution.py:844
  252.7 5.9 %collective-permute-done.12 = bf16[16,32,512]{2,1,0:T(8,128)(2,1)S(1)} collective-permute-done((bf16[16,32,512]{2,1,0:T(8,128)(2,1)S(1)}, bf16[16,32,512]{2,1,0:T(8,128)(2,1)S(1)}, u32[]{:S(2)}, u32[]{:S(2)}) %collective-permute-start.12) | collective-permute-done | bytes 524320 | tf_op jit(solution)/shard_map/ppermute | solution.py:816
  258.6 4.7 collective-permute-done.13
  264.3 16.6 %expert_back.3 = (bf16[32,32,2176]{2,1,0:T(8,128)(2,1)}, bf16[32,32,2048]{2,1,0:T(8,128)(2,1)}, bf16[1024,352]{1,0:T(8,128)(2,1)}, bf16[1024,352]{1,0:T(8,128)(2...) custom-call(s32[1]{0:T(128)} %bitcast.me_ref.refs_0_, s32[1]{0:T(128)} %bitcast.4.refs_1_, ...), custom_call_target="tpu_custom_call" | custom-call | flops 73819750400 | bytes 25165824 | tf_op jit(solution)/shard_map/expert_back/pallas_call | solution.py:390
  281.0 5.4 expert_out.3
  286.4 22.4 %all-to-all-done.2.b_ref = bf16[32,32,2176]{2,1,0:T(8,128)(2,1)} async-done(((bf16[32,32,2176]{2,1,0:T(8,128)(2,1)}), bf16[32,32,2176]{2,1,0:T(8,128)(2,1)}, u32[]{:S(2)}, u32[]{:S(2)}) %all-to-all-start.2) | async-done | bytes 4456480 | tf_op jit(solution)/shard_map/all_to_all | solution.py:844
  308.8 6.8 %all-to-all-start.3 = ((bf16[32,32,2176]{2,1,0:T(8,128)(2,1)}), bf16[32,32,2176]{2,1,0:T(8,128)(2,1)}, u32[]{:S(2)}, u32[]{:S(2)}) async-start(bf16[32,32,2176]{2,1,0:T(8,128)(2,1)} %get-tuple-element.147), calls=%async_computation.5 | async-start | bytes 8912896 | tf_op jit(solution)/shard_map/all_to_all | solution.py:844
  317.9 6.1 %combine_first.1 = (f32[256,2048]{1,0:T(8,128)}, f32[256,128]{1,0:T(8,128)}) custom-call(bf16[256,1024]{1,0:T(8,128)(2,1)} %get-tuple-element.110.t_ref.t0_ref, bf16[32,32,2176]{2,1,0:T(8,128)(2,1)} %all-to-all-done.2.b_ref, f32[256,2048]{1,0:T(8,128)} %get-tuple-element.124.shared_ref), custom_call_target="tpu_custom_call" | custom-call | flops 107374184 | bytes 930611 | tf_op jit(solution)/shard_map/combine_first/pallas_call | solution.py:81
  324.0 19.3 %expert_grads.1 = (f32[2,352,2048]{2,1,0:T(8,128)}, f32[2,352,2048]{2,1,0:T(8,128)}, f32[2,352,2048]{2,1,0:T(8,128)}) custom-call(bf16[32,32,2560]{2,1,0:T(8,128)(2,1)} %all-to-all-done.1.refs_2_.x0_ref, bf16[32,32,2048]{2,1,0:T(8,128)(2,1)} %get-tuple-element.131.c0_ref, bf16[1024,352]{1,0:T(8,128)(2,1)} %get-tuple-element.127.hg_ref.hg0_ref, ...), custom_call_target="tpu_custom_call" | custom-call | flops 738197504 | bytes 4177920 | tf_op jit(solution)/shard_map/expert_grads/pallas_call | solution.py:469
  343.4 9.0 %reduce-scatter.6.cloned.1.call-done = bf16[1,32,32,512]{3,2,1,0:T(8,128)(2,1)} async-done(((bf16[4,32,32,512]{3,2,1,0:T(8,128)(2,1)}), bf16[1,32,32,512]{3,2,1,0:T(8,128)(2,1)}) %reduce-scatter.6.cloned.1.call-update) | async-done | bytes 1048592 | tf_op jit(solution)/shard_map/reduce_scatter | solution.py:1038
  354.1 17.2 %all-to-all-done.3.b_ref = bf16[32,32,2176]{2,1,0:T(8,128)(2,1)} async-done(((bf16[32,32,2176]{2,1,0:T(8,128)(2,1)}), bf16[32,32,2176]{2,1,0:T(8,128)(2,1)}, u32[]{:S(2)}, u32[]{:S(2)}) %all-to-all-start.3) | async-done | bytes 4456480 | tf_op jit(solution)/shard_map/all_to_all | solution.py:844
  371.4 5.5 combine.1
  378.4 6.9 %all-to-all-start.4 = ((bf16[32,64,512]{2,1,0:T(8,128)(2,1)}), bf16[32,64,512]{2,1,0:T(8,128)(2,1)S(1)}, u32[]{:S(2)}, u32[]{:S(2)}) async-start(bf16[32,64,512]{2,1,0:T(8,128)(2,1)} %bitcast.38), calls=%async_computation.6 | async-start | bytes 4194304 | tf_op jit(solution)/shard_map/all_to_all | solution.py:844
  388.5 15.1 %collective-permute-done.17.r1_ref = bf16[256,640]{1,0:T(8,128)(2,1)S(1)} collective-permute-done((bf16[256,640]{1,0:T(8,128)(2,1)}, bf16[256,640]{1,0:T(8,128)(2,1)S(1)}, u32[]{:S(2)}, u32[]{:S(2)}) %collective-permute-start.17) | collective-permute-done | bytes 327712 | tf_op jit(solution)/shard_map/ppermute | solution.py:816
  405.5 2.2 collective-permute-start.20
  408.9 9.7 %collective-permute-done.20.a1_ref = bf16[256,512]{1,0:T(8,128)(2,1)} collective-permute-done((bf16[256,512]{1,0:T(8,128)(2,1)S(1)}, bf16[256,512]{1,0:T(8,128)(2,1)}, u32[]{:S(2)}, u32[]{:S(2)}) %collective-permute-start.20) | collective-permute-done | bytes 262176 | tf_op jit(solution)/shard_map/ppermute | solution.py:816
  418.7 3.8 collective-permute-done.22.a3_ref
  422.4 19.2 %attend_back.1 = (bf16[16,64,2304]{2,1,0:T(8,128)(2,1)}, bf16[16,64,2304]{2,1,0:T(8,128)(2,1)}, f32[256,2048]{1,0:T(8,128)}, f32[256,512]{1,0:T(8,128)}, bf16[25...) custom-call(s32[1]{0:T(128)} %bitcast.me_ref.refs_0_, s32[1]{0:T(128)} %bitcast.21.core_ref, ...), custom_call_target="tpu_custom_call" | custom-call | flops 845571712 | bytes 3586458 | tf_op jit(solution)/shard_map/attend_back/pallas_call | solution.py:81
  442.6 7.5 %collective-permute-done.29.got_ref = bf16[16,64,2304]{2,1,0:T(8,128)(2,1)} collective-permute-done((bf16[16,64,2304]{2,1,0:T(8,128)(2,1)}, bf16[16,64,2304]{2,1,0:T(8,128)(2,1)}, u32[]{:S(2)}, u32[]{:S(2)}) %collective-permute-start.29) | collective-permute-done | bytes 4718624 | tf_op jit(solution)/shard_map/ppermute | solution.py:1131
  450.1 6.4 %pair.1 = (bf16[4,4,64,1152]{3,2,1,0:T(8,128)(2,1)}, bf16[4,64,1152]{2,1,0:T(8,128)(2,1)}, bf16[4,64,1152]{2,1,0:T(8,128)(2,1)}, bf16[4,64,1152]{2,1,0:T(8,128)(2,1)}, bf16[4,64,1152]{2,1,0:T(8,128)(2,1)}) custom-call(s32[2]{0:T(128)} %pad_add_fusion.at_ref, bf16[16,64,2304]{2,1,0:T(8,128)(2,1)} %get-tuple-element.173.keep_ref, ...), custom_call_target="tpu_custom_call" | custom-call | bytes 1415578 | tf_op jit(solution)/shard_map/pair/pallas_call | solution.py:81
  456.5 4.5 all-to-all-start.5
  462.5 1.8 collective-permute-start.25
  466.0 2.8 collective-permute-start.31
  468.8 7.3 %collective-permute-done.23 = bf16[256,512]{1,0:T(8,128)(2,1)S(1)} collective-permute-done((bf16[256,512]{1,0:T(8,128)(2,1)}, bf16[256,512]{1,0:T(8,128)(2,1)S(1)}, u32[]{:S(2)}, u32[]{:S(2)}) %collective-permute-start.23) | collective-permute-done | bytes 262176 | tf_op jit(solution)/shard_map/ppermute | solution.py:816
  476.1 2.8 collective-permute-start.32
  480.2 9.1 %collective-permute-done.26.a1_ref = bf16[256,512]{1,0:T(8,128)(2,1)S(1)} collective-permute-done((bf16[256,512]{1,0:T(8,128)(2,1)S(1)}, bf16[256,512]{1,0:T(8,128)(2,1)S(1)}, u32[]{:S(2)}, u32[]{:S(2)}) %collective-permute-start.26) | collective-permute-done | bytes 262176 | tf_op jit(solution)/shard_map/ppermute | solution.py:816
  489.4 3.7 routed.1.a0_ref
  493.1 3.8 collective-permute-done.28.a3_ref
  497.8 2.6 cross.2
  502.2 2.7 collective-permute-start.34
  507.8 2.6 cross.3
  510.4 5.0 collective-permute-start.36
  517.2 5.0 stream.1
  523.1 3.2 collective-permute-start.37
  527.5 1.8 fusion.1
  532.2 2.3 unpack.1
  535.4 2.7 collective-permute-start.42
  539.4 2.3 collective-permute-start.44
  543.9 3.3 result.1
  (191 shorter events, 61.1 us)
Async XLA Ops:
  7.2 79.8 %all-gather.3.cloned.1.call-start = ((), (), s32[]{:S(2)}) async-start(), calls=%async_computation.9 | async-start | bytes 9732096 | tf_op jit(solution)/shard_map/all_gather | solution.py:907
  10.3 169.7 %all-gather.5.cloned.1.call-start = ((), (), s32[]{:S(2)}) async-start(), calls=%async_computation.10 | async-start | bytes 9191424 | tf_op jit(solution)/shard_map/all_gather | solution.py:908
  17.0 45.4 %copy-start.35 = (s32[1,256]{1,0:T(1,128)S(1)}, s32[1,256]{1,0:T(1,128)}, u32[]{:S(2)}) copy-start(s32[1,256]{1,0:T(1,128)} %seg_row_ref.1) | copy-start | bytes 3076
  57.2 40.8 %copy-start.2 = (bf16[32,64,512]{2,1,0:T(8,128)(2,1)}, bf16[32,64,512]{2,1,0:T(8,128)(2,1)S(1)}, u32[]{:S(2)}) copy-start(bf16[32,64,512]{2,1,0:T(8,128)(2,1)S(1)} %all_to_all.30) | copy-start | bytes 6291460
  57.2 62.2 %collective-permute-start.3 = (bf16[32,2,32,512]{3,2,1,0:T(8,128)(2,1)S(1)}, bf16[32,2,32,512]{3,2,1,0:T(8,128)(2,1)}, u32[]{:S(2)}, u32[]{:S(2)}) collective-permute-start(bf16[32,2,32,512]{3,2,1,0:T(8,128)(2,1)S(1)} %bitcast.40), channel_id=1, source_target_pairs={{0,1},{1,2},{2,3},{3,0},{4,5},{5,6},{6,7},{7,4},{8,9},{9,10},{10,1... | collective-permute-start | bytes 6291464 | tf_op jit(solution)/shard_map/ppermute | solution.py:816
  58.8 60.6 %collective-permute-start.4 = (bf16[32,2,32,512]{3,2,1,0:T(8,128)(2,1)S(1)}, bf16[32,2,32,512]{3,2,1,0:T(8,128)(2,1)}, u32[]{:S(2)}, u32[]{:S(2)}) collective-permute-start(bf16[32,2,32,512]{3,2,1,0:T(8,128)(2,1)S(1)} %bitcast.41), channel_id=1, source_target_pairs={{0,3},{1,0},{2,1},{3,2},{4,7},{5,4},{6,5},{7,6},{8,11},{9,8},{10,9... | collective-permute-start | bytes 6291464 | tf_op jit(solution)/shard_map/ppermute | solution.py:816
  98.0 13.4 %collective-permute-start = (bf16[256,512]{1,0:T(8,128)(2,1)}, bf16[256,512]{1,0:T(8,128)(2,1)S(1)}, u32[]{:S(2)}, u32[]{:S(2)}) collective-permute-start(bf16[256,512]{1,0:T(8,128)(2,1)} %get-tuple-element.115), channel_id=1, source_target_pairs={{0,1},{1,2},{2,3},{3,0},{4,5},{5,6},{6,7},{7,4},{8,9},{9,10},{10,1... | collective-permute-start | bytes 786440 | tf_op jit(solution)/shard_map/ppermute | solution.py:816
  99.6 18.6 %collective-permute-start.1 = (bf16[256,512]{1,0:T(8,128)(2,1)}, bf16[256,512]{1,0:T(8,128)(2,1)S(1)}, u32[]{:S(2)}, u32[]{:S(2)}) collective-permute-start(bf16[256,512]{1,0:T(8,128)(2,1)} %get-tuple-element.116), channel_id=1, source_target_pairs={{0,2},{1,3},{2,0},{3,1},{4,6},{5,7},{6,4},{7,5},{8,10},{9,11},{10,... | collective-permute-start | bytes 786440 | tf_op jit(solution)/shard_map/ppermute | solution.py:816
  102.3 15.9 %collective-permute-start.2 = (bf16[256,512]{1,0:T(8,128)(2,1)}, bf16[256,512]{1,0:T(8,128)(2,1)S(1)}, u32[]{:S(2)}, u32[]{:S(2)}) collective-permute-start(bf16[256,512]{1,0:T(8,128)(2,1)} %get-tuple-element.117), channel_id=1, source_target_pairs={{0,3},{1,0},{2,1},{3,2},{4,7},{5,4},{6,5},{7,6},{8,11},{9,8},{10,9... | collective-permute-start | bytes 786440 | tf_op jit(solution)/shard_map/ppermute | solution.py:816
  119.4 9.3 %collective-permute-start.5 = (bf16[256,512]{1,0:T(8,128)(2,1)S(1)}, bf16[256,512]{1,0:T(8,128)(2,1)S(1)}, u32[]{:S(2)}, u32[]{:S(2)}) collective-permute-start(bf16[256,512]{1,0:T(8,128)(2,1)S(1)} %add_convert_fusion.2.a0_ref), channel_id=1, source_target_pairs={{0,3},{1,0},{2,1},{3,2},{4,7},{5,4},{6,5},{7,6},{8,11},{9,8},{10,9... | collective-permute-start | bytes 786440 | tf_op jit(solution)/shard_map/ppermute | solution.py:816
  121.2 10.8 %collective-permute-start.6 = (bf16[256,512]{1,0:T(8,128)(2,1)S(1)}, bf16[256,512]{1,0:T(8,128)(2,1)S(1)}, u32[]{:S(2)}, u32[]{:S(2)}) collective-permute-start(bf16[256,512]{1,0:T(8,128)(2,1)S(1)} %add_convert_fusion.2.a0_ref), channel_id=1, source_target_pairs={{0,2},{1,3},{2,0},{3,1},{4,6},{5,7},{6,4},{7,5},{8,10},{9,11},{10,... | collective-permute-start | bytes 786440 | tf_op jit(solution)/shard_map/ppermute | solution.py:816
  122.1 12.9 %collective-permute-start.7 = (bf16[256,512]{1,0:T(8,128)(2,1)S(1)}, bf16[256,512]{1,0:T(8,128)(2,1)S(1)}, u32[]{:S(2)}, u32[]{:S(2)}) collective-permute-start(bf16[256,512]{1,0:T(8,128)(2,1)S(1)} %add_convert_fusion.2.a0_ref), channel_id=1, source_target_pairs={{0,1},{1,2},{2,3},{3,0},{4,5},{5,6},{6,7},{7,4},{8,9},{9,10},{10,1... | collective-permute-start | bytes 786440 | tf_op jit(solution)/shard_map/ppermute | solution.py:816
  142.4 69.9 %all-to-all-start.1 = ((bf16[32,32,2560]{2,1,0:T(8,128)(2,1)}), bf16[32,32,2560]{2,1,0:T(8,128)(2,1)}, u32[]{:S(2)}, u32[]{:S(2)}) async-start(bf16[32,32,2560]{2,1,0:T(8,128)(2,1)} %get-tuple-element.126), calls=%async_computation.1 | async-start | bytes 10485760 | tf_op jit(solution)/shard_map/all_to_all | solution.py:844
  147.3 196.1 %reduce-scatter.4.cloned.1.call-start = ((), (), s32[]{:S(2)}) async-start(), calls=%async_computation.11 | async-start | bytes 5242880 | tf_op jit(solution)/shard_map/reduce_scatter | solution.py:1038
  149.6 26.6 %collective-permute-start.8 = (bf16[16,2,32,512]{3,2,1,0:T(8,128)(2,1)}, bf16[16,2,32,512]{3,2,1,0:T(8,128)(2,1)S(1)}, u32[]{:S(2)}, u32[]{:S(2)}) collective-permute-start(bf16[16,2,32,512]{3,2,1,0:T(8,128)(2,1)} %slice.61), channel_id=1, source_target_pairs={{0,1},{1,2},{2,3},{3,0},{4,5},{5,6},{6,7},{7,4},{8,9},{9,10},{10,1... | collective-permute-start | bytes 3145736 | tf_op jit(solution)/shard_map/ppermute | solution.py:816
  150.9 25.7 %collective-permute-start.9 = (bf16[16,2,32,512]{3,2,1,0:T(8,128)(2,1)S(1)}, bf16[16,2,32,512]{3,2,1,0:T(8,128)(2,1)S(1)}, u32[]{:S(2)}, u32[]{:S(2)}) collective-permute-start(bf16[16,2,32,512]{3,2,1,0:T(8,128)(2,1)S(1)} %slice.62), channel_id=1, source_target_pairs={{0,3},{1,0},{2,1},{3,2},{4,7},{5,4},{6,5},{7,6},{8,11},{9,8},{10,9... | collective-permute-start | bytes 3145736 | tf_op jit(solution)/shard_map/ppermute | solution.py:816
  213.6 26.1 %collective-permute-start.11 = (bf16[32,32,512]{2,1,0:T(8,128)(2,1)S(1)}, bf16[32,32,512]{2,1,0:T(8,128)(2,1)S(1)}, u32[]{:S(2)}, u32[]{:S(2)}) collective-permute-start(bf16[32,32,512]{2,1,0:T(8,128)(2,1)S(1)} %slice.63), channel_id=1, source_target_pairs={{0,1},{1,2},{2,3},{3,0},{4,5},{5,6},{6,7},{7,4},{8,9},{9,10},{10,1... | collective-permute-start | bytes 3145736 | tf_op jit(solution)/shard_map/ppermute | solution.py:816
  213.7 26.1 %collective-permute-start.10 = (bf16[32,32,512]{2,1,0:T(8,128)(2,1)S(1)}, bf16[32,32,512]{2,1,0:T(8,128)(2,1)}, u32[]{:S(2)}, u32[]{:S(2)}) collective-permute-start(bf16[32,32,512]{2,1,0:T(8,128)(2,1)S(1)} %slice.63), channel_id=1, source_target_pairs={{0,3},{1,0},{2,1},{3,2},{4,7},{5,4},{6,5},{7,6},{8,11},{9,8},{10,9... | collective-permute-start | bytes 3145736 | tf_op jit(solution)/shard_map/ppermute | solution.py:816
  239.7 18.9 %collective-permute-start.12 = (bf16[16,32,512]{2,1,0:T(8,128)(2,1)S(1)}, bf16[16,32,512]{2,1,0:T(8,128)(2,1)S(1)}, u32[]{:S(2)}, u32[]{:S(2)}) collective-permute-start(bf16[16,32,512]{2,1,0:T(8,128)(2,1)S(1)} %slice.64), channel_id=1, source_target_pairs={{0,1},{1,2},{2,3},{3,0},{4,5},{5,6},{6,7},{7,4},{8,9},{9,10},{10,1... | collective-permute-start | bytes 1572872 | tf_op jit(solution)/shard_map/ppermute | solution.py:816
  241.1 22.1 %collective-permute-start.13 = (bf16[16,32,512]{2,1,0:T(8,128)(2,1)S(1)}, bf16[16,32,512]{2,1,0:T(8,128)(2,1)S(1)}, u32[]{:S(2)}, u32[]{:S(2)}) collective-permute-start(bf16[16,32,512]{2,1,0:T(8,128)(2,1)S(1)} %slice.65), channel_id=1, source_target_pairs={{0,3},{1,0},{2,1},{3,2},{4,7},{5,4},{6,5},{7,6},{8,11},{9,8},{10,9... | collective-permute-start | bytes 1572872 | tf_op jit(solution)/shard_map/ppermute | solution.py:816
  244.3 64.5 %all-to-all-start.2 = ((bf16[32,32,2176]{2,1,0:T(8,128)(2,1)}), bf16[32,32,2176]{2,1,0:T(8,128)(2,1)}, u32[]{:S(2)}, u32[]{:S(2)}) async-start(bf16[32,32,2176]{2,1,0:T(8,128)(2,1)} %get-tuple-element.133), calls=%async_computation.4 | async-start | bytes 8912896 | tf_op jit(solution)/shard_map/all_to_all | solution.py:844
  252.7 99.7 %reduce-scatter.6.cloned.1.call-start = ((), (), s32[]{:S(2)}) async-start(), calls=%async_computation.12 | async-start | bytes 5242880 | tf_op jit(solution)/shard_map/reduce_scatter | solution.py:1038
  308.8 62.6 %all-to-all-start.3 = ((bf16[32,32,2176]{2,1,0:T(8,128)(2,1)}), bf16[32,32,2176]{2,1,0:T(8,128)(2,1)}, u32[]{:S(2)}, u32[]{:S(2)}) async-start(bf16[32,32,2176]{2,1,0:T(8,128)(2,1)} %get-tuple-element.147), calls=%async_computation.5 | async-start | bytes 8912896 | tf_op jit(solution)/shard_map/all_to_all | solution.py:844
  315.5 212.0 %reduce-scatter.8.cloned.1.call-start = ((), (), s32[]{:S(2)}) async-start(), calls=%async_computation.13 | async-start | bytes 9191424 | tf_op jit(solution)/shard_map/reduce_scatter | solution.py:1067
  315.6 38.5 %collective-permute-start.15 = (bf16[256,512]{1,0:T(8,128)(2,1)}, bf16[256,512]{1,0:T(8,128)(2,1)S(1)}, u32[]{:S(2)}, u32[]{:S(2)}) collective-permute-start(bf16[256,512]{1,0:T(8,128)(2,1)} %get-tuple-element.143), channel_id=1, source_target_pairs={{0,2},{1,3},{2,0},{3,1},{4,6},{5,7},{6,4},{7,5},{8,10},{9,11},{10,... | collective-permute-start | bytes 786440 | tf_op jit(solution)/shard_map/ppermute | solution.py:816
  315.7 38.4 %collective-permute-start.16 = (bf16[256,512]{1,0:T(8,128)(2,1)S(1)}, bf16[256,512]{1,0:T(8,128)(2,1)S(1)}, u32[]{:S(2)}, u32[]{:S(2)}) collective-permute-start(bf16[256,512]{1,0:T(8,128)(2,1)S(1)} %copy-done.38), channel_id=1, source_target_pairs={{0,3},{1,0},{2,1},{3,2},{4,7},{5,4},{6,5},{7,6},{8,11},{9,8},{10,9... | collective-permute-start | bytes 786440 | tf_op jit(solution)/shard_map/ppermute | solution.py:816
  317.4 36.7 %collective-permute-start.14 = (bf16[256,512]{1,0:T(8,128)(2,1)S(1)}, bf16[256,512]{1,0:T(8,128)(2,1)S(1)}, u32[]{:S(2)}, u32[]{:S(2)}) collective-permute-start(bf16[256,512]{1,0:T(8,128)(2,1)S(1)} %copy-done.37), channel_id=1, source_target_pairs={{0,1},{1,2},{2,3},{3,0},{4,5},{5,6},{6,7},{7,4},{8,9},{9,10},{10,1... | collective-permute-start | bytes 786440 | tf_op jit(solution)/shard_map/ppermute | solution.py:816
  354.1 22.8 %copy-start.13 = (bf16[256,512]{1,0:T(8,128)(2,1)}, bf16[256,512]{1,0:T(8,128)(2,1)S(1)}, u32[]{:S(2)}) copy-start(bf16[256,512]{1,0:T(8,128)(2,1)S(1)} %collective-permute-done.15.r2_ref) | copy-start | bytes 786436
  354.1 22.8 %copy-start.14 = (bf16[256,512]{1,0:T(8,128)(2,1)}, bf16[256,512]{1,0:T(8,128)(2,1)S(1)}, u32[]{:S(2)}) copy-start(bf16[256,512]{1,0:T(8,128)(2,1)S(1)} %collective-permute-done.16.r3_ref) | copy-start | bytes 786436
  354.1 22.7 %copy-start.15 = (bf16[256,512]{1,0:T(8,128)(2,1)}, bf16[256,512]{1,0:T(8,128)(2,1)S(1)}, u32[]{:S(2)}) copy-start(bf16[256,512]{1,0:T(8,128)(2,1)S(1)} %collective-permute-done.14.r1_ref) | copy-start | bytes 786436
  378.4 63.4 %all-to-all-start.4 = ((bf16[32,64,512]{2,1,0:T(8,128)(2,1)}), bf16[32,64,512]{2,1,0:T(8,128)(2,1)S(1)}, u32[]{:S(2)}, u32[]{:S(2)}) async-start(bf16[32,64,512]{2,1,0:T(8,128)(2,1)} %bitcast.38), calls=%async_computation.6 | async-start | bytes 4194304 | tf_op jit(solution)/shard_map/all_to_all | solution.py:844
  385.2 18.4 %collective-permute-start.17 = (bf16[256,640]{1,0:T(8,128)(2,1)}, bf16[256,640]{1,0:T(8,128)(2,1)S(1)}, u32[]{:S(2)}, u32[]{:S(2)}) collective-permute-start(bf16[256,640]{1,0:T(8,128)(2,1)} %get-tuple-element.154), channel_id=1, source_target_pairs={{0,1},{1,2},{2,3},{3,0},{4,5},{5,6},{6,7},{7,4},{8,9},{9,10},{10,1... | collective-permute-start | bytes 983048 | tf_op jit(solution)/shard_map/ppermute | solution.py:816
  385.3 18.3 %collective-permute-start.18 = (bf16[256,640]{1,0:T(8,128)(2,1)}, bf16[256,640]{1,0:T(8,128)(2,1)S(1)}, u32[]{:S(2)}, u32[]{:S(2)}) collective-permute-start(bf16[256,640]{1,0:T(8,128)(2,1)} %get-tuple-element.155), channel_id=1, source_target_pairs={{0,2},{1,3},{2,0},{3,1},{4,6},{5,7},{6,4},{7,5},{8,10},{9,11},{10,... | collective-permute-start | bytes 983048 | tf_op jit(solution)/shard_map/ppermute | solution.py:816
  386.8 17.5 %collective-permute-start.19 = (bf16[256,640]{1,0:T(8,128)(2,1)S(1)}, bf16[256,640]{1,0:T(8,128)(2,1)S(1)}, u32[]{:S(2)}, u32[]{:S(2)}) collective-permute-start(bf16[256,640]{1,0:T(8,128)(2,1)S(1)} %copy-done.36), channel_id=1, source_target_pairs={{0,3},{1,0},{2,1},{3,2},{4,7},{5,4},{6,5},{7,6},{8,11},{9,8},{10,9... | collective-permute-start | bytes 983048 | tf_op jit(solution)/shard_map/ppermute | solution.py:816
  403.6 18.8 %copy-start.4 = (bf16[256,640]{1,0:T(8,128)(2,1)}, bf16[256,640]{1,0:T(8,128)(2,1)S(1)}, u32[]{:S(2)}) copy-start(bf16[256,640]{1,0:T(8,128)(2,1)S(1)} %collective-permute-done.17.r1_ref) | copy-start | bytes 983044
  403.6 18.8 %copy-start.5 = (bf16[256,640]{1,0:T(8,128)(2,1)}, bf16[256,640]{1,0:T(8,128)(2,1)S(1)}, u32[]{:S(2)}) copy-start(bf16[256,640]{1,0:T(8,128)(2,1)S(1)} %collective-permute-done.18.r2_ref) | copy-start | bytes 983044
  404.2 18.2 %copy-start.6 = (bf16[256,640]{1,0:T(8,128)(2,1)}, bf16[256,640]{1,0:T(8,128)(2,1)S(1)}, u32[]{:S(2)}) copy-start(bf16[256,640]{1,0:T(8,128)(2,1)S(1)} %collective-permute-done.19.r3_ref) | copy-start | bytes 983044
  405.5 13.1 %collective-permute-start.20 = (bf16[256,512]{1,0:T(8,128)(2,1)S(1)}, bf16[256,512]{1,0:T(8,128)(2,1)}, u32[]{:S(2)}, u32[]{:S(2)}) collective-permute-start(bf16[256,512]{1,0:T(8,128)(2,1)S(1)} %add_convert_fusion.1.a0_ref), channel_id=1, source_target_pairs={{0,3},{1,0},{2,1},{3,2},{4,7},{5,4},{6,5},{7,6},{8,11},{9,8},{10,9... | collective-permute-start | bytes 786440 | tf_op jit(solution)/shard_map/ppermute | solution.py:816
  407.8 10.9 %collective-permute-start.21 = (bf16[256,512]{1,0:T(8,128)(2,1)S(1)}, bf16[256,512]{1,0:T(8,128)(2,1)}, u32[]{:S(2)}, u32[]{:S(2)}) collective-permute-start(bf16[256,512]{1,0:T(8,128)(2,1)S(1)} %add_convert_fusion.1.a0_ref), channel_id=1, source_target_pairs={{0,2},{1,3},{2,0},{3,1},{4,6},{5,7},{6,4},{7,5},{8,10},{9,11},{10,... | collective-permute-start | bytes 786440 | tf_op jit(solution)/shard_map/ppermute | solution.py:816
  407.9 14.5 %collective-permute-start.22 = (bf16[256,512]{1,0:T(8,128)(2,1)S(1)}, bf16[256,512]{1,0:T(8,128)(2,1)}, u32[]{:S(2)}, u32[]{:S(2)}) collective-permute-start(bf16[256,512]{1,0:T(8,128)(2,1)S(1)} %add_convert_fusion.1.a0_ref), channel_id=1, source_target_pairs={{0,1},{1,2},{2,3},{3,0},{4,5},{5,6},{6,7},{7,4},{8,9},{9,10},{10,1... | collective-permute-start | bytes 786440 | tf_op jit(solution)/shard_map/ppermute | solution.py:816
  441.7 8.3 %collective-permute-start.29 = (bf16[16,64,2304]{2,1,0:T(8,128)(2,1)}, bf16[16,64,2304]{2,1,0:T(8,128)(2,1)}, u32[]{:S(2)}, u32[]{:S(2)}) collective-permute-start(bf16[16,64,2304]{2,1,0:T(8,128)(2,1)} %get-tuple-element.175), channel_id=1, source_target_pairs={{0,4},{4,0},{8,12},{12,8},{16,20},{20,16},{24,28},{28,24},{32,36},... | collective-permute-start | bytes 14155784 | tf_op jit(solution)/shard_map/ppermute | solution.py:1131
  456.5 49.9 %all-to-all-start.5 = ((bf16[4,256,1152]{2,1,0:T(8,128)(2,1)}), bf16[4,256,1152]{2,1,0:T(8,128)(2,1)S(1)}, u32[]{:S(2)}, u32[]{:S(2)}) async-start(bf16[4,256,1152]{2,1,0:T(8,128)(2,1)} %bitcast.39), calls=%async_computation.7 | async-start | bytes 4718592 | tf_op jit(solution)/shard_map/all_to_all | solution.py:1158
  460.9 15.1 %collective-permute-start.23 = (bf16[256,512]{1,0:T(8,128)(2,1)}, bf16[256,512]{1,0:T(8,128)(2,1)S(1)}, u32[]{:S(2)}, u32[]{:S(2)}) collective-permute-start(bf16[256,512]{1,0:T(8,128)(2,1)} %get-tuple-element.169), channel_id=1, source_target_pairs={{0,1},{1,2},{2,3},{3,0},{4,5},{5,6},{6,7},{7,4},{8,9},{9,10},{10,1... | collective-permute-start | bytes 786440 | tf_op jit(solution)/shard_map/ppermute | solution.py:816
  461.0 17.9 %collective-permute-start.24 = (bf16[256,512]{1,0:T(8,128)(2,1)S(1)}, bf16[256,512]{1,0:T(8,128)(2,1)S(1)}, u32[]{:S(2)}, u32[]{:S(2)}) collective-permute-start(bf16[256,512]{1,0:T(8,128)(2,1)S(1)} %copy-done.40), channel_id=1, source_target_pairs={{0,2},{1,3},{2,0},{3,1},{4,6},{5,7},{6,4},{7,5},{8,10},{9,11},{10,... | collective-permute-start | bytes 786440 | tf_op jit(solution)/shard_map/ppermute | solution.py:816
  462.5 16.4 %collective-permute-start.25 = (bf16[256,512]{1,0:T(8,128)(2,1)S(1)}, bf16[256,512]{1,0:T(8,128)(2,1)S(1)}, u32[]{:S(2)}, u32[]{:S(2)}) collective-permute-start(bf16[256,512]{1,0:T(8,128)(2,1)S(1)} %copy-done.39), channel_id=1, source_target_pairs={{0,3},{1,0},{2,1},{3,2},{4,7},{5,4},{6,5},{7,6},{8,11},{9,8},{10,9... | collective-permute-start | bytes 786440 | tf_op jit(solution)/shard_map/ppermute | solution.py:816
  464.3 32.7 %collective-permute-start.30 = (bf16[4,64,1152]{2,1,0:T(8,128)(2,1)}, bf16[4,64,1152]{2,1,0:T(8,128)(2,1)S(1)}, u32[]{:S(2)}, u32[]{:S(2)}) collective-permute-start(bf16[4,64,1152]{2,1,0:T(8,128)(2,1)} %get-tuple-element.177), channel_id=1, source_target_pairs={{0,32},{4,36},{8,40},{12,44},{16,48},{20,52},{24,56},{28,60},{32,6... | collective-permute-start | bytes 1769480 | tf_op jit(solution)/shard_map/ppermute | solution.py:1147
  466.0 31.0 %collective-permute-start.31 = (bf16[4,64,1152]{2,1,0:T(8,128)(2,1)}, bf16[4,64,1152]{2,1,0:T(8,128)(2,1)}, u32[]{:S(2)}, u32[]{:S(2)}) collective-permute-start(bf16[4,64,1152]{2,1,0:T(8,128)(2,1)} %get-tuple-element.178), channel_id=1, source_target_pairs={{0,64},{4,68},{8,72},{12,76},{16,80},{20,84},{24,88},{28,92},{32,9... | collective-permute-start | bytes 1769480 | tf_op jit(solution)/shard_map/ppermute | solution.py:1147
  476.1 20.9 %collective-permute-start.32 = (bf16[4,64,1152]{2,1,0:T(8,128)(2,1)}, bf16[4,64,1152]{2,1,0:T(8,128)(2,1)}, u32[]{:S(2)}, u32[]{:S(2)}) collective-permute-start(bf16[4,64,1152]{2,1,0:T(8,128)(2,1)} %get-tuple-element.179), channel_id=1, source_target_pairs={{0,96},{4,100},{8,104},{12,108},{16,112},{20,116},{24,120},{28,124... | collective-permute-start | bytes 1769480 | tf_op jit(solution)/shard_map/ppermute | solution.py:1147
  480.1 9.3 %collective-permute-start.26 = (bf16[256,512]{1,0:T(8,128)(2,1)S(1)}, bf16[256,512]{1,0:T(8,128)(2,1)S(1)}, u32[]{:S(2)}, u32[]{:S(2)}) collective-permute-start(bf16[256,512]{1,0:T(8,128)(2,1)S(1)} %add_convert_fusion.a0_ref), channel_id=1, source_target_pairs={{0,3},{1,0},{2,1},{3,2},{4,7},{5,4},{6,5},{7,6},{8,11},{9,8},{10,9... | collective-permute-start | bytes 786440 | tf_op jit(solution)/shard_map/ppermute | solution.py:816
  480.1 13.0 %collective-permute-start.27 = (bf16[256,512]{1,0:T(8,128)(2,1)S(1)}, bf16[256,512]{1,0:T(8,128)(2,1)S(1)}, u32[]{:S(2)}, u32[]{:S(2)}) collective-permute-start(bf16[256,512]{1,0:T(8,128)(2,1)S(1)} %add_convert_fusion.a0_ref), channel_id=1, source_target_pairs={{0,2},{1,3},{2,0},{3,1},{4,6},{5,7},{6,4},{7,5},{8,10},{9,11},{10,... | collective-permute-start | bytes 786440 | tf_op jit(solution)/shard_map/ppermute | solution.py:816
  489.4 7.6 %collective-permute-start.28 = (bf16[256,512]{1,0:T(8,128)(2,1)S(1)}, bf16[256,512]{1,0:T(8,128)(2,1)S(1)}, u32[]{:S(2)}, u32[]{:S(2)}) collective-permute-start(bf16[256,512]{1,0:T(8,128)(2,1)S(1)} %add_convert_fusion.a0_ref), channel_id=1, source_target_pairs={{0,1},{1,2},{2,3},{3,0},{4,5},{5,6},{6,7},{7,4},{8,9},{9,10},{10,1... | collective-permute-start | bytes 786440 | tf_op jit(solution)/shard_map/ppermute | solution.py:816
  497.8 17.6 %copy-start.10 = (bf16[256,512]{1,0:T(8,128)(2,1)S(1)}, bf16[256,512]{1,0:T(8,128)(2,1)}, u32[]{:S(2)}) copy-start(bf16[256,512]{1,0:T(8,128)(2,1)} %routed.1.a0_ref) | copy-start | bytes 786436
  500.5 21.7 %collective-permute-start.33 = (bf16[64,1152]{1,0:T(8,128)(2,1)}, bf16[64,1152]{1,0:T(8,128)(2,1)S(1)}, u32[]{:S(2)}, u32[]{:S(2)}) collective-permute-start(bf16[64,1152]{1,0:T(8,128)(2,1)} %get-tuple-element.188), channel_id=1, source_target_pairs={{0,8},{4,12},{8,16},{12,20},{16,24},{20,28},{24,0},{28,4},{32,40},... | collective-permute-start | bytes 442376 | tf_op jit(solution)/shard_map/ppermute | solution.py:1147
  502.2 20.0 %collective-permute-start.34 = (bf16[64,1152]{1,0:T(8,128)(2,1)}, bf16[64,1152]{1,0:T(8,128)(2,1)S(1)}, u32[]{:S(2)}, u32[]{:S(2)}) collective-permute-start(bf16[64,1152]{1,0:T(8,128)(2,1)} %get-tuple-element.189), channel_id=1, source_target_pairs={{0,16},{4,20},{8,24},{12,28},{16,0},{20,4},{24,8},{28,12},{32,48},... | collective-permute-start | bytes 442376 | tf_op jit(solution)/shard_map/ppermute | solution.py:1147
  504.9 18.2 %collective-permute-start.35 = (bf16[64,1152]{1,0:T(8,128)(2,1)}, bf16[64,1152]{1,0:T(8,128)(2,1)S(1)}, u32[]{:S(2)}, u32[]{:S(2)}) collective-permute-start(bf16[64,1152]{1,0:T(8,128)(2,1)} %get-tuple-element.190), channel_id=1, source_target_pairs={{0,24},{4,28},{8,0},{12,4},{16,8},{20,12},{24,16},{28,20},{32,56},... | collective-permute-start | bytes 442376 | tf_op jit(solution)/shard_map/ppermute | solution.py:1147
  510.4 15.9 %collective-permute-start.36 = (bf16[64,1152]{1,0:T(8,128)(2,1)}, bf16[64,1152]{1,0:T(8,128)(2,1)S(1)}, u32[]{:S(2)}, u32[]{:S(2)}) collective-permute-start(bf16[64,1152]{1,0:T(8,128)(2,1)} %get-tuple-element.191), channel_id=1, source_target_pairs={{0,32},{4,36},{8,40},{12,44},{16,48},{20,52},{24,56},{28,60},{32,6... | collective-permute-start | bytes 442376 | tf_op jit(solution)/shard_map/ppermute | solution.py:1147
  515.4 24.0 %collective-permute-start.39 = (bf16[256,512]{1,0:T(8,128)(2,1)S(1)}, bf16[256,512]{1,0:T(8,128)(2,1)S(1)}, u32[]{:S(2)}, u32[]{:S(2)}) collective-permute-start(bf16[256,512]{1,0:T(8,128)(2,1)S(1)} %copy-done.10), channel_id=1, source_target_pairs={{0,3},{1,0},{2,1},{3,2},{4,7},{5,4},{6,5},{7,6},{8,11},{9,8},{10,9... | collective-permute-start | bytes 786440 | tf_op jit(solution)/shard_map/ppermute | solution.py:816
  522.2 20.3 %collective-permute-start.40 = (bf16[256,512]{1,0:T(8,128)(2,1)S(1)}, bf16[256,512]{1,0:T(8,128)(2,1)S(1)}, u32[]{:S(2)}, u32[]{:S(2)}) collective-permute-start(bf16[256,512]{1,0:T(8,128)(2,1)S(1)} %copy-done.10), channel_id=1, source_target_pairs={{0,2},{1,3},{2,0},{3,1},{4,6},{5,7},{6,4},{7,5},{8,10},{9,11},{10,... | collective-permute-start | bytes 786440 | tf_op jit(solution)/shard_map/ppermute | solution.py:816
  522.2 20.2 %collective-permute-start.41 = (bf16[256,512]{1,0:T(8,128)(2,1)S(1)}, bf16[256,512]{1,0:T(8,128)(2,1)S(1)}, u32[]{:S(2)}, u32[]{:S(2)}) collective-permute-start(bf16[256,512]{1,0:T(8,128)(2,1)S(1)} %copy-done.10), channel_id=1, source_target_pairs={{0,1},{1,2},{2,3},{3,0},{4,5},{5,6},{6,7},{7,4},{8,9},{9,10},{10,1... | collective-permute-start | bytes 786440 | tf_op jit(solution)/shard_map/ppermute | solution.py:816
  523.1 6.7 %collective-permute-start.37 = (bf16[64,1152]{1,0:T(8,128)(2,1)S(1)}, bf16[64,1152]{1,0:T(8,128)(2,1)S(1)}, u32[]{:S(2)}, u32[]{:S(2)}) collective-permute-start(bf16[64,1152]{1,0:T(8,128)(2,1)S(1)} %copy-done.42), channel_id=1, source_target_pairs={{0,64},{4,68},{8,72},{12,76},{16,80},{20,84},{24,88},{28,92},{32,9... | collective-permute-start | bytes 442376 | tf_op jit(solution)/shard_map/ppermute | solution.py:1147
  526.3 5.2 collective-permute-start.38
  535.4 11.8 %collective-permute-start.42 = (bf16[64,640]{1,0:T(8,128)(2,1)S(1)}, bf16[64,640]{1,0:T(8,128)(2,1)S(1)}, u32[]{:S(2)}, u32[]{:S(2)}) collective-permute-start(bf16[64,640]{1,0:T(8,128)(2,1)S(1)} %convert_element_type.87), channel_id=1, source_target_pairs={{0,1},{1,2},{2,3},{3,0},{4,5},{5,6},{6,7},{7,4},{8,9},{9,10},{10,1... | collective-permute-start | bytes 245768 | tf_op jit(solution)/shard_map/ppermute | solution.py:816
  538.1 9.1 %collective-permute-start.43 = (bf16[64,640]{1,0:T(8,128)(2,1)S(1)}, bf16[64,640]{1,0:T(8,128)(2,1)S(1)}, u32[]{:S(2)}, u32[]{:S(2)}) collective-permute-start(bf16[64,640]{1,0:T(8,128)(2,1)S(1)} %convert_element_type.87), channel_id=1, source_target_pairs={{0,2},{1,3},{2,0},{3,1},{4,6},{5,7},{6,4},{7,5},{8,10},{9,11},{10,... | collective-permute-start | bytes 245768 | tf_op jit(solution)/shard_map/ppermute | solution.py:816
  539.4 7.8 %collective-permute-start.44 = (bf16[64,640]{1,0:T(8,128)(2,1)S(1)}, bf16[64,640]{1,0:T(8,128)(2,1)S(1)}, u32[]{:S(2)}, u32[]{:S(2)}) collective-permute-start(bf16[64,640]{1,0:T(8,128)(2,1)S(1)} %convert_element_type.87), channel_id=1, source_target_pairs={{0,3},{1,0},{2,1},{3,2},{4,7},{5,4},{6,5},{7,6},{8,11},{9,8},{10,9... | collective-permute-start | bytes 245768 | tf_op jit(solution)/shard_map/ppermute | solution.py:816
  (34 other events, 204.3 us)
Sparse Core Ops, SparseCore 0:
  10.8 76.0 all-gather.2
  89.2 53.7 all-gather.4
  239.1 50.0 reduce-scatter.3
  291.6 60.6 reduce-scatter.5
  377.0 93.5 reduce-scatter.7
